TPU v7x, 32 devices: a whole 2x2x4 slice. The times are simulated.
32 devices in a mesh: lat: 8 (over y, x, core), lon: 4 (over z).
Axes of the slice: x: 2, y: 2, z: 4, core: 2. Of those that a mesh axis runs over, the one named last changes fastest.
Arguments:
- state: float32 [3, 384, 49152], P(None, 'lat', 'lon'), may hold values from -6 to 6
- sigma: float32 [3, 384, 768], P(None, 'lat', 'lon'), may hold values from 0.3 to 3
- vert: float32 [3, 64, 64], replicated, may hold values from -0.75 to 0.75
- bal_temp: float32 [64, 64], replicated, may hold values from -0.75 to 0.75
- chi_coef: float32 [64], replicated, may hold values from -1 to 1
- scales: float32 [8], replicated, may hold values from 6 to 40
- classes: int32 [192], replicated, may hold values from 0 to 7
- owner: int32 [192], replicated, may hold values from 0 to 31, as said below
Outputs:
- applied: float32 [3, 384, 49152], P(None, 'lat', 'lon')
- slab_energy: float32 [32, 7], P(('lat', 'lon'))
Inputs may be any that keep to these rules, and one draw needn't show every extreme that they name: `owner`: every device owns at most 7 slabs, and some device owns exactly 7.
All inputs are finite; a program needn't handle non-finite values.
Results may differ from a plain program's by a relative error of at most 0.0003.
Values sent between devices are 32-bit elements; how exact they have to be, the bound alone decides.
No kernel may reach another device: no remote copies, remote signals or barrier semaphores. Data moves between devices by JAX's collectives and lax.ppermute only.
A program may use at most 128 MiB of HBM per device.

v0:
```python
import jax
import jax.numpy as jnp
from jax import lax
from jax.sharding import PartitionSpec as P

highest = lax.Precision.HIGHEST


def with_halo(x, sides, width):
    for axis, dim in sides:
        devices, length = (lax.axis_size(axis), x.shape[dim])
        up = [(i, (i + 1) % devices) for i in range(devices - 1)]
        down = [(j, i) for i, j in up]
        last = lax.slice_in_dim(x, length - width, length, axis=dim)
        leading = lax.slice_in_dim(x, 0, width, axis=dim)
        before = lax.ppermute(last, axis, up)
        after = lax.ppermute(leading, axis, down)
        x = jnp.concatenate([before, x, after], axis=dim)
    return x


def laplace_tile(field):
    padded = with_halo(field, (("lat", 1), ("lon", 2)), 1)
    return (
        4.0 * field
        - padded[:, 2:, 1:-1]
        - padded[:, :-2, 1:-1]
        - padded[:, 1:-1, 2:]
        - padded[:, 1:-1, :-2]
    )


def filter_tables(length):
    idx = jnp.arange(128, dtype=jnp.float32)
    gap = idx[:, None] - idx[None, :]
    decay = jnp.exp(-1.0 / length)
    powers = jnp.exp(-jnp.maximum(gap, 0.0)[None] / length[:, None, None])
    lower = jnp.where(gap[None] >= 0.0, (1.0 - decay)[:, None, None] * powers, 0.0)
    ramp = jnp.exp(-(idx[None, :] + 1.0) / length[:, None])
    span = jnp.exp(-128.0 / length)
    return (lower, ramp, span)


def recursion(field, tables, along_lat, backward):
    lower, ramp, span = tables
    edge_pos = 0 if backward else 127
    if along_lat:
        form = "ckbj,cbd->ckdj" if backward else "ckbj,cdb->ckdj"
        local = jnp.einsum(form, field, lower, precision=highest)
        edges = local[:, :, edge_pos, :]
        blocks = local.shape[1]
    else:
        form = "cjkb,cbd->cjkd" if backward else "cjkb,cdb->cjkd"
        local = jnp.einsum(form, field, lower, precision=highest)
        edges = local[:, :, :, edge_pos]
        blocks = local.shape[2]
    order = list(range(blocks))
    if backward:
        order = order[::-1]
    state = jnp.zeros_like(edges[:, 0, :] if along_lat else edges[:, :, 0])
    carries = [state] * blocks
    for block in order:
        carries[block] = state
        edge = edges[:, block, :] if along_lat else edges[:, :, block]
        state = edge + span[:, None] * state
    weights = ramp[:, ::-1] if backward else ramp
    if along_lat:
        carry = jnp.stack(carries, axis=1)
        return local + carry[:, :, None, :] * weights[:, None, :, None]
    carry = jnp.stack(carries, axis=2)
    return local + carry[:, :, :, None] * weights[:, None, None, :]


def smooth(slabs, tables, amp):
    count, rows, cols = slabs.shape
    field = slabs.reshape(count, rows, cols // 128, 128)
    field = recursion(field, tables, False, False)
    field = recursion(field, tables, False, True)
    field = field.reshape(count, rows // 128, 128, cols)
    field = recursion(field, tables, True, False)
    field = recursion(field, tables, True, True)
    return field.reshape(count, rows, cols) * amp[:, None, None]


def shards(state, sigma, vert, bal_temp, chi_coef, scales, classes, owner):
    n_lat = lax.axis_size("lat")
    n_lon = lax.axis_size("lon")
    devices = n_lat * n_lon
    nvars = state.shape[0]
    levels = vert.shape[1]
    tile_lat = state.shape[1]
    tile_lon = state.shape[2] // levels
    tile_cells = tile_lat * tile_lon
    count = nvars * levels
    capacity = (count + devices - 1) // devices + 1
    index = jnp.arange(count, dtype=jnp.int32)
    same = (owner[:, None] == owner[None, :]) & (index[None, :] < index[:, None])
    slot = jnp.sum(same.astype(jnp.int32), axis=1)
    target = owner * capacity + slot
    source_of = jnp.full((devices * capacity,), count, jnp.int32).at[target].set(index)
    field = state.reshape(nvars, tile_lat, tile_lon, levels).transpose(0, 3, 1, 2)
    folded = jnp.einsum("lk,lij->kij", bal_temp, field[2], precision=highest)
    adj_psi = field[0] + chi_coef[:, None, None] * field[1] + laplace_tile(folded)
    scaled = jnp.stack([adj_psi, field[1], field[2]]) * sigma[:, None]
    w = jnp.einsum("vkl,vkij->vlij", vert, scaled, precision=highest)
    rows_ext = jnp.concatenate(
        [w.reshape(count, tile_cells), jnp.zeros((1, tile_cells), jnp.float32)], axis=0
    )
    outgoing = jnp.take(rows_ext, source_of, axis=0)
    arrived = lax.all_to_all(
        outgoing.reshape(devices, capacity, tile_cells),
        ("lat", "lon"),
        split_axis=0,
        concat_axis=0,
        tiled=True,
    )
    whole = arrived.reshape(n_lat, n_lon, capacity, tile_lat, tile_lon)
    whole = whole.transpose(2, 0, 3, 1, 4).reshape(capacity, n_lat * tile_lat, n_lon * tile_lon)
    rank = lax.axis_index("lat") * n_lon + lax.axis_index("lon")
    mine = lax.dynamic_slice_in_dim(source_of, rank * capacity, capacity)
    picks = (mine[:, None] == index[None, :]).astype(jnp.int32)
    my_class = jnp.sum(picks * classes[None, :], axis=1)
    class_ids = jnp.arange(scales.shape[0], dtype=jnp.int32)
    length = jnp.sum(
        jnp.where(my_class[:, None] == class_ids[None, :], scales[None, :], 0.0), axis=1
    )
    tables = filter_tables(length)
    amp = length**0.75
    ctrl = smooth(whole, tables, amp)
    slab_energy = jnp.mean(ctrl * ctrl, axis=(1, 2))[None, :]
    back = smooth(ctrl, tables, amp)
    pieces = back.reshape(capacity, n_lat, tile_lat, n_lon, tile_lon).transpose(1, 3, 0, 2, 4)
    pieces = pieces.reshape(n_lat, n_lon, capacity, tile_cells)
    returned = lax.all_to_all(
        pieces.reshape(devices, capacity, tile_cells),
        ("lat", "lon"),
        split_axis=0,
        concat_axis=0,
        tiled=True,
    )
    tiles = jnp.take(returned.reshape(devices * capacity, tile_cells), target, axis=0)
    tiles = tiles.reshape(nvars, levels, tile_lat, tile_lon)
    z = jnp.einsum("vlk,vkij->vlij", vert, tiles, precision=highest) * sigma[:, None]
    out_chi = z[1] + chi_coef[:, None, None] * z[0]
    out_temp = z[2] + jnp.einsum("lk,kij->lij", bal_temp, laplace_tile(z[0]), precision=highest)
    mixed = jnp.stack([z[0], out_chi, out_temp])
    applied = mixed.transpose(0, 2, 3, 1).reshape(nvars, tile_lat, tile_lon * levels)
    return (applied, slab_energy)


def solution(mesh):
    return jax.shard_map(
        shards,
        mesh=mesh,
        in_specs=(P(None, "lat", "lon"), P(None, "lat", "lon"), P(), P(), P(), P(), P(), P()),
        out_specs=(P(None, "lat", "lon"), P(("lat", "lon"), None)),
        check_vma=False,
    )
```

profile of v0, /device:TPU:0, one launch (start us, length us, event | category | flops | bytes accessed | tf_op | source)
XLA Modules:
  0.0 924.4 jit_solution(13706247468264301291)
XLA Ops:
  0.6 12.4 %reshape.577 = f32[3,48,192,64]{3,2,1,0:T(8,128)} reshape(f32[3,48,12288]{2,1,0:T(8,128)} %param.8) | data formatting | bytes 14155776 | tf_op jit(solution)/shard_map/reshape | solution.py:101
  13.0 12.9 %copy.231 = f32[3,48,192,64]{2,3,1,0:T(8,128)} copy(f32[3,48,192,64]{3,2,1,0:T(8,128)} %reshape.577) | data formatting | bytes 14155776 | tf_op jit(solution)/shard_map/reshape | solution.py:101
  25.9 4.7 fusion.69
  30.6 2.4 collective-permute-start.1
  36.2 2.0 collective-permute-done
  38.4 2.3 fusion.151
  40.7 2.0 copy.233
  42.7 2.0 copy.235
  44.7 3.6 collective-permute-start.3
  49.9 6.3 slice.259
  58.1 1.8 copy.236
  59.9 5.9 fusion.65
  65.8 12.6 %fusion.35 = f32[3,64,48,192]{3,1,2,0:T(8,128)S(1)} fusion(f32[2,64,48,192]{3,1,2,0:T(8,128)} %slice.259, f32[1,64,48,192]{3,1,2,0:T(8,128)S(1)} %fusion.65, f32[3,48,192]{2,1,0:T(8,128)S(1)} %copy-done.4, f32[3,64,64]{2,1,0:T(8,128)S(1)} %copy-done), kind=kOutput, calls=%fused_computation.50 | convolution fusion | flops 1362493440 | bytes 14315520 | tf_op jit(solution)/shard_map/vkl,vkij->vlij/dot_general | solution.py:105
  78.4 9.1 copy.238
  87.5 9.6 %reshape.578 = f32[192,9216]{1,0:T(8,128)} reshape(f32[3,64,48,192]{3,2,1,0:T(8,128)} %copy.238) | data formatting | bytes 14155776 | tf_op jit(solution)/shard_map/reshape | solution.py:107
  97.1 6.8 concatenate.40
  103.9 12.8 %gather_fusion = f32[224,9216]{1,0:T(8,128)} fusion(f32[193,9216]{1,0:T(8,128)} %concatenate.40, s32[1024]{0:T(1024)S(1)} %pad_clamp_fusion.1), kind=kCustom, calls=%fused_computation | custom fusion | bytes 16515968 | tf_op jit(solution)/shard_map/jit(_take)/gather | solution.py:109
  116.7 7.5 gather.13
  124.2 9.1 broadcast_select_fusion
  133.2 9.2 all-to-all-start
  143.1 203.1 %all-to-all-done = f32[32,7,9216]{2,1,0:T(8,128)} async-done(((f32[32,7,9216]{2,1,0:T(8,128)}), f32[32,7,9216]{2,1,0:T(8,128)}, u32[]{:S(2)}, u32[]{:S(2)}) %all-to-all-start) | async-done | bytes 8257568 | tf_op jit(solution)/shard_map/all_to_all | solution.py:110
  346.3 11.7 %copy.239 = f32[32,7,9216]{2,0,1:T(8,128)} copy(f32[32,7,9216]{2,1,0:T(8,128)} %all-to-all-done) | data formatting | bytes 16515072 | tf_op jit(solution)/shard_map/all_to_all | solution.py:110
  358.0 11.7 %reshape.579 = f32[8,4,7,48,192]{4,3,1,0,2:T(8,128)} reshape(f32[32,7,9216]{2,0,1:T(8,128)} %copy.239) | data formatting | bytes 16515072 | tf_op jit(solution)/shard_map/reshape | solution.py:117
  369.7 14.9 %copy.240 = f32[7,8,48,4,192]{4,3,2,1,0:T(4,128)} copy(f32[7,8,48,4,192]{4,2,3,1,0:T(8,128)} %bitcast.131) | data formatting | bytes 16515072 | tf_op jit(solution)/shard_map/transpose | solution.py:118
  384.6 14.3 %reshape_reshape.6 = f32[7,384,6,128]{3,2,1,0:T(8,128)} reshape(f32[7,8,48,4,192]{4,3,2,1,0:T(4,128)} %copy.240) | data formatting | bytes 16515072 | tf_op jit(solution)/shard_map/reshape;reshape | solution.py:76
  398.9 15.3 %fusion.10 = f32[7,384,6,128]{1,3,2,0:T(8,128)S(1)} fusion(f32[7,384,6,128]{3,2,1,0:T(8,128)} %reshape_reshape.6, f32[7]{0:T(128)S(1)} %select_reduce_fusion.1, f32[128,128]{0,1:T(8,128)S(1)} %maximum_negate_fusion, f32[7]{0:T(128)S(1)} %get-tuple-element.36, pred[128,128]{0,1:T(8,128)(4,1)S(1)} %fusion.132), kind=kOutput, calls=%fused_computation.18 | convolution fusion | flops 3171237888 | bytes 16597048 | tf_op jit(solution)/shard_map/cjkb,cdb->cjkd/dot_general | solution.py:54
  414.7 9.3 %fusion.21 = f32[7,384,6,128]{1,3,2,0:T(8,128)S(1)} fusion(f32[7,384,6,128]{1,3,2,0:T(8,128)S(1)} %fusion.10, f32[7,128]{1,0:T(8,128)S(1)} %divide_exponential_fusion.1, f32[7,384,6]{1,2,0:T(8,128)S(1)} %copy.244, f32[7]{0:T(128)S(1)} %select_reduce_fusion.1, f32[128,128]{0,1:T(8,128)S(1)} %maximum_negate_fusion, f32[7]{0:T(128)S(1)} %get-tuple-element.36, ...), kind=kOutput, calls=%fused_computation.34 | convolution fusion | flops 3175366656 | bytes 16665144 | tf_op jit(solution)/shard_map/cjkb,cbd->cjkd/dot_general | solution.py:54
  424.4 4.3 multiply_add_fusion.3
  428.8 13.0 %reshape.622 = f32[7,3,128,768]{2,1,3,0:T(4,128)} reshape(f32[7,384,6,128]{1,3,2,0:T(8,128)} %multiply_add_fusion.3) | data formatting | bytes 16515072 | tf_op jit(solution)/shard_map/reshape | solution.py:79
  441.8 15.0 %fusion.42 = f32[7,3,128,768]{3,2,1,0:T(8,128)S(1)} fusion(f32[7,3,128,768]{2,1,3,0:T(4,128)} %reshape.622, f32[7]{0:T(128)S(1)} %select_reduce_fusion.1, f32[128,128]{0,1:T(8,128)S(1)} %maximum_negate_fusion, f32[7]{0:T(128)S(1)} %get-tuple-element.36, pred[128,128]{0,1:T(8,128)(4,1)S(1)} %fusion.132), kind=kOutput, calls=%fused_computation.55 | convolution fusion | flops 3171237888 | bytes 16597048 | tf_op jit(solution)/shard_map/ckbj,cdb->ckdj/dot_general | solution.py:49
  457.0 8.1 fusion.36
  465.3 4.6 multiply_reduce_fusion
  469.9 10.7 %reshape.581 = f32[7,384,6,128]{3,2,1,0:T(8,128)} reshape(f32[7,3,128,768]{3,2,1,0:T(8,128)} %get-tuple-element.3) | data formatting | bytes 16515072 | tf_op jit(solution)/shard_map/reshape | solution.py:82
  480.6 5.0 broadcast_multiply_fusion
  485.6 10.3 %fusion.8 = f32[7,384,6,128]{1,3,2,0:T(8,128)} fusion(f32[7,384,6,128]{3,2,1,0:T(8,128)S(1)} %broadcast_multiply_fusion, f32[7]{0:T(128)S(1)} %select_reduce_fusion.1, f32[128,128]{0,1:T(8,128)S(1)} %maximum_negate_fusion, f32[7]{0:T(128)S(1)} %get-tuple-element.36, pred[128,128]{0,1:T(8,128)(4,1)S(1)} %fusion.132), kind=kOutput, calls=%fused_computation.16 | convolution fusion | flops 3171237888 | bytes 16597048 | tf_op jit(solution)/shard_map/cjkb,cdb->cjkd/dot_general | solution.py:54
  497.4 10.8 %fusion.15 = f32[7,384,6,128]{1,3,2,0:T(8,128)S(1)} fusion(f32[7,384,6,128]{1,3,2,0:T(8,128)} %fusion.8, f32[7,384,6]{1,2,0:T(8,128)S(1)} %copy.257, f32[7,128]{1,0:T(8,128)S(1)} %divide_exponential_fusion.1, f32[7]{0:T(128)S(1)} %select_reduce_fusion.1, f32[128,128]{0,1:T(8,128)S(1)} %maximum_negate_fusion, f32[7]{0:T(128)S(1)} %get-tuple-element.36, ...), kind=kOutput, calls=%fused_computation.26 | convolution fusion | flops 3175366656 | bytes 16665144 | tf_op jit(solution)/shard_map/cjkb,cbd->cjkd/dot_general | solution.py:54
  508.6 4.3 multiply_add_fusion.1
  512.9 13.0 %reshape.623 = f32[7,3,128,768]{2,1,3,0:T(4,128)} reshape(f32[7,384,6,128]{1,3,2,0:T(8,128)} %multiply_add_fusion.1) | data formatting | bytes 16515072 | tf_op jit(solution)/shard_map/reshape | solution.py:79
  525.9 15.2 %fusion.45 = f32[7,3,128,768]{3,2,1,0:T(8,128)S(1)} fusion(f32[7,3,128,768]{2,1,3,0:T(4,128)} %reshape.623, f32[7]{0:T(128)S(1)} %select_reduce_fusion.1, f32[128,128]{0,1:T(8,128)S(1)} %maximum_negate_fusion, f32[7]{0:T(128)S(1)} %get-tuple-element.36, pred[128,128]{0,1:T(8,128)(4,1)S(1)} %fusion.132), kind=kOutput, calls=%fused_computation.56 | convolution fusion | flops 3171237888 | bytes 16597048 | tf_op jit(solution)/shard_map/ckbj,cdb->ckdj/dot_general | solution.py:49
  541.4 8.1 fusion.39
  549.7 4.3 multiply_add_fusion
  553.9 13.2 %reshape.583 = f32[7,8,48,4,192]{4,3,2,1,0:T(4,128)} reshape(f32[7,3,128,768]{3,2,1,0:T(8,128)} %multiply_add_fusion) | data formatting | bytes 16515072 | tf_op jit(solution)/shard_map/reshape | solution.py:82
  567.2 7.1 multiply_bitcast_fusion
  574.3 6.1 copy.298
  580.5 12.0 %reshape.624 = f32[32,7,9216]{2,1,0:T(8,128)} reshape(f32[8,4,7,48,192]{4,3,2,1,0:T(8,128)} %copy.298) | data formatting | bytes 16515072 | tf_op jit(solution)/shard_map/reshape;reshape | solution.py:135
  592.5 9.2 all-to-all-start.1
  601.8 203.7 %all-to-all-done.1 = f32[32,7,9216]{2,1,0:T(8,128)} async-done(((f32[32,7,9216]{2,1,0:T(8,128)}), f32[32,7,9216]{2,1,0:T(8,128)}, u32[]{:S(2)}, u32[]{:S(2)}) %all-to-all-start.1) | async-done | bytes 8257568 | tf_op jit(solution)/shard_map/all_to_all | solution.py:134
  805.5 7.4 reshape.584
  813.0 11.9 %gather_fusion.1 = f32[192,9216]{1,0:T(8,128)} fusion(f32[224,9216]{1,0:T(8,128)} %reshape.584, s32[1024]{0:T(1024)S(1)} %pad_clamp_fusion), kind=kCustom, calls=%fused_computation.1 | custom fusion | bytes 14156544 | tf_op jit(solution)/shard_map/jit(_take)/gather | solution.py:141
  824.9 9.7 %gather.15 = f32[3,64,48,192]{3,2,1,0:T(8,128)} reshape(f32[192,9216]{1,0:T(8,128)} %gather_fusion.1) | data formatting | bytes 14155776 | tf_op jit(solution)/shard_map/jit(_take)/gather | solution.py:141
  834.6 15.5 %multiply_bitcast_fusion.1 = f32[3,64,48,192]{3,1,2,0:T(8,128)S(1)} fusion(f32[3,48,192]{2,1,0:T(8,128)S(1)} %copy-done.5, f32[3,64,48,192]{3,2,1,0:T(8,128)} %gather.15, pred[3,64]{1,0:T(4,128)(4,1)S(1)} %broadcast_in_dim.51, f32[3,64,64]{2,1,0:T(8,128)S(1)} %copy-done), kind=kOutput, calls=%fused_computation.11 | convolution fusion | flops 1362493440 | bytes 14315712 | tf_op jit(solution)/shard_map/vlk,vkij->vlij/dot_general | solution.py:143
  850.1 4.2 fusion.149
  857.0 1.8 collective-permute-done.4
  859.2 2.3 fusion.150
  861.5 2.0 copy.270
  863.5 2.0 copy.272
  865.5 10.5 %collective-permute-start.7 = (f32[64,50,1]{0,2,1:T(1,128)S(1)}, f32[64,50,1]{0,2,1:T(1,128)S(1)}, u32[]{:S(2)}, u32[]{:S(2)}) collective-permute-start(f32[64,50,1]{0,2,1:T(1,128)S(1)} %copy.272), channel_id=1, source_target_pairs={{0,1},{1,2},{2,3},{4,5},{5,6},{6,7},{8,9},{9,10},{10,11},{12,13},{... | collective-permute-start | bytes 38408 | tf_op jit(solution)/shard_map/ppermute | solution.py:16
  877.8 3.9 collective-permute-done.6
  881.7 1.7 copy.271
  883.4 1.7 copy.273
  885.2 9.5 %fusion.62 = f32[1,64,48,192]{3,1,2,0:T(8,128)S(1)} fusion(f32[3,64,48,192]{3,1,2,0:T(8,128)} %copy-done.1, f32[64,50,1]{2,0,1:T(8,128)} %copy.273, f32[64,1,192]{2,0,1:T(8,128)S(1)} %collective-permute-done.4, f32[64,48,192]{2,0,1:T(8,128)S(1)} %get-tuple-element.25, f32[64,1,192]{2,0,1:T(8,128)S(1)} %collective-permute-done.5, f32[64,50,1]{2,0,1:T(8,128)} %copy.271, ...), kind=kOutput, calls=%fused_computation.76 | convolution fusion | flops 461242368 | bytes 7218176 | tf_op jit(solution)/shard_map/lk,kij->lij/dot_general | solution.py:145
  894.7 4.7 maximum_bitcast_fusion
  899.4 11.9 %copy.274 = f32[3,48,192,64]{3,2,1,0:T(8,128)} copy(f32[3,48,192,64]{2,3,1,0:T(8,128)} %maximum_bitcast_fusion) | data formatting | bytes 14155776 | tf_op jit(solution)/shard_map/transpose | solution.py:147
  911.3 12.8 %reshape.585 = f32[3,48,12288]{2,1,0:T(8,128)} reshape(f32[3,48,192,64]{3,2,1,0:T(8,128)} %copy.274) | data formatting | bytes 14155776 | tf_op jit(solution)/shard_map/reshape | solution.py:147
  (124 shorter events, 16.0 us)
Async XLA Ops:
  0.6 65.2 %copy-start = (f32[3,64,64]{2,1,0:T(8,128)S(1)}, f32[3,64,64]{2,1,0:T(8,128)}, u32[]{:S(2)}) copy-start(f32[3,64,64]{2,1,0:T(8,128)} %param.10) | copy-start | bytes 147460
  13.0 12.9 %copy-start.6 = (f32[64,64]{1,0:T(8,128)S(1)}, f32[64,64]{1,0:T(8,128)}, u32[]{:S(2)}) copy-start(f32[64,64]{1,0:T(8,128)} %param.11) | copy-start | bytes 49156
  13.0 21.2 %copy-start.8 = (s32[192]{0:T(256)S(1)}, s32[192]{0:T(256)}, u32[]{:S(2)}) copy-start(s32[192]{0:T(256)} %param.15) | copy-start | bytes 2308
  30.6 5.6 collective-permute-start.1
  32.9 5.3 collective-permute-start
  35.0 21.3 %copy-start.9 = (s32[192]{0:T(256)}, s32[192]{0:T(256)S(1)}, u32[]{:S(2)}) copy-start(s32[192]{0:T(256)S(1)} %get-tuple-element.5) | copy-start | bytes 2308
  44.7 15.2 %copy-start.11 = (f32[64]{0:T(128)S(1)}, f32[64]{0:T(128)}, u32[]{:S(2)}) copy-start(f32[64]{0:T(128)} %param.12) | copy-start | bytes 772
  44.7 13.4 %collective-permute-start.3 = (f32[64,50,1]{0,2,1:T(1,128)S(1)}, f32[64,50,1]{0,2,1:T(1,128)S(1)}, u32[]{:S(2)}, u32[]{:S(2)}) collective-permute-start(f32[64,50,1]{0,2,1:T(1,128)S(1)} %copy.235), channel_id=1, source_target_pairs={{0,1},{1,2},{2,3},{4,5},{5,6},{6,7},{8,9},{9,10},{10,11},{12,13},{... | collective-permute-start | bytes 38408 | tf_op jit(solution)/shard_map/ppermute | solution.py:16
  48.3 8.1 collective-permute-start.2
  59.9 5.9 copy-start.4
  133.2 9.3 %copy-start.13 = (s32[192]{0:T(256)S(1)}, s32[192]{0:T(256)}, u32[]{:S(2)}) copy-start(s32[192]{0:T(256)} %param.14) | copy-start | bytes 2308
  133.2 9.5 %copy-start.15 = (f32[8]{0:T(128)S(1)}, f32[8]{0:T(128)}, u32[]{:S(2)}) copy-start(f32[8]{0:T(128)} %param.13) | copy-start | bytes 100
  133.2 213.0 %all-to-all-start = ((f32[32,7,9216]{2,1,0:T(8,128)}), f32[32,7,9216]{2,1,0:T(8,128)}, u32[]{:S(2)}, u32[]{:S(2)}) async-start(f32[32,7,9216]{2,1,0:T(8,128)} %broadcast_select_fusion), calls=%async_computation | async-start | bytes 18874368 | tf_op jit(solution)/shard_map/all_to_all | solution.py:110
  592.5 9.2 copy-start.14
  592.5 9.3 %copy-start.10 = (s32[192]{0:T(256)S(1)}, s32[192]{0:T(256)}, u32[]{:S(2)}) copy-start(s32[192]{0:T(256)} %copy-done.9) | copy-start | bytes 2308
  592.5 213.1 %all-to-all-start.1 = ((f32[32,7,9216]{2,1,0:T(8,128)}), f32[32,7,9216]{2,1,0:T(8,128)}, u32[]{:S(2)}, u32[]{:S(2)}) async-start(f32[32,7,9216]{2,1,0:T(8,128)} %reshape.624), calls=%async_computation.1 | async-start | bytes 18874368 | tf_op jit(solution)/shard_map/all_to_all | solution.py:134
  824.9 9.7 %copy-start.5 = (f32[3,48,192]{2,1,0:T(8,128)S(1)}, f32[3,48,192]{2,1,0:T(8,128)}, u32[]{:S(2)}) copy-start(f32[3,48,192]{2,1,0:T(8,128)} %param.9) | copy-start | bytes 331780
  834.6 15.5 %copy-start.12 = (f32[64]{0:T(128)S(1)}, f32[64]{0:T(128)}, u32[]{:S(2)}) copy-start(f32[64]{0:T(128)} %param.12) | copy-start | bytes 772
  850.1 9.1 copy-start.1
  854.3 2.6 collective-permute-start.5
  855.6 29.5 %copy-start.7 = (f32[64,64]{1,0:T(8,128)S(1)}, f32[64,64]{1,0:T(8,128)}, u32[]{:S(2)}) copy-start(f32[64,64]{1,0:T(8,128)} %param.11) | copy-start | bytes 49156
  855.7 3.1 collective-permute-start.4
  865.5 18.0 %collective-permute-start.7 = (f32[64,50,1]{0,2,1:T(1,128)S(1)}, f32[64,50,1]{0,2,1:T(1,128)S(1)}, u32[]{:S(2)}, u32[]{:S(2)}) collective-permute-start(f32[64,50,1]{0,2,1:T(1,128)S(1)} %copy.272), channel_id=1, source_target_pairs={{0,1},{1,2},{2,3},{4,5},{5,6},{6,7},{8,9},{9,10},{10,11},{12,13},{... | collective-permute-start | bytes 38408 | tf_op jit(solution)/shard_map/ppermute | solution.py:16
  876.0 5.7 collective-permute-start.6
  885.2 9.5 %copy-start.2 = (f32[1,64,48,192]{3,1,2,0:T(8,128)S(1)}, f32[1,64,48,192]{3,1,2,0:T(8,128)}, u32[]{:S(2)}) copy-start(f32[1,64,48,192]{3,1,2,0:T(8,128)} %get-tuple-element.24) | copy-start | bytes 7077892
  885.2 9.5 %copy-start.3 = (f32[1,64,48,192]{3,1,2,0:T(8,128)S(1)}, f32[1,64,48,192]{3,1,2,0:T(8,128)}, u32[]{:S(2)}) copy-start(f32[1,64,48,192]{3,1,2,0:T(8,128)} %get-tuple-element.26) | copy-start | bytes 7077892
where the time goes:
time: 934 us; the launch traced here: 924 us
  waiting for transfers between devices  415 us (44%)
  local copies, waits for them, and re-layouts  275 us (29%)
  matrix products  134 us (14%)
  other arithmetic  57.6 us (6%)
  starting transfers between devices  41.6 us (4%)
    all_to_all x1, waiting for transfers between devices, shards(): lax.all_to_all(pieces.reshape(devices, capacity, tile_cells), ('lat', 'lo...  204 us
    all_to_all x1, waiting for transfers between devices, shards(): lax.all_to_all(outgoing.reshape(devices, capacity, tile_cells), ('lat', '...  203 us
    dot_general x8, matrix products, recursion(): local = jnp.einsum(form, field, lower, precision=highest)  92.1 us
    reshape x2, local copies, waits for them, and re-layouts, smooth(): field = field.reshape(count, rows // 128, 128, cols)  26 us
    reshape x2, local copies, waits for them, and re-layouts, shards(): state.reshape(nvars, tile_lat, tile_lon, levels).transpose(0, 3, 1, 2)  25.2 us
    reshape x2, local copies, waits for them, and re-layouts, smooth(): return field.reshape(count, rows, cols) * amp[:, None, None]  23.9 us
    gather x2, local copies, waits for them, and re-layouts, shards(): jnp.take(returned.reshape(devices * capacity, tile_cells), target, axis=0)  21.6 us
    gather x2, local copies, waits for them, and re-layouts, shards(): outgoing = jnp.take(rows_ext, source_of, axis=0)  20.2 us
  transfers between devices with their start and end apart: 10, of which 5 were waited for; matrix products, arithmetic and copies ran while one was open for 1% of the time, Pallas kernels for 0%

commit v1 on v0

v1 whole, which is shorter than its diff:
```python
import functools

import jax
import jax.numpy as jnp
from jax import lax
from jax.experimental import pallas as pl
from jax.experimental.pallas import tpu as pltpu
from jax.sharding import PartitionSpec as P

highest = lax.Precision.HIGHEST
f32 = jnp.float32
bf16 = jnp.bfloat16
LANES = 128
PAIRS = 8
LIMIT = 60 * 1024 * 1024


def params():
    return pltpu.CompilerParams(vmem_limit_bytes=LIMIT)


def full(shape):
    return pl.BlockSpec(shape, lambda g: (0,) * len(shape))


def swap(x):
    return pltpu.roll(x, 64, x.ndim - 1)


def low_lanes(shape):
    return lax.broadcasted_iota(jnp.int32, shape, len(shape) - 1) < 64


def halves(x):
    hi = x.astype(bf16)
    return hi, (x - hi.astype(f32)).astype(bf16)


def dot(x, y):
    return jnp.dot(x, y, preferred_element_type=f32)


def product(x, wh, wl):
    hi, lo = halves(x)
    return dot(hi, wh) + dot(lo, wh) + dot(hi, wl)


def expand(mat, mixed):
    wide = jnp.concatenate([mat, mat], axis=1)
    wide = jnp.concatenate([wide, wide], axis=0)
    src = lax.broadcasted_iota(jnp.int32, (256, 256), 0) // 64
    dst = lax.broadcasted_iota(jnp.int32, (256, 256), 1) // 64
    if mixed:
        src = jnp.where(src == 1, 2, jnp.where(src == 2, 1, src))
    return halves(jnp.where(src == dst, wide, 0.0))


def constants(length, decay, m):
    span = jnp.exp(-float(m) / length)
    d = 1.0 - decay * decay
    k1 = decay * (1.0 - span * span) / d
    k2 = (m * span - decay * decay * (span - span * span * span) / d) / d
    tail = decay * decay * (1.0 + span * span) * (1.0 - span * span) / d
    k3 = decay / (d * d) * (1.0 - (2.0 * m + 1.0) * span * span + tail)
    return span, k1, k2, k3


def responses(length, decay, m):
    j = lax.broadcasted_iota(jnp.int32, (m, LANES), 0).astype(f32)
    up = jnp.exp(-j / length)
    down = jnp.exp(-(m - j) / length)
    span = jnp.exp(-float(m) / length)
    d = 1.0 - decay * decay
    diff = up - span * down
    g3 = decay * diff / d
    g2 = ((m - j) * down - decay * decay * (span * up - span * span * down) / d) / d
    part = decay * decay * (1.0 + span * span) * diff / d
    g1 = decay / (d * d) * ((j + 1.0) * up - (2.0 * m + 1.0 - j) * span * down + part)
    return g1, g2, g3, down


def solve_carries(n, edge, const, me):
    span, k1, k2, k3 = const
    first = edge(0, 0)
    zero = jnp.zeros_like(first)
    e1 = [first] + [edge(t, 0) for t in range(1, n)]
    c1, c2, c3, c4 = ([None] * n for _ in range(4))
    c = zero
    for t in range(n):
        c1[t] = c
        c = e1[t] + span * c
    c = zero
    for t in reversed(range(n)):
        c2[t] = c
        c = edge(t, 1) + k1 * c1[t] + span * c
    c = zero
    for t in range(n):
        c3[t] = c
        c = edge(t, 2) + k2 * c1[t] + k1 * c2[t] + span * c
    c = zero
    for t in reversed(range(n)):
        c4[t] = c
        c = edge(t, 3) + k3 * c1[t] + k2 * c2[t] + k1 * c3[t] + span * c
    out = []
    for cs in (c1, c2, c3, c4):
        mine = cs[0]
        for t in range(1, n):
            mine = jnp.where(me == t, cs[t], mine)
        out.append(mine)
    return out


def cascade(count, load, store, decay, start):
    step = 8
    edges = []
    for stage in range(4):
        back = stage % 2 == 1

        def body(b, states, back=back):
            base = (count // step - 1 - b) * step if back else b * step
            order = range(step - 1, -1, -1) if back else range(step)
            for o in order:
                new = [decay_k * s + x for decay_k, s, x in zip(decay, states, load(base + o))]
                store(base + o, new)
                states = new
            return tuple(states)

        states = lax.fori_loop(0, count // step, body, tuple(start))
        edges.append(list(states))
    return edges


def filter_tile(u_ref, k0, nv, rows, decay):
    count = u_ref.shape[2]
    zero = jnp.zeros((count, LANES), f32)

    def load(i):
        return [u_ref[k, i] for k in range(nv)]

    def store(i, values):
        for k in range(nv):
            u_ref[k, i] = values[k]

    return cascade(rows, load, store, decay, [zero] * nv)


def prepare_mats(mats, wh, wl, mixed):
    for k in range(mats.shape[0]):
        hi, lo = expand(mats[k], mixed[k])
        wh[k] = hi
        wl[k] = lo


def sigma_tile(sig, idx):
    return jnp.take_along_axis(sig, idx, axis=1)


def lat_finish(vs, rows, prm, results, w_ref, u_ref, e_ref):
    for k, res in enumerate(results):
        for p in range(PAIRS):
            part = res[p * rows : (p + 1) * rows]
            w_ref[k, 2 * p] = part[:, :LANES]
            w_ref[k, 2 * p + 1] = part[:, LANES:]
        u_ref[k] = jnp.swapaxes(w_ref[k], 0, 1)
    decay = [prm[v, 1:2, :] for v in vs]
    edges = filter_tile(u_ref, 0, len(vs), rows, decay)
    for e in range(4):
        for k in range(len(vs)):
            e_ref[k, e] = edges[e][k]


def lat_plain(vs, rows, prm, sig, mats, b1lo, b1hi, b2lo, b2hi, w_ref, u_ref, e_ref, xs, wh, wl):
    g = pl.program_id(0)

    @pl.when(g == 0)
    def _():
        prepare_mats(mats, wh, wl, (True, True))

    lane = lax.broadcasted_iota(jnp.int32, (rows, LANES), 1)
    high = (lane >= 64).astype(jnp.int32)
    for p in range(PAIRS):
        at = slice(p * rows, (p + 1) * rows)
        cols = slice(p * LANES, (p + 1) * LANES)
        idx = 2 * (g * PAIRS + p) + high
        for k, sides in enumerate(((b1lo, b1hi), (b2lo, b2hi))):
            for side in range(2):
                s = sigma_tile(sig[vs[k], side], idx)
                xs[k, at, side * LANES : (side + 1) * LANES] = sides[side][0, :, cols] * s
    results = [product(xs[k], wh[k], wl[k]) for k in range(2)]
    lat_finish(vs, rows, prm, results, w_ref, u_ref, e_ref)


def lat_balance(
    rows, pairs, prm, sig, mats, plo, phi, clo, chi, temp, north, south, west, east,
    w_ref, u_ref, e_ref, xs, wh, wl,
):
    g = pl.program_id(0)

    @pl.when(g == 0)
    def _():
        prepare_mats(mats, wh, wl, (True, True))

    lane = lax.broadcasted_iota(jnp.int32, (rows, LANES), 1)
    row_id = lax.broadcasted_iota(jnp.int32, (rows, LANES), 0)
    high = (lane >= 64).astype(jnp.int32)
    chi_row = prm[0, 2:3, :]
    last = 2 * pairs - 1

    def at_tile(m):
        return pl.ds(pl.multiple_of(m * LANES, LANES), LANES)

    def laplace(m):
        x = temp[0, :, at_tile(m)]
        left = jnp.where(m == 0, swap(west[...]), temp[0, :, at_tile(jnp.maximum(m - 1, 0))])
        right = jnp.where(m == last, east[...], temp[0, :, at_tile(jnp.minimum(m + 1, last))])
        beside = swap(x + jnp.where(lane >= 64, left, right))
        above = jnp.where(row_id == 0, north[:, at_tile(m)], pltpu.roll(x, 1, 0))
        below = jnp.where(row_id == rows - 1, south[:, at_tile(m)], pltpu.roll(x, rows - 1, 0))
        return 4.0 * x - beside - above - below

    for p in range(PAIRS):
        at = slice(p * rows, (p + 1) * rows)
        cols = slice(p * LANES, (p + 1) * LANES)
        m = g * PAIRS + p
        for side, (pr, cr) in enumerate(((plo, clo), (phi, chi))):
            s = sigma_tile(sig[0, side], 2 * m + high)
            to = slice(side * LANES, (side + 1) * LANES)
            xs[0, at, to] = (pr[0, :, cols] + chi_row * cr[0, :, cols]) * s
            xs[1, at, to] = laplace(m + side * pairs) * s
    result = product(xs[0], wh[0], wl[0]) + product(xs[1], wh[1], wl[1])
    lat_finish((0,), rows, prm, [result], w_ref, u_ref, e_ref)


def lon_kernel(vs, n_lat, rows, rb, ext, place, prm, u_ref, gathered, *rest):
    if ext:
        o_ref, ox_ref, el_ref, es_ref, carry, resp = rest
    else:
        o_ref, el_ref, es_ref, carry, resp = rest
    nv = len(vs)
    g = pl.program_id(0)
    half = u_ref.shape[2]
    me = place[0]

    @pl.when(g == 0)
    def _():
        for k, v in enumerate(vs):
            length = prm[v, 0:1, :]
            decay = prm[v, 1:2, :]
            const = constants(length, decay, rows)

            def body(b, _, k=k, const=const):
                at = pl.ds(pl.multiple_of(b * 8, 8), 8)
                c = solve_carries(n_lat, lambda t, e: gathered[t, k, e, at, :], const, me)
                for e in range(4):
                    carry[k, e, at, :] = c[e]
                return 0

            lax.fori_loop(0, half // 8, body, 0)
            for e, r in enumerate(responses(length, decay, rows)):
                for s in range(rows // rb):
                    resp[s, k, e] = r[s * rb : (s + 1) * rb]

    def fix(b, _):
        at = pl.ds(pl.multiple_of(b * 8, 8), 8)
        for k in range(nv):
            c = [carry[k, e, at, :] for e in range(4)]
            lines = []
            for i in range(rb):
                y = u_ref[k, i, at, :]
                for e in range(4):
                    y = y + resp[g, k, e, i : i + 1, :] * c[e]
                lines.append(y)
            for q in range(rb // 8):
                block = jnp.stack(lines[q * 8 : (q + 1) * 8], axis=0)
                o_ref[k, at, q * 8 : (q + 1) * 8, :] = jnp.swapaxes(block, 0, 1)
            if ext:
                above = jnp.where(me > 0, c[2] + prm[vs[k], 1:2, :] * lines[0], 0.0)
                zero = jnp.zeros_like(above)
                block = jnp.stack([above, c[3]] + [zero] * 6, axis=0)
                ox_ref[at] = jnp.swapaxes(block, 0, 1)
        return 0

    lax.fori_loop(0, half // 8, fix, 0)

    decay = [prm[v, 1:2, :] for v in vs]

    def load(j):
        out = [o_ref[k, j] for k in range(nv)]
        return out + [ox_ref[j]] if ext else out

    def store(j, values):
        for k in range(nv):
            o_ref[k, j] = values[k]
        if ext:
            ox_ref[j] = values[nv]

    start = [jnp.zeros((rb, LANES), f32)] * nv
    if ext:
        start = start + [jnp.zeros((8, LANES), f32)]
        decay = decay + [decay[0]]
    edges = cascade(half, load, store, decay, start)
    for k in range(nv + ext):
        v = vs[min(k, nv - 1)]
        count = 8 if k == nv else rb
        at = pl.ds(rows, 8) if k == nv else pl.ds(pl.multiple_of(g * rb, 8), rb)
        kk = min(k, nv - 1)
        span, k1, k2, k3 = constants(prm[v, 0:1, :], prm[v, 1:2, :], half)
        low = low_lanes((count, LANES))
        e1, e2, e3, e4 = (edges[e][k] for e in range(4))
        c1 = jnp.where(low, 0.0, swap(e1))
        t1 = e1 + span * c1
        t2 = e2 + k1 * c1
        c2 = jnp.where(low, swap(t2), 0.0)
        t2 = t2 + span * c2
        t3 = e3 + k2 * c1 + k1 * c2
        c3 = jnp.where(low, 0.0, swap(t3))
        t3 = t3 + span * c3
        t4 = e4 + k3 * c1 + k2 * c2 + k1 * c3
        c4 = jnp.where(low, swap(t4), 0.0)
        t4 = t4 + span * c4
        es_ref[kk, 0, at, :] = jnp.where(low, t2, t1)
        es_ref[kk, 1, at, :] = jnp.where(low, t4, t3)
        for e, x in enumerate((e1, e2, e3, e4)):
            el_ref[kk, e, at, :] = x


def end_kernel(
    n_lon, rows, pairs, place, prm, sig, sigx, west, east, mats, balm,
    u0, ux, ua, w0, wa, el0, ela, es0, esa,
    out, energy, carry, resp, cols, zx, xs, wh, wl,
):
    g = pl.program_id(0)
    me = place[1]
    half = 2 * pairs
    wide = 2 * half * 64
    ext = rows + 8
    low8 = low_lanes((8, LANES))

    @pl.when(g == 0)
    def _():
        prepare_mats(mats, wh, wl, (True, True, True))
        hi, lo = expand(balm[0], False)
        wh[3] = hi
        wl[3] = lo
        energy[...] = jnp.zeros_like(energy)
        for v in range(3):
            length = prm[v, 0:1, :]
            decay = prm[v, 1:2, :]
            whole = constants(length, decay, 2 * half)
            span, k1, k2, k3 = constants(length, decay, half)
            sent, own, k = (es0, el0, 0) if v == 0 else (esa, ela, v - 1)
            count = ext if v == 0 else rows

            def body(b, _, v=v, whole=whole, half_c=(span, k1, k2, k3), sent=sent, own=own, k=k):
                span, k1, k2, k3 = half_c
                at = pl.ds(pl.multiple_of(b * 8, 8), 8)
                cache = {}

                def edge(t, e):
                    if (t, e // 2) not in cache:
                        x = sent[t, k, e // 2, at, :]
                        y = swap(x)
                        cache[t, e // 2] = (jnp.where(low8, y, x), jnp.where(low8, x, y))
                    return cache[t, e // 2][e % 2]

                d1, d2, d3, d4 = solve_carries(n_lon, edge, whole, me)
                e1, e2, e3, e4 = (own[k, e, at, :] for e in range(4))
                c1 = jnp.where(low8, d1, swap(e1 + span * d1))
                c2 = jnp.where(low8, swap(e2 + k1 * c1 + span * d2), d2)
                c3 = jnp.where(low8, d3, swap(e3 + k2 * c1 + k1 * c2 + span * d3))
                c4 = jnp.where(low8, swap(e4 + k3 * c1 + k2 * c2 + k1 * c3 + span * d4), d4)
                for e, c in enumerate((c1, c2, c3, c4)):
                    carry[v, e, at, :] = c
                if v == 0:
                    cols[0, at, :] = d3
                    cols[1, at, :] = d4
                return 0

            lax.fori_loop(0, count // 8, body, 0)
            for e, r in enumerate(responses(length, decay, half)):
                resp[v, e] = r
        first = u0[0, 0]
        for e in range(4):
            first = first + resp[0, e, 0:1, :] * carry[0, e, 0:rows, :]
        beside = jnp.where(me > 0, cols[0, 0:rows, :] + prm[0, 1:2, :] * first, 0.0)
        low = low_lanes((rows, LANES))
        lhs = jnp.where(low, beside, cols[1, 0:rows, :])
        lhs = jnp.concatenate([lhs, jnp.zeros_like(lhs)], axis=1)
        res = product(lhs, wh[0], wl[0])
        cols[0, 0:rows, :] = swap(res[:, :LANES] * swap(west[...]))
        cols[1, 0:rows, :] = res[:, LANES:] * swap(east[...])

    lane = lax.broadcasted_iota(jnp.int32, (rows, LANES), 1)
    high = (lane >= 64).astype(jnp.int32)
    chi_row = prm[0, 2:3, :]

    def at_tile(m):
        return pl.ds(pl.multiple_of(m * LANES, LANES), LANES)

    for v in range(3):
        u_ref, w_ref, k = (u0, w0, 0) if v == 0 else (ua, wa, v - 1)
        c = [carry[v, e, 0:rows, :] for e in range(4)]
        total = jnp.zeros((rows, LANES), f32)
        for p in range(2 * PAIRS):
            y = u_ref[k, p]
            jh = g * 2 * PAIRS + p
            for e in range(4):
                y = y + resp[v, e, pl.ds(jh, 1), :] * c[e]
            total = total + y * w_ref[k, p]
            at = slice((p // 2) * rows, (p // 2 + 1) * rows)
            to = slice((p % 2) * LANES, (p % 2 + 1) * LANES)
            xs[v, at, to] = y
        energy[v] += jnp.sum(total.reshape(rows // 8, 8, LANES), axis=0)
    c = [carry[0, e, rows:ext, :] for e in range(4)]
    pieces = []
    for p in range(2 * PAIRS):
        y = ux[p]
        jh = g * 2 * PAIRS + p
        for e in range(4):
            y = y + resp[0, e, pl.ds(jh, 1), :] * c[e]
        pieces.append(y)
    lhs = jnp.concatenate(
        [jnp.concatenate([pieces[2 * p], pieces[2 * p + 1]], axis=1) for p in range(PAIRS)], axis=0
    )
    res = product(lhs, wh[0], wl[0])
    high8 = 1 - low8.astype(jnp.int32)
    for p in range(PAIRS):
        m = g * PAIRS + p
        for side in range(2):
            s = sigma_tile(sigx[side], 2 * m + high8)
            part = res[p * 8 : (p + 1) * 8, side * LANES : (side + 1) * LANES]
            zx[:, at_tile(m + side * pairs)] = part * s
    results = [product(xs[v], wh[v], wl[v]) for v in range(3)]
    for p in range(PAIRS):
        m = g * PAIRS + p
        idx = 2 * m + high
        for side in range(2):
            at = at_tile(m + side * pairs)
            z = [
                results[v][p * rows : (p + 1) * rows, side * LANES : (side + 1) * LANES]
                * sigma_tile(sig[v, side], idx)
                for v in range(3)
            ]
            out[0, :, at] = z[0]
            out[1, :, at] = z[1] + chi_row * z[0]
            out[2, :, at] = z[2]

    @pl.when(g == pl.num_programs(0) - 1)
    def _():
        row_id = lax.broadcasted_iota(jnp.int32, (rows, LANES), 0)
        last = half - 1

        def body(b, _):
            for p in range(PAIRS):
                for side in range(2):
                    m = b * PAIRS + p + side * pairs
                    x = out[0, :, at_tile(m)]
                    left = jnp.where(m == 0, cols[0, 0:rows, :], out[0, :, at_tile(jnp.maximum(m - 1, 0))])
                    right = jnp.where(
                        m == last, cols[1, 0:rows, :], out[0, :, at_tile(jnp.minimum(m + 1, last))]
                    )
                    beside = swap(x + jnp.where(lane >= 64, left, right))
                    above = jnp.where(row_id == 0, zx[0:1, at_tile(m)], pltpu.roll(x, 1, 0))
                    below = jnp.where(row_id == rows - 1, zx[1:2, at_tile(m)], pltpu.roll(x, rows - 1, 0))
                    lap = 4.0 * x - beside - above - below
                    xs[0, p * rows : (p + 1) * rows, side * LANES : (side + 1) * LANES] = lap
            res = product(xs[0], wh[3], wl[3])
            for p in range(PAIRS):
                for side in range(2):
                    at = at_tile(b * PAIRS + p + side * pairs)
                    part = res[p * rows : (p + 1) * rows, side * LANES : (side + 1) * LANES]
                    out[2, :, at] = out[2, :, at] + part
            return 0

        lax.fori_loop(0, pairs // PAIRS, body, 0)


def shards(state, sigma, vert, bal_temp, chi_coef, scales, classes, owner):
    n_lat = lax.axis_size("lat")
    n_lon = lax.axis_size("lon")
    devices = n_lat * n_lon
    nvars, rows, merged = state.shape
    levels = vert.shape[1]
    lon = merged // levels
    half = lon // 2
    pairs = half // 2
    steps = pairs // PAIRS
    count = nvars * levels
    capacity = (count + devices - 1) // devices + 1
    i_lat = lax.axis_index("lat")
    i_lon = lax.axis_index("lon")

    ups, downs = ([(i, i + 1) for i in range(n - 1)] for n in (n_lat, n_lon))
    back_lat = [(j, i) for i, j in ups]
    back_lon = [(j, i) for i, j in downs]

    def row(i):
        return jnp.concatenate([state[2, i : i + 1, :], sigma[0, i : i + 1, :]], axis=1)

    def column(j):
        temp = state[2, :, j * levels : (j + 1) * levels]
        sig = jnp.broadcast_to(sigma[0, :, j : j + 1], (rows, levels))
        return jnp.concatenate([temp, sig], axis=1)

    north = lax.ppermute(row(rows - 1), "lat", ups)
    south = lax.ppermute(row(0), "lat", back_lat)
    west = lax.ppermute(column(lon - 1), "lon", downs)
    east = lax.ppermute(column(0), "lon", back_lon)

    class_ids = jnp.arange(scales.shape[0], dtype=jnp.int32)
    length = jnp.sum(jnp.where(classes[:, None] == class_ids[None, :], scales[None, :], 0.0), axis=1)
    length = length.reshape(nvars, levels)
    decay = jnp.exp(-1.0 / length)
    norm = 1.0 - decay
    norm = norm * norm
    norm = norm * norm
    gain = length**1.5 * norm * norm
    table = jnp.stack([length, decay, jnp.broadcast_to(chi_coef, (nvars, levels))], axis=1)
    prm = jnp.pad(jnp.concatenate([table, table], axis=2), ((0, 0), (0, 5), (0, 0)))

    def spread(m):
        return jnp.tile(m, (1, 2, 2))

    fold = jnp.dot(bal_temp, vert[0], precision=highest)
    mats_a = spread(vert[1:])
    mats_0 = spread(jnp.stack([vert[0], fold]))
    mats_z = spread(jnp.swapaxes(vert, 1, 2) * gain[:, :, None])
    mats_b = spread(bal_temp.T[None])

    def by_half(s):
        s = s.reshape(s.shape[0], s.shape[1], 2, half).transpose(0, 2, 1, 3)
        return jnp.pad(s, ((0, 0), (0, 0), (0, 0), (0, LANES - half)))

    sig = by_half(sigma)
    place = jnp.stack([i_lat, i_lon]).astype(jnp.int32)

    block = PAIRS * LANES
    packed = 2 * PAIRS

    def part(v, side):
        return pl.BlockSpec((1, rows, block), lambda g: (v, 0, g + side * steps))

    def lat_call(vs, body, mats, arrays, specs):
        nv = len(vs)
        return pl.pallas_call(
            body,
            grid=(steps,),
            in_specs=[full(prm.shape), full(sig.shape), full(mats.shape)] + specs,
            out_specs=[
                pl.BlockSpec((nv, packed, rows, LANES), lambda g: (0, g, 0, 0)),
                pl.BlockSpec((nv, rows, packed, LANES), lambda g: (0, 0, g, 0)),
                pl.BlockSpec((nv, 4, packed, LANES), lambda g: (0, 0, g, 0)),
            ],
            out_shape=[
                jax.ShapeDtypeStruct((nv, half, rows, LANES), f32),
                jax.ShapeDtypeStruct((nv, rows, half, LANES), f32),
                jax.ShapeDtypeStruct((nv, 4, half, LANES), f32),
            ],
            scratch_shapes=[
                pltpu.VMEM((2, PAIRS * rows, 256), f32),
                pltpu.VMEM((2, 256, 256), bf16),
                pltpu.VMEM((2, 256, 256), bf16),
            ],
            compiler_params=params(),
            cost_estimate=pl.CostEstimate(
                flops=nv * 60000000, bytes_accessed=nv * 3 * rows * merged * 4, transcendentals=0
            ),
            name="lat_" + "".join(map(str, vs)),
        )(prm, sig, mats, *arrays)

    wa, ua, ea = lat_call(
        (1, 2),
        functools.partial(lat_plain, (1, 2), rows),
        mats_a,
        [state] * 4,
        [part(1, 0), part(1, 1), part(2, 0), part(2, 1)],
    )
    ga = lax.all_gather(ea, "lat")
    w0, u0, e0 = lat_call(
        (0,),
        functools.partial(lat_balance, rows, pairs),
        mats_0,
        [state] * 5 + [north, south, west, east],
        [part(0, 0), part(0, 1), part(1, 0), part(1, 1)]
        + [pl.BlockSpec((1, rows, merged), lambda g: (2, 0, 0))]
        + [full(north.shape), full(south.shape), full(west.shape), full(east.shape)],
    )
    g0 = lax.all_gather(e0, "lat")

    def lon_call(vs, u, gathered, ext):
        nv = len(vs)
        rb = rows if ext else (16 if rows % 16 == 0 else 8)
        total = rows + 8 * ext
        shapes = [(nv, half, rows, LANES)]
        specs = [pl.BlockSpec((nv, half, rb, LANES), lambda g: (0, 0, g, 0))]
        if ext:
            shapes.append((half, 8, LANES))
            specs.append(full((half, 8, LANES)))
        for s in ((nv, 4, total, LANES), (nv, 2, total, LANES)):
            shapes.append(s)
            specs.append(full(s))
        return pl.pallas_call(
            functools.partial(lon_kernel, vs, n_lat, rows, rb, ext),
            grid=(rows // rb,),
            in_specs=[
                pl.BlockSpec(memory_space=pltpu.SMEM),
                full(prm.shape),
                pl.BlockSpec((nv, rb, half, LANES), lambda g: (0, g, 0, 0)),
                full(gathered.shape),
            ],
            out_specs=specs,
            out_shape=[jax.ShapeDtypeStruct(s, f32) for s in shapes],
            scratch_shapes=[
                pltpu.VMEM((nv, 4, half, LANES), f32),
                pltpu.VMEM((rows // rb, nv, 4, rb, LANES), f32),
            ],
            compiler_params=params(),
            cost_estimate=pl.CostEstimate(
                flops=nv * 60000000, bytes_accessed=nv * 3 * rows * merged * 4, transcendentals=0
            ),
            name="lon_" + "".join(map(str, vs)),
        )(place, prm, u, gathered)

    xa, ela, esa = lon_call((1, 2), ua, ga, False)
    ha = lax.all_gather(esa, "lon")
    x0, xx, el0, es0 = lon_call((0,), u0, g0, True)
    h0 = lax.all_gather(es0, "lon")

    sigx = jnp.concatenate([north[:, merged:], south[:, merged:]], axis=0)
    sigx = by_half(jnp.pad(sigx, ((0, 6), (0, 0)))[None])[0]

    def columns(nv):
        return pl.BlockSpec((nv, packed, rows, LANES), lambda g: (0, g, 0, 0))

    ins = [place, prm, sig, sigx, west, east, mats_z, mats_b, x0, xx, xa, w0, wa, el0, ela, h0, ha]
    specs = [full(x.shape) for x in ins]
    specs[0] = pl.BlockSpec(memory_space=pltpu.SMEM)
    specs[8] = columns(1)
    specs[9] = pl.BlockSpec((packed, 8, LANES), lambda g: (g, 0, 0))
    specs[10] = columns(2)
    specs[11] = columns(1)
    specs[12] = columns(2)
    applied, energy = pl.pallas_call(
        functools.partial(end_kernel, n_lon, rows, pairs),
        grid=(steps,),
        in_specs=specs,
        out_specs=[full(state.shape), full((nvars, 8, LANES))],
        out_shape=[
            jax.ShapeDtypeStruct(state.shape, f32),
            jax.ShapeDtypeStruct((nvars, 8, LANES), f32),
        ],
        scratch_shapes=[
            pltpu.VMEM((nvars, 4, rows + 8, LANES), f32),
            pltpu.VMEM((nvars, 4, half, LANES), f32),
            pltpu.VMEM((2, rows + 8, LANES), f32),
            pltpu.VMEM((8, merged), f32),
            pltpu.VMEM((nvars, PAIRS * rows, 256), f32),
            pltpu.VMEM((4, 256, 256), bf16),
            pltpu.VMEM((4, 256, 256), bf16),
        ],
        compiler_params=params(),
        cost_estimate=pl.CostEstimate(
            flops=300000000, bytes_accessed=9 * rows * merged * 4, transcendentals=0
        ),
        name="finish",
    )(*ins)

    energy = jnp.sum(energy.reshape(nvars, 8, 2, levels), axis=(1, 2)) * gain
    energy = lax.psum(energy.reshape(count), ("lat", "lon")) / (devices * rows * lon)
    index = jnp.arange(count, dtype=jnp.int32)
    same = (owner[:, None] == owner[None, :]) & (index[None, :] < index[:, None])
    slot = jnp.sum(same.astype(jnp.int32), axis=1)
    rank = i_lat * n_lon + i_lon
    hit = (owner[:, None] == rank) & (slot[:, None] == jnp.arange(capacity)[None, :])
    slab_energy = jnp.sum(jnp.where(hit, energy[:, None], 0.0), axis=0)[None, :]
    return (applied, slab_energy)


def solution(mesh):
    return jax.shard_map(
        shards,
        mesh=mesh,
        in_specs=(P(None, "lat", "lon"), P(None, "lat", "lon"), P(), P(), P(), P(), P(), P()),
        out_specs=(P(None, "lat", "lon"), P(("lat", "lon"), None)),
        check_vma=False,
    )
```

time: 934 us -> 204 us (0.22)
  waiting for transfers between devices: 415 us -> 23.9 us
  local copies, waits for them, and re-layouts: 275 us -> 13.1 us
  matrix products: 134 us -> 0.93 us
  blocking collectives: 0 us -> 70.7 us
  Pallas kernels: 0 us -> 65.3 us
  other arithmetic: 57.6 us -> 4.01 us
  starting transfers between devices: 41.6 us -> 10.6 us
  between operations: 1.53 us -> 14.3 us
    all_to_all x2 -> x0, waiting for transfers between devices: 407 us -> none  [the longest x1 204 us: shards(): lax.all_to_all(pieces.reshape(devices, capacity, tile_cells), ('lat', 'lo...]
    dot_general x12 -> x1, matrix products: 134 us -> 0.93 us  [shards(): fold = jnp.dot(bal_temp, vert[0], precision=highest)]
    reshape x10 -> x2, local copies, waits for them, and re-layouts: 117 us -> 1.06 us  [by_half(): s = s.reshape(s.shape[0], s.shape[1], 2, half).transpose(0, 2, 1, 3)]
    pallas_call x0 -> x5, Pallas kernels: none -> 65.3 us  [the longest x1 23.8 us: shards(): pl.pallas_call(functools.partial(end_kernel, n_lon, rows, pairs), grid=(s...]
    gather x4 -> x0, local copies, waits for them, and re-layouts: 41.8 us -> none  [the longest x2 21.6 us: shards(): jnp.take(returned.reshape(devices * capacity, tile_cells), target, axis=0)]
    psum x0 -> x1, blocking collectives: none -> 38.1 us  [shards(): lax.psum(energy.reshape(count), ('lat', 'lon')) / (devices * rows * lon)]
    all_gather x0 -> x2, blocking collectives: none -> 32.5 us  [the longest x1 16.8 us: shards(): ha = lax.all_gather(esa, 'lon')]
    another operation x14 -> x12, local copies, waits for them, and re-layouts: 32.8 us -> 4.47 us  [the longest x8 3.64 us: spread(): return jnp.tile(m, (1, 2, 2))]
  transfers between devices with their start and end apart: 10 -> 6, of which waited for: 5 -> 2; matrix products, arithmetic and copies ran while one was open for 1% -> 7% of each run, Pallas kernels for 0% -> 9%
where the time goes in v1:
time: 204 us; the launch traced here: 203 us
  blocking collectives  70.7 us (35%)
  Pallas kernels  65.3 us (32%)
  waiting for transfers between devices  23.9 us (12%)
  between operations  14.3 us (7%)
  local copies, waits for them, and re-layouts  13.1 us (6%)
  starting transfers between devices  10.6 us (5%)
  other arithmetic  4.01 us (2%)
    psum x1, blocking collectives, shards(): lax.psum(energy.reshape(count), ('lat', 'lon')) / (devices * rows * lon)  38.1 us
    pallas_call x1, Pallas kernels, shards(): pl.pallas_call(functools.partial(end_kernel, n_lon, rows, pairs), grid=(s...  23.8 us
    pallas_call x2, Pallas kernels, lat_call(): pl.pallas_call(body, grid=(steps,), in_specs=[full(prm.shape), full(sig.s...  22.9 us
    pallas_call x2, Pallas kernels, lon_call(): pl.pallas_call(functools.partial(lon_kernel, vs, n_lat, rows, rb, ext), g...  18.7 us
    all_gather x1, blocking collectives, shards(): ha = lax.all_gather(esa, 'lon')  16.8 us
    all_gather x1, blocking collectives, shards(): h0 = lax.all_gather(es0, 'lon')  15.8 us
    all_gather x1, waiting for transfers between devices, shards(): g0 = lax.all_gather(e0, 'lat')  12.3 us
    all_gather x1, waiting for transfers between devices, shards(): ga = lax.all_gather(ea, 'lat')  11.5 us
  transfers between devices with their start and end apart: 6, of which 2 were waited for; matrix products, arithmetic and copies ran while one was open for 7% of the time, Pallas kernels for 9%

profile of v1, /device:TPU:0, one launch (start us, length us, event | category | flops | bytes accessed | tf_op | source)
XLA Modules:
  0.0 202.9 jit_solution(13552995591493696464)
XLA Ops:
  7.2 0.0 all-gather.7.cloned.1.call-start
  7.2 0.7 slice_bitcast_fusion.5
  7.9 1.2 slice_bitcast_fusion.1
  9.2 1.3 collective-permute-start.1
  10.5 3.0 %collective-permute-start = (f32[1,12480]{1,0:T(1,128)S(1)}, f32[1,12480]{1,0:T(1,128)S(1)}, u32[]{:S(2)}, u32[]{:S(2)}) collective-permute-start(f32[1,12480]{1,0:T(1,128)S(1)} %pad_maximum_fusion.1), channel_id=1, source_target_pairs={{0,4},{4,8},{8,12},{12,16},{16,20},{20,24},{24,28},{1,5},{5,9},{9,... | collective-permute-start | bytes 149768 | tf_op jit(solution)/shard_map/ppermute | solution.py:505
  13.6 0.9 slice_reduce_fusion
  14.5 0.8 slice_bitcast_fusion.2
  15.3 0.1 broadcast_in_dim.56
  15.4 0.1 pad_maximum_fusion.3
  15.5 4.9 %collective-permute-start.2 = (f32[48,128]{1,0:T(8,128)S(1)}, f32[48,128]{1,0:T(8,128)S(1)}, u32[]{:S(2)}, u32[]{:S(2)}) collective-permute-start(f32[48,128]{1,0:T(8,128)S(1)} %pad_maximum_fusion.3), channel_id=1, source_target_pairs={{0,1},{1,2},{2,3},{4,5},{5,6},{6,7},{8,9},{9,10},{10,11},{12,13},{... | collective-permute-start | bytes 73736 | tf_op jit(solution)/shard_map/ppermute | solution.py:507
  20.4 0.1 broadcast_in_dim.58
  20.5 0.1 pad_maximum_fusion.4
  20.6 1.3 collective-permute-start.3
  21.9 0.8 select_reduce_fusion.1
  22.6 0.1 stack_reshape.3
  22.7 0.8 slice.47
  23.5 0.9 convolution_bitcast_fusion
  24.5 0.7 stack_broadcast_in_dim.3
  25.1 0.7 fusion.2.prm
  25.8 1.1 reshape.76
  26.9 0.1 tile.39
  27.0 0.8 tile.40.mats
  27.8 0.7 pad.17.sig
  28.5 0.0 collective-permute-done.2.west
  28.5 0.0 collective-permute-done.3.east
  28.5 0.0 copy-start.3
  28.5 0.0 collective-permute-done.1.south
  28.5 0.0 collective-permute-done.north
  28.5 0.6 copy-done.2
  29.1 0.0 copy-done.3
  29.1 0.0 copy-done.4
  29.2 0.6 copy-done.5
  29.8 11.7 %lat_0.1 = (f32[1,96,48,128]{3,2,1,0:T(8,128)}, f32[1,48,96,128]{3,2,1,0:T(8,128)}, f32[1,4,96,128]{3,2,1,0:T(8,128)}) custom-call(f32[3,8,128]{2,1,0:T(8,128)} %fusion.2.prm, f32[3,2,48,128]{3,2,1,0:T(8,128)} %pad.17.sig, f32[2,128,128]{2,1,0:T(8,128)} %tile.40.mats, f32[3,48,12288]{2,1,0:T(8,128)} %b2hi.1, f32[3,48,12288]{2,1,0:T(8,128)} %b2hi.1, ...), custom_call_target="tpu_custom_call" | custom-call | flops 60000000 | bytes 7077888 | tf_op jit(solution)/shard_map/lat_0/pallas_call | solution.py:545
  41.5 0.0 all-gather.7.cloned.1.call-update
  41.5 0.0 all-gather.9.cloned.1.call-start
  41.6 0.1 tile.41
  41.7 0.8 tile.42.mats
  42.5 0.0 slice-start.2
  42.5 11.1 %lat_12.1 = (f32[2,96,48,128]{3,2,1,0:T(8,128)}, f32[2,48,96,128]{3,2,1,0:T(8,128)}, f32[2,4,96,128]{3,2,1,0:T(8,128)}) custom-call(f32[3,8,128]{2,1,0:T(8,128)} %fusion.2.prm, f32[3,2,48,128]{3,2,1,0:T(8,128)} %pad.17.sig, f32[2,128,128]{2,1,0:T(8,128)} %tile.42.mats, f32[3,48,12288]{2,1,0:T(8,128)} %b2hi.1, f32[3,48,12288]{2,1,0:T(8,128)} %b2hi.1, ...), custom_call_target="tpu_custom_call" | custom-call | flops 120000000 | bytes 14155776 | tf_op jit(solution)/shard_map/lat_12/pallas_call | solution.py:545
  53.6 0.0 all-gather.9.cloned.1.call-update
  53.7 0.1 reshape.77
  53.8 0.1 pow.16
  53.9 0.1 copy.22
  54.0 0.1 tile.16
  54.1 0.9 tile.17.mats
  55.0 0.1 copy.23
  55.2 0.8 tile.38.balm
  55.9 0.6 pad_add_fusion.place
  56.6 0.0 copy-done.6
  56.6 0.2 convert_reduce_fusion
  56.8 0.1 reshape_broadcast_in_dim.3
  56.9 0.6 pad_bitcast_fusion.sigx
  57.5 12.3 %all-gather.7.cloned.1.call-done = f32[8,4,96,128]{3,2,1,0:T(8,128)} async-done(((f32[1,4,96,128]{3,2,1,0:T(8,128)}), f32[8,4,96,128]{3,2,1,0:T(8,128)}) %all-gather.7.cloned.1.call-update) | async-done | bytes 1572880 | tf_op jit(solution)/shard_map/all_gather | solution.py:588
  69.8 6.9 %lon_0.1 = (f32[1,96,48,128]{3,2,1,0:T(8,128)}, f32[96,8,128]{2,1,0:T(8,128)}, f32[1,4,56,128]{3,2,1,0:T(8,128)}, f32[1,2,56,128]{3,2,1,0:T(8,128)}) custom-call(s32[2]{0:T(128)} %pad_add_fusion.place, f32[3,8,128]{2,1,0:T(8,128)} %fusion.2.prm, f32[1,48,96,128]{3,2,1,0:T(8,128)} %get-tuple-element.17.u_ref, f32[8,1,4,96,128]{4,3,2,1,0:T(8,128)} %bitcast.37), custom_call_target="tpu_custom_call" | custom-call | flops 60000000 | bytes 7077888 | tf_op jit(solution)/shard_map/lon_0/pallas_call | solution.py:602
  76.7 15.8 %all-gather.2 = f32[4,2,56,128]{3,2,1,0:T(8,128)} all-gather(f32[1,2,56,128]{3,2,1,0:T(8,128)} %get-tuple-element.28), channel_id=4, replica_groups=mesh['lat'=8,'lon'=4] {'lon'}, dimensions={0}, use_global_device_ids=true | all-gather | bytes 286720 | tf_op jit(solution)/shard_map/all_gather | solution.py:627
  92.5 11.5 %all-gather.9.cloned.1.call-done = f32[16,4,96,128]{3,2,1,0:T(8,128)} async-done(((f32[2,4,96,128]{3,2,1,0:T(8,128)}), f32[16,4,96,128]{3,2,1,0:T(8,128)}) %all-gather.9.cloned.1.call-update) | async-done | bytes 3145744 | tf_op jit(solution)/shard_map/all_gather | solution.py:578
  104.0 11.7 %lon_12.1 = (f32[2,96,48,128]{3,2,1,0:T(8,128)}, f32[2,4,48,128]{3,2,1,0:T(8,128)}, f32[2,2,48,128]{3,2,1,0:T(8,128)}) custom-call(s32[2]{0:T(128)} %pad_add_fusion.place, f32[3,8,128]{2,1,0:T(8,128)} %fusion.2.prm, f32[2,48,96,128]{3,2,1,0:T(8,128)} %get-tuple-element.21.u_ref, f32[8,2,4,96,128]{4,3,2,1,0:T(8,128)} %bitcast.36), custom_call_target="tpu_custom_call" | custom-call | flops 120000000 | bytes 14155776 | tf_op jit(solution)/shard_map/lon_12/pallas_call | solution.py:602
  115.8 16.8 %all-gather.3 = f32[8,2,48,128]{3,2,1,0:T(8,128)} all-gather(f32[2,2,48,128]{3,2,1,0:T(8,128)} %get-tuple-element.29), channel_id=5, replica_groups=mesh['lat'=8,'lon'=4] {'lon'}, dimensions={0}, use_global_device_ids=true | all-gather | bytes 491520 | tf_op jit(solution)/shard_map/all_gather | solution.py:625
  132.5 23.8 %finish.1 = (f32[3,48,12288]{2,1,0:T(8,128)}, f32[3,8,128]{2,1,0:T(8,128)}) custom-call(s32[2]{0:T(128)} %pad_add_fusion.place, f32[3,8,128]{2,1,0:T(8,128)} %fusion.2.prm, f32[3,2,48,128]{3,2,1,0:T(8,128)} %pad.17.sig, f32[2,8,128]{2,1,0:T(8,128)} %pad_bitcast_fusion.sigx, f32[48,128]{1,0:T(8,128)} %copy-done.2, f32[48,128]{1,0:T(8,128)} %copy-done.3, ...), custom_call_target="tpu_custom_call" | custom-call | flops 300000000 | bytes 21233664 | tf_op jit(solution)/shard_map/finish/pallas_call | solution.py:643
  156.3 0.7 reduce_sum.47
  157.0 0.1 reduce_sum.48
  157.1 0.1 reduce_sum.50
  157.2 38.1 %psum.7 = f32[192]{0:T(256)S(1)} all-reduce(f32[192]{0:T(256)S(1)} %fusion.4), channel_id=1, replica_groups=mesh['lat'=8,'lon'=4] {'lat','lon'}, use_global_device_ids=true, to_apply=%region_4.5 | all-reduce | flops 192 | bytes 1536 | tf_op jit(solution)/shard_map/psum | solution.py:669
  195.4 0.6 select_reduce_fusion
  (28 shorter events, 0.3 us)
Async XLA Ops:
  7.2 62.6 %all-gather.7.cloned.1.call-start = ((), (), s32[]{:S(2)}) async-start(), calls=%async_computation | async-start | bytes 1769472 | tf_op jit(solution)/shard_map/all_gather | solution.py:588
  9.2 19.4 %collective-permute-start.1 = (f32[1,12480]{1,0:T(1,128)S(1)}, f32[1,12480]{1,0:T(1,128)S(1)}, u32[]{:S(2)}, u32[]{:S(2)}) collective-permute-start(f32[1,12480]{1,0:T(1,128)S(1)} %pad_maximum_fusion.2), channel_id=1, source_target_pairs={{4,0},{8,4},{12,8},{16,12},{20,16},{24,20},{28,24},{5,1},{9,5},{13... | collective-permute-start | bytes 149768 | tf_op jit(solution)/shard_map/ppermute | solution.py:506
  10.5 18.0 %collective-permute-start = (f32[1,12480]{1,0:T(1,128)S(1)}, f32[1,12480]{1,0:T(1,128)S(1)}, u32[]{:S(2)}, u32[]{:S(2)}) collective-permute-start(f32[1,12480]{1,0:T(1,128)S(1)} %pad_maximum_fusion.1), channel_id=1, source_target_pairs={{0,4},{4,8},{8,12},{12,16},{16,20},{20,24},{24,28},{1,5},{5,9},{9,... | collective-permute-start | bytes 149768 | tf_op jit(solution)/shard_map/ppermute | solution.py:505
  15.5 13.0 %collective-permute-start.2 = (f32[48,128]{1,0:T(8,128)S(1)}, f32[48,128]{1,0:T(8,128)S(1)}, u32[]{:S(2)}, u32[]{:S(2)}) collective-permute-start(f32[48,128]{1,0:T(8,128)S(1)} %pad_maximum_fusion.3), channel_id=1, source_target_pairs={{0,1},{1,2},{2,3},{4,5},{5,6},{6,7},{8,9},{9,10},{10,11},{12,13},{... | collective-permute-start | bytes 73736 | tf_op jit(solution)/shard_map/ppermute | solution.py:507
  20.6 7.9 %collective-permute-start.3 = (f32[48,128]{1,0:T(8,128)S(1)}, f32[48,128]{1,0:T(8,128)S(1)}, u32[]{:S(2)}, u32[]{:S(2)}) collective-permute-start(f32[48,128]{1,0:T(8,128)S(1)} %pad_maximum_fusion.4), channel_id=1, source_target_pairs={{1,0},{2,1},{3,2},{5,4},{6,5},{7,6},{9,8},{10,9},{11,10},{13,12},{... | collective-permute-start | bytes 73736 | tf_op jit(solution)/shard_map/ppermute | solution.py:508
  28.5 13.1 %slice-start = ((f32[3,64,64]{2,1,0:T(8,128)}), f32[2,64,64]{2,1,0:T(8,128)S(1)}, s32[]{:S(2)}) async-start(f32[3,64,64]{2,1,0:T(8,128)} %param.10), calls=%async_computation.2 | async-start | bytes 131072 | tf_op jit(solution)/shard_map/slice | solution.py:525
  28.5 0.6 copy-start.2
  28.5 0.6 copy-start.3
  28.5 0.6 copy-start.4
  29.1 0.6 copy-start.5
  41.5 62.5 %all-gather.9.cloned.1.call-start = ((), (), s32[]{:S(2)}) async-start(), calls=%async_computation.1 | async-start | bytes 3538944 | tf_op jit(solution)/shard_map/all_gather | solution.py:578
  42.5 11.4 %copy-start = (f32[3,64,64]{2,1,0:T(8,128)S(1)}, f32[3,64,64]{2,1,0:T(8,128)}, u32[]{:S(2)}) copy-start(f32[3,64,64]{2,1,0:T(8,128)} %param.10) | copy-start | bytes 147460
  42.5 12.5 %copy-start.1 = (f32[64,64]{1,0:T(8,128)S(1)}, f32[64,64]{1,0:T(8,128)}, u32[]{:S(2)}) copy-start(f32[64,64]{1,0:T(8,128)} %param.11) | copy-start | bytes 49156
  42.5 14.1 %copy-start.6 = (s32[192]{0:T(256)S(1)}, s32[192]{0:T(256)}, u32[]{:S(2)}) copy-start(s32[192]{0:T(256)} %param.15) | copy-start | bytes 2308
  42.5 14.3 %slice-start.1 = ((f32[1,12480]{1,0:T(1,128)}), f32[1,192]{1,0:T(1,128)S(1)}, s32[]{:S(2)}) async-start(f32[1,12480]{1,0:T(1,128)} %copy-done.4), calls=%async_computation.3 | async-start | bytes 2048 | tf_op jit(solution)/shard_map/slice | solution.py:629
  42.5 14.3 %slice-start.2 = ((f32[1,12480]{1,0:T(1,128)}), f32[1,192]{1,0:T(1,128)S(1)}, s32[]{:S(2)}) async-start(f32[1,12480]{1,0:T(1,128)} %copy-done.5), calls=%async_computation.4 | async-start | bytes 2048 | tf_op jit(solution)/shard_map/slice | solution.py:629
Sparse Core Ops, SparseCore 0:
  41.6 28.1 all-gather.6
  71.7 32.3 all-gather.8

commit v2 on v1

v2 whole, which is shorter than its diff:
```python
import functools

import jax
import jax.numpy as jnp
from jax import lax
from jax.experimental import pallas as pl
from jax.experimental.pallas import tpu as pltpu
from jax.sharding import PartitionSpec as P

highest = lax.Precision.HIGHEST
f32 = jnp.float32
bf16 = jnp.bfloat16
LANES = 128
PAIRS = 8
BLOCK = 24
ORDER = (1, 2, 0)
LIMIT = 60 * 1024 * 1024


def params():
    return pltpu.CompilerParams(vmem_limit_bytes=LIMIT)


def full(shape):
    return pl.BlockSpec(shape, lambda g: (0,) * len(shape))


def swap(x):
    return pltpu.roll(x, 64, x.ndim - 1)


def low_lanes(shape):
    return lax.broadcasted_iota(jnp.int32, shape, len(shape) - 1) < 64


def halves(x):
    hi = x.astype(bf16)
    return hi, (x - hi.astype(f32)).astype(bf16)


def dot(x, y):
    return jnp.dot(x, y, preferred_element_type=f32)


def product(x, wh, wl):
    hi, lo = halves(x)
    return dot(hi, wh) + dot(lo, wh) + dot(hi, wl)


def expand(mat, mixed):
    wide = quad(mat)
    wide = jnp.concatenate([wide, wide], axis=1)
    wide = jnp.concatenate([wide, wide], axis=0)
    src = lax.broadcasted_iota(jnp.int32, (256, 256), 0) // 64
    dst = lax.broadcasted_iota(jnp.int32, (256, 256), 1) // 64
    if mixed:
        src = jnp.where(src == 1, 2, jnp.where(src == 2, 1, src))
    return halves(jnp.where(src == dst, wide, 0.0))


def quad(mat):
    if mat.shape[0] == LANES:
        return mat
    wide = jnp.concatenate([mat, mat], axis=1)
    return jnp.concatenate([wide, wide], axis=0)


def constants(length, decay, m):
    span = jnp.exp(-float(m) / length)
    d = 1.0 - decay * decay
    k1 = decay * (1.0 - span * span) / d
    k2 = (m * span - decay * decay * (span - span * span * span) / d) / d
    tail = decay * decay * (1.0 + span * span) * (1.0 - span * span) / d
    k3 = decay / (d * d) * (1.0 - (2.0 * m + 1.0) * span * span + tail)
    return span, k1, k2, k3


def responses(length, decay, m):
    j = lax.broadcasted_iota(jnp.int32, (m, LANES), 0).astype(f32)
    up = jnp.exp(-j / length)
    down = jnp.exp(-(m - j) / length)
    span = jnp.exp(-float(m) / length)
    d = 1.0 - decay * decay
    diff = up - span * down
    g3 = decay * diff / d
    g2 = ((m - j) * down - decay * decay * (span * up - span * span * down) / d) / d
    part = decay * decay * (1.0 + span * span) * diff / d
    g1 = decay / (d * d) * ((j + 1.0) * up - (2.0 * m + 1.0 - j) * span * down + part)
    return g1, g2, g3, down


def solve_carries(n, edge, const, me):
    span, k1, k2, k3 = const
    first = edge(0, 0)
    zero = jnp.zeros_like(first)
    e1 = [first] + [edge(t, 0) for t in range(1, n)]
    c1, c2, c3, c4 = ([None] * n for _ in range(4))
    c = zero
    for t in range(n):
        c1[t] = c
        c = e1[t] + span * c
    c = zero
    for t in reversed(range(n)):
        c2[t] = c
        c = edge(t, 1) + k1 * c1[t] + span * c
    c = zero
    for t in range(n):
        c3[t] = c
        c = edge(t, 2) + k2 * c1[t] + k1 * c2[t] + span * c
    c = zero
    for t in reversed(range(n)):
        c4[t] = c
        c = edge(t, 3) + k3 * c1[t] + k2 * c2[t] + k1 * c3[t] + span * c
    out = []
    for cs in (c1, c2, c3, c4):
        mine = cs[0]
        for t in range(1, n):
            mine = jnp.where(me == t, cs[t], mine)
        out.append(mine)
    return out


def cascade(count, load, store, decay, start):
    step = 8
    edges = []
    for stage in range(4):
        back = stage % 2 == 1

        def body(b, states, back=back):
            base = (count // step - 1 - b) * step if back else b * step
            order = range(step - 1, -1, -1) if back else range(step)
            for o in order:
                new = [decay_k * s + x for decay_k, s, x in zip(decay, states, load(base + o))]
                store(base + o, new)
                states = new
            return tuple(states)

        states = lax.fori_loop(0, count // step, body, tuple(start))
        edges.append(list(states))
    return edges


def stage_sigma(sigma, sg, variables):
    lon = sigma.shape[2]
    for v in variables:
        for at in range(0, lon, LANES):
            width = min(LANES, lon - at)
            sg[v, at // LANES, :, 0:width] = sigma[v, :, at : at + width]


def sigma_tile(sg, v, m, high):
    idx = 2 * (m & 63) + high
    return jnp.take_along_axis(sg[v, m >> 6], idx, axis=1, mode="promise_in_bounds")


def set_weights(wh, wl, k, mat, mixed):
    hi, lo = expand(mat, mixed)
    wh[k] = hi
    wl[k] = lo


def lat_filter(vs, rows, prm, u_ref, e_ref):
    nv = len(vs)
    decay = [prm[v, 1:2, :] for v in vs]

    def load(i):
        return [u_ref[k, i] for k in range(nv)]

    def store(i, values):
        for k in range(nv):
            u_ref[k, i] = values[k]

    zero = jnp.zeros((u_ref.shape[2], LANES), f32)
    edges = cascade(rows, load, store, decay, [zero] * nv)
    for e in range(4):
        for k in range(nv):
            e_ref[k, e] = edges[e][k]


def put_mixed(k, b, rows, res, w_ref, u_ref):
    base = b * 2 * PAIRS
    for p in range(PAIRS):
        part = res[p * rows : (p + 1) * rows]
        w_ref[k, base + 2 * p] = part[:, :LANES]
        w_ref[k, base + 2 * p + 1] = part[:, LANES:]
    at = pl.ds(pl.multiple_of(base, 2 * PAIRS), 2 * PAIRS)
    u_ref[k, :, at, :] = jnp.swapaxes(w_ref[k, at], 0, 1)


def lat_plain(rows, pairs, prm, sigma, vert, b1lo, b1hi, b2lo, b2hi, w_ref, u_ref, e_ref, xs, wh, wl, sg):
    g = pl.program_id(0)

    @pl.when(g == 0)
    def _():
        set_weights(wh, wl, 0, vert[1], True)
        set_weights(wh, wl, 1, vert[2], True)
        stage_sigma(sigma, sg, (1, 2))

    lane = lax.broadcasted_iota(jnp.int32, (rows, LANES), 1)
    high = (lane >= 64).astype(jnp.int32)

    def body(b, _):
        for p in range(PAIRS):
            at = slice(p * rows, (p + 1) * rows)
            cols = pl.ds(pl.multiple_of((b * PAIRS + p) * LANES, LANES), LANES)
            m = g * BLOCK + b * PAIRS + p
            for k, sides in enumerate(((b1lo, b1hi), (b2lo, b2hi))):
                for side in range(2):
                    s = sigma_tile(sg, k + 1, m + side * pairs, high)
                    xs[k, at, side * LANES : (side + 1) * LANES] = sides[side][0, :, cols] * s
        for k in range(2):
            put_mixed(k, b, rows, product(xs[k], wh[k], wl[k]), w_ref, u_ref)
        return 0

    lax.fori_loop(0, BLOCK // PAIRS, body, 0)
    lat_filter((1, 2), rows, prm, u_ref, e_ref)


def lat_balance(
    rows, pairs, prm, sigma, vert, bal, plo, phi, clo, chi, temp, north, south, west, east, w_in, u_in, e_in,
    w_ref, u_ref, e_ref, xs, wh, wl, sg,
):
    del w_in, u_in, e_in
    g = pl.program_id(0)

    @pl.when(g == 0)
    def _():
        set_weights(wh, wl, 0, vert[0], True)
        vh, vl = halves(vert[0])
        set_weights(wh, wl, 1, product(bal[...], vh, vl), True)
        stage_sigma(sigma, sg, (0,))

    lane = lax.broadcasted_iota(jnp.int32, (rows, LANES), 1)
    row_id = lax.broadcasted_iota(jnp.int32, (rows, LANES), 0)
    high = (lane >= 64).astype(jnp.int32)
    chi_row = prm[0, 2:3, :]
    last = 2 * pairs - 1

    def at_tile(m):
        return pl.ds(pl.multiple_of(m * LANES, LANES), LANES)

    def laplace(m):
        x = temp[0, :, at_tile(m)]
        left = jnp.where(m == 0, swap(west[...]), temp[0, :, at_tile(jnp.maximum(m - 1, 0))])
        right = jnp.where(m == last, east[...], temp[0, :, at_tile(jnp.minimum(m + 1, last))])
        beside = swap(x + jnp.where(lane >= 64, left, right))
        above = jnp.where(row_id == 0, north[:, at_tile(m)], pltpu.roll(x, 1, 0))
        below = jnp.where(row_id == rows - 1, south[:, at_tile(m)], pltpu.roll(x, rows - 1, 0))
        return 4.0 * x - beside - above - below

    def body(b, _):
        for p in range(PAIRS):
            at = slice(p * rows, (p + 1) * rows)
            cols = at_tile(b * PAIRS + p)
            m = g * BLOCK + b * PAIRS + p
            for side, (pr, cr) in enumerate(((plo, clo), (phi, chi))):
                s = sigma_tile(sg, 0, m + side * pairs, high)
                to = slice(side * LANES, (side + 1) * LANES)
                xs[0, at, to] = (pr[0, :, cols] + chi_row * cr[0, :, cols]) * s
                xs[1, at, to] = laplace(m + side * pairs) * s
        res = product(xs[0], wh[0], wl[0]) + product(xs[1], wh[1], wl[1])
        put_mixed(0, b, rows, res, w_ref, u_ref)
        return 0

    lax.fori_loop(0, BLOCK // PAIRS, body, 0)
    lat_filter((0,), rows, prm, u_ref, e_ref)


def lon_filter(prm, rb, o_ref, el_ref, es_ref, at):
    half = o_ref.shape[1]
    nv = len(ORDER)
    decay = [prm[v, 1:2, :] for v in ORDER]

    def load(j):
        return [o_ref[k, j] for k in range(nv)]

    def store(j, values):
        for k in range(nv):
            o_ref[k, j] = values[k]

    edges = cascade(half, load, store, decay, [jnp.zeros((rb, LANES), f32)] * nv)
    low = low_lanes((rb, LANES))
    for k, v in enumerate(ORDER):
        span, k1, k2, k3 = constants(prm[v, 0:1, :], prm[v, 1:2, :], half)
        e1, e2, e3, e4 = (edges[e][k] for e in range(4))
        c1 = jnp.where(low, 0.0, swap(e1))
        t1 = e1 + span * c1
        t2 = e2 + k1 * c1
        c2 = jnp.where(low, swap(t2), 0.0)
        t2 = t2 + span * c2
        t3 = e3 + k2 * c1 + k1 * c2
        c3 = jnp.where(low, 0.0, swap(t3))
        t3 = t3 + span * c3
        t4 = e4 + k3 * c1 + k2 * c2 + k1 * c3
        c4 = jnp.where(low, swap(t4), 0.0)
        t4 = t4 + span * c4
        es_ref[k, 0, at, :] = jnp.where(low, t2, t1)
        es_ref[k, 1, at, :] = jnp.where(low, t4, t3)
        for e, x in enumerate((e1, e2, e3, e4)):
            el_ref[k, e, at, :] = x


def lon_kernel(rb, prm, u_ref, o_ref, el_ref, es_ref):
    g = pl.program_id(0)
    half = u_ref.shape[2]

    def turn(b, _):
        at = pl.ds(pl.multiple_of(b * 8, 8), 8)
        for k in range(len(ORDER)):
            for q in range(0, rb, 8):
                o_ref[k, at, q : q + 8, :] = jnp.swapaxes(u_ref[k, q : q + 8, at, :], 0, 1)
        return 0

    lax.fori_loop(0, half // 8, turn, 0)
    lon_filter(prm, rb, o_ref, el_ref, es_ref, pl.ds(pl.multiple_of(g * rb, 8), rb))


def carry_kernel(n_lat, rows, place, prm, gathered, o_ref, el_ref, es_ref):
    half = o_ref.shape[1]
    me = place[0]
    for k, v in enumerate(ORDER):
        const = constants(prm[v, 0:1, :], prm[v, 1:2, :], rows)

        def body(b, _, k=k, const=const):
            at = pl.ds(pl.multiple_of(b * 8, 8), 8)
            c = solve_carries(n_lat, lambda t, e: gathered[t, k, e, at, :], const, me)
            block = jnp.stack(c + [jnp.zeros_like(c[0])] * 4, axis=0)
            o_ref[k, at] = jnp.swapaxes(block, 0, 1)
            return 0

        lax.fori_loop(0, half // 8, body, 0)
    lon_filter(prm, 8, o_ref, el_ref, es_ref, pl.ds(0, 8))


def join_kernel(n_lon, rows, packed, rq, place, prm, u_ref, w_ref, x_ref, el, es, elc, *rest):
    sent = rest[:n_lon]
    y_ref, yx_ref, col_ref, energy, carry, extra, resp_x, resp_y, esx = rest[n_lon:]
    g = pl.program_id(0)
    half = resp_x.shape[2]
    lat, me = place[0], place[1]
    low8 = low_lanes((8, LANES))

    @pl.when(g == 0)
    def _():
        energy[...] = jnp.zeros_like(energy)
        for s in range(n_lon):
            esx[lax.rem(me - s + n_lon, n_lon)] = sent[s][...]
        for k, v in enumerate(ORDER):
            length = prm[v, 0:1, :]
            decay = prm[v, 1:2, :]
            whole = constants(length, decay, 2 * half)
            span, k1, k2, k3 = constants(length, decay, half)

            def solve(gathered, own, at, k=k, whole=whole, half_c=(span, k1, k2, k3)):
                span, k1, k2, k3 = half_c
                cache = {}

                def edge(t, e):
                    if (t, e // 2) not in cache:
                        x = gathered[t, k, e // 2, at, :]
                        y = swap(x)
                        cache[t, e // 2] = (jnp.where(low8, y, x), jnp.where(low8, x, y))
                    return cache[t, e // 2][e % 2]

                d1, d2, d3, d4 = solve_carries(n_lon, edge, whole, me)
                e1, e2, e3, e4 = (own[k, e, at, :] for e in range(4))
                c1 = jnp.where(low8, d1, swap(e1 + span * d1))
                c2 = jnp.where(low8, swap(e2 + k1 * c1 + span * d2), d2)
                c3 = jnp.where(low8, d3, swap(e3 + k2 * c1 + k1 * c2 + span * d3))
                c4 = jnp.where(low8, swap(e4 + k3 * c1 + k2 * c2 + k1 * c3 + span * d4), d4)
                return (c1, c2, c3, c4), d3, d4

            for e, r in enumerate(responses(length, decay, half)):
                resp_x[k, e] = r
            for e, r in enumerate(responses(length, decay, rows)):
                resp_y[k, e] = r
            cc, f3, f4 = solve(esx, elc, slice(0, 8))
            for e in range(4):
                extra[k, e] = cc[e]

            def body(b, _, k=k, v=v, cc=cc, f3=f3, f4=f4, solve=solve):
                at = pl.ds(pl.multiple_of(b * 8, 8), 8)
                c, d3, d4 = solve(es, el, at)
                ry = [resp_y[k, e, at, :] for e in range(4)]

                def total(x, rows_of):
                    for e in range(4):
                        x = x + ry[e] * rows_of[e : e + 1, :]
                    return x

                for e in range(4):
                    carry[k, e, at, :] = total(c[e], cc[e])
                if v == 0:
                    col_ref[0, at, :] = total(d3, f3)
                    col_ref[1, at, :] = total(d4, f4)
                return 0

            lax.fori_loop(0, rows // 8, body, 0)

    row8 = lax.broadcasted_iota(jnp.int32, (8, LANES), 0)
    for k, v in enumerate(ORDER):
        total = jnp.zeros((8, LANES), f32)
        for q in range(0, rows, rq):
            at = slice(q, q + rq)
            c = [carry[k, e, at, :] for e in range(4)]
            ry = [resp_y[k, e, at, :] for e in range(4)]

            def body(b, total, k=k, v=v, q=q, at=at, c=c, ry=ry):
                base = g * packed + b * 8
                rx = [resp_x[k, e, pl.ds(pl.multiple_of(base, 8), 8), :] for e in range(4)]
                for o in range(8):
                    p = b * 8 + o
                    x = x_ref[k, p]
                    y = u_ref[k, p, at, :]
                    for e in range(4):
                        y = y + rx[e][o : o + 1, :] * c[e] + ry[e] * x[e : e + 1, :]
                    y_ref[k, p, at, :] = y
                    t = y * w_ref[k, p, at, :]
                    for i in range(0, rq, 8):
                        total = total + t[i : i + 8]
                    if v == 0 and q == 0:
                        for e in range(4):
                            x = x + rx[e][o : o + 1, :] * extra[k, e]
                        x = pltpu.roll(x, 6, 0)
                        above = jnp.where(lat > 0, x + prm[0, 1:2, :] * y[0:1, :], 0.0)
                        yx_ref[p] = jnp.where(row8 == 0, above, jnp.where(row8 == 1, x, 0.0))
                return total

            total = lax.fori_loop(0, packed // 8, body, total)
        energy[k] += total

    @pl.when(g == 0)
    def _():
        beside = col_ref[0] + prm[0, 1:2, :] * y_ref[ORDER.index(0), 0]
        col_ref[0] = jnp.where(me > 0, beside, 0.0)


def end_kernel(
    rows, pairs, prm, sigma, north, south, west, east, vert, bal, col, y_ref, yx_ref,
    out, xs, zx, zc, wh, wl, sg, sx,
):
    g = pl.program_id(0)
    half = 2 * pairs
    merged = out.shape[2]
    lon = sigma.shape[2]

    @pl.when(g == 0)
    def _():
        for v in range(3):
            scaled = quad(vert[v]) * prm[v, 3:4, :]
            set_weights(wh, wl, v, scaled.T, True)
        set_weights(wh, wl, 3, quad(bal[...]).T, False)
        stage_sigma(sigma, sg, (0, 1, 2))
        for at in range(0, lon, LANES):
            width = min(LANES, lon - at)
            sx[at // LANES, 0:1, 0:width] = north[:, merged + at : merged + at + width]
            sx[at // LANES, 1:2, 0:width] = south[:, merged + at : merged + at + width]
        lhs = jnp.where(low_lanes((rows, LANES)), col[0], col[1])
        lhs = jnp.concatenate([lhs, jnp.zeros_like(lhs)], axis=1)
        res = product(lhs, wh[0], wl[0])
        zc[0] = swap(res[:, :LANES] * swap(west[...]))
        zc[1] = res[:, LANES:] * swap(east[...])

    lane = lax.broadcasted_iota(jnp.int32, (rows, LANES), 1)
    high = (lane >= 64).astype(jnp.int32)
    high8 = high[0:8]
    chi_row = prm[0, 2:3, :]

    def at_tile(m):
        return pl.ds(pl.multiple_of(m * LANES, LANES), LANES)

    lhs = jnp.concatenate(
        [jnp.concatenate([yx_ref[2 * p], yx_ref[2 * p + 1]], axis=1) for p in range(PAIRS)], axis=0
    )
    res = product(lhs, wh[0], wl[0])
    for p in range(PAIRS):
        m = g * PAIRS + p
        for side in range(2):
            tile = m + side * pairs
            s = jnp.take_along_axis(sx[tile >> 6], 2 * (tile & 63) + high8, axis=1, mode="promise_in_bounds")
            part = res[p * 8 : (p + 1) * 8, side * LANES : (side + 1) * LANES]
            zx[:, at_tile(tile)] = jnp.where(lax.broadcasted_iota(jnp.int32, (8, LANES), 0) < 2, part * s, 0.0)
    for k in range(3):
        for p in range(2 * PAIRS):
            at = slice((p // 2) * rows, (p // 2 + 1) * rows)
            xs[k, at, (p % 2) * LANES : (p % 2 + 1) * LANES] = y_ref[k, p]
    results = {v: product(xs[k], wh[v], wl[v]) for k, v in enumerate(ORDER)}
    for p in range(PAIRS):
        m = g * PAIRS + p
        for side in range(2):
            at = at_tile(m + side * pairs)
            z = [
                results[v][p * rows : (p + 1) * rows, side * LANES : (side + 1) * LANES]
                * sigma_tile(sg, v, m + side * pairs, high)
                for v in range(3)
            ]
            out[0, :, at] = z[0]
            out[1, :, at] = z[1] + chi_row * z[0]
            out[2, :, at] = z[2]

    @pl.when(g == pl.num_programs(0) - 1)
    def _():
        row_id = lax.broadcasted_iota(jnp.int32, (rows, LANES), 0)
        last = half - 1

        def body(b, _):
            for p in range(PAIRS):
                for side in range(2):
                    m = b * PAIRS + p + side * pairs
                    x = out[0, :, at_tile(m)]
                    left = jnp.where(m == 0, zc[0], out[0, :, at_tile(jnp.maximum(m - 1, 0))])
                    right = jnp.where(m == last, zc[1], out[0, :, at_tile(jnp.minimum(m + 1, last))])
                    beside = swap(x + jnp.where(lane >= 64, left, right))
                    above = jnp.where(row_id == 0, zx[0:1, at_tile(m)], pltpu.roll(x, 1, 0))
                    below = jnp.where(row_id == rows - 1, zx[1:2, at_tile(m)], pltpu.roll(x, rows - 1, 0))
                    lap = 4.0 * x - beside - above - below
                    xs[0, p * rows : (p + 1) * rows, side * LANES : (side + 1) * LANES] = lap
            res = product(xs[0], wh[3], wl[3])
            for p in range(PAIRS):
                for side in range(2):
                    at = at_tile(b * PAIRS + p + side * pairs)
                    part = res[p * rows : (p + 1) * rows, side * LANES : (side + 1) * LANES]
                    out[2, :, at] = out[2, :, at] + part
            return 0

        lax.fori_loop(0, pairs // PAIRS, body, 0)


def shards(state, sigma, vert, bal_temp, chi_coef, scales, classes, owner):
    n_lat = lax.axis_size("lat")
    n_lon = lax.axis_size("lon")
    devices = n_lat * n_lon
    nvars, rows, merged = state.shape
    levels = vert.shape[1]
    lon = merged // levels
    half = lon // 2
    pairs = half // 2
    pieces = (lon + LANES - 1) // LANES
    count = nvars * levels
    capacity = (count + devices - 1) // devices + 1
    i_lat = lax.axis_index("lat")
    i_lon = lax.axis_index("lon")

    up_lat, up_lon = ([(i, i + 1) for i in range(n - 1)] for n in (n_lat, n_lon))
    down_lat, down_lon = ([(j, i) for i, j in up] for up in (up_lat, up_lon))

    def row(i):
        return jnp.concatenate([state[2, i : i + 1, :], sigma[0, i : i + 1, :]], axis=1)

    def column(j):
        temp = state[2, :, j * levels : (j + 1) * levels]
        sig = jnp.broadcast_to(sigma[0, :, j : j + 1], (rows, levels))
        return jnp.concatenate([temp, sig], axis=1)

    north = lax.ppermute(row(rows - 1), "lat", up_lat)
    south = lax.ppermute(row(0), "lat", down_lat)
    west = lax.ppermute(column(lon - 1), "lon", up_lon)
    east = lax.ppermute(column(0), "lon", down_lon)

    class_ids = jnp.arange(scales.shape[0], dtype=jnp.int32)
    kind = classes.reshape(nvars, levels)
    kind = jnp.concatenate([kind, kind], axis=1)
    length = jnp.sum(jnp.where(kind[:, None, :] == class_ids[None, :, None], scales[None, :, None], 0.0), axis=1)
    decay = jnp.exp(-1.0 / length)
    norm = 1.0 - decay
    norm = norm * norm
    norm = norm * norm
    gain = length * jnp.sqrt(length) * norm * norm
    coef = jnp.broadcast_to(jnp.concatenate([chi_coef, chi_coef]), (nvars, 2 * levels))
    prm = jnp.stack([length, decay, coef, gain], axis=1)
    place = jnp.stack([i_lat, i_lon]).astype(jnp.int32)

    anywhere = pl.BlockSpec(memory_space=pl.ANY)
    steps = pairs // BLOCK

    def part(v, side):
        return pl.BlockSpec((1, rows, BLOCK * LANES), lambda g: (v, 0, g + side * steps))

    packed_shapes = [(nvars, half, rows, LANES), (nvars, rows, half, LANES), (nvars, 4, half, LANES)]

    def lat_call(nv, first, body, arrays, specs, name, aliases):
        return pl.pallas_call(
            body,
            grid=(steps,),
            in_specs=specs,
            out_specs=[
                pl.BlockSpec((nv, 2 * BLOCK, rows, LANES), lambda g: (first, g, 0, 0)),
                pl.BlockSpec((nv, rows, 2 * BLOCK, LANES), lambda g: (first, 0, g, 0)),
                pl.BlockSpec((nv, 4, 2 * BLOCK, LANES), lambda g: (first, 0, g, 0)),
            ],
            out_shape=[jax.ShapeDtypeStruct(s, f32) for s in packed_shapes],
            scratch_shapes=[
                pltpu.VMEM((2, PAIRS * rows, 256), f32),
                pltpu.VMEM((2, 256, 256), bf16),
                pltpu.VMEM((2, 256, 256), bf16),
                pltpu.VMEM((nvars, pieces, rows, LANES), f32),
            ],
            compiler_params=params(),
            cost_estimate=pl.CostEstimate(
                flops=nv * 60000000, bytes_accessed=nv * 3 * rows * merged * 4, transcendentals=0
            ),
            input_output_aliases=aliases,
            name=name,
        )(*arrays)

    ins = [prm, sigma, vert] + [state] * 4
    specs = [full(x.shape) for x in ins[:3]] + [part(1, 0), part(1, 1), part(2, 0), part(2, 1)]
    wue = lat_call(2, 0, functools.partial(lat_plain, rows, pairs), ins, specs, "lat_chi_temp", {})
    ins = [prm, sigma, vert, bal_temp] + [state] * 5 + [north, south, west, east] + list(wue)
    specs = [full(x.shape) for x in ins[:4]] + [part(0, 0), part(0, 1), part(1, 0), part(1, 1)]
    specs += [pl.BlockSpec((1, rows, merged), lambda g: (2, 0, 0))]
    specs += [full(x.shape) for x in (north, south, west, east)] + [anywhere] * 3
    aliases = {13: 0, 14: 1, 15: 2}
    w, u, edges = lat_call(1, 2, functools.partial(lat_balance, rows, pairs), ins, specs, "lat_psi", aliases)
    gathered = lax.all_gather(edges, "lat")

    rb = BLOCK
    local, el, es = pl.pallas_call(
        functools.partial(lon_kernel, rb),
        grid=(rows // rb,),
        in_specs=[full(prm.shape), pl.BlockSpec((nvars, rb, half, LANES), lambda g: (0, g, 0, 0))],
        out_specs=[
            pl.BlockSpec((nvars, half, rb, LANES), lambda g: (0, 0, g, 0)),
            full((nvars, 4, rows, LANES)),
            full((nvars, 2, rows, LANES)),
        ],
        out_shape=[
            jax.ShapeDtypeStruct((nvars, half, rows, LANES), f32),
            jax.ShapeDtypeStruct((nvars, 4, rows, LANES), f32),
            jax.ShapeDtypeStruct((nvars, 2, rows, LANES), f32),
        ],
        compiler_params=params(),
        cost_estimate=pl.CostEstimate(
            flops=180000000, bytes_accessed=6 * rows * merged * 4, transcendentals=0
        ),
        name="lon_tile",
    )(prm, u)
    es_all = lax.all_gather(es, "lon")

    crossed, elc, esc = pl.pallas_call(
        functools.partial(carry_kernel, n_lat, rows),
        grid=(1,),
        in_specs=[pl.BlockSpec(memory_space=pltpu.SMEM), full(prm.shape), full(gathered.shape)],
        out_specs=[full((nvars, half, 8, LANES)), full((nvars, 4, 8, LANES)), full((nvars, 2, 8, LANES))],
        out_shape=[
            jax.ShapeDtypeStruct((nvars, half, 8, LANES), f32),
            jax.ShapeDtypeStruct((nvars, 4, 8, LANES), f32),
            jax.ShapeDtypeStruct((nvars, 2, 8, LANES), f32),
        ],
        compiler_params=params(),
        cost_estimate=pl.CostEstimate(
            flops=30000000, bytes_accessed=4 * nvars * 5 * n_lat * half * LANES, transcendentals=0
        ),
        name="lon_carry",
    )(place, prm, gathered)
    sent = [esc] + [
        lax.ppermute(esc, "lon", [(i, (i + s) % n_lon) for i in range(n_lon)]) for s in range(1, n_lon)
    ]

    packed = 2 * PAIRS

    def columns(r):
        return pl.BlockSpec((nvars, packed, r, LANES), lambda g: (0, g, 0, 0))

    ins = [place, prm, local, w, crossed, el, es_all, elc] + sent
    specs = [full(x.shape) for x in ins]
    specs[0] = pl.BlockSpec(memory_space=pltpu.SMEM)
    specs[2:5] = [columns(rows), columns(rows), columns(8)]
    y, yx, col, energy = pl.pallas_call(
        functools.partial(join_kernel, n_lon, rows, packed, 24),
        grid=(half // packed,),
        in_specs=specs,
        out_specs=[
            columns(rows),
            pl.BlockSpec((packed, 8, LANES), lambda g: (g, 0, 0)),
            full((2, rows, LANES)),
            full((nvars, 8, LANES)),
        ],
        out_shape=[
            jax.ShapeDtypeStruct((nvars, half, rows, LANES), f32),
            jax.ShapeDtypeStruct((half, 8, LANES), f32),
            jax.ShapeDtypeStruct((2, rows, LANES), f32),
            jax.ShapeDtypeStruct((nvars, 8, LANES), f32),
        ],
        scratch_shapes=[
            pltpu.VMEM((nvars, 4, rows, LANES), f32),
            pltpu.VMEM((nvars, 4, 8, LANES), f32),
            pltpu.VMEM((nvars, 4, half, LANES), f32),
            pltpu.VMEM((nvars, 4, rows, LANES), f32),
            pltpu.VMEM((n_lon, nvars, 2, 8, LANES), f32),
        ],
        compiler_params=params(),
        cost_estimate=pl.CostEstimate(
            flops=60000000, bytes_accessed=9 * rows * merged * 4, transcendentals=0
        ),
        name="join",
    )(*ins)

    index = jnp.arange(count, dtype=jnp.int32)
    same = (owner[:, None] == owner[None, :]) & (index[None, :] < index[:, None])
    slot = jnp.sum(same.astype(jnp.int32), axis=1)
    target = owner * capacity + slot
    hit = target[:, None] == jnp.arange(devices * capacity)[None, :]
    energy = jnp.stack([energy[ORDER.index(v)] for v in range(nvars)])
    energy = jnp.sum(energy, axis=1) * gain
    energy = (energy[:, :levels] + energy[:, levels:]).reshape(count)
    table = jnp.sum(jnp.where(hit, energy[:, None], 0.0), axis=0).reshape(devices, capacity)
    table = lax.all_to_all(table, ("lat", "lon"), split_axis=0, concat_axis=0, tiled=True)
    slab_energy = (jnp.sum(table, axis=0) / (devices * rows * lon))[None, :]

    ins = [prm, sigma, north, south, west, east, vert, bal_temp, col, y, yx]
    specs = [full(x.shape) for x in ins]
    specs[9] = columns(rows)
    specs[10] = pl.BlockSpec((packed, 8, LANES), lambda g: (g, 0, 0))
    applied = pl.pallas_call(
        functools.partial(end_kernel, rows, pairs),
        grid=(half // packed,),
        in_specs=specs,
        out_specs=full(state.shape),
        out_shape=jax.ShapeDtypeStruct(state.shape, f32),
        scratch_shapes=[
            pltpu.VMEM((nvars, PAIRS * rows, 256), f32),
            pltpu.VMEM((8, merged), f32),
            pltpu.VMEM((2, rows, LANES), f32),
            pltpu.VMEM((4, 256, 256), bf16),
            pltpu.VMEM((4, 256, 256), bf16),
            pltpu.VMEM((nvars, pieces, rows, LANES), f32),
            pltpu.VMEM((pieces, 8, LANES), f32),
        ],
        compiler_params=params(),
        cost_estimate=pl.CostEstimate(
            flops=300000000, bytes_accessed=6 * rows * merged * 4, transcendentals=0
        ),
        name="finish",
    )(*ins)
    return (applied, slab_energy)


def solution(mesh):
    return jax.shard_map(
        shards,
        mesh=mesh,
        in_specs=(P(None, "lat", "lon"), P(None, "lat", "lon"), P(), P(), P(), P(), P(), P()),
        out_specs=(P(None, "lat", "lon"), P(("lat", "lon"), None)),
        check_vma=False,
    )
```

time: 204 us -> 169 us (0.83)
  blocking collectives: 70.7 us -> 16.1 us
  waiting for transfers between devices: 23.9 us -> 34.4 us
  starting transfers between devices: 10.6 us -> 19.1 us
  Pallas kernels: 65.3 us -> 71.9 us
  local copies, waits for them, and re-layouts: 13.1 us -> 7.99 us
    psum x1 -> x0, blocking collectives: 38.1 us -> none  [shards(): lax.psum(energy.reshape(count), ('lat', 'lon')) / (devices * rows * lon)]
    all_gather x2 -> x1, blocking collectives: 32.5 us -> 16.1 us  [shards(): es_all = lax.all_gather(es, 'lon')]
    all_gather x2 -> x1, waiting for transfers between devices: 23.9 us -> 34.4 us  [shards(): gathered = lax.all_gather(edges, 'lat')]
    pallas_call x5 -> x6, Pallas kernels: 65.3 us -> 71.9 us  [the longest x2 22.6 us: lat_call(): pl.pallas_call(body, grid=(steps,), in_specs=specs, out_specs=[pl.BlockSp...]
    all_to_all x0 -> x1, starting transfers between devices: none -> 4.46 us  [shards(): lax.all_to_all(table, ('lat', 'lon'), split_axis=0, concat_axis=0, tiled=...]
    another operation x12 -> x2, local copies, waits for them, and re-layouts: 4.47 us -> 0.01 us  [shards(): prm = jnp.stack([length, decay, coef, gain], axis=1)]
    ppermute x4 -> x7, starting transfers between devices: 10.5 us -> 14.6 us  [the longest x3 5.33 us: shards(): lax.ppermute(esc, 'lon', [(i, (i + s) % n_lon) for i in range(n_lon)])]
  transfers between devices with their start and end apart: 6 -> 9, of which waited for: 2 -> 1; matrix products, arithmetic and copies ran while one was open for 7% -> 4% of each run, Pallas kernels for 9% -> 20%
where the time goes in v2:
time: 169 us; the launch traced here: 168 us
  Pallas kernels  71.9 us (43%)
  waiting for transfers between devices  34.4 us (20%)
  starting transfers between devices  19.1 us (11%)
  blocking collectives  16.1 us (10%)
  between operations  14.2 us (8%)
  local copies, waits for them, and re-layouts  7.99 us (5%)
  other arithmetic  4.12 us (2%)
    all_gather x1, waiting for transfers between devices, shards(): gathered = lax.all_gather(edges, 'lat')  34.4 us
    pallas_call x2, Pallas kernels, lat_call(): pl.pallas_call(body, grid=(steps,), in_specs=specs, out_specs=[pl.BlockSp...  22.6 us
    pallas_call x1, Pallas kernels, shards(): pl.pallas_call(functools.partial(join_kernel, n_lon, rows, packed, 24), g...  19.5 us
    all_gather x1, blocking collectives, shards(): es_all = lax.all_gather(es, 'lon')  16.1 us
    pallas_call x1, Pallas kernels, shards(): pl.pallas_call(functools.partial(end_kernel, rows, pairs), grid=(half //...  14 us
    pallas_call x1, Pallas kernels, shards(): pl.pallas_call(functools.partial(lon_kernel, rb), grid=(rows // rb,), in_...  8.7 us
    pallas_call x1, Pallas kernels, shards(): pl.pallas_call(functools.partial(carry_kernel, n_lat, rows), grid=(1,), i...  7.1 us
    ppermute x3, starting transfers between devices, shards(): lax.ppermute(esc, 'lon', [(i, (i + s) % n_lon) for i in range(n_lon)])  5.33 us
  transfers between devices with their start and end apart: 9, of which 1 were waited for; matrix products, arithmetic and copies ran while one was open for 4% of the time, Pallas kernels for 20%

profile of v2, /device:TPU:0, one launch (start us, length us, event | category | flops | bytes accessed | tf_op | source)
XLA Modules:
  0.0 167.8 jit_solution(16299500785929337094)
XLA Ops:
  7.2 0.0 all-gather.4.cloned.1.call-start
  7.2 1.2 slice_bitcast_fusion
  8.4 0.7 slice_bitcast_fusion.4
  9.2 2.4 %collective-permute-start = (f32[1,12480]{1,0:T(1,128)S(1)}, f32[1,12480]{1,0:T(1,128)S(1)}, u32[]{:S(2)}, u32[]{:S(2)}) collective-permute-start(f32[1,12480]{1,0:T(1,128)S(1)} %pad_maximum_fusion), channel_id=1, source_target_pairs={{0,4},{4,8},{8,12},{12,16},{16,20},{20,24},{24,28},{1,5},{5,9},{9,... | collective-permute-start | bytes 149768 | tf_op jit(solution)/shard_map/ppermute | solution.py:555
  11.6 1.3 collective-permute-start.1
  12.9 0.8 slice_bitcast_fusion.2
  13.7 0.9 slice_reduce_fusion
  14.7 0.1 broadcast_in_dim.53
  14.7 0.1 pad_maximum_fusion.2
  14.8 4.3 %collective-permute-start.2 = (f32[48,128]{1,0:T(8,128)S(1)}, f32[48,128]{1,0:T(8,128)S(1)}, u32[]{:S(2)}, u32[]{:S(2)}) collective-permute-start(f32[48,128]{1,0:T(8,128)S(1)} %pad_maximum_fusion.2), channel_id=1, source_target_pairs={{0,1},{1,2},{2,3},{4,5},{5,6},{6,7},{8,9},{9,10},{10,11},{12,13},{... | collective-permute-start | bytes 73736 | tf_op jit(solution)/shard_map/ppermute | solution.py:557
  19.1 0.1 broadcast_in_dim.55
  19.2 0.1 pad_maximum_fusion.3
  19.3 1.3 collective-permute-start.3
  20.6 0.8 reshape.63
  21.3 0.1 pad_add_fusion
  21.4 0.7 select_reduce_fusion.1
  22.2 0.8 pad_maximum_fusion.5
  23.0 0.6 pad_maximum_fusion.4.prm
  23.6 11.2 %lat_chi_temp.1 = (f32[3,96,48,128]{3,2,1,0:T(8,128)}, f32[3,48,96,128]{3,2,1,0:T(8,128)}, f32[3,4,96,128]{3,2,1,0:T(8,128)}) custom-call(f32[3,4,128]{2,1,0:T(4,128)} %pad_maximum_fusion.4.prm, f32[3,48,192]{2,1,0:T(8,128)} %sigma.5, f32[3,64,64]{2,1,0:T(8,128)} %vert.5, f32[3,48,12288]{2,1,0:T(8,128)} %temp.1, f32[3,48,12288]{2,1,0:T(8,128)} %temp.1, ...), custom_call_target="tpu_custom_call" | custom-call | flops 120000000 | bytes 14155776 | tf_op jit(solution)/shard_map/lat_chi_temp/pallas_call | solution.py:582
  34.8 0.0 collective-permute-done.2.west
  34.8 0.0 copy-start.2
  34.8 0.0 collective-permute-done.3.east
  34.9 0.0 copy-start.3
  34.9 0.0 collective-permute-done.north
  34.9 0.0 copy-start
  34.9 0.0 collective-permute-done.1.south
  34.9 0.0 copy-start.1
  34.9 0.5 copy-done.2
  35.4 0.0 copy-done.3
  35.5 0.0 copy-done
  35.5 0.0 copy-done.1
  35.5 0.0 copy-start.7
  35.5 11.3 %lat_psi.1 = (f32[3,96,48,128]{3,2,1,0:T(8,128)}, f32[3,48,96,128]{3,2,1,0:T(8,128)}, f32[3,4,96,128]{3,2,1,0:T(8,128)}) custom-call(f32[3,4,128]{2,1,0:T(4,128)} %pad_maximum_fusion.4.prm, f32[3,48,192]{2,1,0:T(8,128)} %sigma.5, f32[3,64,64]{2,1,0:T(8,128)} %vert.5, f32[64,64]{1,0:T(8,128)} %bal.3, ...), custom_call_target="tpu_custom_call", output_to_operand_aliasing={{0}: (13, {}), {1}: (14, {}), {2}: (15, {})} | custom-call | flops 60000000 | bytes 7077888 | tf_op jit(solution)/shard_map/lat_psi/pallas_call | solution.py:582
  46.9 0.0 all-gather.4.cloned.1.call-update
  46.9 0.6 pad_add_fusion.1.place
  47.5 0.0 copy-done.7
  47.5 0.2 convert_reduce_fusion
  47.7 8.7 %lon_tile.1 = (f32[3,96,48,128]{3,2,1,0:T(8,128)}, f32[3,4,48,128]{3,2,1,0:T(8,128)}, f32[3,2,48,128]{3,2,1,0:T(8,128)}) custom-call(f32[3,4,128]{2,1,0:T(4,128)} %pad_maximum_fusion.4.prm, f32[3,48,96,128]{3,2,1,0:T(8,128)} %get-tuple-element.21.u_ref), custom_call_target="tpu_custom_call" | custom-call | flops 180000000 | bytes 14155776 | tf_op jit(solution)/shard_map/lon_tile/pallas_call | solution.py:618
  56.4 34.4 %all-gather.4.cloned.1.call-done = f32[24,4,96,128]{3,2,1,0:T(8,128)} async-done(((f32[3,4,96,128]{3,2,1,0:T(8,128)}), f32[24,4,96,128]{3,2,1,0:T(8,128)}) %all-gather.4.cloned.1.call-update) | async-done | bytes 4718608 | tf_op jit(solution)/shard_map/all_gather | solution.py:615
  90.8 7.1 %lon_carry.1 = (f32[3,96,8,128]{3,2,1,0:T(8,128)}, f32[3,4,8,128]{3,2,1,0:T(8,128)}, f32[3,2,8,128]{3,2,1,0:T(8,128)}) custom-call(s32[2]{0:T(128)} %pad_add_fusion.1.place, f32[3,4,128]{2,1,0:T(4,128)} %pad_maximum_fusion.4.prm, f32[8,3,4,96,128]{4,3,2,1,0:T(8,128)} %bitcast.19), custom_call_target="tpu_custom_call" | custom-call | flops 30000000 | bytes 5898240 | tf_op jit(solution)/shard_map/lon_carry/pallas_call | solution.py:640
  97.9 1.5 collective-permute-start.4
  99.4 2.4 %collective-permute-start.5 = (f32[3,2,8,128]{3,2,1,0:T(8,128)}, f32[3,2,8,128]{3,2,1,0:T(8,128)S(1)}, u32[]{:S(2)}, u32[]{:S(2)}) collective-permute-start(f32[3,2,8,128]{3,2,1,0:T(8,128)} %get-tuple-element.29.rest_0_), channel_id=1, source_target_pairs={{0,2},{1,3},{2,0},{3,1},{4,6},{5,7},{6,4},{7,5},{8,10},{9,11},{10,... | collective-permute-start | bytes 73736 | tf_op jit(solution)/shard_map/ppermute | solution.py:657
  101.8 1.4 collective-permute-start.6
  103.2 16.1 %all-gather.1 = f32[12,2,48,128]{3,2,1,0:T(8,128)} all-gather(f32[3,2,48,128]{3,2,1,0:T(8,128)} %get-tuple-element.27), channel_id=3, replica_groups=mesh['lat'=8,'lon'=4] {'lon'}, dimensions={0}, use_global_device_ids=true | all-gather | bytes 737280 | tf_op jit(solution)/shard_map/all_gather | solution.py:638
  119.3 0.0 collective-permute-done.4.rest_1_
  119.3 0.0 collective-permute-done.5.rest_2_
  119.3 0.0 copy-start.5
  119.3 0.0 collective-permute-done.6.rest_3_
  119.3 0.0 copy-start.6
  119.4 0.6 copy-done.4
  119.9 0.0 copy-done.5
  120.0 0.0 copy-done.6
  120.0 19.5 %join.1 = (f32[3,96,48,128]{3,2,1,0:T(8,128)}, f32[96,8,128]{2,1,0:T(8,128)}, f32[2,48,128]{2,1,0:T(8,128)}, f32[3,8,128]{2,1,0:T(8,128)}) custom-call(s32[2]{0:T(128)} %pad_add_fusion.1.place, f32[3,4,128]{2,1,0:T(4,128)} %pad_maximum_fusion.4.prm, f32[3,96,48,128]{3,2,1,0:T(8,128)} %get-tuple-element.22.u_ref, f32[3,96,48,128]{3,2,1,0:T(8,128)} %get-tuple-element.23.w_ref, ...), custom_call_target="tpu_custom_call" | custom-call | flops 60000000 | bytes 21233664 | tf_op jit(solution)/shard_map/join/pallas_call | solution.py:669
  139.5 0.7 slice.47
  140.2 0.7 slice.46
  140.9 0.1 slice_add_fusion
  140.9 0.1 broadcast_in_dim.56
  141.0 0.1 select_reduce_fusion
  141.2 0.7 all_to_all.6
  141.9 4.5 %all-to-all-start = ((f32[32,1,7]{2,1,0:T(1,128)}), f32[32,1,7]{2,1,0:T(1,128)S(1)}, u32[]{:S(2)}, u32[]{:S(2)}) async-start(f32[32,1,7]{2,1,0:T(1,128)} %bitcast.10), calls=%async_computation | async-start | bytes 32768 | tf_op jit(solution)/shard_map/all_to_all | solution.py:708
  146.4 14.0 %finish.1 = f32[3,48,12288]{2,1,0:T(8,128)} custom-call(f32[3,4,128]{2,1,0:T(4,128)} %pad_maximum_fusion.4.prm, f32[3,48,192]{2,1,0:T(8,128)} %sigma.5, f32[1,12480]{1,0:T(1,128)} %copy-done, f32[1,12480]{1,0:T(1,128)} %copy-done.1, f32[48,128]{1,0:T(8,128)} %copy-done.2, f32[48,128]{1,0:T(8,128)} %copy-done.3, f32[3,64,64]{2,1,0:T(8,128)} %vert.5, ...), custom_call_target="tpu_custom_call" | custom-call | flops 300000000 | bytes 14155776 | tf_op jit(solution)/shard_map/finish/pallas_call | solution.py:715
  160.4 0.0 all-to-all-done
  160.4 0.1 reduce_sum.49
  160.5 0.5 multiply_bitcast_fusion
  (9 shorter events, 0.2 us)
Async XLA Ops:
  7.2 83.6 %all-gather.4.cloned.1.call-start = ((), (), s32[]{:S(2)}) async-start(), calls=%async_computation.1 | async-start | bytes 5308416 | tf_op jit(solution)/shard_map/all_gather | solution.py:615
  9.2 25.7 %collective-permute-start = (f32[1,12480]{1,0:T(1,128)S(1)}, f32[1,12480]{1,0:T(1,128)S(1)}, u32[]{:S(2)}, u32[]{:S(2)}) collective-permute-start(f32[1,12480]{1,0:T(1,128)S(1)} %pad_maximum_fusion), channel_id=1, source_target_pairs={{0,4},{4,8},{8,12},{12,16},{16,20},{20,24},{24,28},{1,5},{5,9},{9,... | collective-permute-start | bytes 149768 | tf_op jit(solution)/shard_map/ppermute | solution.py:555
  11.6 23.3 %collective-permute-start.1 = (f32[1,12480]{1,0:T(1,128)S(1)}, f32[1,12480]{1,0:T(1,128)S(1)}, u32[]{:S(2)}, u32[]{:S(2)}) collective-permute-start(f32[1,12480]{1,0:T(1,128)S(1)} %pad_maximum_fusion.1), channel_id=1, source_target_pairs={{4,0},{8,4},{12,8},{16,12},{20,16},{24,20},{28,24},{5,1},{9,5},{13... | collective-permute-start | bytes 149768 | tf_op jit(solution)/shard_map/ppermute | solution.py:556
  14.8 20.0 %collective-permute-start.2 = (f32[48,128]{1,0:T(8,128)S(1)}, f32[48,128]{1,0:T(8,128)S(1)}, u32[]{:S(2)}, u32[]{:S(2)}) collective-permute-start(f32[48,128]{1,0:T(8,128)S(1)} %pad_maximum_fusion.2), channel_id=1, source_target_pairs={{0,1},{1,2},{2,3},{4,5},{5,6},{6,7},{8,9},{9,10},{10,11},{12,13},{... | collective-permute-start | bytes 73736 | tf_op jit(solution)/shard_map/ppermute | solution.py:557
  19.3 15.6 %collective-permute-start.3 = (f32[48,128]{1,0:T(8,128)S(1)}, f32[48,128]{1,0:T(8,128)S(1)}, u32[]{:S(2)}, u32[]{:S(2)}) collective-permute-start(f32[48,128]{1,0:T(8,128)S(1)} %pad_maximum_fusion.3), channel_id=1, source_target_pairs={{1,0},{2,1},{3,2},{5,4},{6,5},{7,6},{9,8},{10,9},{11,10},{13,12},{... | collective-permute-start | bytes 73736 | tf_op jit(solution)/shard_map/ppermute | solution.py:558
  34.8 0.6 copy-start.2
  34.9 0.6 copy-start.3
  34.9 0.6 copy-start
  34.9 0.6 copy-start.1
  35.5 12.0 %copy-start.7 = (s32[192]{0:T(256)S(1)}, s32[192]{0:T(256)}, u32[]{:S(2)}) copy-start(s32[192]{0:T(256)} %param.15) | copy-start | bytes 2308
  97.9 21.4 %collective-permute-start.4 = (f32[3,2,8,128]{3,2,1,0:T(8,128)}, f32[3,2,8,128]{3,2,1,0:T(8,128)S(1)}, u32[]{:S(2)}, u32[]{:S(2)}) collective-permute-start(f32[3,2,8,128]{3,2,1,0:T(8,128)} %get-tuple-element.29.rest_0_), channel_id=1, source_target_pairs={{0,1},{1,2},{2,3},{3,0},{4,5},{5,6},{6,7},{7,4},{8,9},{9,10},{10,1... | collective-permute-start | bytes 73736 | tf_op jit(solution)/shard_map/ppermute | solution.py:657
  99.4 19.9 %collective-permute-start.5 = (f32[3,2,8,128]{3,2,1,0:T(8,128)}, f32[3,2,8,128]{3,2,1,0:T(8,128)S(1)}, u32[]{:S(2)}, u32[]{:S(2)}) collective-permute-start(f32[3,2,8,128]{3,2,1,0:T(8,128)} %get-tuple-element.29.rest_0_), channel_id=1, source_target_pairs={{0,2},{1,3},{2,0},{3,1},{4,6},{5,7},{6,4},{7,5},{8,10},{9,11},{10,... | collective-permute-start | bytes 73736 | tf_op jit(solution)/shard_map/ppermute | solution.py:657
  101.8 17.5 %collective-permute-start.6 = (f32[3,2,8,128]{3,2,1,0:T(8,128)}, f32[3,2,8,128]{3,2,1,0:T(8,128)S(1)}, u32[]{:S(2)}, u32[]{:S(2)}) collective-permute-start(f32[3,2,8,128]{3,2,1,0:T(8,128)} %get-tuple-element.29.rest_0_), channel_id=1, source_target_pairs={{0,3},{1,0},{2,1},{3,2},{4,7},{5,4},{6,5},{7,6},{8,11},{9,8},{10,9... | collective-permute-start | bytes 73736 | tf_op jit(solution)/shard_map/ppermute | solution.py:657
  119.3 0.6 copy-start.4
  119.3 0.6 copy-start.5
  119.3 0.6 copy-start.6
  141.9 18.5 %all-to-all-start = ((f32[32,1,7]{2,1,0:T(1,128)}), f32[32,1,7]{2,1,0:T(1,128)S(1)}, u32[]{:S(2)}, u32[]{:S(2)}) async-start(f32[32,1,7]{2,1,0:T(1,128)} %bitcast.10), calls=%async_computation | async-start | bytes 32768 | tf_op jit(solution)/shard_map/all_to_all | solution.py:708
Sparse Core Ops, SparseCore 0:
  47.0 43.7 all-gather.3

commit v3 on v2

--- a/solution.py
+++ b/solution.py
@@ -89,7 +89,17 @@
     return g1, g2, g3, down
 
 
-def solve_carries(n, edge, const, me):
+def pick(all_carries, me):
+    out = []
+    for cs in all_carries:
+        mine = cs[0]
+        for t in range(1, len(cs)):
+            mine = jnp.where(me == t, cs[t], mine)
+        out.append(mine)
+    return out
+
+
+def solve_carries(n, edge, const):
     span, k1, k2, k3 = const
     first = edge(0, 0)
     zero = jnp.zeros_like(first)
@@ -111,13 +121,7 @@
     for t in reversed(range(n)):
         c4[t] = c
         c = edge(t, 3) + k3 * c1[t] + k2 * c2[t] + k1 * c3[t] + span * c
-    out = []
-    for cs in (c1, c2, c3, c4):
-        mine = cs[0]
-        for t in range(1, n):
-            mine = jnp.where(me == t, cs[t], mine)
-        out.append(mine)
-    return out
+    return c1, c2, c3, c4
 
 
 def cascade(count, load, store, decay, start):
@@ -172,9 +176,11 @@
 
     zero = jnp.zeros((u_ref.shape[2], LANES), f32)
     edges = cascade(rows, load, store, decay, [zero] * nv)
+    width = e_ref.shape[2] // 4
     for e in range(4):
         for k in range(nv):
-            e_ref[k, e] = edges[e][k]
+            for c in range(e_ref.shape[0]):
+                e_ref[c, k, e * width : (e + 1) * width] = edges[e][k][c * width : (c + 1) * width]
 
 
 def put_mixed(k, b, rows, res, w_ref, u_ref):
@@ -187,11 +193,33 @@
     u_ref[k, :, at, :] = jnp.swapaxes(w_ref[k, at], 0, 1)
 
 
-def lat_plain(rows, pairs, prm, sigma, vert, b1lo, b1hi, b2lo, b2hi, w_ref, u_ref, e_ref, xs, wh, wl, sg):
+def set_params(scales, classes, chi_coef, prm):
+    coef = jnp.concatenate([chi_coef[...], chi_coef[...]], axis=1)
+    for v in range(3):
+        kind = classes[:, 64 * v : 64 * (v + 1)]
+        kind = jnp.concatenate([kind, kind], axis=1)
+        length = jnp.zeros((1, LANES), f32)
+        for n in range(scales.shape[0]):
+            length = jnp.where(kind == n, scales[n], length)
+        decay = jnp.exp(-1.0 / length)
+        norm = 1.0 - decay
+        norm = norm * norm
+        norm = norm * norm
+        prm[v, 0:1, :] = length
+        prm[v, 1:2, :] = decay
+        prm[v, 2:3, :] = coef
+        prm[v, 3:4, :] = length * jnp.sqrt(length) * norm * norm
+
+
+def lat_plain(
+    rows, pairs, scales, classes, chi_coef, sigma, vert, b1lo, b1hi, b2lo, b2hi,
+    w_ref, u_ref, e_ref, prm, xs, wh, wl, sg,
+):
     g = pl.program_id(0)
 
     @pl.when(g == 0)
     def _():
+        set_params(scales, classes, chi_coef, prm)
         set_weights(wh, wl, 0, vert[1], True)
         set_weights(wh, wl, 1, vert[2], True)
         stage_sigma(sigma, sg, (1, 2))
@@ -235,14 +263,15 @@
     high = (lane >= 64).astype(jnp.int32)
     chi_row = prm[0, 2:3, :]
     last = 2 * pairs - 1
+    beyond = [jnp.concatenate([x[...], x[...]], axis=1) for x in (west, east)]
 
     def at_tile(m):
         return pl.ds(pl.multiple_of(m * LANES, LANES), LANES)
 
     def laplace(m):
         x = temp[0, :, at_tile(m)]
-        left = jnp.where(m == 0, swap(west[...]), temp[0, :, at_tile(jnp.maximum(m - 1, 0))])
-        right = jnp.where(m == last, east[...], temp[0, :, at_tile(jnp.minimum(m + 1, last))])
+        left = jnp.where(m == 0, beyond[0], temp[0, :, at_tile(jnp.maximum(m - 1, 0))])
+        right = jnp.where(m == last, beyond[1], temp[0, :, at_tile(jnp.minimum(m + 1, last))])
         beside = swap(x + jnp.where(lane >= 64, left, right))
         above = jnp.where(row_id == 0, north[:, at_tile(m)], pltpu.roll(x, 1, 0))
         below = jnp.where(row_id == rows - 1, south[:, at_tile(m)], pltpu.roll(x, rows - 1, 0))
@@ -294,15 +323,21 @@
         t4 = e4 + k3 * c1 + k2 * c2 + k1 * c3
         c4 = jnp.where(low, swap(t4), 0.0)
         t4 = t4 + span * c4
-        es_ref[k, 0, at, :] = jnp.where(low, t2, t1)
-        es_ref[k, 1, at, :] = jnp.where(low, t4, t3)
+        es_ref[2 * k, at, :] = jnp.where(low, t2, t1)
+        es_ref[2 * k + 1, at, :] = jnp.where(low, t4, t3)
         for e, x in enumerate((e1, e2, e3, e4)):
             el_ref[k, e, at, :] = x
 
 
-def lon_kernel(rb, prm, u_ref, o_ref, el_ref, es_ref):
+def lon_kernel(rb, prm, sigma, u_ref, o_ref, el_ref, es_ref):
     g = pl.program_id(0)
     half = u_ref.shape[2]
+
+    @pl.when(g == 0)
+    def _():
+        x = sigma[0]
+        lon = x.shape[1]
+        es_ref[6] = jnp.where(low_lanes((x.shape[0], LANES)), x[:, 0:1], x[:, lon - 1 : lon])
 
     def turn(b, _):
         at = pl.ds(pl.multiple_of(b * 8, 8), 8)
@@ -315,91 +350,98 @@
     lon_filter(prm, rb, o_ref, el_ref, es_ref, pl.ds(pl.multiple_of(g * rb, 8), rb))
 
 
-def carry_kernel(n_lat, rows, place, prm, gathered, o_ref, el_ref, es_ref):
-    half = o_ref.shape[1]
-    me = place[0]
+def solve_kernel(n_lat, rows, prm, edges, carries):
+    width = edges.shape[2] // 4
     for k, v in enumerate(ORDER):
         const = constants(prm[v, 0:1, :], prm[v, 1:2, :], rows)
-
-        def body(b, _, k=k, const=const):
-            at = pl.ds(pl.multiple_of(b * 8, 8), 8)
-            c = solve_carries(n_lat, lambda t, e: gathered[t, k, e, at, :], const, me)
-            block = jnp.stack(c + [jnp.zeros_like(c[0])] * 4, axis=0)
-            o_ref[k, at] = jnp.swapaxes(block, 0, 1)
-            return 0
-
-        lax.fori_loop(0, half // 8, body, 0)
-    lon_filter(prm, 8, o_ref, el_ref, es_ref, pl.ds(0, 8))
-
-
-def join_kernel(n_lon, rows, packed, rq, place, prm, u_ref, w_ref, x_ref, el, es, elc, *rest):
-    sent = rest[:n_lon]
-    y_ref, yx_ref, col_ref, energy, carry, extra, resp_x, resp_y, esx = rest[n_lon:]
+        c = solve_carries(n_lat, lambda t, e: edges[t, k, e * width : (e + 1) * width, :], const)
+        for e in range(4):
+            for t in range(n_lat):
+                carries[t, k, e * width : (e + 1) * width, :] = c[e][t]
+
+
+def carry_kernel(prm, carries, o_ref, el_ref, es_ref):
+    width = carries.shape[2] // 4
+    zero = jnp.zeros((8, LANES), f32)
+
+    def body(d, _):
+        for k in range(len(ORDER)):
+            for j in range(width):
+                at = d * width + j
+                o_ref[k, at] = zero
+                for e in range(4):
+                    o_ref[k, at, e : e + 1, :] = carries[d, k, e * width + j : e * width + j + 1, :]
+        return 0
+
+    lax.fori_loop(0, carries.shape[0], body, 0)
+    lon_filter(prm, 8, o_ref, el_ref, es_ref, slice(0, 8))
+
+
+def join_kernel(n_lon, rows, packed, rq, place, prm, u_ref, w_ref, x_ref, el, elc, *rest):
+    sent, sent_x = rest[:n_lon], rest[n_lon : 2 * n_lon]
+    y_ref, yx_ref, col_ref, side_ref, energy, carry, extra, resp_x, resp_y, esm, esx = rest[2 * n_lon :]
     g = pl.program_id(0)
     half = resp_x.shape[2]
     lat, me = place[0], place[1]
-    low8 = low_lanes((8, LANES))
 
     @pl.when(g == 0)
     def _():
         energy[...] = jnp.zeros_like(energy)
         for s in range(n_lon):
-            esx[lax.rem(me - s + n_lon, n_lon)] = sent[s][...]
+            t = lax.rem(me - s + n_lon, n_lon)
+            esm[t] = sent[s][...]
+            esx[t] = sent_x[s][...]
+        side_ref[0] = esm[jnp.maximum(me - 1, 0), 6]
+        side_ref[1] = esm[jnp.minimum(me + 1, n_lon - 1), 6]
         for k, v in enumerate(ORDER):
             length = prm[v, 0:1, :]
             decay = prm[v, 1:2, :]
             whole = constants(length, decay, 2 * half)
             span, k1, k2, k3 = constants(length, decay, half)
 
-            def solve(gathered, own, at, k=k, whole=whole, half_c=(span, k1, k2, k3)):
+            def solve(gathered, own, k=k, whole=whole, half_c=(span, k1, k2, k3)):
                 span, k1, k2, k3 = half_c
+                low = low_lanes(own.shape[2:])
                 cache = {}
 
                 def edge(t, e):
                     if (t, e // 2) not in cache:
-                        x = gathered[t, k, e // 2, at, :]
+                        x = gathered[t, 2 * k + e // 2]
                         y = swap(x)
-                        cache[t, e // 2] = (jnp.where(low8, y, x), jnp.where(low8, x, y))
+                        cache[t, e // 2] = (jnp.where(low, y, x), jnp.where(low, x, y))
                     return cache[t, e // 2][e % 2]
 
-                d1, d2, d3, d4 = solve_carries(n_lon, edge, whole, me)
-                e1, e2, e3, e4 = (own[k, e, at, :] for e in range(4))
-                c1 = jnp.where(low8, d1, swap(e1 + span * d1))
-                c2 = jnp.where(low8, swap(e2 + k1 * c1 + span * d2), d2)
-                c3 = jnp.where(low8, d3, swap(e3 + k2 * c1 + k1 * c2 + span * d3))
-                c4 = jnp.where(low8, swap(e4 + k3 * c1 + k2 * c2 + k1 * c3 + span * d4), d4)
+                d1, d2, d3, d4 = pick(solve_carries(n_lon, edge, whole), me)
+                e1, e2, e3, e4 = (own[k, e] for e in range(4))
+                c1 = jnp.where(low, d1, swap(e1 + span * d1))
+                c2 = jnp.where(low, swap(e2 + k1 * c1 + span * d2), d2)
+                c3 = jnp.where(low, d3, swap(e3 + k2 * c1 + k1 * c2 + span * d3))
+                c4 = jnp.where(low, swap(e4 + k3 * c1 + k2 * c2 + k1 * c3 + span * d4), d4)
                 return (c1, c2, c3, c4), d3, d4
 
             for e, r in enumerate(responses(length, decay, half)):
                 resp_x[k, e] = r
-            for e, r in enumerate(responses(length, decay, rows)):
-                resp_y[k, e] = r
-            cc, f3, f4 = solve(esx, elc, slice(0, 8))
+            ry = responses(length, decay, rows)
+            for e in range(4):
+                resp_y[k, e] = ry[e]
+            cc, f3, f4 = solve(esx, elc)
+            c, d3, d4 = solve(esm, el)
+
+            def total(x, rows_of, ry=ry):
+                for e in range(4):
+                    x = x + ry[e] * rows_of[e : e + 1, :]
+                return x
+
             for e in range(4):
                 extra[k, e] = cc[e]
-
-            def body(b, _, k=k, v=v, cc=cc, f3=f3, f4=f4, solve=solve):
-                at = pl.ds(pl.multiple_of(b * 8, 8), 8)
-                c, d3, d4 = solve(es, el, at)
-                ry = [resp_y[k, e, at, :] for e in range(4)]
-
-                def total(x, rows_of):
-                    for e in range(4):
-                        x = x + ry[e] * rows_of[e : e + 1, :]
-                    return x
-
-                for e in range(4):
-                    carry[k, e, at, :] = total(c[e], cc[e])
-                if v == 0:
-                    col_ref[0, at, :] = total(d3, f3)
-                    col_ref[1, at, :] = total(d4, f4)
-                return 0
-
-            lax.fori_loop(0, rows // 8, body, 0)
+                carry[k, e] = total(c[e], cc[e])
+            if v == 0:
+                col_ref[0] = total(d3, f3)
+                col_ref[1] = total(d4, f4)
 
     row8 = lax.broadcasted_iota(jnp.int32, (8, LANES), 0)
     for k, v in enumerate(ORDER):
-        total = jnp.zeros((8, LANES), f32)
+        total = jnp.zeros((rq, LANES), f32)
         for q in range(0, rows, rq):
             at = slice(q, q + rq)
             c = [carry[k, e, at, :] for e in range(4)]
@@ -415,9 +457,7 @@
                     for e in range(4):
                         y = y + rx[e][o : o + 1, :] * c[e] + ry[e] * x[e : e + 1, :]
                     y_ref[k, p, at, :] = y
-                    t = y * w_ref[k, p, at, :]
-                    for i in range(0, rq, 8):
-                        total = total + t[i : i + 8]
+                    total = total + y * w_ref[k, p, at, :]
                     if v == 0 and q == 0:
                         for e in range(4):
                             x = x + rx[e][o : o + 1, :] * extra[k, e]
@@ -427,7 +467,7 @@
                 return total
 
             total = lax.fori_loop(0, packed // 8, body, total)
-        energy[k] += total
+        energy[k] += jnp.sum(total.reshape(rq // 8, 8, LANES), axis=0)
 
     @pl.when(g == 0)
     def _():
@@ -436,12 +476,11 @@
 
 
 def end_kernel(
-    rows, pairs, prm, sigma, north, south, west, east, vert, bal, col, y_ref, yx_ref,
+    rows, pairs, prm, sigma, north, south, vert, bal, col, side, y_ref, yx_ref,
     out, xs, zx, zc, wh, wl, sg, sx,
 ):
     g = pl.program_id(0)
     half = 2 * pairs
-    merged = out.shape[2]
     lon = sigma.shape[2]
 
     @pl.when(g == 0)
@@ -453,13 +492,13 @@
         stage_sigma(sigma, sg, (0, 1, 2))
         for at in range(0, lon, LANES):
             width = min(LANES, lon - at)
-            sx[at // LANES, 0:1, 0:width] = north[:, merged + at : merged + at + width]
-            sx[at // LANES, 1:2, 0:width] = south[:, merged + at : merged + at + width]
+            sx[at // LANES, 0:1, 0:width] = north[:, at : at + width]
+            sx[at // LANES, 1:2, 0:width] = south[:, at : at + width]
         lhs = jnp.where(low_lanes((rows, LANES)), col[0], col[1])
         lhs = jnp.concatenate([lhs, jnp.zeros_like(lhs)], axis=1)
         res = product(lhs, wh[0], wl[0])
-        zc[0] = swap(res[:, :LANES] * swap(west[...]))
-        zc[1] = res[:, LANES:] * swap(east[...])
+        zc[0] = swap(res[:, :LANES] * swap(side[0]))
+        zc[1] = res[:, LANES:] * side[1]
 
     lane = lax.broadcasted_iota(jnp.int32, (rows, LANES), 1)
     high = (lane >= 64).astype(jnp.int32)
@@ -543,31 +582,10 @@
 
     up_lat, up_lon = ([(i, i + 1) for i in range(n - 1)] for n in (n_lat, n_lon))
     down_lat, down_lon = ([(j, i) for i, j in up] for up in (up_lat, up_lon))
-
-    def row(i):
-        return jnp.concatenate([state[2, i : i + 1, :], sigma[0, i : i + 1, :]], axis=1)
-
-    def column(j):
-        temp = state[2, :, j * levels : (j + 1) * levels]
-        sig = jnp.broadcast_to(sigma[0, :, j : j + 1], (rows, levels))
-        return jnp.concatenate([temp, sig], axis=1)
-
-    north = lax.ppermute(row(rows - 1), "lat", up_lat)
-    south = lax.ppermute(row(0), "lat", down_lat)
-    west = lax.ppermute(column(lon - 1), "lon", up_lon)
-    east = lax.ppermute(column(0), "lon", down_lon)
-
-    class_ids = jnp.arange(scales.shape[0], dtype=jnp.int32)
-    kind = classes.reshape(nvars, levels)
-    kind = jnp.concatenate([kind, kind], axis=1)
-    length = jnp.sum(jnp.where(kind[:, None, :] == class_ids[None, :, None], scales[None, :, None], 0.0), axis=1)
-    decay = jnp.exp(-1.0 / length)
-    norm = 1.0 - decay
-    norm = norm * norm
-    norm = norm * norm
-    gain = length * jnp.sqrt(length) * norm * norm
-    coef = jnp.broadcast_to(jnp.concatenate([chi_coef, chi_coef]), (nvars, 2 * levels))
-    prm = jnp.stack([length, decay, coef, gain], axis=1)
+    north = lax.ppermute(state[2, rows - 1 : rows, :], "lat", up_lat)
+    south = lax.ppermute(state[2, 0:1, :], "lat", down_lat)
+    west = lax.ppermute(state[2, :, merged - levels :], "lon", up_lon)
+    east = lax.ppermute(state[2, :, :levels], "lon", down_lon)
     place = jnp.stack([i_lat, i_lon]).astype(jnp.int32)
 
     anywhere = pl.BlockSpec(memory_space=pl.ANY)
@@ -576,9 +594,10 @@
     def part(v, side):
         return pl.BlockSpec((1, rows, BLOCK * LANES), lambda g: (v, 0, g + side * steps))
 
-    packed_shapes = [(nvars, half, rows, LANES), (nvars, rows, half, LANES), (nvars, 4, half, LANES)]
-
-    def lat_call(nv, first, body, arrays, specs, name, aliases):
+    width = half // n_lat
+    shapes = [(nvars, half, rows, LANES), (nvars, rows, half, LANES), (n_lat, nvars, 4 * width, LANES)]
+
+    def lat_call(nv, first, body, arrays, specs, name, aliases, more=()):
         return pl.pallas_call(
             body,
             grid=(steps,),
@@ -586,9 +605,10 @@
             out_specs=[
                 pl.BlockSpec((nv, 2 * BLOCK, rows, LANES), lambda g: (first, g, 0, 0)),
                 pl.BlockSpec((nv, rows, 2 * BLOCK, LANES), lambda g: (first, 0, g, 0)),
-                pl.BlockSpec((nv, 4, 2 * BLOCK, LANES), lambda g: (first, 0, g, 0)),
-            ],
-            out_shape=[jax.ShapeDtypeStruct(s, f32) for s in packed_shapes],
+                pl.BlockSpec((2 * BLOCK // width, nv, 4 * width, LANES), lambda g: (g, first, 0, 0)),
+            ]
+            + [full(s) for s in more],
+            out_shape=[jax.ShapeDtypeStruct(s, f32) for s in shapes + list(more)],
             scratch_shapes=[
                 pltpu.VMEM((2, PAIRS * rows, 256), f32),
                 pltpu.VMEM((2, 256, 256), bf16),
@@ -603,70 +623,98 @@
             name=name,
         )(*arrays)
 
-    ins = [prm, sigma, vert] + [state] * 4
-    specs = [full(x.shape) for x in ins[:3]] + [part(1, 0), part(1, 1), part(2, 0), part(2, 1)]
-    wue = lat_call(2, 0, functools.partial(lat_plain, rows, pairs), ins, specs, "lat_chi_temp", {})
+    ins = [scales, classes.reshape(1, count), chi_coef.reshape(1, levels), sigma, vert] + [state] * 4
+    specs = [full(x.shape) for x in ins[:5]] + [part(1, 0), part(1, 1), part(2, 0), part(2, 1)]
+    specs[0] = pl.BlockSpec(memory_space=pltpu.SMEM)
+    body = functools.partial(lat_plain, rows, pairs)
+    *wue, prm = lat_call(2, 0, body, ins, specs, "lat_chi_temp", {}, [(nvars, 4, LANES)])
     ins = [prm, sigma, vert, bal_temp] + [state] * 5 + [north, south, west, east] + list(wue)
     specs = [full(x.shape) for x in ins[:4]] + [part(0, 0), part(0, 1), part(1, 0), part(1, 1)]
     specs += [pl.BlockSpec((1, rows, merged), lambda g: (2, 0, 0))]
     specs += [full(x.shape) for x in (north, south, west, east)] + [anywhere] * 3
     aliases = {13: 0, 14: 1, 15: 2}
     w, u, edges = lat_call(1, 2, functools.partial(lat_balance, rows, pairs), ins, specs, "lat_psi", aliases)
-    gathered = lax.all_gather(edges, "lat")
+    def trade(x):
+        return lax.all_to_all(x, "lat", split_axis=0, concat_axis=0, tiled=True)
+
+    shares = trade(edges)
 
     rb = BLOCK
     local, el, es = pl.pallas_call(
         functools.partial(lon_kernel, rb),
         grid=(rows // rb,),
-        in_specs=[full(prm.shape), pl.BlockSpec((nvars, rb, half, LANES), lambda g: (0, g, 0, 0))],
+        in_specs=[
+            full(prm.shape),
+            pl.BlockSpec((1, rows, lon), lambda g: (0, 0, 0)),
+            pl.BlockSpec((nvars, rb, half, LANES), lambda g: (0, g, 0, 0)),
+        ],
         out_specs=[
             pl.BlockSpec((nvars, half, rb, LANES), lambda g: (0, 0, g, 0)),
             full((nvars, 4, rows, LANES)),
-            full((nvars, 2, rows, LANES)),
+            full((7, rows, LANES)),
         ],
         out_shape=[
             jax.ShapeDtypeStruct((nvars, half, rows, LANES), f32),
             jax.ShapeDtypeStruct((nvars, 4, rows, LANES), f32),
-            jax.ShapeDtypeStruct((nvars, 2, rows, LANES), f32),
+            jax.ShapeDtypeStruct((7, rows, LANES), f32),
         ],
         compiler_params=params(),
         cost_estimate=pl.CostEstimate(
             flops=180000000, bytes_accessed=6 * rows * merged * 4, transcendentals=0
         ),
         name="lon_tile",
-    )(prm, u)
-    es_all = lax.all_gather(es, "lon")
+    )(prm, sigma, u)
+
+    def round_lon(x):
+        return [x] + [
+            lax.ppermute(x, "lon", [(i, (i + s) % n_lon) for i in range(n_lon)]) for s in range(1, n_lon)
+        ]
+
+    sent = round_lon(es)
+    carries = pl.pallas_call(
+        functools.partial(solve_kernel, n_lat, rows),
+        grid=(1,),
+        in_specs=[full(prm.shape), full(shares.shape)],
+        out_specs=full(shares.shape),
+        out_shape=jax.ShapeDtypeStruct(shares.shape, f32),
+        compiler_params=params(),
+        cost_estimate=pl.CostEstimate(flops=1000000, bytes_accessed=2 * shares.size * 4, transcendentals=0),
+        name="solve",
+    )(prm, shares)
+    carries = trade(carries)
+
+    row, _ = lax.optimization_barrier((sigma[0], es))
+    sig_n = lax.ppermute(row[rows - 1 : rows], "lat", up_lat)
+    sig_s = lax.ppermute(row[0:1], "lat", down_lat)
 
     crossed, elc, esc = pl.pallas_call(
-        functools.partial(carry_kernel, n_lat, rows),
+        carry_kernel,
         grid=(1,),
-        in_specs=[pl.BlockSpec(memory_space=pltpu.SMEM), full(prm.shape), full(gathered.shape)],
-        out_specs=[full((nvars, half, 8, LANES)), full((nvars, 4, 8, LANES)), full((nvars, 2, 8, LANES))],
+        in_specs=[full(prm.shape), full(carries.shape)],
+        out_specs=[full((nvars, half, 8, LANES)), full((nvars, 4, 8, LANES)), full((6, 8, LANES))],
         out_shape=[
             jax.ShapeDtypeStruct((nvars, half, 8, LANES), f32),
             jax.ShapeDtypeStruct((nvars, 4, 8, LANES), f32),
-            jax.ShapeDtypeStruct((nvars, 2, 8, LANES), f32),
+            jax.ShapeDtypeStruct((6, 8, LANES), f32),
         ],
         compiler_params=params(),
         cost_estimate=pl.CostEstimate(
-            flops=30000000, bytes_accessed=4 * nvars * 5 * n_lat * half * LANES, transcendentals=0
+            flops=30000000, bytes_accessed=4 * nvars * 12 * half * LANES, transcendentals=0
         ),
         name="lon_carry",
-    )(place, prm, gathered)
-    sent = [esc] + [
-        lax.ppermute(esc, "lon", [(i, (i + s) % n_lon) for i in range(n_lon)]) for s in range(1, n_lon)
-    ]
+    )(prm, carries)
+    sent_x = round_lon(esc)
 
     packed = 2 * PAIRS
 
     def columns(r):
         return pl.BlockSpec((nvars, packed, r, LANES), lambda g: (0, g, 0, 0))
 
-    ins = [place, prm, local, w, crossed, el, es_all, elc] + sent
+    ins = [place, prm, local, w, crossed, el, elc] + sent + sent_x
     specs = [full(x.shape) for x in ins]
     specs[0] = pl.BlockSpec(memory_space=pltpu.SMEM)
     specs[2:5] = [columns(rows), columns(rows), columns(8)]
-    y, yx, col, energy = pl.pallas_call(
+    y, yx, col, side, energy = pl.pallas_call(
         functools.partial(join_kernel, n_lon, rows, packed, 24),
         grid=(half // packed,),
         in_specs=specs,
@@ -674,11 +722,13 @@
             columns(rows),
             pl.BlockSpec((packed, 8, LANES), lambda g: (g, 0, 0)),
             full((2, rows, LANES)),
+            full((2, rows, LANES)),
             full((nvars, 8, LANES)),
         ],
         out_shape=[
             jax.ShapeDtypeStruct((nvars, half, rows, LANES), f32),
             jax.ShapeDtypeStruct((half, 8, LANES), f32),
+            jax.ShapeDtypeStruct((2, rows, LANES), f32),
             jax.ShapeDtypeStruct((2, rows, LANES), f32),
             jax.ShapeDtypeStruct((nvars, 8, LANES), f32),
         ],
@@ -687,7 +737,8 @@
             pltpu.VMEM((nvars, 4, 8, LANES), f32),
             pltpu.VMEM((nvars, 4, half, LANES), f32),
             pltpu.VMEM((nvars, 4, rows, LANES), f32),
-            pltpu.VMEM((n_lon, nvars, 2, 8, LANES), f32),
+            pltpu.VMEM((n_lon, 7, rows, LANES), f32),
+            pltpu.VMEM((n_lon, 6, 8, LANES), f32),
         ],
         compiler_params=params(),
         cost_estimate=pl.CostEstimate(
@@ -702,16 +753,16 @@
     target = owner * capacity + slot
     hit = target[:, None] == jnp.arange(devices * capacity)[None, :]
     energy = jnp.stack([energy[ORDER.index(v)] for v in range(nvars)])
-    energy = jnp.sum(energy, axis=1) * gain
+    energy = jnp.sum(energy, axis=1) * prm[:, 3]
     energy = (energy[:, :levels] + energy[:, levels:]).reshape(count)
     table = jnp.sum(jnp.where(hit, energy[:, None], 0.0), axis=0).reshape(devices, capacity)
     table = lax.all_to_all(table, ("lat", "lon"), split_axis=0, concat_axis=0, tiled=True)
     slab_energy = (jnp.sum(table, axis=0) / (devices * rows * lon))[None, :]
 
-    ins = [prm, sigma, north, south, west, east, vert, bal_temp, col, y, yx]
+    ins = [prm, sigma, sig_n, sig_s, vert, bal_temp, col, side, y, yx]
     specs = [full(x.shape) for x in ins]
-    specs[9] = columns(rows)
-    specs[10] = pl.BlockSpec((packed, 8, LANES), lambda g: (g, 0, 0))
+    specs[8] = columns(rows)
+    specs[9] = pl.BlockSpec((packed, 8, LANES), lambda g: (g, 0, 0))
     applied = pl.pallas_call(
         functools.partial(end_kernel, rows, pairs),
         grid=(half // packed,),

time: 169 us -> 133 us (0.79)
  starting transfers between devices: 19.1 us -> 44.4 us
  waiting for transfers between devices: 34.4 us -> 12.5 us
  blocking collectives: 16.1 us -> 0 us
  between operations: 14.2 us -> 0.89 us
  Pallas kernels: 71.9 us -> 63.4 us
  other arithmetic: 4.12 us -> 1.63 us
    all_gather x1 -> x0, waiting for transfers between devices: 34.4 us -> none  [shards(): gathered = lax.all_gather(edges, 'lat')]
    all_gather x1 -> x0, blocking collectives: 16.1 us -> none  [shards(): es_all = lax.all_gather(es, 'lon')]
    ppermute x7 -> x12, starting transfers between devices: 14.6 us -> 25.1 us  [the longest x6 12.8 us: round_lon(): lax.ppermute(x, 'lon', [(i, (i + s) % n_lon) for i in range(n_lon)])]
    all_to_all x0 -> x2, waiting for transfers between devices: none -> 10.3 us  [trade(): return lax.all_to_all(x, 'lat', split_axis=0, concat_axis=0, tiled=True)]
    all_to_all x0 -> x2, starting transfers between devices: none -> 9.8 us  [trade(): return lax.all_to_all(x, 'lat', split_axis=0, concat_axis=0, tiled=True)]
    pallas_call x1, Pallas kernels: 19.5 us -> 12.8 us  [shards(): pl.pallas_call(functools.partial(join_kernel, n_lon, rows, packed, 24), g...]
    all_to_all x1, starting transfers between devices: 4.46 us -> 9.51 us  [shards(): lax.all_to_all(table, ('lat', 'lon'), split_axis=0, concat_axis=0, tiled=...]
    ppermute x7 -> x12, waiting for transfers between devices: 0.02 us -> 2.29 us  [the longest x6 2.27 us: round_lon(): lax.ppermute(x, 'lon', [(i, (i + s) % n_lon) for i in range(n_lon)])]
  transfers between devices with their start and end apart: 9 -> 15, of which waited for: 1 -> 3; matrix products, arithmetic and copies ran while one was open for 4% -> 4% of each run, Pallas kernels for 20% -> 38%
where the time goes in v3:
time: 133 us; the launch traced here: 132 us
  Pallas kernels  63.4 us (48%)
  starting transfers between devices  44.4 us (33%)
  waiting for transfers between devices  12.5 us (9%)
  local copies, waits for them, and re-layouts  9.12 us (7%)
  other arithmetic  1.63 us (1%)
    pallas_call x2, Pallas kernels, lat_call(): pl.pallas_call(body, grid=(steps,), in_specs=specs, out_specs=[pl.BlockSp...  22.2 us
    pallas_call x1, Pallas kernels, shards(): pl.pallas_call(functools.partial(end_kernel, rows, pairs), grid=(half //...  14 us
    pallas_call x1, Pallas kernels, shards(): pl.pallas_call(functools.partial(join_kernel, n_lon, rows, packed, 24), g...  12.8 us
    ppermute x6, starting transfers between devices, round_lon(): lax.ppermute(x, 'lon', [(i, (i + s) % n_lon) for i in range(n_lon)])  12.8 us
    all_to_all x2, waiting for transfers between devices, trade(): return lax.all_to_all(x, 'lat', split_axis=0, concat_axis=0, tiled=True)  10.3 us
    all_to_all x2, starting transfers between devices, trade(): return lax.all_to_all(x, 'lat', split_axis=0, concat_axis=0, tiled=True)  9.8 us
    all_to_all x1, starting transfers between devices, shards(): lax.all_to_all(table, ('lat', 'lon'), split_axis=0, concat_axis=0, tiled=...  9.51 us
    pallas_call x1, Pallas kernels, shards(): pl.pallas_call(functools.partial(lon_kernel, rb), grid=(rows // rb,), in_...  8.77 us
  transfers between devices with their start and end apart: 15, of which 3 were waited for; matrix products, arithmetic and copies ran while one was open for 4% of the time, Pallas kernels for 38%

profile of v3, /device:TPU:0, one launch (start us, length us, event | category | flops | bytes accessed | tf_op | source)
XLA Modules:
  0.0 132.0 jit_solution(48983520951084099)
XLA Ops:
  0.6 1.2 slice_bitcast_fusion
  1.8 2.4 %collective-permute-start = (f32[1,12288]{1,0:T(1,128)S(1)}, f32[1,12288]{1,0:T(1,128)S(1)}, u32[]{:S(2)}, u32[]{:S(2)}) collective-permute-start(f32[1,12288]{1,0:T(1,128)S(1)} %get-tuple-element.43), channel_id=1, source_target_pairs={{0,4},{4,8},{8,12},{12,16},{16,20},{20,24},{24,28},{1,5},{5,9},{9,... | collective-permute-start | bytes 147464 | tf_op jit(solution)/shard_map/ppermute | solution.py:585
  4.2 1.3 collective-permute-start.1
  5.5 0.8 slice_bitcast_fusion.3
  6.3 4.3 %collective-permute-start.2 = (f32[48,64]{1,0:T(8,128)S(1)}, f32[48,64]{1,0:T(8,128)S(1)}, u32[]{:S(2)}, u32[]{:S(2)}) collective-permute-start(f32[48,64]{1,0:T(8,128)S(1)} %get-tuple-element.41), channel_id=1, source_target_pairs={{0,1},{1,2},{2,3},{4,5},{5,6},{6,7},{8,9},{9,10},{10,11},{12,13},{... | collective-permute-start | bytes 36872 | tf_op jit(solution)/shard_map/ppermute | solution.py:587
  10.6 1.3 collective-permute-start.3
  11.9 11.2 %lat_chi_temp.1 = (f32[3,96,48,128]{3,2,1,0:T(8,128)}, f32[3,48,96,128]{3,2,1,0:T(8,128)}, f32[8,3,48,128]{3,2,1,0:T(8,128)}, f32[3,4,128]{2,1,0:T(4,128)}) custom-call(f32[8]{0:T(128)} %scales.1, s32[1,192]{1,0:T(1,128)} %bitcast.19, f32[1,64]{1,0:T(1,128)} %bitcast.20, f32[3,48,192]{2,1,0:T(8,128)} %sigma.7, f32[3,64,64]{2,1,0:T(8,128)} %vert.5, ...), custom_call_target="tpu_custom_call" | custom-call | flops 120000000 | bytes 14155776 | tf_op jit(solution)/shard_map/lat_chi_temp/pallas_call | solution.py:601
  23.2 0.0 collective-permute-done.2.west
  23.2 0.0 copy-start.10
  23.2 0.0 collective-permute-done.3.east
  23.2 0.0 copy-start.11
  23.2 0.0 collective-permute-done.north
  23.2 0.0 collective-permute-done.1.south
  23.2 0.5 copy-done.10
  23.8 0.0 copy-done.11
  23.8 0.1 copy-done.5
  23.8 11.0 %lat_psi.1 = (f32[3,96,48,128]{3,2,1,0:T(8,128)}, f32[3,48,96,128]{3,2,1,0:T(8,128)}, f32[8,3,48,128]{3,2,1,0:T(8,128)}) custom-call(f32[3,4,128]{2,1,0:T(4,128)} %get-tuple-element.21.prm, f32[3,48,192]{2,1,0:T(8,128)} %sigma.7, f32[3,64,64]{2,1,0:T(8,128)} %vert.5, f32[64,64]{1,0:T(8,128)} %bal.3, ...), custom_call_target="tpu_custom_call", output_to_operand_aliasing={{0}: (13, {}), {1}: (14, {}), {2}: (15, {})} | custom-call | flops 60000000 | bytes 7077888 | tf_op jit(solution)/shard_map/lat_psi/pallas_call | solution.py:601
  34.8 6.3 %all-to-all-start = ((f32[8,3,48,128]{3,2,1,0:T(8,128)}), f32[8,3,48,128]{3,2,1,0:T(8,128)S(1)}, u32[]{:S(2)}, u32[]{:S(2)}) async-start(f32[8,3,48,128]{3,2,1,0:T(8,128)} %get-tuple-element.30), calls=%async_computation | async-start | bytes 1179648 | tf_op jit(solution)/shard_map/all_to_all | solution.py:638
  41.1 0.0 copy-done.12
  41.1 0.2 convert_reduce_fusion
  41.3 10.3 %all-to-all-done.edges = f32[8,3,48,128]{3,2,1,0:T(8,128)S(1)} async-done(((f32[8,3,48,128]{3,2,1,0:T(8,128)}), f32[8,3,48,128]{3,2,1,0:T(8,128)S(1)}, u32[]{:S(2)}, u32[]{:S(2)}) %all-to-all-start) | async-done | bytes 589856 | tf_op jit(solution)/shard_map/all_to_all | solution.py:638
  51.5 0.8 copy-done.1
  52.4 2.1 %solve.1 = f32[8,3,48,128]{3,2,1,0:T(8,128)} custom-call(f32[3,4,128]{2,1,0:T(4,128)} %get-tuple-element.21.prm, f32[8,3,48,128]{3,2,1,0:T(8,128)} %copy-done.1), custom_call_target="tpu_custom_call" | custom-call | flops 1000000 | bytes 1179648 | tf_op jit(solution)/shard_map/solve/pallas_call | solution.py:674
  54.4 3.5 %all-to-all-start.1 = ((f32[8,3,48,128]{3,2,1,0:T(8,128)}), f32[8,3,48,128]{3,2,1,0:T(8,128)S(1)}, u32[]{:S(2)}, u32[]{:S(2)}) async-start(f32[8,3,48,128]{3,2,1,0:T(8,128)} %solve.1), calls=%async_computation.1 | async-start | bytes 1179648 | tf_op jit(solution)/shard_map/all_to_all | solution.py:638
  58.0 0.7 pad_add_fusion.place
  58.6 0.7 slice.47
  59.3 0.8 slice_bitcast_fusion.2
  60.1 8.8 %lon_tile.1 = (f32[3,96,48,128]{3,2,1,0:T(8,128)}, f32[3,4,48,128]{3,2,1,0:T(8,128)}, f32[7,48,128]{2,1,0:T(8,128)}) custom-call(f32[3,4,128]{2,1,0:T(4,128)} %get-tuple-element.21.prm, f32[3,48,192]{2,1,0:T(8,128)} %sigma.7, f32[3,48,96,128]{3,2,1,0:T(8,128)} %get-tuple-element.25.u_ref), custom_call_target="tpu_custom_call" | custom-call | flops 180000000 | bytes 14155776 | tf_op jit(solution)/shard_map/lon_tile/pallas_call | solution.py:643
  68.9 2.6 %collective-permute-start.6 = (f32[7,48,128]{2,1,0:T(8,128)}, f32[7,48,128]{2,1,0:T(8,128)S(1)}, u32[]{:S(2)}, u32[]{:S(2)}) collective-permute-start(f32[7,48,128]{2,1,0:T(8,128)} %get-tuple-element.26.rest_0_), channel_id=1, source_target_pairs={{0,1},{1,2},{2,3},{3,0},{4,5},{5,6},{6,7},{7,4},{8,9},{9,10},{10,1... | collective-permute-start | bytes 516104 | tf_op jit(solution)/shard_map/ppermute | solution.py:670
  71.5 2.6 %collective-permute-start.7 = (f32[7,48,128]{2,1,0:T(8,128)}, f32[7,48,128]{2,1,0:T(8,128)S(1)}, u32[]{:S(2)}, u32[]{:S(2)}) collective-permute-start(f32[7,48,128]{2,1,0:T(8,128)} %get-tuple-element.26.rest_0_), channel_id=1, source_target_pairs={{0,2},{1,3},{2,0},{3,1},{4,6},{5,7},{6,4},{7,5},{8,10},{9,11},{10,... | collective-permute-start | bytes 516104 | tf_op jit(solution)/shard_map/ppermute | solution.py:670
  74.1 1.4 %collective-permute-start.8 = (f32[7,48,128]{2,1,0:T(8,128)}, f32[7,48,128]{2,1,0:T(8,128)S(1)}, u32[]{:S(2)}, u32[]{:S(2)}) collective-permute-start(f32[7,48,128]{2,1,0:T(8,128)} %get-tuple-element.26.rest_0_), channel_id=1, source_target_pairs={{0,3},{1,0},{2,1},{3,2},{4,7},{5,4},{6,5},{7,6},{8,11},{9,8},{10,9... | collective-permute-start | bytes 516104 | tf_op jit(solution)/shard_map/ppermute | solution.py:670
  75.5 0.0 all-to-all-done.1.carries
  75.5 0.8 copy-done
  76.3 3.6 %lon_carry.1 = (f32[3,96,8,128]{3,2,1,0:T(8,128)}, f32[3,4,8,128]{3,2,1,0:T(8,128)}, f32[6,8,128]{2,1,0:T(8,128)}) custom-call(f32[3,4,128]{2,1,0:T(4,128)} %get-tuple-element.21.prm, f32[8,3,48,128]{3,2,1,0:T(8,128)} %copy-done), custom_call_target="tpu_custom_call" | custom-call | flops 30000000 | bytes 1769472 | tf_op jit(solution)/shard_map/lon_carry/pallas_call | solution.py:690
  79.9 0.2 collective-permute-start.10
  80.1 2.8 %collective-permute-start.11 = (f32[6,8,128]{2,1,0:T(8,128)}, f32[6,8,128]{2,1,0:T(8,128)S(1)}, u32[]{:S(2)}, u32[]{:S(2)}) collective-permute-start(f32[6,8,128]{2,1,0:T(8,128)} %get-tuple-element.34.rest_4_), channel_id=1, source_target_pairs={{0,3},{1,0},{2,1},{3,2},{4,7},{5,4},{6,5},{7,6},{8,11},{9,8},{10,9... | collective-permute-start | bytes 73736 | tf_op jit(solution)/shard_map/ppermute | solution.py:670
  83.0 0.0 collective-permute-done.6.rest_1_
  83.0 3.2 %collective-permute-start.9 = (f32[6,8,128]{2,1,0:T(8,128)}, f32[6,8,128]{2,1,0:T(8,128)S(1)}, u32[]{:S(2)}, u32[]{:S(2)}) collective-permute-start(f32[6,8,128]{2,1,0:T(8,128)} %get-tuple-element.34.rest_4_), channel_id=1, source_target_pairs={{0,1},{1,2},{2,3},{3,0},{4,5},{5,6},{6,7},{7,4},{8,9},{9,10},{10,1... | collective-permute-start | bytes 73736 | tf_op jit(solution)/shard_map/ppermute | solution.py:670
  86.1 0.4 collective-permute-done.7.rest_2_
  86.5 1.8 %collective-permute-start.4 = (f32[1,192]{1,0:T(1,128)S(1)}, f32[1,192]{1,0:T(1,128)S(1)}, u32[]{:S(2)}, u32[]{:S(2)}) collective-permute-start(f32[1,192]{1,0:T(1,128)S(1)} %get-tuple-element.45), channel_id=1, source_target_pairs={{0,4},{4,8},{8,12},{12,16},{16,20},{20,24},{24,28},{1,5},{5,9},{9,... | collective-permute-start | bytes 2312 | tf_op jit(solution)/shard_map/ppermute | solution.py:687
  88.3 0.0 collective-permute-done.8.rest_3_
  88.3 0.0 copy-start.4
  88.3 1.3 collective-permute-start.5
  89.6 1.9 %collective-permute-done.10.rest_6_ = f32[6,8,128]{2,1,0:T(8,128)S(1)} collective-permute-done((f32[6,8,128]{2,1,0:T(8,128)}, f32[6,8,128]{2,1,0:T(8,128)S(1)}, u32[]{:S(2)}, u32[]{:S(2)}) %collective-permute-start.10) | collective-permute-done | bytes 24608 | tf_op jit(solution)/shard_map/ppermute | solution.py:670
  91.5 0.0 collective-permute-done.11.rest_7_
  91.5 0.0 collective-permute-done.9.rest_5_
  91.6 0.6 copy-done.7
  92.1 0.0 copy-done.8
  92.1 0.0 copy-done.9
  92.1 12.8 %join.1 = (f32[3,96,48,128]{3,2,1,0:T(8,128)}, f32[96,8,128]{2,1,0:T(8,128)}, f32[2,48,128]{2,1,0:T(8,128)}, f32[2,48,128]{2,1,0:T(8,128)}, f32[3,8,128]{2,1,0:T(8,128)}) custom-call(s32[2]{0:T(128)} %pad_add_fusion.place, f32[3,4,128]{2,1,0:T(4,128)} %get-tuple-element.21.prm, f32[3,96,48,128]{3,2,1,0:T(8,128)} %get-tuple-element.28.u_ref, ...), custom_call_target="tpu_custom_call" | custom-call | flops 60000000 | bytes 21233664 | tf_op jit(solution)/shard_map/join/pallas_call | solution.py:717
  105.0 0.7 slice.46
  105.7 0.7 slice.45
  106.4 0.1 slice_add_fusion
  106.5 0.1 broadcast_in_dim.14
  106.5 0.1 select_reduce_fusion
  106.7 0.7 all_to_all.14
  107.4 9.5 %all-to-all-start.2 = ((f32[32,1,7]{2,1,0:T(1,128)}), f32[32,1,7]{2,1,0:T(1,128)S(1)}, u32[]{:S(2)}, u32[]{:S(2)}) async-start(f32[32,1,7]{2,1,0:T(1,128)} %bitcast.9), calls=%async_computation.2 | async-start | bytes 32768 | tf_op jit(solution)/shard_map/all_to_all | solution.py:759
  116.9 0.0 collective-permute-done.4.north
  116.9 0.0 collective-permute-done.5.south
  116.9 0.6 copy-done.13
  117.5 14.0 %finish.1 = f32[3,48,12288]{2,1,0:T(8,128)} custom-call(f32[3,4,128]{2,1,0:T(4,128)} %get-tuple-element.21.prm, f32[3,48,192]{2,1,0:T(8,128)} %sigma.7, f32[1,192]{1,0:T(1,128)} %copy-done.13, f32[1,192]{1,0:T(1,128)} %copy-done.14, f32[3,64,64]{2,1,0:T(8,128)} %vert.5, f32[64,64]{1,0:T(8,128)} %bal.3, f32[2,48,128]{2,1,0:T(8,128)} %get-tuple-element.35.col, ...), custom_call_target="tpu_custom_call" | custom-call | flops 300000000 | bytes 14155776 | tf_op jit(solution)/shard_map/finish/pallas_call | solution.py:766
  131.5 0.0 all-to-all-done.2
  131.5 0.1 reduce_sum.39
  131.5 0.5 multiply_bitcast_fusion
  (21 shorter events, 0.1 us)
Async XLA Ops:
  1.8 21.4 %collective-permute-start = (f32[1,12288]{1,0:T(1,128)S(1)}, f32[1,12288]{1,0:T(1,128)S(1)}, u32[]{:S(2)}, u32[]{:S(2)}) collective-permute-start(f32[1,12288]{1,0:T(1,128)S(1)} %get-tuple-element.43), channel_id=1, source_target_pairs={{0,4},{4,8},{8,12},{12,16},{16,20},{20,24},{24,28},{1,5},{5,9},{9,... | collective-permute-start | bytes 147464 | tf_op jit(solution)/shard_map/ppermute | solution.py:585
  4.2 19.0 %collective-permute-start.1 = (f32[1,12288]{1,0:T(1,128)S(1)}, f32[1,12288]{1,0:T(1,128)S(1)}, u32[]{:S(2)}, u32[]{:S(2)}) collective-permute-start(f32[1,12288]{1,0:T(1,128)S(1)} %get-tuple-element.42), channel_id=1, source_target_pairs={{4,0},{8,4},{12,8},{16,12},{20,16},{24,20},{28,24},{5,1},{9,5},{13... | collective-permute-start | bytes 147464 | tf_op jit(solution)/shard_map/ppermute | solution.py:586
  6.3 16.8 %collective-permute-start.2 = (f32[48,64]{1,0:T(8,128)S(1)}, f32[48,64]{1,0:T(8,128)S(1)}, u32[]{:S(2)}, u32[]{:S(2)}) collective-permute-start(f32[48,64]{1,0:T(8,128)S(1)} %get-tuple-element.41), channel_id=1, source_target_pairs={{0,1},{1,2},{2,3},{4,5},{5,6},{6,7},{8,9},{9,10},{10,11},{12,13},{... | collective-permute-start | bytes 36872 | tf_op jit(solution)/shard_map/ppermute | solution.py:587
  10.6 12.6 %collective-permute-start.3 = (f32[48,64]{1,0:T(8,128)S(1)}, f32[48,64]{1,0:T(8,128)S(1)}, u32[]{:S(2)}, u32[]{:S(2)}) collective-permute-start(f32[48,64]{1,0:T(8,128)S(1)} %get-tuple-element.40), channel_id=1, source_target_pairs={{1,0},{2,1},{3,2},{5,4},{6,5},{7,6},{9,8},{10,9},{11,10},{13,12},{... | collective-permute-start | bytes 36872 | tf_op jit(solution)/shard_map/ppermute | solution.py:588
  23.2 0.6 copy-start.10
  23.2 0.6 copy-start.11
  23.2 0.6 copy-start.5
  23.2 0.6 copy-start.6
  23.8 17.2 %copy-start.12 = (s32[192]{0:T(256)S(1)}, s32[192]{0:T(256)}, u32[]{:S(2)}) copy-start(s32[192]{0:T(256)} %param.15) | copy-start | bytes 2308
  34.8 16.7 %all-to-all-start = ((f32[8,3,48,128]{3,2,1,0:T(8,128)}), f32[8,3,48,128]{3,2,1,0:T(8,128)S(1)}, u32[]{:S(2)}, u32[]{:S(2)}) async-start(f32[8,3,48,128]{3,2,1,0:T(8,128)} %get-tuple-element.30), calls=%async_computation | async-start | bytes 1179648 | tf_op jit(solution)/shard_map/all_to_all | solution.py:638
  51.5 0.8 copy-start.1
  54.4 21.1 %all-to-all-start.1 = ((f32[8,3,48,128]{3,2,1,0:T(8,128)}), f32[8,3,48,128]{3,2,1,0:T(8,128)S(1)}, u32[]{:S(2)}, u32[]{:S(2)}) async-start(f32[8,3,48,128]{3,2,1,0:T(8,128)} %solve.1), calls=%async_computation.1 | async-start | bytes 1179648 | tf_op jit(solution)/shard_map/all_to_all | solution.py:638
  68.9 14.1 %collective-permute-start.6 = (f32[7,48,128]{2,1,0:T(8,128)}, f32[7,48,128]{2,1,0:T(8,128)S(1)}, u32[]{:S(2)}, u32[]{:S(2)}) collective-permute-start(f32[7,48,128]{2,1,0:T(8,128)} %get-tuple-element.26.rest_0_), channel_id=1, source_target_pairs={{0,1},{1,2},{2,3},{3,0},{4,5},{5,6},{6,7},{7,4},{8,9},{9,10},{10,1... | collective-permute-start | bytes 516104 | tf_op jit(solution)/shard_map/ppermute | solution.py:670
  71.5 15.0 %collective-permute-start.7 = (f32[7,48,128]{2,1,0:T(8,128)}, f32[7,48,128]{2,1,0:T(8,128)S(1)}, u32[]{:S(2)}, u32[]{:S(2)}) collective-permute-start(f32[7,48,128]{2,1,0:T(8,128)} %get-tuple-element.26.rest_0_), channel_id=1, source_target_pairs={{0,2},{1,3},{2,0},{3,1},{4,6},{5,7},{6,4},{7,5},{8,10},{9,11},{10,... | collective-permute-start | bytes 516104 | tf_op jit(solution)/shard_map/ppermute | solution.py:670
  74.1 14.2 %collective-permute-start.8 = (f32[7,48,128]{2,1,0:T(8,128)}, f32[7,48,128]{2,1,0:T(8,128)S(1)}, u32[]{:S(2)}, u32[]{:S(2)}) collective-permute-start(f32[7,48,128]{2,1,0:T(8,128)} %get-tuple-element.26.rest_0_), channel_id=1, source_target_pairs={{0,3},{1,0},{2,1},{3,2},{4,7},{5,4},{6,5},{7,6},{8,11},{9,8},{10,9... | collective-permute-start | bytes 516104 | tf_op jit(solution)/shard_map/ppermute | solution.py:670
  75.5 0.8 copy-start
  79.9 11.6 %collective-permute-start.10 = (f32[6,8,128]{2,1,0:T(8,128)}, f32[6,8,128]{2,1,0:T(8,128)S(1)}, u32[]{:S(2)}, u32[]{:S(2)}) collective-permute-start(f32[6,8,128]{2,1,0:T(8,128)} %get-tuple-element.34.rest_4_), channel_id=1, source_target_pairs={{0,2},{1,3},{2,0},{3,1},{4,6},{5,7},{6,4},{7,5},{8,10},{9,11},{10,... | collective-permute-start | bytes 73736 | tf_op jit(solution)/shard_map/ppermute | solution.py:670
  80.1 11.4 %collective-permute-start.11 = (f32[6,8,128]{2,1,0:T(8,128)}, f32[6,8,128]{2,1,0:T(8,128)S(1)}, u32[]{:S(2)}, u32[]{:S(2)}) collective-permute-start(f32[6,8,128]{2,1,0:T(8,128)} %get-tuple-element.34.rest_4_), channel_id=1, source_target_pairs={{0,3},{1,0},{2,1},{3,2},{4,7},{5,4},{6,5},{7,6},{8,11},{9,8},{10,9... | collective-permute-start | bytes 73736 | tf_op jit(solution)/shard_map/ppermute | solution.py:670
  83.0 8.6 %copy-start.2 = (f32[7,48,128]{2,1,0:T(8,128)}, f32[7,48,128]{2,1,0:T(8,128)S(1)}, u32[]{:S(2)}) copy-start(f32[7,48,128]{2,1,0:T(8,128)S(1)} %collective-permute-done.6.rest_1_) | copy-start | bytes 516100
  83.0 8.5 %collective-permute-start.9 = (f32[6,8,128]{2,1,0:T(8,128)}, f32[6,8,128]{2,1,0:T(8,128)S(1)}, u32[]{:S(2)}, u32[]{:S(2)}) collective-permute-start(f32[6,8,128]{2,1,0:T(8,128)} %get-tuple-element.34.rest_4_), channel_id=1, source_target_pairs={{0,1},{1,2},{2,3},{3,0},{4,5},{5,6},{6,7},{7,4},{8,9},{9,10},{10,1... | collective-permute-start | bytes 73736 | tf_op jit(solution)/shard_map/ppermute | solution.py:670
  86.5 5.0 %copy-start.3 = (f32[7,48,128]{2,1,0:T(8,128)}, f32[7,48,128]{2,1,0:T(8,128)S(1)}, u32[]{:S(2)}) copy-start(f32[7,48,128]{2,1,0:T(8,128)S(1)} %collective-permute-done.7.rest_2_) | copy-start | bytes 516100
  86.5 30.4 %collective-permute-start.4 = (f32[1,192]{1,0:T(1,128)S(1)}, f32[1,192]{1,0:T(1,128)S(1)}, u32[]{:S(2)}, u32[]{:S(2)}) collective-permute-start(f32[1,192]{1,0:T(1,128)S(1)} %get-tuple-element.45), channel_id=1, source_target_pairs={{0,4},{4,8},{8,12},{12,16},{16,20},{20,24},{24,28},{1,5},{5,9},{9,... | collective-permute-start | bytes 2312 | tf_op jit(solution)/shard_map/ppermute | solution.py:687
  88.3 3.2 %copy-start.4 = (f32[7,48,128]{2,1,0:T(8,128)}, f32[7,48,128]{2,1,0:T(8,128)S(1)}, u32[]{:S(2)}) copy-start(f32[7,48,128]{2,1,0:T(8,128)S(1)} %collective-permute-done.8.rest_3_) | copy-start | bytes 516100
  88.3 28.6 %collective-permute-start.5 = (f32[1,192]{1,0:T(1,128)S(1)}, f32[1,192]{1,0:T(1,128)S(1)}, u32[]{:S(2)}, u32[]{:S(2)}) collective-permute-start(f32[1,192]{1,0:T(1,128)S(1)} %get-tuple-element.44), channel_id=1, source_target_pairs={{4,0},{8,4},{12,8},{16,12},{20,16},{24,20},{28,24},{5,1},{9,5},{13... | collective-permute-start | bytes 2312 | tf_op jit(solution)/shard_map/ppermute | solution.py:688
  91.5 0.6 copy-start.7
  91.5 0.6 copy-start.8
  91.5 0.6 copy-start.9
  107.4 24.1 %all-to-all-start.2 = ((f32[32,1,7]{2,1,0:T(1,128)}), f32[32,1,7]{2,1,0:T(1,128)S(1)}, u32[]{:S(2)}, u32[]{:S(2)}) async-start(f32[32,1,7]{2,1,0:T(1,128)} %bitcast.9), calls=%async_computation.2 | async-start | bytes 32768 | tf_op jit(solution)/shard_map/all_to_all | solution.py:759
  116.9 0.6 copy-start.13
  116.9 0.6 copy-start.14

commit v4 on v3

--- a/solution.py
+++ b/solution.py
@@ -42,9 +42,13 @@
     return jnp.dot(x, y, preferred_element_type=f32)
 
 
-def product(x, wh, wl):
+def split(x):
     hi, lo = halves(x)
-    return dot(hi, wh) + dot(lo, wh) + dot(hi, wl)
+    return jnp.concatenate([hi, lo, hi], axis=1)
+
+
+def product(x, weights):
+    return dot(split(x), weights)
 
 
 def expand(mat, mixed):
@@ -157,10 +161,15 @@
     return jnp.take_along_axis(sg[v, m >> 6], idx, axis=1, mode="promise_in_bounds")
 
 
-def set_weights(wh, wl, k, mat, mixed):
+def set_weights(weights, k, mat, mixed):
     hi, lo = expand(mat, mixed)
-    wh[k] = hi
-    wl[k] = lo
+    weights[768 * k : 768 * k + 256] = hi
+    weights[768 * k + 256 : 768 * k + 512] = hi
+    weights[768 * k + 512 : 768 * k + 768] = lo
+
+
+def weight(weights, k):
+    return weights[768 * k : 768 * (k + 1)]
 
 
 def lat_filter(vs, rows, prm, u_ref, e_ref):
@@ -213,15 +222,15 @@
 
 def lat_plain(
     rows, pairs, scales, classes, chi_coef, sigma, vert, b1lo, b1hi, b2lo, b2hi,
-    w_ref, u_ref, e_ref, prm, xs, wh, wl, sg,
+    w_ref, u_ref, e_ref, prm, xs, wt, sg,
 ):
     g = pl.program_id(0)
 
     @pl.when(g == 0)
     def _():
         set_params(scales, classes, chi_coef, prm)
-        set_weights(wh, wl, 0, vert[1], True)
-        set_weights(wh, wl, 1, vert[2], True)
+        set_weights(wt, 0, vert[1], True)
+        set_weights(wt, 1, vert[2], True)
         stage_sigma(sigma, sg, (1, 2))
 
     lane = lax.broadcasted_iota(jnp.int32, (rows, LANES), 1)
@@ -237,7 +246,7 @@
                     s = sigma_tile(sg, k + 1, m + side * pairs, high)
                     xs[k, at, side * LANES : (side + 1) * LANES] = sides[side][0, :, cols] * s
         for k in range(2):
-            put_mixed(k, b, rows, product(xs[k], wh[k], wl[k]), w_ref, u_ref)
+            put_mixed(k, b, rows, product(xs[k], weight(wt, k)), w_ref, u_ref)
         return 0
 
     lax.fori_loop(0, BLOCK // PAIRS, body, 0)
@@ -246,16 +255,16 @@
 
 def lat_balance(
     rows, pairs, prm, sigma, vert, bal, plo, phi, clo, chi, temp, north, south, west, east, w_in, u_in, e_in,
-    w_ref, u_ref, e_ref, xs, wh, wl, sg,
+    w_ref, u_ref, e_ref, xs, wt, sg,
 ):
     del w_in, u_in, e_in
     g = pl.program_id(0)
 
     @pl.when(g == 0)
     def _():
-        set_weights(wh, wl, 0, vert[0], True)
-        vh, vl = halves(vert[0])
-        set_weights(wh, wl, 1, product(bal[...], vh, vl), True)
+        set_weights(wt, 0, vert[0], True)
+        (bh, bl), (vh, vl) = halves(bal[...]), halves(vert[0])
+        set_weights(wt, 1, dot(bh, vh) + dot(bl, vh) + dot(bh, vl), True)
         stage_sigma(sigma, sg, (0,))
 
     lane = lax.broadcasted_iota(jnp.int32, (rows, LANES), 1)
@@ -287,7 +296,7 @@
                 to = slice(side * LANES, (side + 1) * LANES)
                 xs[0, at, to] = (pr[0, :, cols] + chi_row * cr[0, :, cols]) * s
                 xs[1, at, to] = laplace(m + side * pairs) * s
-        res = product(xs[0], wh[0], wl[0]) + product(xs[1], wh[1], wl[1])
+        res = dot(jnp.concatenate([split(xs[0]), split(xs[1])], axis=1), wt[...])
         put_mixed(0, b, rows, res, w_ref, u_ref)
         return 0
 
@@ -467,7 +476,7 @@
                 return total
 
             total = lax.fori_loop(0, packed // 8, body, total)
-        energy[k] += jnp.sum(total.reshape(rq // 8, 8, LANES), axis=0)
+        energy[v] += jnp.sum(total.reshape(rq // 8, 8, LANES), axis=0)
 
     @pl.when(g == 0)
     def _():
@@ -477,26 +486,27 @@
 
 def end_kernel(
     rows, pairs, prm, sigma, north, south, vert, bal, col, side, y_ref, yx_ref,
-    out, xs, zx, zc, wh, wl, sg, sx,
+    out, xs, zx, zc, wt, sg, sx,
 ):
     g = pl.program_id(0)
     half = 2 * pairs
     lon = sigma.shape[2]
+    merged = out.shape[2]
 
     @pl.when(g == 0)
     def _():
         for v in range(3):
             scaled = quad(vert[v]) * prm[v, 3:4, :]
-            set_weights(wh, wl, v, scaled.T, True)
-        set_weights(wh, wl, 3, quad(bal[...]).T, False)
+            set_weights(wt, v, scaled.T, True)
+        set_weights(wt, 3, quad(bal[...]).T, False)
         stage_sigma(sigma, sg, (0, 1, 2))
         for at in range(0, lon, LANES):
             width = min(LANES, lon - at)
-            sx[at // LANES, 0:1, 0:width] = north[:, at : at + width]
-            sx[at // LANES, 1:2, 0:width] = south[:, at : at + width]
+            sx[at // LANES, 0:1, 0:width] = north[:, merged + at : merged + at + width]
+            sx[at // LANES, 1:2, 0:width] = south[:, merged + at : merged + at + width]
         lhs = jnp.where(low_lanes((rows, LANES)), col[0], col[1])
         lhs = jnp.concatenate([lhs, jnp.zeros_like(lhs)], axis=1)
-        res = product(lhs, wh[0], wl[0])
+        res = product(lhs, weight(wt, 0))
         zc[0] = swap(res[:, :LANES] * swap(side[0]))
         zc[1] = res[:, LANES:] * side[1]
 
@@ -511,7 +521,7 @@
     lhs = jnp.concatenate(
         [jnp.concatenate([yx_ref[2 * p], yx_ref[2 * p + 1]], axis=1) for p in range(PAIRS)], axis=0
     )
-    res = product(lhs, wh[0], wl[0])
+    res = product(lhs, weight(wt, 0))
     for p in range(PAIRS):
         m = g * PAIRS + p
         for side in range(2):
@@ -523,7 +533,7 @@
         for p in range(2 * PAIRS):
             at = slice((p // 2) * rows, (p // 2 + 1) * rows)
             xs[k, at, (p % 2) * LANES : (p % 2 + 1) * LANES] = y_ref[k, p]
-    results = {v: product(xs[k], wh[v], wl[v]) for k, v in enumerate(ORDER)}
+    results = {v: product(xs[k], weight(wt, v)) for k, v in enumerate(ORDER)}
     for p in range(PAIRS):
         m = g * PAIRS + p
         for side in range(2):
@@ -554,7 +564,7 @@
                     below = jnp.where(row_id == rows - 1, zx[1:2, at_tile(m)], pltpu.roll(x, rows - 1, 0))
                     lap = 4.0 * x - beside - above - below
                     xs[0, p * rows : (p + 1) * rows, side * LANES : (side + 1) * LANES] = lap
-            res = product(xs[0], wh[3], wl[3])
+            res = product(xs[0], weight(wt, 3))
             for p in range(PAIRS):
                 for side in range(2):
                     at = at_tile(b * PAIRS + p + side * pairs)
@@ -582,8 +592,12 @@
 
     up_lat, up_lon = ([(i, i + 1) for i in range(n - 1)] for n in (n_lat, n_lon))
     down_lat, down_lon = ([(j, i) for i, j in up] for up in (up_lat, up_lon))
-    north = lax.ppermute(state[2, rows - 1 : rows, :], "lat", up_lat)
-    south = lax.ppermute(state[2, 0:1, :], "lat", down_lat)
+
+    def row(i):
+        return jnp.concatenate([state[2, i : i + 1, :], sigma[0, i : i + 1, :]], axis=1)
+
+    north = lax.ppermute(row(rows - 1), "lat", up_lat)
+    south = lax.ppermute(row(0), "lat", down_lat)
     west = lax.ppermute(state[2, :, merged - levels :], "lon", up_lon)
     east = lax.ppermute(state[2, :, :levels], "lon", down_lon)
     place = jnp.stack([i_lat, i_lon]).astype(jnp.int32)
@@ -611,8 +625,7 @@
             out_shape=[jax.ShapeDtypeStruct(s, f32) for s in shapes + list(more)],
             scratch_shapes=[
                 pltpu.VMEM((2, PAIRS * rows, 256), f32),
-                pltpu.VMEM((2, 256, 256), bf16),
-                pltpu.VMEM((2, 256, 256), bf16),
+                pltpu.VMEM((2 * 768, 256), bf16),
                 pltpu.VMEM((nvars, pieces, rows, LANES), f32),
             ],
             compiler_params=params(),
@@ -670,6 +683,7 @@
             lax.ppermute(x, "lon", [(i, (i + s) % n_lon) for i in range(n_lon)]) for s in range(1, n_lon)
         ]
 
+    shares, _ = lax.optimization_barrier((shares, es))
     sent = round_lon(es)
     carries = pl.pallas_call(
         functools.partial(solve_kernel, n_lat, rows),
@@ -682,10 +696,6 @@
         name="solve",
     )(prm, shares)
     carries = trade(carries)
-
-    row, _ = lax.optimization_barrier((sigma[0], es))
-    sig_n = lax.ppermute(row[rows - 1 : rows], "lat", up_lat)
-    sig_s = lax.ppermute(row[0:1], "lat", down_lat)
 
     crossed, elc, esc = pl.pallas_call(
         carry_kernel,
@@ -752,14 +762,13 @@
     slot = jnp.sum(same.astype(jnp.int32), axis=1)
     target = owner * capacity + slot
     hit = target[:, None] == jnp.arange(devices * capacity)[None, :]
-    energy = jnp.stack([energy[ORDER.index(v)] for v in range(nvars)])
     energy = jnp.sum(energy, axis=1) * prm[:, 3]
     energy = (energy[:, :levels] + energy[:, levels:]).reshape(count)
     table = jnp.sum(jnp.where(hit, energy[:, None], 0.0), axis=0).reshape(devices, capacity)
     table = lax.all_to_all(table, ("lat", "lon"), split_axis=0, concat_axis=0, tiled=True)
     slab_energy = (jnp.sum(table, axis=0) / (devices * rows * lon))[None, :]
 
-    ins = [prm, sigma, sig_n, sig_s, vert, bal_temp, col, side, y, yx]
+    ins = [prm, sigma, north, south, vert, bal_temp, col, side, y, yx]
     specs = [full(x.shape) for x in ins]
     specs[8] = columns(rows)
     specs[9] = pl.BlockSpec((packed, 8, LANES), lambda g: (g, 0, 0))
@@ -773,8 +782,7 @@
             pltpu.VMEM((nvars, PAIRS * rows, 256), f32),
             pltpu.VMEM((8, merged), f32),
             pltpu.VMEM((2, rows, LANES), f32),
-            pltpu.VMEM((4, 256, 256), bf16),
-            pltpu.VMEM((4, 256, 256), bf16),
+            pltpu.VMEM((4 * 768, 256), bf16),
             pltpu.VMEM((nvars, pieces, rows, LANES), f32),
             pltpu.VMEM((pieces, 8, LANES), f32),
         ],

time: 133 us -> 117 us (0.88)
  starting transfers between devices: 44.4 us -> 35.8 us
  waiting for transfers between devices: 12.5 us -> 6.42 us
  local copies, waits for them, and re-layouts: 9.12 us -> 7.14 us
    all_to_all x1, starting transfers between devices: 9.51 us -> 3.51 us  [shards(): lax.all_to_all(table, ('lat', 'lon'), split_axis=0, concat_axis=0, tiled=...]
    all_to_all x2, waiting for transfers between devices: 10.3 us -> 5.07 us  [trade(): return lax.all_to_all(x, 'lat', split_axis=0, concat_axis=0, tiled=True)]
    ppermute x4 -> x2, starting transfers between devices: 6.7 us -> 3.65 us  [the longest x1 2.36 us: shards(): north = lax.ppermute(row(rows - 1), 'lat', up_lat)]
    slice x3 -> x0, local copies, waits for them, and re-layouts: 1.39 us -> none  [the longest x2 1.38 us: shards(): energy = jnp.stack([energy[ORDER.index(v)] for v in range(nvars)])]
    unnamed x30 -> x26, local copies, waits for them, and re-layouts: 3.42 us -> 2.91 us
  transfers between devices with their start and end apart: 15 -> 13, of which waited for: 3 -> 3; matrix products, arithmetic and copies ran while one was open for 4% -> 2% of each run, Pallas kernels for 38% -> 32%
where the time goes in v4:
time: 117 us; the launch traced here: 116 us
  Pallas kernels  63.7 us (54%)
  starting transfers between devices  35.8 us (31%)
  local copies, waits for them, and re-layouts  7.14 us (6%)
  waiting for transfers between devices  6.42 us (5%)
  other arithmetic  2.39 us (2%)
    pallas_call x2, Pallas kernels, lat_call(): pl.pallas_call(body, grid=(steps,), in_specs=specs, out_specs=[pl.BlockSp...  22.3 us
    pallas_call x1, Pallas kernels, shards(): pl.pallas_call(functools.partial(end_kernel, rows, pairs), grid=(half //...  14 us
    ppermute x6, starting transfers between devices, round_lon(): lax.ppermute(x, 'lon', [(i, (i + s) % n_lon) for i in range(n_lon)])  13.2 us
    pallas_call x1, Pallas kernels, shards(): pl.pallas_call(functools.partial(join_kernel, n_lon, rows, packed, 24), g...  12.8 us
    all_to_all x2, starting transfers between devices, trade(): return lax.all_to_all(x, 'lat', split_axis=0, concat_axis=0, tiled=True)  9.8 us
    pallas_call x1, Pallas kernels, shards(): pl.pallas_call(functools.partial(lon_kernel, rb), grid=(rows // rb,), in_...  8.93 us
    all_to_all x2, waiting for transfers between devices, trade(): return lax.all_to_all(x, 'lat', split_axis=0, concat_axis=0, tiled=True)  5.07 us
    ppermute x1, starting transfers between devices, shards(): west = lax.ppermute(state[2, :, merged - levels:], 'lon', up_lon)  4.3 us
  transfers between devices with their start and end apart: 13, of which 3 were waited for; matrix products, arithmetic and copies ran while one was open for 2% of the time, Pallas kernels for 32%

profile of v4, /device:TPU:0, one launch (start us, length us, event | category | flops | bytes accessed | tf_op | source)
XLA Modules:
  0.0 116.3 jit_solution(13956451974168172756)
XLA Ops:
  0.6 1.2 %slice_bitcast_fusion = (f32[1,12288]{1,0:T(1,128)S(1)}, f32[1,12288]{1,0:T(1,128)S(1)}) fusion(f32[3,48,12288]{2,1,0:T(8,128)} %temp.1), kind=kLoop, calls=%fused_computation.7 | loop fusion | bytes 196608 | tf_op jit(solution)/shard_map/squeeze | solution.py:597
  1.8 0.7 slice_bitcast_fusion.4
  2.6 2.4 %collective-permute-start = (f32[1,12480]{1,0:T(1,128)S(1)}, f32[1,12480]{1,0:T(1,128)S(1)}, u32[]{:S(2)}, u32[]{:S(2)}) collective-permute-start(f32[1,12480]{1,0:T(1,128)S(1)} %pad_maximum_fusion), channel_id=1, source_target_pairs={{0,4},{4,8},{8,12},{12,16},{16,20},{20,24},{24,28},{1,5},{5,9},{9,... | collective-permute-start | bytes 149768 | tf_op jit(solution)/shard_map/ppermute | solution.py:599
  5.0 1.3 %collective-permute-start.1 = (f32[1,12480]{1,0:T(1,128)S(1)}, f32[1,12480]{1,0:T(1,128)S(1)}, u32[]{:S(2)}, u32[]{:S(2)}) collective-permute-start(f32[1,12480]{1,0:T(1,128)S(1)} %pad_maximum_fusion.1), channel_id=1, source_target_pairs={{4,0},{8,4},{12,8},{16,12},{20,16},{24,20},{28,24},{5,1},{9,5},{13... | collective-permute-start | bytes 149768 | tf_op jit(solution)/shard_map/ppermute | solution.py:600
  6.3 0.8 slice_bitcast_fusion.2
  7.1 4.3 %collective-permute-start.2 = (f32[48,64]{1,0:T(8,128)S(1)}, f32[48,64]{1,0:T(8,128)S(1)}, u32[]{:S(2)}, u32[]{:S(2)}) collective-permute-start(f32[48,64]{1,0:T(8,128)S(1)} %get-tuple-element.41), channel_id=1, source_target_pairs={{0,1},{1,2},{2,3},{4,5},{5,6},{6,7},{8,9},{9,10},{10,11},{12,13},{... | collective-permute-start | bytes 36872 | tf_op jit(solution)/shard_map/ppermute | solution.py:601
  11.5 1.3 %collective-permute-start.3 = (f32[48,64]{1,0:T(8,128)S(1)}, f32[48,64]{1,0:T(8,128)S(1)}, u32[]{:S(2)}, u32[]{:S(2)}) collective-permute-start(f32[48,64]{1,0:T(8,128)S(1)} %get-tuple-element.40), channel_id=1, source_target_pairs={{1,0},{2,1},{3,2},{5,4},{6,5},{7,6},{9,8},{10,9},{11,10},{13,12},{... | collective-permute-start | bytes 36872 | tf_op jit(solution)/shard_map/ppermute | solution.py:602
  12.8 11.3 %lat_chi_temp.1 = (f32[3,96,48,128]{3,2,1,0:T(8,128)}, f32[3,48,96,128]{3,2,1,0:T(8,128)}, f32[8,3,48,128]{3,2,1,0:T(8,128)}, f32[3,4,128]{2,1,0:T(4,128)}) custom-call(f32[8]{0:T(128)} %scales.1, s32[1,192]{1,0:T(1,128)} %bitcast.21, f32[1,64]{1,0:T(1,128)} %bitcast.22, f32[3,48,192]{2,1,0:T(8,128)} %sigma.7, f32[3,64,64]{2,1,0:T(8,128)} %vert.5, ...), custom_call_target="tpu_custom_call" | custom-call | flops 120000000 | bytes 14155776 | tf_op jit(solution)/shard_map/lat_chi_temp/pallas_call | solution.py:615
  24.0 0.0 collective-permute-done.2.west
  24.1 0.0 copy-start.10
  24.1 0.0 collective-permute-done.3.east
  24.1 0.0 copy-start.11
  24.1 0.0 collective-permute-done.north
  24.1 0.0 copy-start.2
  24.1 0.0 collective-permute-done.1.south
  24.1 0.0 copy-start.3
  24.1 0.5 copy-done.10
  24.6 0.0 copy-done.11
  24.7 0.0 copy-done.2
  24.7 0.0 copy-done.3
  24.7 11.0 %lat_psi.1 = (f32[3,96,48,128]{3,2,1,0:T(8,128)}, f32[3,48,96,128]{3,2,1,0:T(8,128)}, f32[8,3,48,128]{3,2,1,0:T(8,128)}) custom-call(f32[3,4,128]{2,1,0:T(4,128)} %get-tuple-element.21.prm, f32[3,48,192]{2,1,0:T(8,128)} %sigma.7, f32[3,64,64]{2,1,0:T(8,128)} %vert.5, f32[64,64]{1,0:T(8,128)} %bal.3, ...), custom_call_target="tpu_custom_call", output_to_operand_aliasing={{0}: (13, {}), {1}: (14, {}), {2}: (15, {})} | custom-call | flops 60000000 | bytes 7077888 | tf_op jit(solution)/shard_map/lat_psi/pallas_call | solution.py:615
  35.8 0.0 copy-start.12
  35.8 6.3 %all-to-all-start = ((f32[8,3,48,128]{3,2,1,0:T(8,128)}), f32[8,3,48,128]{3,2,1,0:T(8,128)S(1)}, u32[]{:S(2)}, u32[]{:S(2)}) async-start(f32[8,3,48,128]{3,2,1,0:T(8,128)} %get-tuple-element.28), calls=%async_computation | async-start | bytes 1179648 | tf_op jit(solution)/shard_map/all_to_all | solution.py:651
  42.1 8.9 %lon_tile.1 = (f32[3,96,48,128]{3,2,1,0:T(8,128)}, f32[3,4,48,128]{3,2,1,0:T(8,128)}, f32[7,48,128]{2,1,0:T(8,128)}) custom-call(f32[3,4,128]{2,1,0:T(4,128)} %get-tuple-element.21.prm, f32[3,48,192]{2,1,0:T(8,128)} %sigma.7, f32[3,48,96,128]{3,2,1,0:T(8,128)} %get-tuple-element.25.u_ref), custom_call_target="tpu_custom_call" | custom-call | flops 180000000 | bytes 14155776 | tf_op jit(solution)/shard_map/lon_tile/pallas_call | solution.py:656
  51.0 1.5 %all-to-all-done.edges = f32[8,3,48,128]{3,2,1,0:T(8,128)S(1)} async-done(((f32[8,3,48,128]{3,2,1,0:T(8,128)}), f32[8,3,48,128]{3,2,1,0:T(8,128)S(1)}, u32[]{:S(2)}, u32[]{:S(2)}) %all-to-all-start) | async-done | bytes 589856 | tf_op jit(solution)/shard_map/all_to_all | solution.py:651
  52.5 0.9 copy-done.1
  53.4 2.1 %solve.1 = f32[8,3,48,128]{3,2,1,0:T(8,128)} custom-call(f32[3,4,128]{2,1,0:T(4,128)} %get-tuple-element.21.prm, f32[8,3,48,128]{3,2,1,0:T(8,128)} %copy-done.1), custom_call_target="tpu_custom_call" | custom-call | flops 1000000 | bytes 1179648 | tf_op jit(solution)/shard_map/solve/pallas_call | solution.py:688
  55.4 3.5 %all-to-all-start.1 = ((f32[8,3,48,128]{3,2,1,0:T(8,128)}), f32[8,3,48,128]{3,2,1,0:T(8,128)S(1)}, u32[]{:S(2)}, u32[]{:S(2)}) async-start(f32[8,3,48,128]{3,2,1,0:T(8,128)} %solve.1), calls=%async_computation.1 | async-start | bytes 1179648 | tf_op jit(solution)/shard_map/all_to_all | solution.py:651
  59.0 0.0 copy-done.12
  59.0 0.2 convert_reduce_fusion
  59.2 2.7 %collective-permute-start.4 = (f32[7,48,128]{2,1,0:T(8,128)}, f32[7,48,128]{2,1,0:T(8,128)S(1)}, u32[]{:S(2)}, u32[]{:S(2)}) collective-permute-start(f32[7,48,128]{2,1,0:T(8,128)} %get-tuple-element.29.rest_0_), channel_id=1, source_target_pairs={{0,1},{1,2},{2,3},{3,0},{4,5},{5,6},{6,7},{7,4},{8,9},{9,10},{10,1... | collective-permute-start | bytes 516104 | tf_op jit(solution)/shard_map/ppermute | solution.py:683
  61.9 2.6 %collective-permute-start.5 = (f32[7,48,128]{2,1,0:T(8,128)}, f32[7,48,128]{2,1,0:T(8,128)S(1)}, u32[]{:S(2)}, u32[]{:S(2)}) collective-permute-start(f32[7,48,128]{2,1,0:T(8,128)} %get-tuple-element.29.rest_0_), channel_id=1, source_target_pairs={{0,2},{1,3},{2,0},{3,1},{4,6},{5,7},{6,4},{7,5},{8,10},{9,11},{10,... | collective-permute-start | bytes 516104 | tf_op jit(solution)/shard_map/ppermute | solution.py:683
  64.5 1.3 %collective-permute-start.6 = (f32[7,48,128]{2,1,0:T(8,128)}, f32[7,48,128]{2,1,0:T(8,128)S(1)}, u32[]{:S(2)}, u32[]{:S(2)}) collective-permute-start(f32[7,48,128]{2,1,0:T(8,128)} %get-tuple-element.29.rest_0_), channel_id=1, source_target_pairs={{0,3},{1,0},{2,1},{3,2},{4,7},{5,4},{6,5},{7,6},{8,11},{9,8},{10,9... | collective-permute-start | bytes 516104 | tf_op jit(solution)/shard_map/ppermute | solution.py:683
  65.8 3.5 %all-to-all-done.1.carries = f32[8,3,48,128]{3,2,1,0:T(8,128)S(1)} async-done(((f32[8,3,48,128]{3,2,1,0:T(8,128)}), f32[8,3,48,128]{3,2,1,0:T(8,128)S(1)}, u32[]{:S(2)}, u32[]{:S(2)}) %all-to-all-start.1) | async-done | bytes 589856 | tf_op jit(solution)/shard_map/all_to_all | solution.py:651
  69.4 0.8 copy-done
  70.2 3.6 %lon_carry.1 = (f32[3,96,8,128]{3,2,1,0:T(8,128)}, f32[3,4,8,128]{3,2,1,0:T(8,128)}, f32[6,8,128]{2,1,0:T(8,128)}) custom-call(f32[3,4,128]{2,1,0:T(4,128)} %get-tuple-element.21.prm, f32[8,3,48,128]{3,2,1,0:T(8,128)} %copy-done), custom_call_target="tpu_custom_call" | custom-call | flops 30000000 | bytes 1769472 | tf_op jit(solution)/shard_map/lon_carry/pallas_call | solution.py:700
  73.8 2.6 %collective-permute-start.7 = (f32[6,8,128]{2,1,0:T(8,128)}, f32[6,8,128]{2,1,0:T(8,128)S(1)}, u32[]{:S(2)}, u32[]{:S(2)}) collective-permute-start(f32[6,8,128]{2,1,0:T(8,128)} %get-tuple-element.34.rest_4_), channel_id=1, source_target_pairs={{0,1},{1,2},{2,3},{3,0},{4,5},{5,6},{6,7},{7,4},{8,9},{9,10},{10,1... | collective-permute-start | bytes 73736 | tf_op jit(solution)/shard_map/ppermute | solution.py:683
  76.4 2.6 %collective-permute-start.8 = (f32[6,8,128]{2,1,0:T(8,128)}, f32[6,8,128]{2,1,0:T(8,128)S(1)}, u32[]{:S(2)}, u32[]{:S(2)}) collective-permute-start(f32[6,8,128]{2,1,0:T(8,128)} %get-tuple-element.34.rest_4_), channel_id=1, source_target_pairs={{0,2},{1,3},{2,0},{3,1},{4,6},{5,7},{6,4},{7,5},{8,10},{9,11},{10,... | collective-permute-start | bytes 73736 | tf_op jit(solution)/shard_map/ppermute | solution.py:683
  79.0 0.0 collective-permute-done.4.rest_1_
  79.0 1.3 %collective-permute-start.9 = (f32[6,8,128]{2,1,0:T(8,128)}, f32[6,8,128]{2,1,0:T(8,128)S(1)}, u32[]{:S(2)}, u32[]{:S(2)}) collective-permute-start(f32[6,8,128]{2,1,0:T(8,128)} %get-tuple-element.34.rest_4_), channel_id=1, source_target_pairs={{0,3},{1,0},{2,1},{3,2},{4,7},{5,4},{6,5},{7,6},{8,11},{9,8},{10,9... | collective-permute-start | bytes 73736 | tf_op jit(solution)/shard_map/ppermute | solution.py:683
  80.4 0.6 pad_add_fusion.place
  81.0 0.7 slice.33
  81.7 0.0 collective-permute-done.5.rest_2_
  81.7 0.0 collective-permute-done.6.rest_3_
  81.7 0.0 copy-start.6
  81.7 0.0 collective-permute-done.7.rest_5_
  81.7 0.0 copy-start.7
  81.7 0.0 collective-permute-done.8.rest_6_
  81.7 0.0 copy-start.8
  81.7 1.3 %collective-permute-done.9.rest_7_ = f32[6,8,128]{2,1,0:T(8,128)S(1)} collective-permute-done((f32[6,8,128]{2,1,0:T(8,128)}, f32[6,8,128]{2,1,0:T(8,128)S(1)}, u32[]{:S(2)}, u32[]{:S(2)}) %collective-permute-start.9) | collective-permute-done | bytes 24608 | tf_op jit(solution)/shard_map/ppermute | solution.py:683
  83.1 0.0 copy-done.4
  83.1 0.0 copy-done.5
  83.1 0.6 copy-done.9
  83.7 12.8 %join.1 = (f32[3,96,48,128]{3,2,1,0:T(8,128)}, f32[96,8,128]{2,1,0:T(8,128)}, f32[2,48,128]{2,1,0:T(8,128)}, f32[2,48,128]{2,1,0:T(8,128)}, f32[3,8,128]{2,1,0:T(8,128)}) custom-call(s32[2]{0:T(128)} %pad_add_fusion.place, f32[3,4,128]{2,1,0:T(4,128)} %get-tuple-element.21.prm, f32[3,96,48,128]{3,2,1,0:T(8,128)} %get-tuple-element.26.u_ref, ...), custom_call_target="tpu_custom_call" | custom-call | flops 60000000 | bytes 21233664 | tf_op jit(solution)/shard_map/join/pallas_call | solution.py:727
  96.5 0.7 reduce_sum.37
  97.2 0.1 slice_add_fusion
  97.3 0.1 broadcast_in_dim.14
  97.4 0.1 select_reduce_fusion
  97.5 0.7 all_to_all.14
  98.2 3.5 %all-to-all-start.2 = ((f32[32,1,7]{2,1,0:T(1,128)}), f32[32,1,7]{2,1,0:T(1,128)S(1)}, u32[]{:S(2)}, u32[]{:S(2)}) async-start(f32[32,1,7]{2,1,0:T(1,128)} %bitcast.10), calls=%async_computation.2 | async-start | bytes 32768 | tf_op jit(solution)/shard_map/all_to_all | solution.py:768
  101.7 14.0 %finish.1 = f32[3,48,12288]{2,1,0:T(8,128)} custom-call(f32[3,4,128]{2,1,0:T(4,128)} %get-tuple-element.21.prm, f32[3,48,192]{2,1,0:T(8,128)} %sigma.7, f32[1,12480]{1,0:T(1,128)} %copy-done.2, f32[1,12480]{1,0:T(1,128)} %copy-done.3, f32[3,64,64]{2,1,0:T(8,128)} %vert.5, f32[64,64]{1,0:T(8,128)} %bal.3, f32[2,48,128]{2,1,0:T(8,128)} %get-tuple-element.35.col, ...), custom_call_target="tpu_custom_call" | custom-call | flops 300000000 | bytes 14155776 | tf_op jit(solution)/shard_map/finish/pallas_call | solution.py:775
  115.7 0.0 all-to-all-done.2
  115.7 0.1 reduce_sum.39
  115.7 0.5 multiply_bitcast_fusion
  (12 shorter events, 0.1 us)
Async XLA Ops:
  2.6 21.5 %collective-permute-start = (f32[1,12480]{1,0:T(1,128)S(1)}, f32[1,12480]{1,0:T(1,128)S(1)}, u32[]{:S(2)}, u32[]{:S(2)}) collective-permute-start(f32[1,12480]{1,0:T(1,128)S(1)} %pad_maximum_fusion), channel_id=1, source_target_pairs={{0,4},{4,8},{8,12},{12,16},{16,20},{20,24},{24,28},{1,5},{5,9},{9,... | collective-permute-start | bytes 149768 | tf_op jit(solution)/shard_map/ppermute | solution.py:599
  5.0 19.1 %collective-permute-start.1 = (f32[1,12480]{1,0:T(1,128)S(1)}, f32[1,12480]{1,0:T(1,128)S(1)}, u32[]{:S(2)}, u32[]{:S(2)}) collective-permute-start(f32[1,12480]{1,0:T(1,128)S(1)} %pad_maximum_fusion.1), channel_id=1, source_target_pairs={{4,0},{8,4},{12,8},{16,12},{20,16},{24,20},{28,24},{5,1},{9,5},{13... | collective-permute-start | bytes 149768 | tf_op jit(solution)/shard_map/ppermute | solution.py:600
  7.1 16.9 %collective-permute-start.2 = (f32[48,64]{1,0:T(8,128)S(1)}, f32[48,64]{1,0:T(8,128)S(1)}, u32[]{:S(2)}, u32[]{:S(2)}) collective-permute-start(f32[48,64]{1,0:T(8,128)S(1)} %get-tuple-element.41), channel_id=1, source_target_pairs={{0,1},{1,2},{2,3},{4,5},{5,6},{6,7},{8,9},{9,10},{10,11},{12,13},{... | collective-permute-start | bytes 36872 | tf_op jit(solution)/shard_map/ppermute | solution.py:601
  11.5 12.6 %collective-permute-start.3 = (f32[48,64]{1,0:T(8,128)S(1)}, f32[48,64]{1,0:T(8,128)S(1)}, u32[]{:S(2)}, u32[]{:S(2)}) collective-permute-start(f32[48,64]{1,0:T(8,128)S(1)} %get-tuple-element.40), channel_id=1, source_target_pairs={{1,0},{2,1},{3,2},{5,4},{6,5},{7,6},{9,8},{10,9},{11,10},{13,12},{... | collective-permute-start | bytes 36872 | tf_op jit(solution)/shard_map/ppermute | solution.py:602
  24.1 0.6 copy-start.10
  24.1 0.6 copy-start.11
  24.1 0.6 copy-start.2
  24.1 0.6 copy-start.3
  35.8 23.2 %copy-start.12 = (s32[192]{0:T(256)S(1)}, s32[192]{0:T(256)}, u32[]{:S(2)}) copy-start(s32[192]{0:T(256)} %param.15) | copy-start | bytes 2308
  35.8 16.7 %all-to-all-start = ((f32[8,3,48,128]{3,2,1,0:T(8,128)}), f32[8,3,48,128]{3,2,1,0:T(8,128)S(1)}, u32[]{:S(2)}, u32[]{:S(2)}) async-start(f32[8,3,48,128]{3,2,1,0:T(8,128)} %get-tuple-element.28), calls=%async_computation | async-start | bytes 1179648 | tf_op jit(solution)/shard_map/all_to_all | solution.py:651
  52.5 0.9 copy-start.1
  55.4 13.9 %all-to-all-start.1 = ((f32[8,3,48,128]{3,2,1,0:T(8,128)}), f32[8,3,48,128]{3,2,1,0:T(8,128)S(1)}, u32[]{:S(2)}, u32[]{:S(2)}) async-start(f32[8,3,48,128]{3,2,1,0:T(8,128)} %solve.1), calls=%async_computation.1 | async-start | bytes 1179648 | tf_op jit(solution)/shard_map/all_to_all | solution.py:651
  59.2 19.8 %collective-permute-start.4 = (f32[7,48,128]{2,1,0:T(8,128)}, f32[7,48,128]{2,1,0:T(8,128)S(1)}, u32[]{:S(2)}, u32[]{:S(2)}) collective-permute-start(f32[7,48,128]{2,1,0:T(8,128)} %get-tuple-element.29.rest_0_), channel_id=1, source_target_pairs={{0,1},{1,2},{2,3},{3,0},{4,5},{5,6},{6,7},{7,4},{8,9},{9,10},{10,1... | collective-permute-start | bytes 516104 | tf_op jit(solution)/shard_map/ppermute | solution.py:683
  61.9 19.8 %collective-permute-start.5 = (f32[7,48,128]{2,1,0:T(8,128)}, f32[7,48,128]{2,1,0:T(8,128)S(1)}, u32[]{:S(2)}, u32[]{:S(2)}) collective-permute-start(f32[7,48,128]{2,1,0:T(8,128)} %get-tuple-element.29.rest_0_), channel_id=1, source_target_pairs={{0,2},{1,3},{2,0},{3,1},{4,6},{5,7},{6,4},{7,5},{8,10},{9,11},{10,... | collective-permute-start | bytes 516104 | tf_op jit(solution)/shard_map/ppermute | solution.py:683
  64.5 17.2 %collective-permute-start.6 = (f32[7,48,128]{2,1,0:T(8,128)}, f32[7,48,128]{2,1,0:T(8,128)S(1)}, u32[]{:S(2)}, u32[]{:S(2)}) collective-permute-start(f32[7,48,128]{2,1,0:T(8,128)} %get-tuple-element.29.rest_0_), channel_id=1, source_target_pairs={{0,3},{1,0},{2,1},{3,2},{4,7},{5,4},{6,5},{7,6},{8,11},{9,8},{10,9... | collective-permute-start | bytes 516104 | tf_op jit(solution)/shard_map/ppermute | solution.py:683
  69.4 0.8 copy-start
  73.8 7.9 %collective-permute-start.7 = (f32[6,8,128]{2,1,0:T(8,128)}, f32[6,8,128]{2,1,0:T(8,128)S(1)}, u32[]{:S(2)}, u32[]{:S(2)}) collective-permute-start(f32[6,8,128]{2,1,0:T(8,128)} %get-tuple-element.34.rest_4_), channel_id=1, source_target_pairs={{0,1},{1,2},{2,3},{3,0},{4,5},{5,6},{6,7},{7,4},{8,9},{9,10},{10,1... | collective-permute-start | bytes 73736 | tf_op jit(solution)/shard_map/ppermute | solution.py:683
  76.4 5.3 %collective-permute-start.8 = (f32[6,8,128]{2,1,0:T(8,128)}, f32[6,8,128]{2,1,0:T(8,128)S(1)}, u32[]{:S(2)}, u32[]{:S(2)}) collective-permute-start(f32[6,8,128]{2,1,0:T(8,128)} %get-tuple-element.34.rest_4_), channel_id=1, source_target_pairs={{0,2},{1,3},{2,0},{3,1},{4,6},{5,7},{6,4},{7,5},{8,10},{9,11},{10,... | collective-permute-start | bytes 73736 | tf_op jit(solution)/shard_map/ppermute | solution.py:683
  79.0 4.0 %copy-start.4 = (f32[7,48,128]{2,1,0:T(8,128)}, f32[7,48,128]{2,1,0:T(8,128)S(1)}, u32[]{:S(2)}) copy-start(f32[7,48,128]{2,1,0:T(8,128)S(1)} %collective-permute-done.4.rest_1_) | copy-start | bytes 516100
  79.0 4.0 %collective-permute-start.9 = (f32[6,8,128]{2,1,0:T(8,128)}, f32[6,8,128]{2,1,0:T(8,128)S(1)}, u32[]{:S(2)}, u32[]{:S(2)}) collective-permute-start(f32[6,8,128]{2,1,0:T(8,128)} %get-tuple-element.34.rest_4_), channel_id=1, source_target_pairs={{0,3},{1,0},{2,1},{3,2},{4,7},{5,4},{6,5},{7,6},{8,11},{9,8},{10,9... | collective-permute-start | bytes 73736 | tf_op jit(solution)/shard_map/ppermute | solution.py:683
  81.7 1.4 %copy-start.5 = (f32[7,48,128]{2,1,0:T(8,128)}, f32[7,48,128]{2,1,0:T(8,128)S(1)}, u32[]{:S(2)}) copy-start(f32[7,48,128]{2,1,0:T(8,128)S(1)} %collective-permute-done.5.rest_2_) | copy-start | bytes 516100
  81.7 1.4 %copy-start.6 = (f32[7,48,128]{2,1,0:T(8,128)}, f32[7,48,128]{2,1,0:T(8,128)S(1)}, u32[]{:S(2)}) copy-start(f32[7,48,128]{2,1,0:T(8,128)S(1)} %collective-permute-done.6.rest_3_) | copy-start | bytes 516100
  81.7 1.4 %copy-start.7 = (f32[6,8,128]{2,1,0:T(8,128)}, f32[6,8,128]{2,1,0:T(8,128)S(1)}, u32[]{:S(2)}) copy-start(f32[6,8,128]{2,1,0:T(8,128)S(1)} %collective-permute-done.7.rest_5_) | copy-start | bytes 73732
  81.7 1.4 %copy-start.8 = (f32[6,8,128]{2,1,0:T(8,128)}, f32[6,8,128]{2,1,0:T(8,128)S(1)}, u32[]{:S(2)}) copy-start(f32[6,8,128]{2,1,0:T(8,128)S(1)} %collective-permute-done.8.rest_6_) | copy-start | bytes 73732
  83.1 0.6 copy-start.9
  98.2 17.5 %all-to-all-start.2 = ((f32[32,1,7]{2,1,0:T(1,128)}), f32[32,1,7]{2,1,0:T(1,128)S(1)}, u32[]{:S(2)}, u32[]{:S(2)}) async-start(f32[32,1,7]{2,1,0:T(1,128)} %bitcast.10), calls=%async_computation.2 | async-start | bytes 32768 | tf_op jit(solution)/shard_map/all_to_all | solution.py:768

commit v5 on v4

--- a/solution.py
+++ b/solution.py
@@ -38,17 +38,31 @@
     return hi, (x - hi.astype(f32)).astype(bf16)
 
 
-def dot(x, y):
-    return jnp.dot(x, y, preferred_element_type=f32)
-
-
-def split(x):
-    hi, lo = halves(x)
-    return jnp.concatenate([hi, lo, hi], axis=1)
-
-
-def product(x, weights):
-    return dot(split(x), weights)
+def products(sources, wh, wl, store, pieces=3):
+    count = sources[0][0].shape[0] // (2 * pieces)
+
+    def run(*acc):
+        for x, k in sources:
+            for unit in range(2):
+                pltpu.matmul_push_rhs(wh[k], 0, unit)
+                pltpu.matmul_push_rhs(wl[k], 1, unit)
+            parts = {}
+            for c in range(pieces):
+                for unit in range(2):
+                    at = (unit * pieces + c) * count
+                    parts[unit, c] = hi, lo = halves(x[at : at + count])
+                    ref = acc[unit * pieces + c]
+                    pltpu.matmul_acc_lhs(ref, hi, load_staged_rhs=0 if c == 0 else None)
+                    pltpu.matmul_acc_lhs(ref, lo)
+            for c in range(pieces):
+                for unit in range(2):
+                    ref = acc[unit * pieces + c]
+                    pltpu.matmul_acc_lhs(ref, parts[unit, c][0], load_staged_rhs=1 if c == 0 else None)
+        for c in range(pieces):
+            for unit in range(2):
+                store((unit * pieces + c) * count, pltpu.matmul_pop(acc[unit * pieces + c]))
+
+    pl.run_scoped(run, *[pltpu.ACC(unit)((count, 256), f32) for unit in (0, 1) for _ in range(pieces)])
 
 
 def expand(mat, mixed):
@@ -59,7 +73,7 @@
     dst = lax.broadcasted_iota(jnp.int32, (256, 256), 1) // 64
     if mixed:
         src = jnp.where(src == 1, 2, jnp.where(src == 2, 1, src))
-    return halves(jnp.where(src == dst, wide, 0.0))
+    return jnp.where(src == dst, wide, 0.0)
 
 
 def quad(mat):
@@ -161,15 +175,10 @@
     return jnp.take_along_axis(sg[v, m >> 6], idx, axis=1, mode="promise_in_bounds")
 
 
-def set_weights(weights, k, mat, mixed):
-    hi, lo = expand(mat, mixed)
-    weights[768 * k : 768 * k + 256] = hi
-    weights[768 * k + 256 : 768 * k + 512] = hi
-    weights[768 * k + 512 : 768 * k + 768] = lo
-
-
-def weight(weights, k):
-    return weights[768 * k : 768 * (k + 1)]
+def set_weights(wh, wl, k, wide):
+    hi, lo = halves(wide)
+    wh[k] = hi
+    wl[k] = lo
 
 
 def lat_filter(vs, rows, prm, u_ref, e_ref):
@@ -192,14 +201,18 @@
                 e_ref[c, k, e * width : (e + 1) * width] = edges[e][k][c * width : (c + 1) * width]
 
 
-def put_mixed(k, b, rows, res, w_ref, u_ref):
-    base = b * 2 * PAIRS
-    for p in range(PAIRS):
-        part = res[p * rows : (p + 1) * rows]
-        w_ref[k, base + 2 * p] = part[:, :LANES]
-        w_ref[k, base + 2 * p + 1] = part[:, LANES:]
-    at = pl.ds(pl.multiple_of(base, 2 * PAIRS), 2 * PAIRS)
-    u_ref[k, :, at, :] = jnp.swapaxes(w_ref[k, at], 0, 1)
+def put_mixed(k, rows, res, w_ref, u_ref):
+    def body(b, _):
+        base = pl.multiple_of(b * 8, 8)
+        for o in range(4):
+            at = pl.ds(pl.multiple_of((b * 4 + o) * rows, 8), rows)
+            w_ref[k, base + 2 * o] = res[at, 0:LANES]
+            w_ref[k, base + 2 * o + 1] = res[at, LANES:]
+        at = pl.ds(base, 8)
+        u_ref[k, :, at, :] = jnp.swapaxes(w_ref[k, at], 0, 1)
+        return 0
+
+    lax.fori_loop(0, BLOCK // 4, body, 0)
 
 
 def set_params(scales, classes, chi_coef, prm):
@@ -222,49 +235,59 @@
 
 def lat_plain(
     rows, pairs, scales, classes, chi_coef, sigma, vert, b1lo, b1hi, b2lo, b2hi,
-    w_ref, u_ref, e_ref, prm, xs, wt, sg,
+    w_ref, u_ref, e_ref, prm, xs, wh, wl, sg,
 ):
     g = pl.program_id(0)
 
     @pl.when(g == 0)
     def _():
         set_params(scales, classes, chi_coef, prm)
-        set_weights(wt, 0, vert[1], True)
-        set_weights(wt, 1, vert[2], True)
+        set_weights(wh, wl, 0, expand(vert[1], True))
+        set_weights(wh, wl, 1, expand(vert[2], True))
         stage_sigma(sigma, sg, (1, 2))
 
     lane = lax.broadcasted_iota(jnp.int32, (rows, LANES), 1)
     high = (lane >= 64).astype(jnp.int32)
 
     def body(b, _):
-        for p in range(PAIRS):
-            at = slice(p * rows, (p + 1) * rows)
-            cols = pl.ds(pl.multiple_of((b * PAIRS + p) * LANES, LANES), LANES)
-            m = g * BLOCK + b * PAIRS + p
+        for o in range(4):
+            p = b * 4 + o
+            at = pl.ds(pl.multiple_of(p * rows, 8), rows)
+            cols = pl.ds(pl.multiple_of(p * LANES, LANES), LANES)
             for k, sides in enumerate(((b1lo, b1hi), (b2lo, b2hi))):
                 for side in range(2):
-                    s = sigma_tile(sg, k + 1, m + side * pairs, high)
+                    s = sigma_tile(sg, k + 1, g * BLOCK + p + side * pairs, high)
                     xs[k, at, side * LANES : (side + 1) * LANES] = sides[side][0, :, cols] * s
-        for k in range(2):
-            put_mixed(k, b, rows, product(xs[k], weight(wt, k)), w_ref, u_ref)
         return 0
 
-    lax.fori_loop(0, BLOCK // PAIRS, body, 0)
+    lax.fori_loop(0, BLOCK // 4, body, 0)
+    for k in range(2):
+
+        def store(first, res, k=k):
+            xs[k, first : first + res.shape[0], :] = res
+
+        products([(xs.at[k], k)], wh, wl, store)
+        put_mixed(k, rows, xs.at[k], w_ref, u_ref)
     lat_filter((1, 2), rows, prm, u_ref, e_ref)
 
 
 def lat_balance(
     rows, pairs, prm, sigma, vert, bal, plo, phi, clo, chi, temp, north, south, west, east, w_in, u_in, e_in,
-    w_ref, u_ref, e_ref, xs, wt, sg,
+    w_ref, u_ref, e_ref, xs, wh, wl, sg,
 ):
     del w_in, u_in, e_in
     g = pl.program_id(0)
 
     @pl.when(g == 0)
     def _():
-        set_weights(wt, 0, vert[0], True)
-        (bh, bl), (vh, vl) = halves(bal[...]), halves(vert[0])
-        set_weights(wt, 1, dot(bh, vh) + dot(bl, vh) + dot(bh, vl), True)
+        set_weights(wh, wl, 0, expand(vert[0], True))
+        xs[0, 0:256, :] = expand(bal[...], False)
+
+        def fold(first, res):
+            set_rows = slice(first, first + res.shape[0])
+            wh[1, set_rows], wl[1, set_rows] = halves(res)
+
+        products([(xs.at[0, 0:256], 0)], wh, wl, fold, 1)
         stage_sigma(sigma, sg, (0,))
 
     lane = lax.broadcasted_iota(jnp.int32, (rows, LANES), 1)
@@ -287,20 +310,24 @@
         return 4.0 * x - beside - above - below
 
     def body(b, _):
-        for p in range(PAIRS):
-            at = slice(p * rows, (p + 1) * rows)
-            cols = at_tile(b * PAIRS + p)
-            m = g * BLOCK + b * PAIRS + p
+        for o in range(4):
+            p = b * 4 + o
+            at = pl.ds(pl.multiple_of(p * rows, 8), rows)
+            m = g * BLOCK + p
             for side, (pr, cr) in enumerate(((plo, clo), (phi, chi))):
                 s = sigma_tile(sg, 0, m + side * pairs, high)
                 to = slice(side * LANES, (side + 1) * LANES)
-                xs[0, at, to] = (pr[0, :, cols] + chi_row * cr[0, :, cols]) * s
+                xs[0, at, to] = (pr[0, :, at_tile(p)] + chi_row * cr[0, :, at_tile(p)]) * s
                 xs[1, at, to] = laplace(m + side * pairs) * s
-        res = dot(jnp.concatenate([split(xs[0]), split(xs[1])], axis=1), wt[...])
-        put_mixed(0, b, rows, res, w_ref, u_ref)
         return 0
 
-    lax.fori_loop(0, BLOCK // PAIRS, body, 0)
+    lax.fori_loop(0, BLOCK // 4, body, 0)
+
+    def store(first, res):
+        xs[0, first : first + res.shape[0], :] = res
+
+    products([(xs.at[0], 0), (xs.at[1], 1)], wh, wl, store)
+    put_mixed(0, rows, xs.at[0], w_ref, u_ref)
     lat_filter((0,), rows, prm, u_ref, e_ref)
 
 
@@ -332,8 +359,9 @@
         t4 = e4 + k3 * c1 + k2 * c2 + k1 * c3
         c4 = jnp.where(low, swap(t4), 0.0)
         t4 = t4 + span * c4
-        es_ref[2 * k, at, :] = jnp.where(low, t2, t1)
-        es_ref[2 * k + 1, at, :] = jnp.where(low, t4, t3)
+        for t in range(es_ref.shape[0]):
+            es_ref[t, 2 * k, at, :] = jnp.where(low, t2, t1)
+            es_ref[t, 2 * k + 1, at, :] = jnp.where(low, t4, t3)
         for e, x in enumerate((e1, e2, e3, e4)):
             el_ref[k, e, at, :] = x
 
@@ -346,7 +374,9 @@
     def _():
         x = sigma[0]
         lon = x.shape[1]
-        es_ref[6] = jnp.where(low_lanes((x.shape[0], LANES)), x[:, 0:1], x[:, lon - 1 : lon])
+        outer = jnp.where(low_lanes((x.shape[0], LANES)), x[:, 0:1], x[:, lon - 1 : lon])
+        for t in range(es_ref.shape[0]):
+            es_ref[t, 6] = outer
 
     def turn(b, _):
         at = pl.ds(pl.multiple_of(b * 8, 8), 8)
@@ -386,9 +416,10 @@
     lon_filter(prm, 8, o_ref, el_ref, es_ref, slice(0, 8))
 
 
-def join_kernel(n_lon, rows, packed, rq, place, prm, u_ref, w_ref, x_ref, el, elc, *rest):
-    sent, sent_x = rest[:n_lon], rest[n_lon : 2 * n_lon]
-    y_ref, yx_ref, col_ref, side_ref, energy, carry, extra, resp_x, resp_y, esm, esx = rest[2 * n_lon :]
+def join_kernel(
+    n_lon, rows, packed, rq, place, prm, u_ref, w_ref, x_ref, el, elc, esm, esx,
+    y_ref, yx_ref, col_ref, side_ref, energy, carry, extra, resp_x, resp_y,
+):
     g = pl.program_id(0)
     half = resp_x.shape[2]
     lat, me = place[0], place[1]
@@ -396,10 +427,6 @@
     @pl.when(g == 0)
     def _():
         energy[...] = jnp.zeros_like(energy)
-        for s in range(n_lon):
-            t = lax.rem(me - s + n_lon, n_lon)
-            esm[t] = sent[s][...]
-            esx[t] = sent_x[s][...]
         side_ref[0] = esm[jnp.maximum(me - 1, 0), 6]
         side_ref[1] = esm[jnp.minimum(me + 1, n_lon - 1), 6]
         for k, v in enumerate(ORDER):
@@ -486,7 +513,7 @@
 
 def end_kernel(
     rows, pairs, prm, sigma, north, south, vert, bal, col, side, y_ref, yx_ref,
-    out, xs, zx, zc, wt, sg, sx,
+    out, xs, xe, zx, zc, wh, wl, sg, sx,
 ):
     g = pl.program_id(0)
     half = 2 * pairs
@@ -497,18 +524,13 @@
     def _():
         for v in range(3):
             scaled = quad(vert[v]) * prm[v, 3:4, :]
-            set_weights(wt, v, scaled.T, True)
-        set_weights(wt, 3, quad(bal[...]).T, False)
+            set_weights(wh, wl, v, expand(scaled.T, True))
+        set_weights(wh, wl, 3, expand(quad(bal[...]).T, False))
         stage_sigma(sigma, sg, (0, 1, 2))
         for at in range(0, lon, LANES):
             width = min(LANES, lon - at)
             sx[at // LANES, 0:1, 0:width] = north[:, merged + at : merged + at + width]
             sx[at // LANES, 1:2, 0:width] = south[:, merged + at : merged + at + width]
-        lhs = jnp.where(low_lanes((rows, LANES)), col[0], col[1])
-        lhs = jnp.concatenate([lhs, jnp.zeros_like(lhs)], axis=1)
-        res = product(lhs, weight(wt, 0))
-        zc[0] = swap(res[:, :LANES] * swap(side[0]))
-        zc[1] = res[:, LANES:] * side[1]
 
     lane = lax.broadcasted_iota(jnp.int32, (rows, LANES), 1)
     high = (lane >= 64).astype(jnp.int32)
@@ -518,61 +540,104 @@
     def at_tile(m):
         return pl.ds(pl.multiple_of(m * LANES, LANES), LANES)
 
-    lhs = jnp.concatenate(
-        [jnp.concatenate([yx_ref[2 * p], yx_ref[2 * p + 1]], axis=1) for p in range(PAIRS)], axis=0
-    )
-    res = product(lhs, weight(wt, 0))
-    for p in range(PAIRS):
-        m = g * PAIRS + p
-        for side in range(2):
-            tile = m + side * pairs
+    row8 = lax.broadcasted_iota(jnp.int32, (8, LANES), 0)
+    for p in range(BLOCK):
+        xe[p * 8 : (p + 1) * 8, 0:LANES] = yx_ref[2 * p]
+        xe[p * 8 : (p + 1) * 8, LANES:] = yx_ref[2 * p + 1]
+    at_cols = slice(BLOCK * 8, BLOCK * 8 + rows)
+    xe[at_cols, 0:LANES] = jnp.where(lane < 64, col[0], col[1])
+    xe[at_cols, LANES:] = jnp.zeros((rows, LANES), f32)
+
+    def keep(first, res):
+        xe[first : first + res.shape[0], :] = res
+
+    products([(xe, 0)], wh, wl, keep, 1)
+    zc[0] = swap(xe[at_cols, 0:LANES] * swap(side[0]))
+    zc[1] = xe[at_cols, LANES:] * side[1]
+    for p in range(BLOCK):
+        for half_at in range(2):
+            tile = g * BLOCK + p + half_at * pairs
             s = jnp.take_along_axis(sx[tile >> 6], 2 * (tile & 63) + high8, axis=1, mode="promise_in_bounds")
-            part = res[p * 8 : (p + 1) * 8, side * LANES : (side + 1) * LANES]
-            zx[:, at_tile(tile)] = jnp.where(lax.broadcasted_iota(jnp.int32, (8, LANES), 0) < 2, part * s, 0.0)
-    for k in range(3):
-        for p in range(2 * PAIRS):
-            at = slice((p // 2) * rows, (p // 2 + 1) * rows)
-            xs[k, at, (p % 2) * LANES : (p % 2 + 1) * LANES] = y_ref[k, p]
-    results = {v: product(xs[k], weight(wt, v)) for k, v in enumerate(ORDER)}
-    for p in range(PAIRS):
-        m = g * PAIRS + p
-        for side in range(2):
-            at = at_tile(m + side * pairs)
-            z = [
-                results[v][p * rows : (p + 1) * rows, side * LANES : (side + 1) * LANES]
-                * sigma_tile(sg, v, m + side * pairs, high)
-                for v in range(3)
-            ]
-            out[0, :, at] = z[0]
-            out[1, :, at] = z[1] + chi_row * z[0]
-            out[2, :, at] = z[2]
+            part = xe[p * 8 : (p + 1) * 8, half_at * LANES : (half_at + 1) * LANES]
+            zx[:, at_tile(tile)] = jnp.where(row8 < 2, part * s, 0.0)
+
+    def gather_rows(b, _):
+        for o in range(4):
+            p = b * 4 + o
+            at = pl.ds(pl.multiple_of(p * rows, 8), rows)
+            for k in range(3):
+                xs[k, at, 0:LANES] = y_ref[k, 2 * p]
+                xs[k, at, LANES:] = y_ref[k, 2 * p + 1]
+        return 0
+
+    lax.fori_loop(0, BLOCK // 4, gather_rows, 0)
+    for k, v in enumerate(ORDER):
+
+        def store(first, res, k=k):
+            xs[k, first : first + res.shape[0], :] = res
+
+        products([(xs.at[k], v)], wh, wl, store)
+
+    def scale(b, _):
+        for o in range(4):
+            p = b * 4 + o
+            for half_at in range(2):
+                m = g * BLOCK + p + half_at * pairs
+                z = [
+                    xs[
+                        ORDER.index(v),
+                        pl.ds(pl.multiple_of(p * rows, 8), rows),
+                        half_at * LANES : (half_at + 1) * LANES,
+                    ]
+                    * sigma_tile(sg, v, m, high)
+                    for v in range(3)
+                ]
+                out[0, :, at_tile(m)] = z[0]
+                out[1, :, at_tile(m)] = z[1] + chi_row * z[0]
+                out[2, :, at_tile(m)] = z[2]
+        return 0
+
+    lax.fori_loop(0, BLOCK // 4, scale, 0)
 
     @pl.when(g == pl.num_programs(0) - 1)
     def _():
         row_id = lax.broadcasted_iota(jnp.int32, (rows, LANES), 0)
         last = half - 1
 
-        def body(b, _):
-            for p in range(PAIRS):
+        def laplace(b, base):
+            for o in range(4):
+                p = b * 4 + o
                 for side in range(2):
-                    m = b * PAIRS + p + side * pairs
+                    m = base + p + side * pairs
                     x = out[0, :, at_tile(m)]
                     left = jnp.where(m == 0, zc[0], out[0, :, at_tile(jnp.maximum(m - 1, 0))])
                     right = jnp.where(m == last, zc[1], out[0, :, at_tile(jnp.minimum(m + 1, last))])
                     beside = swap(x + jnp.where(lane >= 64, left, right))
                     above = jnp.where(row_id == 0, zx[0:1, at_tile(m)], pltpu.roll(x, 1, 0))
                     below = jnp.where(row_id == rows - 1, zx[1:2, at_tile(m)], pltpu.roll(x, rows - 1, 0))
-                    lap = 4.0 * x - beside - above - below
-                    xs[0, p * rows : (p + 1) * rows, side * LANES : (side + 1) * LANES] = lap
-            res = product(xs[0], weight(wt, 3))
-            for p in range(PAIRS):
+                    at = pl.ds(pl.multiple_of(p * rows, 8), rows)
+                    xs[0, at, side * LANES : (side + 1) * LANES] = 4.0 * x - beside - above - below
+            return base
+
+        def add(b, base):
+            for o in range(4):
+                p = b * 4 + o
+                at = pl.ds(pl.multiple_of(p * rows, 8), rows)
                 for side in range(2):
-                    at = at_tile(b * PAIRS + p + side * pairs)
-                    part = res[p * rows : (p + 1) * rows, side * LANES : (side + 1) * LANES]
-                    out[2, :, at] = out[2, :, at] + part
+                    to = at_tile(base + p + side * pairs)
+                    out[2, :, to] = out[2, :, to] + xs[0, at, side * LANES : (side + 1) * LANES]
+            return base
+
+        def store(first, res):
+            xs[0, first : first + res.shape[0], :] = res
+
+        def block(n, _):
+            lax.fori_loop(0, BLOCK // 4, laplace, n * BLOCK)
+            products([(xs.at[0], 3)], wh, wl, store)
+            lax.fori_loop(0, BLOCK // 4, add, n * BLOCK)
             return 0
 
-        lax.fori_loop(0, pairs // PAIRS, body, 0)
+        lax.fori_loop(0, pairs // BLOCK, block, 0)
 
 
 def shards(state, sigma, vert, bal_temp, chi_coef, scales, classes, owner):
@@ -624,8 +689,9 @@
             + [full(s) for s in more],
             out_shape=[jax.ShapeDtypeStruct(s, f32) for s in shapes + list(more)],
             scratch_shapes=[
-                pltpu.VMEM((2, PAIRS * rows, 256), f32),
-                pltpu.VMEM((2 * 768, 256), bf16),
+                pltpu.VMEM((2, BLOCK * rows, 256), f32),
+                pltpu.VMEM((2, 256, 256), bf16),
+                pltpu.VMEM((2, 256, 256), bf16),
                 pltpu.VMEM((nvars, pieces, rows, LANES), f32),
             ],
             compiler_params=params(),
@@ -647,10 +713,10 @@
     specs += [full(x.shape) for x in (north, south, west, east)] + [anywhere] * 3
     aliases = {13: 0, 14: 1, 15: 2}
     w, u, edges = lat_call(1, 2, functools.partial(lat_balance, rows, pairs), ins, specs, "lat_psi", aliases)
-    def trade(x):
-        return lax.all_to_all(x, "lat", split_axis=0, concat_axis=0, tiled=True)
-
-    shares = trade(edges)
+    def trade(x, axis):
+        return lax.all_to_all(x, axis, split_axis=0, concat_axis=0, tiled=True)
+
+    shares = trade(edges, "lat")
 
     rb = BLOCK
     local, el, es = pl.pallas_call(
@@ -664,12 +730,12 @@
         out_specs=[
             pl.BlockSpec((nvars, half, rb, LANES), lambda g: (0, 0, g, 0)),
             full((nvars, 4, rows, LANES)),
-            full((7, rows, LANES)),
+            full((n_lon, 7, rows, LANES)),
         ],
         out_shape=[
             jax.ShapeDtypeStruct((nvars, half, rows, LANES), f32),
             jax.ShapeDtypeStruct((nvars, 4, rows, LANES), f32),
-            jax.ShapeDtypeStruct((7, rows, LANES), f32),
+            jax.ShapeDtypeStruct((n_lon, 7, rows, LANES), f32),
         ],
         compiler_params=params(),
         cost_estimate=pl.CostEstimate(
@@ -678,13 +744,8 @@
         name="lon_tile",
     )(prm, sigma, u)
 
-    def round_lon(x):
-        return [x] + [
-            lax.ppermute(x, "lon", [(i, (i + s) % n_lon) for i in range(n_lon)]) for s in range(1, n_lon)
-        ]
-
     shares, _ = lax.optimization_barrier((shares, es))
-    sent = round_lon(es)
+    sent = trade(es, "lon")
     carries = pl.pallas_call(
         functools.partial(solve_kernel, n_lat, rows),
         grid=(1,),
@@ -695,17 +756,17 @@
         cost_estimate=pl.CostEstimate(flops=1000000, bytes_accessed=2 * shares.size * 4, transcendentals=0),
         name="solve",
     )(prm, shares)
-    carries = trade(carries)
+    carries = trade(carries, "lat")
 
     crossed, elc, esc = pl.pallas_call(
         carry_kernel,
         grid=(1,),
         in_specs=[full(prm.shape), full(carries.shape)],
-        out_specs=[full((nvars, half, 8, LANES)), full((nvars, 4, 8, LANES)), full((6, 8, LANES))],
+        out_specs=[full((nvars, half, 8, LANES)), full((nvars, 4, 8, LANES)), full((n_lon, 6, 8, LANES))],
         out_shape=[
             jax.ShapeDtypeStruct((nvars, half, 8, LANES), f32),
             jax.ShapeDtypeStruct((nvars, 4, 8, LANES), f32),
-            jax.ShapeDtypeStruct((6, 8, LANES), f32),
+            jax.ShapeDtypeStruct((n_lon, 6, 8, LANES), f32),
         ],
         compiler_params=params(),
         cost_estimate=pl.CostEstimate(
@@ -713,14 +774,14 @@
         ),
         name="lon_carry",
     )(prm, carries)
-    sent_x = round_lon(esc)
+    sent_x = trade(esc, "lon")
 
     packed = 2 * PAIRS
 
     def columns(r):
         return pl.BlockSpec((nvars, packed, r, LANES), lambda g: (0, g, 0, 0))
 
-    ins = [place, prm, local, w, crossed, el, elc] + sent + sent_x
+    ins = [place, prm, local, w, crossed, el, elc, sent, sent_x]
     specs = [full(x.shape) for x in ins]
     specs[0] = pl.BlockSpec(memory_space=pltpu.SMEM)
     specs[2:5] = [columns(rows), columns(rows), columns(8)]
@@ -747,8 +808,6 @@
             pltpu.VMEM((nvars, 4, 8, LANES), f32),
             pltpu.VMEM((nvars, 4, half, LANES), f32),
             pltpu.VMEM((nvars, 4, rows, LANES), f32),
-            pltpu.VMEM((n_lon, 7, rows, LANES), f32),
-            pltpu.VMEM((n_lon, 6, 8, LANES), f32),
         ],
         compiler_params=params(),
         cost_estimate=pl.CostEstimate(
@@ -770,19 +829,21 @@
 
     ins = [prm, sigma, north, south, vert, bal_temp, col, side, y, yx]
     specs = [full(x.shape) for x in ins]
-    specs[8] = columns(rows)
-    specs[9] = pl.BlockSpec((packed, 8, LANES), lambda g: (g, 0, 0))
+    specs[8] = pl.BlockSpec((nvars, 2 * BLOCK, rows, LANES), lambda g: (0, g, 0, 0))
+    specs[9] = pl.BlockSpec((2 * BLOCK, 8, LANES), lambda g: (g, 0, 0))
     applied = pl.pallas_call(
         functools.partial(end_kernel, rows, pairs),
-        grid=(half // packed,),
+        grid=(steps,),
         in_specs=specs,
         out_specs=full(state.shape),
         out_shape=jax.ShapeDtypeStruct(state.shape, f32),
         scratch_shapes=[
-            pltpu.VMEM((nvars, PAIRS * rows, 256), f32),
+            pltpu.VMEM((nvars, BLOCK * rows, 256), f32),
+            pltpu.VMEM((256, 256), f32),
             pltpu.VMEM((8, merged), f32),
             pltpu.VMEM((2, rows, LANES), f32),
-            pltpu.VMEM((4 * 768, 256), bf16),
+            pltpu.VMEM((4, 256, 256), bf16),
+            pltpu.VMEM((4, 256, 256), bf16),
             pltpu.VMEM((nvars, pieces, rows, LANES), f32),
             pltpu.VMEM((pieces, 8, LANES), f32),
         ],

time: 117 us -> 140 us (1.20)
  blocking collectives: 0 us -> 14.6 us
  waiting for transfers between devices: 6.42 us -> 20.1 us
  starting transfers between devices: 35.8 us -> 27.3 us
  Pallas kernels: 63.7 us -> 68.1 us
    all_to_all x2 -> x3, waiting for transfers between devices: 5.07 us -> 20 us  [trade(): return lax.all_to_all(x, axis, split_axis=0, concat_axis=0, tiled=True)]
    all_to_all x0 -> x1, blocking collectives: none -> 14.6 us  [trade(): return lax.all_to_all(x, axis, split_axis=0, concat_axis=0, tiled=True)]
    ppermute x6 -> x0, starting transfers between devices: 13.2 us -> none  [round_lon(): lax.ppermute(x, 'lon', [(i, (i + s) % n_lon) for i in range(n_lon)])]
    all_to_all x2 -> x3, starting transfers between devices: 9.8 us -> 15.5 us  [trade(): return lax.all_to_all(x, axis, split_axis=0, concat_axis=0, tiled=True)]
    pallas_call x1, Pallas kernels: 14 us -> 16.6 us  [shards(): pl.pallas_call(functools.partial(end_kernel, rows, pairs), grid=(steps,),...]
    pallas_call x2, Pallas kernels: 22.3 us -> 23.9 us  [lat_call(): pl.pallas_call(body, grid=(steps,), in_specs=specs, out_specs=[pl.BlockSp...]
    unnamed x26 -> x16, local copies, waits for them, and re-layouts: 2.91 us -> 2.06 us
  transfers between devices with their start and end apart: 13 -> 8, of which waited for: 3 -> 3; matrix products, arithmetic and copies ran while one was open for 2% -> 2% of each run, Pallas kernels for 32% -> 30%
where the time goes in v5:
time: 140 us
  Pallas kernels  68.1 us (49%)
  starting transfers between devices  27.3 us (20%)
  waiting for transfers between devices  20.1 us (14%)
  blocking collectives  14.6 us (10%)
  local copies, waits for them, and re-layouts  6.3 us (4%)
  other arithmetic  2.36 us (2%)
    pallas_call x2, Pallas kernels, lat_call(): pl.pallas_call(body, grid=(steps,), in_specs=specs, out_specs=[pl.BlockSp...  23.9 us
    all_to_all x3, waiting for transfers between devices, trade(): return lax.all_to_all(x, axis, split_axis=0, concat_axis=0, tiled=True)  20 us
    pallas_call x1, Pallas kernels, shards(): pl.pallas_call(functools.partial(end_kernel, rows, pairs), grid=(steps,),...  16.6 us
    all_to_all x3, starting transfers between devices, trade(): return lax.all_to_all(x, axis, split_axis=0, concat_axis=0, tiled=True)  15.5 us
    all_to_all x1, blocking collectives, trade(): return lax.all_to_all(x, axis, split_axis=0, concat_axis=0, tiled=True)  14.6 us
    pallas_call x1, Pallas kernels, shards(): pl.pallas_call(functools.partial(join_kernel, n_lon, rows, packed, 24), g...  12.8 us
    pallas_call x1, Pallas kernels, shards(): pl.pallas_call(functools.partial(lon_kernel, rb), grid=(rows // rb,), in_...  9.05 us
    ppermute x1, starting transfers between devices, shards(): west = lax.ppermute(state[2, :, merged - levels:], 'lon', up_lon)  4.3 us
  transfers between devices with their start and end apart: 8, of which 3 were waited for; matrix products, arithmetic and copies ran while one was open for 2% of the time, Pallas kernels for 30%

profile of v5, /device:TPU:0, one launch (start us, length us, event | category | flops | bytes accessed | tf_op | source)
XLA Modules:
  0.0 139.5 jit_solution(1199513392856938380)
XLA Ops:
  0.6 1.2 slice_bitcast_fusion
  1.8 0.7 slice_bitcast_fusion.4
  2.6 2.4 %collective-permute-start = (f32[1,12480]{1,0:T(1,128)S(1)}, f32[1,12480]{1,0:T(1,128)S(1)}, u32[]{:S(2)}, u32[]{:S(2)}) collective-permute-start(f32[1,12480]{1,0:T(1,128)S(1)} %pad_maximum_fusion), channel_id=1, source_target_pairs={{0,4},{4,8},{8,12},{12,16},{16,20},{20,24},{24,28},{1,5},{5,9},{9,... | collective-permute-start | bytes 149768 | tf_op jit(solution)/shard_map/ppermute | solution.py:664
  5.0 1.3 collective-permute-start.1
  6.3 0.8 slice_bitcast_fusion.2
  7.1 4.3 %collective-permute-start.2 = (f32[48,64]{1,0:T(8,128)S(1)}, f32[48,64]{1,0:T(8,128)S(1)}, u32[]{:S(2)}, u32[]{:S(2)}) collective-permute-start(f32[48,64]{1,0:T(8,128)S(1)} %get-tuple-element.41), channel_id=1, source_target_pairs={{0,1},{1,2},{2,3},{4,5},{5,6},{6,7},{8,9},{9,10},{10,11},{12,13},{... | collective-permute-start | bytes 36872 | tf_op jit(solution)/shard_map/ppermute | solution.py:666
  11.5 1.3 collective-permute-start.3
  12.8 12.4 %lat_chi_temp.1 = (f32[3,96,48,128]{3,2,1,0:T(8,128)}, f32[3,48,96,128]{3,2,1,0:T(8,128)}, f32[8,3,48,128]{3,2,1,0:T(8,128)}, f32[3,4,128]{2,1,0:T(4,128)}) custom-call(f32[8]{0:T(128)} %scales.1, s32[1,192]{1,0:T(1,128)} %bitcast.21, f32[1,64]{1,0:T(1,128)} %bitcast.22, f32[3,48,192]{2,1,0:T(8,128)} %sigma.7, f32[3,64,64]{2,1,0:T(8,128)} %vert.5, ...), custom_call_target="tpu_custom_call" | custom-call | flops 120000000 | bytes 14155776 | tf_op jit(solution)/shard_map/lat_chi_temp/pallas_call | solution.py:680
  25.1 0.0 collective-permute-done.2.west
  25.1 0.0 copy-start.5
  25.1 0.0 collective-permute-done.3.east
  25.2 0.0 copy-start.6
  25.2 0.0 collective-permute-done.north
  25.2 0.0 copy-start.3
  25.2 0.0 collective-permute-done.1.south
  25.2 0.0 copy-start.4
  25.2 0.5 copy-done.5
  25.7 0.0 copy-done.6
  25.8 0.0 copy-done.3
  25.8 0.0 copy-done.4
  25.8 11.6 %lat_psi.1 = (f32[3,96,48,128]{3,2,1,0:T(8,128)}, f32[3,48,96,128]{3,2,1,0:T(8,128)}, f32[8,3,48,128]{3,2,1,0:T(8,128)}) custom-call(f32[3,4,128]{2,1,0:T(4,128)} %get-tuple-element.21.prm, f32[3,48,192]{2,1,0:T(8,128)} %sigma.7, f32[3,64,64]{2,1,0:T(8,128)} %vert.5, f32[64,64]{1,0:T(8,128)} %bal.3, ...), custom_call_target="tpu_custom_call", output_to_operand_aliasing={{0}: (13, {}), {1}: (14, {}), {2}: (15, {})} | custom-call | flops 60000000 | bytes 7077888 | tf_op jit(solution)/shard_map/lat_psi/pallas_call | solution.py:680
  37.4 0.0 copy-start.7
  37.4 6.3 %all-to-all-start = ((f32[8,3,48,128]{3,2,1,0:T(8,128)}), f32[8,3,48,128]{3,2,1,0:T(8,128)S(1)}, u32[]{:S(2)}, u32[]{:S(2)}) async-start(f32[8,3,48,128]{3,2,1,0:T(8,128)} %get-tuple-element.28), calls=%async_computation | async-start | bytes 1179648 | tf_op jit(solution)/shard_map/all_to_all | solution.py:717
  43.7 9.0 %lon_tile.1 = (f32[3,96,48,128]{3,2,1,0:T(8,128)}, f32[3,4,48,128]{3,2,1,0:T(8,128)}, f32[4,7,48,128]{3,2,1,0:T(8,128)}) custom-call(f32[3,4,128]{2,1,0:T(4,128)} %get-tuple-element.21.prm, f32[3,48,192]{2,1,0:T(8,128)} %sigma.7, f32[3,48,96,128]{3,2,1,0:T(8,128)} %get-tuple-element.25.u_ref), custom_call_target="tpu_custom_call" | custom-call | flops 180000000 | bytes 14155776 | tf_op jit(solution)/shard_map/lon_tile/pallas_call | solution.py:722
  52.7 1.4 %all-to-all-done.edges = f32[8,3,48,128]{3,2,1,0:T(8,128)S(1)} async-done(((f32[8,3,48,128]{3,2,1,0:T(8,128)}), f32[8,3,48,128]{3,2,1,0:T(8,128)S(1)}, u32[]{:S(2)}, u32[]{:S(2)}) %all-to-all-start) | async-done | bytes 589856 | tf_op jit(solution)/shard_map/all_to_all | solution.py:717
  54.1 0.0 copy-start.1
  54.1 0.8 copy-done.1
  54.9 2.1 %solve.1 = f32[8,3,48,128]{3,2,1,0:T(8,128)} custom-call(f32[3,4,128]{2,1,0:T(4,128)} %get-tuple-element.21.prm, f32[8,3,48,128]{3,2,1,0:T(8,128)} %copy-done.1), custom_call_target="tpu_custom_call" | custom-call | flops 1000000 | bytes 1179648 | tf_op jit(solution)/shard_map/solve/pallas_call | solution.py:749
  57.1 14.6 %all_to_all.29.carries = f32[8,3,48,128]{3,2,1,0:T(8,128)} all-to-all(f32[8,3,48,128]{3,2,1,0:T(8,128)} %solve.1), channel_id=1, replica_groups=mesh['lat'=8,'lon'=4] {'lat'}, dimensions={0} | all-to-all | bytes 1179648 | tf_op jit(solution)/shard_map/all_to_all | solution.py:717
  71.7 5.9 %all-to-all-start.2 = ((f32[4,7,48,128]{3,2,1,0:T(8,128)}), f32[4,7,48,128]{3,2,1,0:T(8,128)S(1)}, u32[]{:S(2)}, u32[]{:S(2)}) async-start(f32[4,7,48,128]{3,2,1,0:T(8,128)} %get-tuple-element.29), calls=%async_computation.2 | async-start | bytes 1376256 | tf_op jit(solution)/shard_map/all_to_all | solution.py:717
  77.6 0.0 copy-done.7
  77.6 0.2 convert_reduce_fusion
  77.8 3.6 %lon_carry.1 = (f32[3,96,8,128]{3,2,1,0:T(8,128)}, f32[3,4,8,128]{3,2,1,0:T(8,128)}, f32[4,6,8,128]{3,2,1,0:T(8,128)}) custom-call(f32[3,4,128]{2,1,0:T(4,128)} %get-tuple-element.21.prm, f32[8,3,48,128]{3,2,1,0:T(8,128)} %all_to_all.29.carries), custom_call_target="tpu_custom_call" | custom-call | flops 30000000 | bytes 1769472 | tf_op jit(solution)/shard_map/lon_carry/pallas_call | solution.py:761
  81.4 14.1 %all-to-all-done.2.esm = f32[4,7,48,128]{3,2,1,0:T(8,128)S(1)} async-done(((f32[4,7,48,128]{3,2,1,0:T(8,128)}), f32[4,7,48,128]{3,2,1,0:T(8,128)S(1)}, u32[]{:S(2)}, u32[]{:S(2)}) %all-to-all-start.2) | async-done | bytes 688160 | tf_op jit(solution)/shard_map/all_to_all | solution.py:717
  95.6 0.0 copy-start
  95.6 3.3 %all-to-all-start.3 = ((f32[4,6,8,128]{3,2,1,0:T(8,128)}), f32[4,6,8,128]{3,2,1,0:T(8,128)S(1)}, u32[]{:S(2)}, u32[]{:S(2)}) async-start(f32[4,6,8,128]{3,2,1,0:T(8,128)} %get-tuple-element.34), calls=%async_computation.3 | async-start | bytes 196608 | tf_op jit(solution)/shard_map/all_to_all | solution.py:717
  98.9 0.7 slice.33
  99.6 0.6 pad_add_fusion.place
  100.2 4.5 %all-to-all-done.3.esx = f32[4,6,8,128]{3,2,1,0:T(8,128)S(1)} async-done(((f32[4,6,8,128]{3,2,1,0:T(8,128)}), f32[4,6,8,128]{3,2,1,0:T(8,128)S(1)}, u32[]{:S(2)}, u32[]{:S(2)}) %all-to-all-start.3) | async-done | bytes 98336 | tf_op jit(solution)/shard_map/all_to_all | solution.py:717
  104.7 0.0 copy-start.2
  104.7 0.0 copy-done
  104.7 0.6 copy-done.2
  105.3 12.8 %join.1 = (f32[3,96,48,128]{3,2,1,0:T(8,128)}, f32[96,8,128]{2,1,0:T(8,128)}, f32[2,48,128]{2,1,0:T(8,128)}, f32[2,48,128]{2,1,0:T(8,128)}, f32[3,8,128]{2,1,0:T(8,128)}) custom-call(s32[2]{0:T(128)} %pad_add_fusion.place, f32[3,4,128]{2,1,0:T(4,128)} %get-tuple-element.21.prm, f32[3,96,48,128]{3,2,1,0:T(8,128)} %get-tuple-element.26.u_ref, ...), custom_call_target="tpu_custom_call" | custom-call | flops 60000000 | bytes 21233664 | tf_op jit(solution)/shard_map/join/pallas_call | solution.py:788
  118.1 0.7 reduce_sum.37
  118.8 0.1 slice_add_fusion
  118.9 0.1 broadcast_in_dim.14
  119.0 0.1 select_reduce_fusion
  119.1 0.7 all_to_all.22
  119.8 2.6 %all-to-all-start.4 = ((f32[32,1,7]{2,1,0:T(1,128)}), f32[32,1,7]{2,1,0:T(1,128)S(1)}, u32[]{:S(2)}, u32[]{:S(2)}) async-start(f32[32,1,7]{2,1,0:T(1,128)} %bitcast.10), calls=%async_computation.4 | async-start | bytes 32768 | tf_op jit(solution)/shard_map/all_to_all | solution.py:827
  122.4 16.6 %finish.1 = f32[3,48,12288]{2,1,0:T(8,128)} custom-call(f32[3,4,128]{2,1,0:T(4,128)} %get-tuple-element.21.prm, f32[3,48,192]{2,1,0:T(8,128)} %sigma.7, f32[1,12480]{1,0:T(1,128)} %copy-done.3, f32[1,12480]{1,0:T(1,128)} %copy-done.4, f32[3,64,64]{2,1,0:T(8,128)} %vert.5, f32[64,64]{1,0:T(8,128)} %bal.3, f32[2,48,128]{2,1,0:T(8,128)} %get-tuple-element.35.col, ...), custom_call_target="tpu_custom_call" | custom-call | flops 300000000 | bytes 14155776 | tf_op jit(solution)/shard_map/finish/pallas_call | solution.py:834
  138.9 0.0 all-to-all-done.4
  138.9 0.1 reduce_sum.39
  139.0 0.5 multiply_bitcast_fusion
  (4 shorter events, 0.1 us)
Async XLA Ops:
  2.6 22.6 %collective-permute-start = (f32[1,12480]{1,0:T(1,128)S(1)}, f32[1,12480]{1,0:T(1,128)S(1)}, u32[]{:S(2)}, u32[]{:S(2)}) collective-permute-start(f32[1,12480]{1,0:T(1,128)S(1)} %pad_maximum_fusion), channel_id=1, source_target_pairs={{0,4},{4,8},{8,12},{12,16},{16,20},{20,24},{24,28},{1,5},{5,9},{9,... | collective-permute-start | bytes 149768 | tf_op jit(solution)/shard_map/ppermute | solution.py:664
  5.0 20.2 %collective-permute-start.1 = (f32[1,12480]{1,0:T(1,128)S(1)}, f32[1,12480]{1,0:T(1,128)S(1)}, u32[]{:S(2)}, u32[]{:S(2)}) collective-permute-start(f32[1,12480]{1,0:T(1,128)S(1)} %pad_maximum_fusion.1), channel_id=1, source_target_pairs={{4,0},{8,4},{12,8},{16,12},{20,16},{24,20},{28,24},{5,1},{9,5},{13... | collective-permute-start | bytes 149768 | tf_op jit(solution)/shard_map/ppermute | solution.py:665
  7.1 18.0 %collective-permute-start.2 = (f32[48,64]{1,0:T(8,128)S(1)}, f32[48,64]{1,0:T(8,128)S(1)}, u32[]{:S(2)}, u32[]{:S(2)}) collective-permute-start(f32[48,64]{1,0:T(8,128)S(1)} %get-tuple-element.41), channel_id=1, source_target_pairs={{0,1},{1,2},{2,3},{4,5},{5,6},{6,7},{8,9},{9,10},{10,11},{12,13},{... | collective-permute-start | bytes 36872 | tf_op jit(solution)/shard_map/ppermute | solution.py:666
  11.5 13.7 %collective-permute-start.3 = (f32[48,64]{1,0:T(8,128)S(1)}, f32[48,64]{1,0:T(8,128)S(1)}, u32[]{:S(2)}, u32[]{:S(2)}) collective-permute-start(f32[48,64]{1,0:T(8,128)S(1)} %get-tuple-element.40), channel_id=1, source_target_pairs={{1,0},{2,1},{3,2},{5,4},{6,5},{7,6},{9,8},{10,9},{11,10},{13,12},{... | collective-permute-start | bytes 36872 | tf_op jit(solution)/shard_map/ppermute | solution.py:667
  25.1 0.6 copy-start.5
  25.2 0.6 copy-start.6
  25.2 0.6 copy-start.3
  25.2 0.6 copy-start.4
  37.4 40.2 %copy-start.7 = (s32[192]{0:T(256)S(1)}, s32[192]{0:T(256)}, u32[]{:S(2)}) copy-start(s32[192]{0:T(256)} %param.15) | copy-start | bytes 2308
  37.4 16.7 %all-to-all-start = ((f32[8,3,48,128]{3,2,1,0:T(8,128)}), f32[8,3,48,128]{3,2,1,0:T(8,128)S(1)}, u32[]{:S(2)}, u32[]{:S(2)}) async-start(f32[8,3,48,128]{3,2,1,0:T(8,128)} %get-tuple-element.28), calls=%async_computation | async-start | bytes 1179648 | tf_op jit(solution)/shard_map/all_to_all | solution.py:717
  54.1 0.8 copy-start.1
  71.7 23.9 %all-to-all-start.2 = ((f32[4,7,48,128]{3,2,1,0:T(8,128)}), f32[4,7,48,128]{3,2,1,0:T(8,128)S(1)}, u32[]{:S(2)}, u32[]{:S(2)}) async-start(f32[4,7,48,128]{3,2,1,0:T(8,128)} %get-tuple-element.29), calls=%async_computation.2 | async-start | bytes 1376256 | tf_op jit(solution)/shard_map/all_to_all | solution.py:717
  95.6 9.1 %copy-start = (f32[4,7,48,128]{3,2,1,0:T(8,128)}, f32[4,7,48,128]{3,2,1,0:T(8,128)S(1)}, u32[]{:S(2)}) copy-start(f32[4,7,48,128]{3,2,1,0:T(8,128)S(1)} %all-to-all-done.2.esm) | copy-start | bytes 2064388
  95.6 9.1 %all-to-all-start.3 = ((f32[4,6,8,128]{3,2,1,0:T(8,128)}), f32[4,6,8,128]{3,2,1,0:T(8,128)S(1)}, u32[]{:S(2)}, u32[]{:S(2)}) async-start(f32[4,6,8,128]{3,2,1,0:T(8,128)} %get-tuple-element.34), calls=%async_computation.3 | async-start | bytes 196608 | tf_op jit(solution)/shard_map/all_to_all | solution.py:717
  104.7 0.6 copy-start.2
  119.8 19.1 %all-to-all-start.4 = ((f32[32,1,7]{2,1,0:T(1,128)}), f32[32,1,7]{2,1,0:T(1,128)S(1)}, u32[]{:S(2)}, u32[]{:S(2)}) async-start(f32[32,1,7]{2,1,0:T(1,128)} %bitcast.10), calls=%async_computation.4 | async-start | bytes 32768 | tf_op jit(solution)/shard_map/all_to_all | solution.py:827

commit v6 on v4

--- a/solution.py
+++ b/solution.py
@@ -14,7 +14,7 @@
 PAIRS = 8
 BLOCK = 24
 ORDER = (1, 2, 0)
-LIMIT = 60 * 1024 * 1024
+LIMIT = 22 * 1024 * 1024
 
 
 def params():
@@ -129,7 +129,7 @@
 
 
 def cascade(count, load, store, decay, start):
-    step = 8
+    step = 24
     edges = []
     for stage in range(4):
         back = stage % 2 == 1
@@ -402,51 +402,50 @@
             esx[t] = sent_x[s][...]
         side_ref[0] = esm[jnp.maximum(me - 1, 0), 6]
         side_ref[1] = esm[jnp.minimum(me + 1, n_lon - 1), 6]
+        length = jnp.stack([prm[v, 0:1, :] for v in ORDER])
+        decay = jnp.stack([prm[v, 1:2, :] for v in ORDER])
+        whole = constants(length, decay, 2 * half)
+        span, k1, k2, k3 = constants(length, decay, half)
+        low = low_lanes((len(ORDER), rows + 8, LANES))
+        cache = {}
+
+        def both(main, more):
+            parts = [jnp.concatenate([main(k), more(k)], axis=0) for k in range(len(ORDER))]
+            return jnp.stack(parts)
+
+        def edge(t, e):
+            i = e // 2
+            if (t, i) not in cache:
+                x = both(lambda k: esm[t, 2 * k + i], lambda k: esx[t, 2 * k + i])
+                y = swap(x)
+                cache[t, i] = (jnp.where(low, y, x), jnp.where(low, x, y))
+            return cache[t, i][e % 2]
+
+        d1, d2, d3, d4 = pick(solve_carries(n_lon, edge, whole), me)
+        e1, e2, e3, e4 = (both(lambda k, e=e: el[k, e], lambda k, e=e: elc[k, e]) for e in range(4))
+        c1 = jnp.where(low, d1, swap(e1 + span * d1))
+        c2 = jnp.where(low, swap(e2 + k1 * c1 + span * d2), d2)
+        c3 = jnp.where(low, d3, swap(e3 + k2 * c1 + k1 * c2 + span * d3))
+        c4 = jnp.where(low, swap(e4 + k3 * c1 + k2 * c2 + k1 * c3 + span * d4), d4)
         for k, v in enumerate(ORDER):
-            length = prm[v, 0:1, :]
-            decay = prm[v, 1:2, :]
-            whole = constants(length, decay, 2 * half)
-            span, k1, k2, k3 = constants(length, decay, half)
-
-            def solve(gathered, own, k=k, whole=whole, half_c=(span, k1, k2, k3)):
-                span, k1, k2, k3 = half_c
-                low = low_lanes(own.shape[2:])
-                cache = {}
-
-                def edge(t, e):
-                    if (t, e // 2) not in cache:
-                        x = gathered[t, 2 * k + e // 2]
-                        y = swap(x)
-                        cache[t, e // 2] = (jnp.where(low, y, x), jnp.where(low, x, y))
-                    return cache[t, e // 2][e % 2]
-
-                d1, d2, d3, d4 = pick(solve_carries(n_lon, edge, whole), me)
-                e1, e2, e3, e4 = (own[k, e] for e in range(4))
-                c1 = jnp.where(low, d1, swap(e1 + span * d1))
-                c2 = jnp.where(low, swap(e2 + k1 * c1 + span * d2), d2)
-                c3 = jnp.where(low, d3, swap(e3 + k2 * c1 + k1 * c2 + span * d3))
-                c4 = jnp.where(low, swap(e4 + k3 * c1 + k2 * c2 + k1 * c3 + span * d4), d4)
-                return (c1, c2, c3, c4), d3, d4
-
-            for e, r in enumerate(responses(length, decay, half)):
+            for e, r in enumerate(responses(prm[v, 0:1, :], prm[v, 1:2, :], half)):
                 resp_x[k, e] = r
-            ry = responses(length, decay, rows)
+            ry = responses(prm[v, 0:1, :], prm[v, 1:2, :], rows)
             for e in range(4):
                 resp_y[k, e] = ry[e]
-            cc, f3, f4 = solve(esx, elc)
-            c, d3, d4 = solve(esm, el)
-
-            def total(x, rows_of, ry=ry):
+
+            def total(x, ry=ry):
+                y = x[:rows]
                 for e in range(4):
-                    x = x + ry[e] * rows_of[e : e + 1, :]
-                return x
-
-            for e in range(4):
-                extra[k, e] = cc[e]
-                carry[k, e] = total(c[e], cc[e])
+                    y = y + ry[e] * x[rows + e : rows + e + 1]
+                return y
+
+            for e, c in enumerate((c1, c2, c3, c4)):
+                extra[k, e] = c[k, rows:]
+                carry[k, e] = total(c[k])
             if v == 0:
-                col_ref[0] = total(d3, f3)
-                col_ref[1] = total(d4, f4)
+                col_ref[0] = total(d3[k])
+                col_ref[1] = total(d4[k])
 
     row8 = lax.broadcasted_iota(jnp.int32, (8, LANES), 0)
     for k, v in enumerate(ORDER):

time: 117 us -> 126 us (1.077)
  local copies, waits for them, and re-layouts: 7.14 us -> 34.1 us
  Pallas kernels: 63.7 us -> 44.4 us
  starting transfers between devices: 35.8 us -> 37.5 us
    unnamed x26 -> x38, local copies, waits for them, and re-layouts: 2.91 us -> 30.6 us
    pallas_call x2, Pallas kernels: 22.3 us -> 16.7 us  [lat_call(): pl.pallas_call(body, grid=(steps,), in_specs=specs, out_specs=[pl.BlockSp...]
    pallas_call x1, Pallas kernels: 12.8 us -> 8.18 us  [shards(): pl.pallas_call(functools.partial(join_kernel, n_lon, rows, packed, 24), g...]
    pallas_call x1, Pallas kernels: 8.93 us -> 5.23 us  [shards(): pl.pallas_call(functools.partial(lon_kernel, rb), grid=(rows // rb,), in_...]
    ppermute x6, waiting for transfers between devices: 1.34 us -> 4 us  [round_lon(): lax.ppermute(x, 'lon', [(i, (i + s) % n_lon) for i in range(n_lon)])]
    pallas_call x1, Pallas kernels: 14 us -> 11.8 us  [shards(): pl.pallas_call(functools.partial(end_kernel, rows, pairs), grid=(half //...]
    pallas_call x1, Pallas kernels: 3.61 us -> 1.58 us  [shards(): pl.pallas_call(carry_kernel, grid=(1,), in_specs=[full(prm.shape), full(c...]
    all_to_all x2, waiting for transfers between devices: 5.07 us -> 3.62 us  [trade(): return lax.all_to_all(x, 'lat', split_axis=0, concat_axis=0, tiled=True)]
  transfers between devices with their start and end apart: 13 -> 13, of which waited for: 3 -> 2; matrix products, arithmetic and copies ran while one was open for 2% -> 1% of each run, Pallas kernels for 32% -> 22%
where the time goes in v6:
time: 126 us
  Pallas kernels  44.4 us (35%)
  starting transfers between devices  37.5 us (30%)
  local copies, waits for them, and re-layouts  34.1 us (27%)
  waiting for transfers between devices  7.63 us (6%)
    unnamed x38, local copies, waits for them, and re-layouts  30.6 us
    pallas_call x2, Pallas kernels, lat_call(): pl.pallas_call(body, grid=(steps,), in_specs=specs, out_specs=[pl.BlockSp...  16.7 us
    ppermute x6, starting transfers between devices, round_lon(): lax.ppermute(x, 'lon', [(i, (i + s) % n_lon) for i in range(n_lon)])  13.2 us
    pallas_call x1, Pallas kernels, shards(): pl.pallas_call(functools.partial(end_kernel, rows, pairs), grid=(half //...  11.8 us
    all_to_all x2, starting transfers between devices, trade(): return lax.all_to_all(x, 'lat', split_axis=0, concat_axis=0, tiled=True)  10.6 us
    pallas_call x1, Pallas kernels, shards(): pl.pallas_call(functools.partial(join_kernel, n_lon, rows, packed, 24), g...  8.18 us
    pallas_call x1, Pallas kernels, shards(): pl.pallas_call(functools.partial(lon_kernel, rb), grid=(rows // rb,), in_...  5.23 us
    all_to_all x1, starting transfers between devices, shards(): lax.all_to_all(table, ('lat', 'lon'), split_axis=0, concat_axis=0, tiled=...  4.42 us
  transfers between devices with their start and end apart: 13, of which 2 were waited for; matrix products, arithmetic and copies ran while one was open for 1% of the time, Pallas kernels for 22%

profile of v6, /device:TPU:0, one launch (start us, length us, event | category | flops | bytes accessed | tf_op | source)
XLA Modules:
  0.0 125.6 jit_solution(3452607390233054546)
XLA Ops:
  0.6 1.2 slice_bitcast_fusion
  1.8 0.7 slice_bitcast_fusion.4
  2.6 2.4 %collective-permute-start = (f32[1,12480]{1,0:T(1,128)S(1)}, f32[1,12480]{1,0:T(1,128)S(1)}, u32[]{:S(2)}, u32[]{:S(2)}) collective-permute-start(f32[1,12480]{1,0:T(1,128)S(1)} %pad_maximum_fusion), channel_id=1, source_target_pairs={{0,4},{4,8},{8,12},{12,16},{16,20},{20,24},{24,28},{1,5},{5,9},{9,... | collective-permute-start | bytes 149768 | tf_op jit(solution)/shard_map/ppermute | solution.py:598
  5.0 1.3 %collective-permute-start.1 = (f32[1,12480]{1,0:T(1,128)S(1)}, f32[1,12480]{1,0:T(1,128)S(1)}, u32[]{:S(2)}, u32[]{:S(2)}) collective-permute-start(f32[1,12480]{1,0:T(1,128)S(1)} %pad_maximum_fusion.1), channel_id=1, source_target_pairs={{4,0},{8,4},{12,8},{16,12},{20,16},{24,20},{28,24},{5,1},{9,5},{13... | collective-permute-start | bytes 149768 | tf_op jit(solution)/shard_map/ppermute | solution.py:599
  6.3 0.8 slice_bitcast_fusion.2
  7.1 4.3 %collective-permute-start.2 = (f32[48,64]{1,0:T(8,128)S(1)}, f32[48,64]{1,0:T(8,128)S(1)}, u32[]{:S(2)}, u32[]{:S(2)}) collective-permute-start(f32[48,64]{1,0:T(8,128)S(1)} %get-tuple-element.41), channel_id=1, source_target_pairs={{0,1},{1,2},{2,3},{4,5},{5,6},{6,7},{8,9},{9,10},{10,11},{12,13},{... | collective-permute-start | bytes 36872 | tf_op jit(solution)/shard_map/ppermute | solution.py:600
  11.5 1.3 %collective-permute-start.3 = (f32[48,64]{1,0:T(8,128)S(1)}, f32[48,64]{1,0:T(8,128)S(1)}, u32[]{:S(2)}, u32[]{:S(2)}) collective-permute-start(f32[48,64]{1,0:T(8,128)S(1)} %get-tuple-element.40), channel_id=1, source_target_pairs={{1,0},{2,1},{3,2},{5,4},{6,5},{7,6},{9,8},{10,9},{11,10},{13,12},{... | collective-permute-start | bytes 36872 | tf_op jit(solution)/shard_map/ppermute | solution.py:601
  12.8 0.0 copy-start
  12.8 3.0 %copy-done = f32[3,48,12288]{2,1,0:T(8,128)S(1)} copy-done((f32[3,48,12288]{2,1,0:T(8,128)S(1)}, f32[3,48,12288]{2,1,0:T(8,128)}, u32[]{:S(2)}) %copy-start) | copy-done | bytes 7077912
  15.8 0.9 copy-done.10
  16.7 0.9 copy-done.12
  17.6 0.7 copy-done.15
  18.3 0.7 copy-done.16
  18.9 0.7 copy-done.17
  19.6 8.9 %lat_chi_temp.1 = (f32[3,96,48,128]{3,2,1,0:T(8,128)S(1)}, f32[3,48,96,128]{3,2,1,0:T(8,128)S(1)}, f32[8,3,48,128]{3,2,1,0:T(8,128)}, f32[3,4,128]{2,1,0:T(4,128)S(1)}) custom-call(f32[8]{0:T(128)S(1)} %copy-done.16, s32[1,192]{1,0:T(1,128)S(1)} %bitcast.21, f32[1,64]{1,0:T(1,128)S(1)} %bitcast.22, f32[3,48,192]{2,1,0:T(8,128)S(1)} %copy-done.10, ...), custom_call_target="tpu_custom_call" | custom-call | flops 120000000 | bytes 14155776 | tf_op jit(solution)/shard_map/lat_chi_temp/pallas_call | solution.py:614
  28.5 0.0 collective-permute-done.2.west
  28.5 0.0 collective-permute-done.3.east
  28.5 0.0 collective-permute-done.north
  28.5 0.0 collective-permute-done.1.south
  28.5 0.0 copy-done.1
  28.5 0.0 copy-done.11
  28.5 7.8 %lat_psi.1 = (f32[3,96,48,128]{3,2,1,0:T(8,128)S(1)}, f32[3,48,96,128]{3,2,1,0:T(8,128)S(1)}, f32[8,3,48,128]{3,2,1,0:T(8,128)}) custom-call(f32[3,4,128]{2,1,0:T(4,128)S(1)} %get-tuple-element.21.prm, f32[3,48,192]{2,1,0:T(8,128)S(1)} %copy-done.11, f32[3,64,64]{2,1,0:T(8,128)S(1)} %copy-done.12, ...), custom_call_target="tpu_custom_call", output_to_operand_aliasing={{0}: (13, {}), {1}: (14, {}), {2}: (15, {})} | custom-call | flops 60000000 | bytes 7077888 | tf_op jit(solution)/shard_map/lat_psi/pallas_call | solution.py:614
  36.3 2.9 %copy-done.2 = f32[3,96,48,128]{3,2,1,0:T(8,128)} copy-done((f32[3,96,48,128]{3,2,1,0:T(8,128)}, f32[3,96,48,128]{3,2,1,0:T(8,128)S(1)}, u32[]{:S(2)}) %copy-start.2) | copy-done | bytes 7077912
  39.1 3.0 %copy-done.4 = f32[3,48,96,128]{3,2,1,0:T(8,128)} copy-done((f32[3,48,96,128]{3,2,1,0:T(8,128)}, f32[3,48,96,128]{3,2,1,0:T(8,128)S(1)}, u32[]{:S(2)}) %copy-start.4) | copy-done | bytes 7077912
  42.1 6.4 %all-to-all-start = ((f32[8,3,48,128]{3,2,1,0:T(8,128)}), f32[8,3,48,128]{3,2,1,0:T(8,128)S(1)}, u32[]{:S(2)}, u32[]{:S(2)}) async-start(f32[8,3,48,128]{3,2,1,0:T(8,128)} %get-tuple-element.28), calls=%async_computation | async-start | bytes 1179648 | tf_op jit(solution)/shard_map/all_to_all | solution.py:650
  48.5 3.0 %copy-done.5 = f32[3,48,96,128]{3,2,1,0:T(8,128)S(1)} copy-done((f32[3,48,96,128]{3,2,1,0:T(8,128)S(1)}, f32[3,48,96,128]{3,2,1,0:T(8,128)}, u32[]{:S(2)}) %copy-start.5) | copy-done | bytes 7077912
  51.5 5.2 %lon_tile.1 = (f32[3,96,48,128]{3,2,1,0:T(8,128)S(1)}, f32[3,4,48,128]{3,2,1,0:T(8,128)S(1)}, f32[7,48,128]{2,1,0:T(8,128)S(1)}) custom-call(f32[3,4,128]{2,1,0:T(4,128)S(1)} %get-tuple-element.21.prm, f32[3,48,192]{2,1,0:T(8,128)S(1)} %copy-done.11, f32[3,48,96,128]{3,2,1,0:T(8,128)S(1)} %copy-done.5), custom_call_target="tpu_custom_call" | custom-call | flops 180000000 | bytes 14155776 | tf_op jit(solution)/shard_map/lon_tile/pallas_call | solution.py:655
  56.7 0.0 copy-start.6
  56.8 3.0 %copy-done.6 = f32[3,96,48,128]{3,2,1,0:T(8,128)} copy-done((f32[3,96,48,128]{3,2,1,0:T(8,128)}, f32[3,96,48,128]{3,2,1,0:T(8,128)S(1)}, u32[]{:S(2)}) %copy-start.6) | copy-done | bytes 7077912
  59.7 0.0 all-to-all-done.edges
  59.7 1.0 solve.1
  60.7 4.2 %all-to-all-start.1 = ((f32[8,3,48,128]{3,2,1,0:T(8,128)}), f32[8,3,48,128]{3,2,1,0:T(8,128)S(1)}, u32[]{:S(2)}, u32[]{:S(2)}) async-start(f32[8,3,48,128]{3,2,1,0:T(8,128)} %solve.1), calls=%async_computation.1 | async-start | bytes 1179648 | tf_op jit(solution)/shard_map/all_to_all | solution.py:650
  64.9 0.2 convert_reduce_fusion
  65.1 2.7 %collective-permute-start.4 = (f32[7,48,128]{2,1,0:T(8,128)S(1)}, f32[7,48,128]{2,1,0:T(8,128)S(1)}, u32[]{:S(2)}, u32[]{:S(2)}) collective-permute-start(f32[7,48,128]{2,1,0:T(8,128)S(1)} %get-tuple-element.29.rest_0_), channel_id=1, source_target_pairs={{0,1},{1,2},{2,3},{3,0},{4,5},{5,6},{6,7},{7,4},{8,9},{9,10},{10,1... | collective-permute-start | bytes 516104 | tf_op jit(solution)/shard_map/ppermute | solution.py:682
  67.8 2.6 %collective-permute-start.5 = (f32[7,48,128]{2,1,0:T(8,128)S(1)}, f32[7,48,128]{2,1,0:T(8,128)S(1)}, u32[]{:S(2)}, u32[]{:S(2)}) collective-permute-start(f32[7,48,128]{2,1,0:T(8,128)S(1)} %get-tuple-element.29.rest_0_), channel_id=1, source_target_pairs={{0,2},{1,3},{2,0},{3,1},{4,6},{5,7},{6,4},{7,5},{8,10},{9,11},{10,... | collective-permute-start | bytes 516104 | tf_op jit(solution)/shard_map/ppermute | solution.py:682
  70.4 1.3 %collective-permute-start.6 = (f32[7,48,128]{2,1,0:T(8,128)S(1)}, f32[7,48,128]{2,1,0:T(8,128)S(1)}, u32[]{:S(2)}, u32[]{:S(2)}) collective-permute-start(f32[7,48,128]{2,1,0:T(8,128)S(1)} %get-tuple-element.29.rest_0_), channel_id=1, source_target_pairs={{0,3},{1,0},{2,1},{3,2},{4,7},{5,4},{6,5},{7,6},{8,11},{9,8},{10,9... | collective-permute-start | bytes 516104 | tf_op jit(solution)/shard_map/ppermute | solution.py:682
  71.7 3.6 %all-to-all-done.1.carries = f32[8,3,48,128]{3,2,1,0:T(8,128)S(1)} async-done(((f32[8,3,48,128]{3,2,1,0:T(8,128)}), f32[8,3,48,128]{3,2,1,0:T(8,128)S(1)}, u32[]{:S(2)}, u32[]{:S(2)}) %all-to-all-start.1) | async-done | bytes 589856 | tf_op jit(solution)/shard_map/all_to_all | solution.py:650
  75.3 1.6 %lon_carry.1 = (f32[3,96,8,128]{3,2,1,0:T(8,128)S(1)}, f32[3,4,8,128]{3,2,1,0:T(8,128)S(1)}, f32[6,8,128]{2,1,0:T(8,128)S(1)}) custom-call(f32[3,4,128]{2,1,0:T(4,128)S(1)} %get-tuple-element.21.prm, f32[8,3,48,128]{3,2,1,0:T(8,128)S(1)} %all-to-all-done.1.carries), custom_call_target="tpu_custom_call" | custom-call | flops 30000000 | bytes 1769472 | tf_op jit(solution)/shard_map/lon_carry/pallas_call | solution.py:699
  76.9 2.6 %collective-permute-start.7 = (f32[6,8,128]{2,1,0:T(8,128)S(1)}, f32[6,8,128]{2,1,0:T(8,128)S(1)}, u32[]{:S(2)}, u32[]{:S(2)}) collective-permute-start(f32[6,8,128]{2,1,0:T(8,128)S(1)} %get-tuple-element.34.rest_4_), channel_id=1, source_target_pairs={{0,1},{1,2},{2,3},{3,0},{4,5},{5,6},{6,7},{7,4},{8,9},{9,10},{10,1... | collective-permute-start | bytes 73736 | tf_op jit(solution)/shard_map/ppermute | solution.py:682
  79.6 2.6 %collective-permute-start.8 = (f32[6,8,128]{2,1,0:T(8,128)S(1)}, f32[6,8,128]{2,1,0:T(8,128)S(1)}, u32[]{:S(2)}, u32[]{:S(2)}) collective-permute-start(f32[6,8,128]{2,1,0:T(8,128)S(1)} %get-tuple-element.34.rest_4_), channel_id=1, source_target_pairs={{0,2},{1,3},{2,0},{3,1},{4,6},{5,7},{6,4},{7,5},{8,10},{9,11},{10,... | collective-permute-start | bytes 73736 | tf_op jit(solution)/shard_map/ppermute | solution.py:682
  82.2 0.0 collective-permute-done.4.rest_1_
  82.2 1.3 %collective-permute-start.9 = (f32[6,8,128]{2,1,0:T(8,128)S(1)}, f32[6,8,128]{2,1,0:T(8,128)S(1)}, u32[]{:S(2)}, u32[]{:S(2)}) collective-permute-start(f32[6,8,128]{2,1,0:T(8,128)S(1)} %get-tuple-element.34.rest_4_), channel_id=1, source_target_pairs={{0,3},{1,0},{2,1},{3,2},{4,7},{5,4},{6,5},{7,6},{8,11},{9,8},{10,9... | collective-permute-start | bytes 73736 | tf_op jit(solution)/shard_map/ppermute | solution.py:682
  83.5 0.1 pad_add_fusion.place
  83.6 0.0 collective-permute-done.5.rest_2_
  83.6 0.0 collective-permute-done.6.rest_3_
  83.6 0.0 collective-permute-done.7.rest_5_
  83.6 4.0 %collective-permute-done.8.rest_6_ = f32[6,8,128]{2,1,0:T(8,128)S(1)} collective-permute-done((f32[6,8,128]{2,1,0:T(8,128)S(1)}, f32[6,8,128]{2,1,0:T(8,128)S(1)}, u32[]{:S(2)}, u32[]{:S(2)}) %collective-permute-start.8) | collective-permute-done | bytes 24608 | tf_op jit(solution)/shard_map/ppermute | solution.py:682
  87.6 0.0 collective-permute-done.9.rest_7_
  87.6 3.0 %copy-done.3 = f32[3,96,48,128]{3,2,1,0:T(8,128)S(1)} copy-done((f32[3,96,48,128]{3,2,1,0:T(8,128)S(1)}, f32[3,96,48,128]{3,2,1,0:T(8,128)}, u32[]{:S(2)}) %copy-start.3) | copy-done | bytes 7077912
  90.6 3.0 %copy-done.7 = f32[3,96,48,128]{3,2,1,0:T(8,128)S(1)} copy-done((f32[3,96,48,128]{3,2,1,0:T(8,128)S(1)}, f32[3,96,48,128]{3,2,1,0:T(8,128)}, u32[]{:S(2)}) %copy-start.7) | copy-done | bytes 7077912
  93.6 8.2 %join.1 = (f32[3,96,48,128]{3,2,1,0:T(8,128)S(1)}, f32[96,8,128]{2,1,0:T(8,128)S(1)}, f32[2,48,128]{2,1,0:T(8,128)S(1)}, f32[2,48,128]{2,1,0:T(8,128)S(1)}, f32[3,8,128]{2,1,0:T(8,128)S(1)}) custom-call(s32[2]{0:T(128)S(1)} %pad_add_fusion.place, f32[3,4,128]{2,1,0:T(4,128)S(1)} %get-tuple-element.21.prm, f32[3,96,48,128]{3,2,1,0:T(8,128)S(1)} %copy-done.7, ...), custom_call_target="tpu_custom_call" | custom-call | flops 60000000 | bytes 21233664 | tf_op jit(solution)/shard_map/join/pallas_call | solution.py:726
  101.8 0.0 copy-start.8
  101.8 3.0 %copy-done.8 = f32[3,96,48,128]{3,2,1,0:T(8,128)} copy-done((f32[3,96,48,128]{3,2,1,0:T(8,128)}, f32[3,96,48,128]{3,2,1,0:T(8,128)S(1)}, u32[]{:S(2)}) %copy-start.8) | copy-done | bytes 7077912
  104.8 0.1 slice_add_fusion
  104.9 0.1 broadcast_in_dim.14
  105.0 0.1 select_reduce_fusion
  105.1 0.7 all_to_all.14
  105.8 4.4 %all-to-all-start.2 = ((f32[32,1,7]{2,1,0:T(1,128)}), f32[32,1,7]{2,1,0:T(1,128)S(1)}, u32[]{:S(2)}, u32[]{:S(2)}) async-start(f32[32,1,7]{2,1,0:T(1,128)} %bitcast.10), calls=%async_computation.2 | async-start | bytes 32768 | tf_op jit(solution)/shard_map/all_to_all | solution.py:767
  110.2 0.0 copy-start.9
  110.2 3.0 %copy-done.9 = f32[3,96,48,128]{3,2,1,0:T(8,128)S(1)} copy-done((f32[3,96,48,128]{3,2,1,0:T(8,128)S(1)}, f32[3,96,48,128]{3,2,1,0:T(8,128)}, u32[]{:S(2)}) %copy-start.9) | copy-done | bytes 7077912
  113.2 11.8 %finish.1 = f32[3,48,12288]{2,1,0:T(8,128)} custom-call(f32[3,4,128]{2,1,0:T(4,128)S(1)} %get-tuple-element.21.prm, f32[3,48,192]{2,1,0:T(8,128)S(1)} %copy-done.11, f32[1,12480]{1,0:T(1,128)S(1)} %collective-permute-done.north, f32[1,12480]{1,0:T(1,128)S(1)} %collective-permute-done.1.south, f32[3,64,64]{2,1,0:T(8,128)S(1)} %copy-done.13, ...), custom_call_target="tpu_custom_call" | custom-call | flops 300000000 | bytes 14155776 | tf_op jit(solution)/shard_map/finish/pallas_call | solution.py:774
  125.0 0.0 all-to-all-done.2
  125.0 0.1 reduce_sum.39
  125.1 0.5 multiply_bitcast_fusion
  (24 shorter events, 0.2 us)
Async XLA Ops:
  2.6 25.9 %collective-permute-start = (f32[1,12480]{1,0:T(1,128)S(1)}, f32[1,12480]{1,0:T(1,128)S(1)}, u32[]{:S(2)}, u32[]{:S(2)}) collective-permute-start(f32[1,12480]{1,0:T(1,128)S(1)} %pad_maximum_fusion), channel_id=1, source_target_pairs={{0,4},{4,8},{8,12},{12,16},{16,20},{20,24},{24,28},{1,5},{5,9},{9,... | collective-permute-start | bytes 149768 | tf_op jit(solution)/shard_map/ppermute | solution.py:598
  5.0 23.5 %collective-permute-start.1 = (f32[1,12480]{1,0:T(1,128)S(1)}, f32[1,12480]{1,0:T(1,128)S(1)}, u32[]{:S(2)}, u32[]{:S(2)}) collective-permute-start(f32[1,12480]{1,0:T(1,128)S(1)} %pad_maximum_fusion.1), channel_id=1, source_target_pairs={{4,0},{8,4},{12,8},{16,12},{20,16},{24,20},{28,24},{5,1},{9,5},{13... | collective-permute-start | bytes 149768 | tf_op jit(solution)/shard_map/ppermute | solution.py:599
  7.1 21.3 %collective-permute-start.2 = (f32[48,64]{1,0:T(8,128)S(1)}, f32[48,64]{1,0:T(8,128)S(1)}, u32[]{:S(2)}, u32[]{:S(2)}) collective-permute-start(f32[48,64]{1,0:T(8,128)S(1)} %get-tuple-element.41), channel_id=1, source_target_pairs={{0,1},{1,2},{2,3},{4,5},{5,6},{6,7},{8,9},{9,10},{10,11},{12,13},{... | collective-permute-start | bytes 36872 | tf_op jit(solution)/shard_map/ppermute | solution.py:600
  11.5 17.0 %collective-permute-start.3 = (f32[48,64]{1,0:T(8,128)S(1)}, f32[48,64]{1,0:T(8,128)S(1)}, u32[]{:S(2)}, u32[]{:S(2)}) collective-permute-start(f32[48,64]{1,0:T(8,128)S(1)} %get-tuple-element.40), channel_id=1, source_target_pairs={{1,0},{2,1},{3,2},{5,4},{6,5},{7,6},{9,8},{10,9},{11,10},{13,12},{... | collective-permute-start | bytes 36872 | tf_op jit(solution)/shard_map/ppermute | solution.py:601
  12.8 3.0 %copy-start = (f32[3,48,12288]{2,1,0:T(8,128)S(1)}, f32[3,48,12288]{2,1,0:T(8,128)}, u32[]{:S(2)}) copy-start(f32[3,48,12288]{2,1,0:T(8,128)} %temp.1) | copy-start | bytes 21233668
  15.8 0.9 copy-start.10
  16.7 0.9 copy-start.12
  17.6 0.7 copy-start.15
  18.2 0.7 copy-start.16
  18.9 0.7 copy-start.17
  19.6 8.9 %copy-start.1 = (f32[3,48,12288]{2,1,0:T(8,128)S(1)}, f32[3,48,12288]{2,1,0:T(8,128)}, u32[]{:S(2)}) copy-start(f32[3,48,12288]{2,1,0:T(8,128)} %temp.1) | copy-start | bytes 21233668
  19.6 8.9 %copy-start.11 = (f32[3,48,192]{2,1,0:T(8,128)S(1)}, f32[3,48,192]{2,1,0:T(8,128)}, u32[]{:S(2)}) copy-start(f32[3,48,192]{2,1,0:T(8,128)} %sigma.7) | copy-start | bytes 331780
  19.6 8.9 %copy-start.14 = (f32[64,64]{1,0:T(8,128)S(1)}, f32[64,64]{1,0:T(8,128)}, u32[]{:S(2)}) copy-start(f32[64,64]{1,0:T(8,128)} %bal.3) | copy-start | bytes 49156
  36.3 2.9 %copy-start.2 = (f32[3,96,48,128]{3,2,1,0:T(8,128)}, f32[3,96,48,128]{3,2,1,0:T(8,128)S(1)}, u32[]{:S(2)}) copy-start(f32[3,96,48,128]{3,2,1,0:T(8,128)S(1)} %get-tuple-element.27.w_ref) | copy-start | bytes 21233668
  39.1 3.0 %copy-start.4 = (f32[3,48,96,128]{3,2,1,0:T(8,128)}, f32[3,48,96,128]{3,2,1,0:T(8,128)S(1)}, u32[]{:S(2)}) copy-start(f32[3,48,96,128]{3,2,1,0:T(8,128)S(1)} %get-tuple-element.25.u_ref) | copy-start | bytes 21233668
  42.1 22.8 %copy-start.18 = (s32[192]{0:T(256)S(1)}, s32[192]{0:T(256)}, u32[]{:S(2)}) copy-start(s32[192]{0:T(256)} %param.15) | copy-start | bytes 2308
  42.1 17.6 %all-to-all-start = ((f32[8,3,48,128]{3,2,1,0:T(8,128)}), f32[8,3,48,128]{3,2,1,0:T(8,128)S(1)}, u32[]{:S(2)}, u32[]{:S(2)}) async-start(f32[8,3,48,128]{3,2,1,0:T(8,128)} %get-tuple-element.28), calls=%async_computation | async-start | bytes 1179648 | tf_op jit(solution)/shard_map/all_to_all | solution.py:650
  48.5 3.0 %copy-start.5 = (f32[3,48,96,128]{3,2,1,0:T(8,128)S(1)}, f32[3,48,96,128]{3,2,1,0:T(8,128)}, u32[]{:S(2)}) copy-start(f32[3,48,96,128]{3,2,1,0:T(8,128)} %copy-done.4) | copy-start | bytes 21233668
  56.7 3.0 %copy-start.6 = (f32[3,96,48,128]{3,2,1,0:T(8,128)}, f32[3,96,48,128]{3,2,1,0:T(8,128)S(1)}, u32[]{:S(2)}) copy-start(f32[3,96,48,128]{3,2,1,0:T(8,128)S(1)} %get-tuple-element.26.u_ref) | copy-start | bytes 21233668
  60.7 14.6 %all-to-all-start.1 = ((f32[8,3,48,128]{3,2,1,0:T(8,128)}), f32[8,3,48,128]{3,2,1,0:T(8,128)S(1)}, u32[]{:S(2)}, u32[]{:S(2)}) async-start(f32[8,3,48,128]{3,2,1,0:T(8,128)} %solve.1), calls=%async_computation.1 | async-start | bytes 1179648 | tf_op jit(solution)/shard_map/all_to_all | solution.py:650
  65.1 17.1 %collective-permute-start.4 = (f32[7,48,128]{2,1,0:T(8,128)S(1)}, f32[7,48,128]{2,1,0:T(8,128)S(1)}, u32[]{:S(2)}, u32[]{:S(2)}) collective-permute-start(f32[7,48,128]{2,1,0:T(8,128)S(1)} %get-tuple-element.29.rest_0_), channel_id=1, source_target_pairs={{0,1},{1,2},{2,3},{3,0},{4,5},{5,6},{6,7},{7,4},{8,9},{9,10},{10,1... | collective-permute-start | bytes 516104 | tf_op jit(solution)/shard_map/ppermute | solution.py:682
  67.8 15.8 %collective-permute-start.5 = (f32[7,48,128]{2,1,0:T(8,128)S(1)}, f32[7,48,128]{2,1,0:T(8,128)S(1)}, u32[]{:S(2)}, u32[]{:S(2)}) collective-permute-start(f32[7,48,128]{2,1,0:T(8,128)S(1)} %get-tuple-element.29.rest_0_), channel_id=1, source_target_pairs={{0,2},{1,3},{2,0},{3,1},{4,6},{5,7},{6,4},{7,5},{8,10},{9,11},{10,... | collective-permute-start | bytes 516104 | tf_op jit(solution)/shard_map/ppermute | solution.py:682
  70.4 13.2 %collective-permute-start.6 = (f32[7,48,128]{2,1,0:T(8,128)S(1)}, f32[7,48,128]{2,1,0:T(8,128)S(1)}, u32[]{:S(2)}, u32[]{:S(2)}) collective-permute-start(f32[7,48,128]{2,1,0:T(8,128)S(1)} %get-tuple-element.29.rest_0_), channel_id=1, source_target_pairs={{0,3},{1,0},{2,1},{3,2},{4,7},{5,4},{6,5},{7,6},{8,11},{9,8},{10,9... | collective-permute-start | bytes 516104 | tf_op jit(solution)/shard_map/ppermute | solution.py:682
  76.9 6.7 %collective-permute-start.7 = (f32[6,8,128]{2,1,0:T(8,128)S(1)}, f32[6,8,128]{2,1,0:T(8,128)S(1)}, u32[]{:S(2)}, u32[]{:S(2)}) collective-permute-start(f32[6,8,128]{2,1,0:T(8,128)S(1)} %get-tuple-element.34.rest_4_), channel_id=1, source_target_pairs={{0,1},{1,2},{2,3},{3,0},{4,5},{5,6},{6,7},{7,4},{8,9},{9,10},{10,1... | collective-permute-start | bytes 73736 | tf_op jit(solution)/shard_map/ppermute | solution.py:682
  79.6 8.0 %collective-permute-start.8 = (f32[6,8,128]{2,1,0:T(8,128)S(1)}, f32[6,8,128]{2,1,0:T(8,128)S(1)}, u32[]{:S(2)}, u32[]{:S(2)}) collective-permute-start(f32[6,8,128]{2,1,0:T(8,128)S(1)} %get-tuple-element.34.rest_4_), channel_id=1, source_target_pairs={{0,2},{1,3},{2,0},{3,1},{4,6},{5,7},{6,4},{7,5},{8,10},{9,11},{10,... | collective-permute-start | bytes 73736 | tf_op jit(solution)/shard_map/ppermute | solution.py:682
  82.2 5.4 %collective-permute-start.9 = (f32[6,8,128]{2,1,0:T(8,128)S(1)}, f32[6,8,128]{2,1,0:T(8,128)S(1)}, u32[]{:S(2)}, u32[]{:S(2)}) collective-permute-start(f32[6,8,128]{2,1,0:T(8,128)S(1)} %get-tuple-element.34.rest_4_), channel_id=1, source_target_pairs={{0,3},{1,0},{2,1},{3,2},{4,7},{5,4},{6,5},{7,6},{8,11},{9,8},{10,9... | collective-permute-start | bytes 73736 | tf_op jit(solution)/shard_map/ppermute | solution.py:682
  87.6 3.0 %copy-start.3 = (f32[3,96,48,128]{3,2,1,0:T(8,128)S(1)}, f32[3,96,48,128]{3,2,1,0:T(8,128)}, u32[]{:S(2)}) copy-start(f32[3,96,48,128]{3,2,1,0:T(8,128)} %copy-done.2) | copy-start | bytes 21233668
  90.6 3.0 %copy-start.7 = (f32[3,96,48,128]{3,2,1,0:T(8,128)S(1)}, f32[3,96,48,128]{3,2,1,0:T(8,128)}, u32[]{:S(2)}) copy-start(f32[3,96,48,128]{3,2,1,0:T(8,128)} %copy-done.6) | copy-start | bytes 21233668
  93.6 16.6 %copy-start.13 = (f32[3,64,64]{2,1,0:T(8,128)S(1)}, f32[3,64,64]{2,1,0:T(8,128)}, u32[]{:S(2)}) copy-start(f32[3,64,64]{2,1,0:T(8,128)} %vert.5) | copy-start | bytes 147460
  101.8 3.0 %copy-start.8 = (f32[3,96,48,128]{3,2,1,0:T(8,128)}, f32[3,96,48,128]{3,2,1,0:T(8,128)S(1)}, u32[]{:S(2)}) copy-start(f32[3,96,48,128]{3,2,1,0:T(8,128)S(1)} %get-tuple-element.37.y_ref) | copy-start | bytes 21233668
  105.8 19.2 %all-to-all-start.2 = ((f32[32,1,7]{2,1,0:T(1,128)}), f32[32,1,7]{2,1,0:T(1,128)S(1)}, u32[]{:S(2)}, u32[]{:S(2)}) async-start(f32[32,1,7]{2,1,0:T(1,128)} %bitcast.10), calls=%async_computation.2 | async-start | bytes 32768 | tf_op jit(solution)/shard_map/all_to_all | solution.py:767
  110.2 3.0 %copy-start.9 = (f32[3,96,48,128]{3,2,1,0:T(8,128)S(1)}, f32[3,96,48,128]{3,2,1,0:T(8,128)}, u32[]{:S(2)}) copy-start(f32[3,96,48,128]{3,2,1,0:T(8,128)} %copy-done.8) | copy-start | bytes 21233668

commit v7 on v6

--- a/solution.py
+++ b/solution.py
@@ -14,11 +14,15 @@
 PAIRS = 8
 BLOCK = 24
 ORDER = (1, 2, 0)
-LIMIT = 22 * 1024 * 1024
+LIMIT = 30 * 1024 * 1024
 
 
 def params():
     return pltpu.CompilerParams(vmem_limit_bytes=LIMIT)
+
+
+def in_hbm(x):
+    return pltpu.with_memory_space_constraint(x, pltpu.HBM)
 
 
 def full(shape):
@@ -208,8 +212,8 @@
         kind = classes[:, 64 * v : 64 * (v + 1)]
         kind = jnp.concatenate([kind, kind], axis=1)
         length = jnp.zeros((1, LANES), f32)
-        for n in range(scales.shape[0]):
-            length = jnp.where(kind == n, scales[n], length)
+        for n in range(scales.shape[1]):
+            length = jnp.where(kind == n, scales[:, n : n + 1], length)
         decay = jnp.exp(-1.0 / length)
         norm = 1.0 - decay
         norm = norm * norm
@@ -621,7 +625,8 @@
                 pl.BlockSpec((2 * BLOCK // width, nv, 4 * width, LANES), lambda g: (g, first, 0, 0)),
             ]
             + [full(s) for s in more],
-            out_shape=[jax.ShapeDtypeStruct(s, f32) for s in shapes + list(more)],
+            out_shape=[pltpu.HBM(s, f32) for s in shapes[:2]]
+            + [jax.ShapeDtypeStruct(s, f32) for s in shapes[2:] + list(more)],
             scratch_shapes=[
                 pltpu.VMEM((2, PAIRS * rows, 256), f32),
                 pltpu.VMEM((2 * 768, 256), bf16),
@@ -635,12 +640,13 @@
             name=name,
         )(*arrays)
 
-    ins = [scales, classes.reshape(1, count), chi_coef.reshape(1, levels), sigma, vert] + [state] * 4
+    ins = [scales.reshape(1, -1), classes.reshape(1, count), chi_coef.reshape(1, levels), sigma, vert] + [state] * 4
     specs = [full(x.shape) for x in ins[:5]] + [part(1, 0), part(1, 1), part(2, 0), part(2, 1)]
-    specs[0] = pl.BlockSpec(memory_space=pltpu.SMEM)
+    ins = [in_hbm(x) for x in ins]
     body = functools.partial(lat_plain, rows, pairs)
     *wue, prm = lat_call(2, 0, body, ins, specs, "lat_chi_temp", {}, [(nvars, 4, LANES)])
-    ins = [prm, sigma, vert, bal_temp] + [state] * 5 + [north, south, west, east] + list(wue)
+    ins = [prm, sigma, vert, bal_temp] + [in_hbm(state)] * 5 + [north, south, west, east]
+    ins += [in_hbm(wue[0]), in_hbm(wue[1]), wue[2]]
     specs = [full(x.shape) for x in ins[:4]] + [part(0, 0), part(0, 1), part(1, 0), part(1, 1)]
     specs += [pl.BlockSpec((1, rows, merged), lambda g: (2, 0, 0))]
     specs += [full(x.shape) for x in (north, south, west, east)] + [anywhere] * 3
@@ -666,7 +672,7 @@
             full((7, rows, LANES)),
         ],
         out_shape=[
-            jax.ShapeDtypeStruct((nvars, half, rows, LANES), f32),
+            pltpu.HBM((nvars, half, rows, LANES), f32),
             jax.ShapeDtypeStruct((nvars, 4, rows, LANES), f32),
             jax.ShapeDtypeStruct((7, rows, LANES), f32),
         ],
@@ -675,7 +681,7 @@
             flops=180000000, bytes_accessed=6 * rows * merged * 4, transcendentals=0
         ),
         name="lon_tile",
-    )(prm, sigma, u)
+    )(prm, sigma, in_hbm(u))
 
     def round_lon(x):
         return [x] + [
@@ -719,7 +725,7 @@
     def columns(r):
         return pl.BlockSpec((nvars, packed, r, LANES), lambda g: (0, g, 0, 0))
 
-    ins = [place, prm, local, w, crossed, el, elc] + sent + sent_x
+    ins = [place, prm, in_hbm(local), in_hbm(w), crossed, el, elc] + sent + sent_x
     specs = [full(x.shape) for x in ins]
     specs[0] = pl.BlockSpec(memory_space=pltpu.SMEM)
     specs[2:5] = [columns(rows), columns(rows), columns(8)]
@@ -735,7 +741,7 @@
             full((nvars, 8, LANES)),
         ],
         out_shape=[
-            jax.ShapeDtypeStruct((nvars, half, rows, LANES), f32),
+            pltpu.HBM((nvars, half, rows, LANES), f32),
             jax.ShapeDtypeStruct((half, 8, LANES), f32),
             jax.ShapeDtypeStruct((2, rows, LANES), f32),
             jax.ShapeDtypeStruct((2, rows, LANES), f32),
@@ -767,7 +773,7 @@
     table = lax.all_to_all(table, ("lat", "lon"), split_axis=0, concat_axis=0, tiled=True)
     slab_energy = (jnp.sum(table, axis=0) / (devices * rows * lon))[None, :]
 
-    ins = [prm, sigma, north, south, vert, bal_temp, col, side, y, yx]
+    ins = [prm, sigma, north, south, vert, bal_temp, col, side, in_hbm(y), yx]
     specs = [full(x.shape) for x in ins]
     specs[8] = columns(rows)
     specs[9] = pl.BlockSpec((packed, 8, LANES), lambda g: (g, 0, 0))

time: 126 us -> 111 us (0.88)
  local copies, waits for them, and re-layouts: 34.1 us -> 3.56 us
  Pallas kernels: 44.4 us -> 58.8 us
  waiting for transfers between devices: 7.63 us -> 9.66 us
    unnamed x38 -> x8, local copies, waits for them, and re-layouts: 30.6 us -> 0.02 us
    pallas_call x2, Pallas kernels: 16.7 us -> 22.1 us  [lat_call(): pl.pallas_call(body, grid=(steps,), in_specs=specs, out_specs=[pl.BlockSp...]
    pallas_call x1, Pallas kernels: 8.18 us -> 12.1 us  [shards(): pl.pallas_call(functools.partial(join_kernel, n_lon, rows, packed, 24), g...]
    pallas_call x1, Pallas kernels: 5.23 us -> 8.3 us  [shards(): pl.pallas_call(functools.partial(lon_kernel, rb), grid=(rows // rb,), in_...]
    all_to_all x2, waiting for transfers between devices: 3.62 us -> 5.69 us  [trade(): return lax.all_to_all(x, 'lat', split_axis=0, concat_axis=0, tiled=True)]
    pallas_call x1, Pallas kernels: 11.8 us -> 13.7 us  [shards(): pl.pallas_call(functools.partial(end_kernel, rows, pairs), grid=(half //...]
  transfers between devices with their start and end apart: 13 -> 13, of which waited for: 2 -> 3; matrix products, arithmetic and copies ran while one was open for 1% -> 1% of each run, Pallas kernels for 22% -> 32%
where the time goes in v7:
time: 111 us
  Pallas kernels  58.8 us (53%)
  starting transfers between devices  36.7 us (33%)
  waiting for transfers between devices  9.66 us (9%)
  local copies, waits for them, and re-layouts  3.56 us (3%)
  other arithmetic  1.15 us (1%)
    pallas_call x2, Pallas kernels, lat_call(): pl.pallas_call(body, grid=(steps,), in_specs=specs, out_specs=[pl.BlockSp...  22.1 us
    pallas_call x1, Pallas kernels, shards(): pl.pallas_call(functools.partial(end_kernel, rows, pairs), grid=(half //...  13.7 us
    ppermute x6, starting transfers between devices, round_lon(): lax.ppermute(x, 'lon', [(i, (i + s) % n_lon) for i in range(n_lon)])  13.2 us
    pallas_call x1, Pallas kernels, shards(): pl.pallas_call(functools.partial(join_kernel, n_lon, rows, packed, 24), g...  12.1 us
    all_to_all x2, starting transfers between devices, trade(): return lax.all_to_all(x, 'lat', split_axis=0, concat_axis=0, tiled=True)  9.8 us
    pallas_call x1, Pallas kernels, shards(): pl.pallas_call(functools.partial(lon_kernel, rb), grid=(rows // rb,), in_...  8.3 us
    all_to_all x2, waiting for transfers between devices, trade(): return lax.all_to_all(x, 'lat', split_axis=0, concat_axis=0, tiled=True)  5.69 us
    all_to_all x1, starting transfers between devices, shards(): lax.all_to_all(table, ('lat', 'lon'), split_axis=0, concat_axis=0, tiled=...  4.46 us
  transfers between devices with their start and end apart: 13, of which 3 were waited for; matrix products, arithmetic and copies ran while one was open for 1% of the time, Pallas kernels for 32%

profile of v7, /device:TPU:0, one launch (start us, length us, event | category | flops | bytes accessed | tf_op | source)
XLA Modules:
  0.0 110.7 jit_solution(15698050228930096204)
XLA Ops:
  0.6 1.2 %slice_bitcast_fusion = (f32[1,12288]{1,0:T(1,128)S(1)}, f32[1,12288]{1,0:T(1,128)S(1)}) fusion(f32[3,48,12288]{2,1,0:T(8,128)} %temp.1), kind=kLoop, calls=%fused_computation.7 | loop fusion | bytes 196608 | tf_op jit(solution)/shard_map/squeeze | solution.py:600
  1.8 0.7 slice_bitcast_fusion.4
  2.6 2.4 %collective-permute-start = (f32[1,12480]{1,0:T(1,128)S(1)}, f32[1,12480]{1,0:T(1,128)S(1)}, u32[]{:S(2)}, u32[]{:S(2)}) collective-permute-start(f32[1,12480]{1,0:T(1,128)S(1)} %pad_maximum_fusion), channel_id=1, source_target_pairs={{0,4},{4,8},{8,12},{12,16},{16,20},{20,24},{24,28},{1,5},{5,9},{9,... | collective-permute-start | bytes 149768 | tf_op jit(solution)/shard_map/ppermute | solution.py:602
  5.0 1.3 %collective-permute-start.1 = (f32[1,12480]{1,0:T(1,128)S(1)}, f32[1,12480]{1,0:T(1,128)S(1)}, u32[]{:S(2)}, u32[]{:S(2)}) collective-permute-start(f32[1,12480]{1,0:T(1,128)S(1)} %pad_maximum_fusion.1), channel_id=1, source_target_pairs={{4,0},{8,4},{12,8},{16,12},{20,16},{24,20},{28,24},{5,1},{9,5},{13... | collective-permute-start | bytes 149768 | tf_op jit(solution)/shard_map/ppermute | solution.py:603
  6.3 0.8 slice_bitcast_fusion.2
  7.1 4.3 %collective-permute-start.2 = (f32[48,64]{1,0:T(8,128)S(1)}, f32[48,64]{1,0:T(8,128)S(1)}, u32[]{:S(2)}, u32[]{:S(2)}) collective-permute-start(f32[48,64]{1,0:T(8,128)S(1)} %get-tuple-element.41), channel_id=1, source_target_pairs={{0,1},{1,2},{2,3},{4,5},{5,6},{6,7},{8,9},{9,10},{10,11},{12,13},{... | collective-permute-start | bytes 36872 | tf_op jit(solution)/shard_map/ppermute | solution.py:604
  11.5 1.3 %collective-permute-start.3 = (f32[48,64]{1,0:T(8,128)S(1)}, f32[48,64]{1,0:T(8,128)S(1)}, u32[]{:S(2)}, u32[]{:S(2)}) collective-permute-start(f32[48,64]{1,0:T(8,128)S(1)} %get-tuple-element.40), channel_id=1, source_target_pairs={{1,0},{2,1},{3,2},{5,4},{6,5},{7,6},{9,8},{10,9},{11,10},{13,12},{... | collective-permute-start | bytes 36872 | tf_op jit(solution)/shard_map/ppermute | solution.py:605
  12.8 0.0 copy-start
  12.8 0.0 copy-start.1
  12.8 0.0 copy-start.2
  12.8 11.5 %lat_chi_temp.1 = (f32[3,96,48,128]{3,2,1,0:T(8,128)}, f32[3,48,96,128]{3,2,1,0:T(8,128)}, f32[8,3,48,128]{3,2,1,0:T(8,128)}, f32[3,4,128]{2,1,0:T(4,128)S(1)}) custom-call(f32[1,8]{1,0:T(1,128)} %bitcast.23, s32[1,192]{1,0:T(1,128)} %bitcast.22, f32[1,64]{1,0:T(1,128)} %bitcast.24, f32[3,48,192]{2,1,0:T(8,128)} %sigma.7, f32[3,64,64]{2,1,0:T(8,128)} %vert.5, ...), custom_call_target="tpu_custom_call" | custom-call | flops 120000000 | bytes 14155776 | tf_op jit(solution)/shard_map/lat_chi_temp/pallas_call | solution.py:618
  24.3 0.0 collective-permute-done.2.west
  24.3 0.0 collective-permute-done.3.east
  24.3 0.0 collective-permute-done.north
  24.3 0.0 collective-permute-done.1.south
  24.3 0.0 copy-done
  24.3 0.0 copy-done.1
  24.3 0.0 copy-done.2
  24.3 10.7 %lat_psi.1 = (f32[3,96,48,128]{3,2,1,0:T(8,128)}, f32[3,48,96,128]{3,2,1,0:T(8,128)}, f32[8,3,48,128]{3,2,1,0:T(8,128)}) custom-call(f32[3,4,128]{2,1,0:T(4,128)S(1)} %get-tuple-element.21.prm, f32[3,48,192]{2,1,0:T(8,128)S(1)} %copy-done, f32[3,64,64]{2,1,0:T(8,128)S(1)} %copy-done.1, ...), custom_call_target="tpu_custom_call", output_to_operand_aliasing={{0}: (13, {}), {1}: (14, {}), {2}: (15, {})} | custom-call | flops 60000000 | bytes 7077888 | tf_op jit(solution)/shard_map/lat_psi/pallas_call | solution.py:618
  35.0 0.0 copy-start.3
  35.0 6.3 %all-to-all-start = ((f32[8,3,48,128]{3,2,1,0:T(8,128)}), f32[8,3,48,128]{3,2,1,0:T(8,128)S(1)}, u32[]{:S(2)}, u32[]{:S(2)}) async-start(f32[8,3,48,128]{3,2,1,0:T(8,128)} %get-tuple-element.28), calls=%async_computation | async-start | bytes 1179648 | tf_op jit(solution)/shard_map/all_to_all | solution.py:656
  41.3 8.3 %lon_tile.1 = (f32[3,96,48,128]{3,2,1,0:T(8,128)}, f32[3,4,48,128]{3,2,1,0:T(8,128)S(1)}, f32[7,48,128]{2,1,0:T(8,128)S(1)}) custom-call(f32[3,4,128]{2,1,0:T(4,128)S(1)} %get-tuple-element.21.prm, f32[3,48,192]{2,1,0:T(8,128)S(1)} %copy-done, f32[3,48,96,128]{3,2,1,0:T(8,128)} %get-tuple-element.25.u_ref), custom_call_target="tpu_custom_call" | custom-call | flops 180000000 | bytes 14155776 | tf_op jit(solution)/shard_map/lon_tile/pallas_call | solution.py:661
  49.6 2.1 %all-to-all-done.edges = f32[8,3,48,128]{3,2,1,0:T(8,128)S(1)} async-done(((f32[8,3,48,128]{3,2,1,0:T(8,128)}), f32[8,3,48,128]{3,2,1,0:T(8,128)S(1)}, u32[]{:S(2)}, u32[]{:S(2)}) %all-to-all-start) | async-done | bytes 589856 | tf_op jit(solution)/shard_map/all_to_all | solution.py:656
  51.7 1.0 solve.1
  52.7 3.5 %all-to-all-start.1 = ((f32[8,3,48,128]{3,2,1,0:T(8,128)}), f32[8,3,48,128]{3,2,1,0:T(8,128)S(1)}, u32[]{:S(2)}, u32[]{:S(2)}) async-start(f32[8,3,48,128]{3,2,1,0:T(8,128)} %solve.1), calls=%async_computation.1 | async-start | bytes 1179648 | tf_op jit(solution)/shard_map/all_to_all | solution.py:656
  56.2 0.0 copy-done.3
  56.2 0.2 convert_reduce_fusion
  56.4 2.7 %collective-permute-start.4 = (f32[7,48,128]{2,1,0:T(8,128)S(1)}, f32[7,48,128]{2,1,0:T(8,128)S(1)}, u32[]{:S(2)}, u32[]{:S(2)}) collective-permute-start(f32[7,48,128]{2,1,0:T(8,128)S(1)} %get-tuple-element.29.rest_0_), channel_id=1, source_target_pairs={{0,1},{1,2},{2,3},{3,0},{4,5},{5,6},{6,7},{7,4},{8,9},{9,10},{10,1... | collective-permute-start | bytes 516104 | tf_op jit(solution)/shard_map/ppermute | solution.py:688
  59.1 2.6 %collective-permute-start.5 = (f32[7,48,128]{2,1,0:T(8,128)S(1)}, f32[7,48,128]{2,1,0:T(8,128)S(1)}, u32[]{:S(2)}, u32[]{:S(2)}) collective-permute-start(f32[7,48,128]{2,1,0:T(8,128)S(1)} %get-tuple-element.29.rest_0_), channel_id=1, source_target_pairs={{0,2},{1,3},{2,0},{3,1},{4,6},{5,7},{6,4},{7,5},{8,10},{9,11},{10,... | collective-permute-start | bytes 516104 | tf_op jit(solution)/shard_map/ppermute | solution.py:688
  61.7 1.4 %collective-permute-start.6 = (f32[7,48,128]{2,1,0:T(8,128)S(1)}, f32[7,48,128]{2,1,0:T(8,128)S(1)}, u32[]{:S(2)}, u32[]{:S(2)}) collective-permute-start(f32[7,48,128]{2,1,0:T(8,128)S(1)} %get-tuple-element.29.rest_0_), channel_id=1, source_target_pairs={{0,3},{1,0},{2,1},{3,2},{4,7},{5,4},{6,5},{7,6},{8,11},{9,8},{10,9... | collective-permute-start | bytes 516104 | tf_op jit(solution)/shard_map/ppermute | solution.py:688
  63.1 3.5 %all-to-all-done.1.carries = f32[8,3,48,128]{3,2,1,0:T(8,128)S(1)} async-done(((f32[8,3,48,128]{3,2,1,0:T(8,128)}), f32[8,3,48,128]{3,2,1,0:T(8,128)S(1)}, u32[]{:S(2)}, u32[]{:S(2)}) %all-to-all-start.1) | async-done | bytes 589856 | tf_op jit(solution)/shard_map/all_to_all | solution.py:656
  66.6 1.6 %lon_carry.1 = (f32[3,96,8,128]{3,2,1,0:T(8,128)S(1)}, f32[3,4,8,128]{3,2,1,0:T(8,128)S(1)}, f32[6,8,128]{2,1,0:T(8,128)S(1)}) custom-call(f32[3,4,128]{2,1,0:T(4,128)S(1)} %get-tuple-element.21.prm, f32[8,3,48,128]{3,2,1,0:T(8,128)S(1)} %all-to-all-done.1.carries), custom_call_target="tpu_custom_call" | custom-call | flops 30000000 | bytes 1769472 | tf_op jit(solution)/shard_map/lon_carry/pallas_call | solution.py:705
  68.2 2.6 %collective-permute-start.7 = (f32[6,8,128]{2,1,0:T(8,128)S(1)}, f32[6,8,128]{2,1,0:T(8,128)S(1)}, u32[]{:S(2)}, u32[]{:S(2)}) collective-permute-start(f32[6,8,128]{2,1,0:T(8,128)S(1)} %get-tuple-element.34.rest_4_), channel_id=1, source_target_pairs={{0,1},{1,2},{2,3},{3,0},{4,5},{5,6},{6,7},{7,4},{8,9},{9,10},{10,1... | collective-permute-start | bytes 73736 | tf_op jit(solution)/shard_map/ppermute | solution.py:688
  70.8 2.6 %collective-permute-start.8 = (f32[6,8,128]{2,1,0:T(8,128)S(1)}, f32[6,8,128]{2,1,0:T(8,128)S(1)}, u32[]{:S(2)}, u32[]{:S(2)}) collective-permute-start(f32[6,8,128]{2,1,0:T(8,128)S(1)} %get-tuple-element.34.rest_4_), channel_id=1, source_target_pairs={{0,2},{1,3},{2,0},{3,1},{4,6},{5,7},{6,4},{7,5},{8,10},{9,11},{10,... | collective-permute-start | bytes 73736 | tf_op jit(solution)/shard_map/ppermute | solution.py:688
  73.4 0.0 collective-permute-done.4.rest_1_
  73.4 1.4 %collective-permute-start.9 = (f32[6,8,128]{2,1,0:T(8,128)S(1)}, f32[6,8,128]{2,1,0:T(8,128)S(1)}, u32[]{:S(2)}, u32[]{:S(2)}) collective-permute-start(f32[6,8,128]{2,1,0:T(8,128)S(1)} %get-tuple-element.34.rest_4_), channel_id=1, source_target_pairs={{0,3},{1,0},{2,1},{3,2},{4,7},{5,4},{6,5},{7,6},{8,11},{9,8},{10,9... | collective-permute-start | bytes 73736 | tf_op jit(solution)/shard_map/ppermute | solution.py:688
  74.8 0.1 pad_add_fusion.place
  74.8 0.0 collective-permute-done.5.rest_2_
  74.8 0.0 collective-permute-done.6.rest_3_
  74.9 0.0 collective-permute-done.7.rest_5_
  74.9 3.9 %collective-permute-done.8.rest_6_ = f32[6,8,128]{2,1,0:T(8,128)S(1)} collective-permute-done((f32[6,8,128]{2,1,0:T(8,128)S(1)}, f32[6,8,128]{2,1,0:T(8,128)S(1)}, u32[]{:S(2)}, u32[]{:S(2)}) %collective-permute-start.8) | collective-permute-done | bytes 24608 | tf_op jit(solution)/shard_map/ppermute | solution.py:688
  78.8 0.0 collective-permute-done.9.rest_7_
  78.8 12.1 %join.1 = (f32[3,96,48,128]{3,2,1,0:T(8,128)}, f32[96,8,128]{2,1,0:T(8,128)S(1)}, f32[2,48,128]{2,1,0:T(8,128)S(1)}, f32[2,48,128]{2,1,0:T(8,128)S(1)}, f32[3,8,128]{2,1,0:T(8,128)S(1)}) custom-call(s32[2]{0:T(128)S(1)} %pad_add_fusion.place, f32[3,4,128]{2,1,0:T(4,128)S(1)} %get-tuple-element.21.prm, f32[3,96,48,128]{3,2,1,0:T(8,128)} %get-tuple-element.26.u_ref, ...), custom_call_target="tpu_custom_call" | custom-call | flops 60000000 | bytes 21233664 | tf_op jit(solution)/shard_map/join/pallas_call | solution.py:732
  90.9 0.1 slice_add_fusion
  91.0 0.1 broadcast_in_dim.14
  91.1 0.1 select_reduce_fusion
  91.2 0.7 all_to_all.14
  91.9 4.5 %all-to-all-start.2 = ((f32[32,1,7]{2,1,0:T(1,128)}), f32[32,1,7]{2,1,0:T(1,128)S(1)}, u32[]{:S(2)}, u32[]{:S(2)}) async-start(f32[32,1,7]{2,1,0:T(1,128)} %bitcast.11), calls=%async_computation.2 | async-start | bytes 32768 | tf_op jit(solution)/shard_map/all_to_all | solution.py:773
  96.4 13.7 %finish.1 = f32[3,48,12288]{2,1,0:T(8,128)} custom-call(f32[3,4,128]{2,1,0:T(4,128)S(1)} %get-tuple-element.21.prm, f32[3,48,192]{2,1,0:T(8,128)S(1)} %copy-done, f32[1,12480]{1,0:T(1,128)S(1)} %collective-permute-done.north, f32[1,12480]{1,0:T(1,128)S(1)} %collective-permute-done.1.south, f32[3,64,64]{2,1,0:T(8,128)S(1)} %copy-done.1, ...), custom_call_target="tpu_custom_call" | custom-call | flops 300000000 | bytes 14155776 | tf_op jit(solution)/shard_map/finish/pallas_call | solution.py:780
  110.1 0.0 all-to-all-done.2
  110.1 0.1 reduce_sum.39
  110.1 0.5 multiply_bitcast_fusion
  (6 shorter events, 0.1 us)
Async XLA Ops:
  2.6 21.7 %collective-permute-start = (f32[1,12480]{1,0:T(1,128)S(1)}, f32[1,12480]{1,0:T(1,128)S(1)}, u32[]{:S(2)}, u32[]{:S(2)}) collective-permute-start(f32[1,12480]{1,0:T(1,128)S(1)} %pad_maximum_fusion), channel_id=1, source_target_pairs={{0,4},{4,8},{8,12},{12,16},{16,20},{20,24},{24,28},{1,5},{5,9},{9,... | collective-permute-start | bytes 149768 | tf_op jit(solution)/shard_map/ppermute | solution.py:602
  5.0 19.3 %collective-permute-start.1 = (f32[1,12480]{1,0:T(1,128)S(1)}, f32[1,12480]{1,0:T(1,128)S(1)}, u32[]{:S(2)}, u32[]{:S(2)}) collective-permute-start(f32[1,12480]{1,0:T(1,128)S(1)} %pad_maximum_fusion.1), channel_id=1, source_target_pairs={{4,0},{8,4},{12,8},{16,12},{20,16},{24,20},{28,24},{5,1},{9,5},{13... | collective-permute-start | bytes 149768 | tf_op jit(solution)/shard_map/ppermute | solution.py:603
  7.1 17.1 %collective-permute-start.2 = (f32[48,64]{1,0:T(8,128)S(1)}, f32[48,64]{1,0:T(8,128)S(1)}, u32[]{:S(2)}, u32[]{:S(2)}) collective-permute-start(f32[48,64]{1,0:T(8,128)S(1)} %get-tuple-element.41), channel_id=1, source_target_pairs={{0,1},{1,2},{2,3},{4,5},{5,6},{6,7},{8,9},{9,10},{10,11},{12,13},{... | collective-permute-start | bytes 36872 | tf_op jit(solution)/shard_map/ppermute | solution.py:604
  11.5 12.8 %collective-permute-start.3 = (f32[48,64]{1,0:T(8,128)S(1)}, f32[48,64]{1,0:T(8,128)S(1)}, u32[]{:S(2)}, u32[]{:S(2)}) collective-permute-start(f32[48,64]{1,0:T(8,128)S(1)} %get-tuple-element.40), channel_id=1, source_target_pairs={{1,0},{2,1},{3,2},{5,4},{6,5},{7,6},{9,8},{10,9},{11,10},{13,12},{... | collective-permute-start | bytes 36872 | tf_op jit(solution)/shard_map/ppermute | solution.py:605
  12.8 11.6 %copy-start = (f32[3,48,192]{2,1,0:T(8,128)S(1)}, f32[3,48,192]{2,1,0:T(8,128)}, u32[]{:S(2)}) copy-start(f32[3,48,192]{2,1,0:T(8,128)} %sigma.7) | copy-start | bytes 331780
  12.8 11.5 %copy-start.1 = (f32[3,64,64]{2,1,0:T(8,128)S(1)}, f32[3,64,64]{2,1,0:T(8,128)}, u32[]{:S(2)}) copy-start(f32[3,64,64]{2,1,0:T(8,128)} %vert.5) | copy-start | bytes 147460
  12.8 11.5 %copy-start.2 = (f32[64,64]{1,0:T(8,128)S(1)}, f32[64,64]{1,0:T(8,128)}, u32[]{:S(2)}) copy-start(f32[64,64]{1,0:T(8,128)} %bal.3) | copy-start | bytes 49156
  35.0 21.2 %copy-start.3 = (s32[192]{0:T(256)S(1)}, s32[192]{0:T(256)}, u32[]{:S(2)}) copy-start(s32[192]{0:T(256)} %param.15) | copy-start | bytes 2308
  35.0 16.7 %all-to-all-start = ((f32[8,3,48,128]{3,2,1,0:T(8,128)}), f32[8,3,48,128]{3,2,1,0:T(8,128)S(1)}, u32[]{:S(2)}, u32[]{:S(2)}) async-start(f32[8,3,48,128]{3,2,1,0:T(8,128)} %get-tuple-element.28), calls=%async_computation | async-start | bytes 1179648 | tf_op jit(solution)/shard_map/all_to_all | solution.py:656
  52.7 13.9 %all-to-all-start.1 = ((f32[8,3,48,128]{3,2,1,0:T(8,128)}), f32[8,3,48,128]{3,2,1,0:T(8,128)S(1)}, u32[]{:S(2)}, u32[]{:S(2)}) async-start(f32[8,3,48,128]{3,2,1,0:T(8,128)} %solve.1), calls=%async_computation.1 | async-start | bytes 1179648 | tf_op jit(solution)/shard_map/all_to_all | solution.py:656
  56.4 17.0 %collective-permute-start.4 = (f32[7,48,128]{2,1,0:T(8,128)S(1)}, f32[7,48,128]{2,1,0:T(8,128)S(1)}, u32[]{:S(2)}, u32[]{:S(2)}) collective-permute-start(f32[7,48,128]{2,1,0:T(8,128)S(1)} %get-tuple-element.29.rest_0_), channel_id=1, source_target_pairs={{0,1},{1,2},{2,3},{3,0},{4,5},{5,6},{6,7},{7,4},{8,9},{9,10},{10,1... | collective-permute-start | bytes 516104 | tf_op jit(solution)/shard_map/ppermute | solution.py:688
  59.1 15.7 %collective-permute-start.5 = (f32[7,48,128]{2,1,0:T(8,128)S(1)}, f32[7,48,128]{2,1,0:T(8,128)S(1)}, u32[]{:S(2)}, u32[]{:S(2)}) collective-permute-start(f32[7,48,128]{2,1,0:T(8,128)S(1)} %get-tuple-element.29.rest_0_), channel_id=1, source_target_pairs={{0,2},{1,3},{2,0},{3,1},{4,6},{5,7},{6,4},{7,5},{8,10},{9,11},{10,... | collective-permute-start | bytes 516104 | tf_op jit(solution)/shard_map/ppermute | solution.py:688
  61.7 13.2 %collective-permute-start.6 = (f32[7,48,128]{2,1,0:T(8,128)S(1)}, f32[7,48,128]{2,1,0:T(8,128)S(1)}, u32[]{:S(2)}, u32[]{:S(2)}) collective-permute-start(f32[7,48,128]{2,1,0:T(8,128)S(1)} %get-tuple-element.29.rest_0_), channel_id=1, source_target_pairs={{0,3},{1,0},{2,1},{3,2},{4,7},{5,4},{6,5},{7,6},{8,11},{9,8},{10,9... | collective-permute-start | bytes 516104 | tf_op jit(solution)/shard_map/ppermute | solution.py:688
  68.2 6.7 %collective-permute-start.7 = (f32[6,8,128]{2,1,0:T(8,128)S(1)}, f32[6,8,128]{2,1,0:T(8,128)S(1)}, u32[]{:S(2)}, u32[]{:S(2)}) collective-permute-start(f32[6,8,128]{2,1,0:T(8,128)S(1)} %get-tuple-element.34.rest_4_), channel_id=1, source_target_pairs={{0,1},{1,2},{2,3},{3,0},{4,5},{5,6},{6,7},{7,4},{8,9},{9,10},{10,1... | collective-permute-start | bytes 73736 | tf_op jit(solution)/shard_map/ppermute | solution.py:688
  70.8 8.0 %collective-permute-start.8 = (f32[6,8,128]{2,1,0:T(8,128)S(1)}, f32[6,8,128]{2,1,0:T(8,128)S(1)}, u32[]{:S(2)}, u32[]{:S(2)}) collective-permute-start(f32[6,8,128]{2,1,0:T(8,128)S(1)} %get-tuple-element.34.rest_4_), channel_id=1, source_target_pairs={{0,2},{1,3},{2,0},{3,1},{4,6},{5,7},{6,4},{7,5},{8,10},{9,11},{10,... | collective-permute-start | bytes 73736 | tf_op jit(solution)/shard_map/ppermute | solution.py:688
  73.4 5.4 %collective-permute-start.9 = (f32[6,8,128]{2,1,0:T(8,128)S(1)}, f32[6,8,128]{2,1,0:T(8,128)S(1)}, u32[]{:S(2)}, u32[]{:S(2)}) collective-permute-start(f32[6,8,128]{2,1,0:T(8,128)S(1)} %get-tuple-element.34.rest_4_), channel_id=1, source_target_pairs={{0,3},{1,0},{2,1},{3,2},{4,7},{5,4},{6,5},{7,6},{8,11},{9,8},{10,9... | collective-permute-start | bytes 73736 | tf_op jit(solution)/shard_map/ppermute | solution.py:688
  91.9 18.2 %all-to-all-start.2 = ((f32[32,1,7]{2,1,0:T(1,128)}), f32[32,1,7]{2,1,0:T(1,128)S(1)}, u32[]{:S(2)}, u32[]{:S(2)}) async-start(f32[32,1,7]{2,1,0:T(1,128)} %bitcast.11), calls=%async_computation.2 | async-start | bytes 32768 | tf_op jit(solution)/shard_map/all_to_all | solution.py:773

commit v8 on v7

--- a/solution.py
+++ b/solution.py
@@ -176,7 +176,7 @@
     return weights[768 * k : 768 * (k + 1)]
 
 
-def lat_filter(vs, rows, prm, u_ref, e_ref):
+def lat_filter(vs, rows, prm, u_ref, e_ref, p_ref):
     nv = len(vs)
     decay = [prm[v, 1:2, :] for v in vs]
 
@@ -189,6 +189,11 @@
 
     zero = jnp.zeros((u_ref.shape[2], LANES), f32)
     edges = cascade(rows, load, store, decay, [zero] * nv)
+    for k in range(nv):
+        for j in range(0, u_ref.shape[2], 8):
+            block = [edges[3 - e][k][j : j + 8] * decay[k] for e in range(4)]
+            block = jnp.stack(block + [jnp.zeros((8, LANES), f32)] * 4)
+            p_ref[k, j : j + 8] = jnp.swapaxes(block, 0, 1)
     width = e_ref.shape[2] // 4
     for e in range(4):
         for k in range(nv):
@@ -226,7 +231,7 @@
 
 def lat_plain(
     rows, pairs, scales, classes, chi_coef, sigma, vert, b1lo, b1hi, b2lo, b2hi,
-    w_ref, u_ref, e_ref, prm, xs, wt, sg,
+    w_ref, u_ref, e_ref, p_ref, prm, xs, wt, sg,
 ):
     g = pl.program_id(0)
 
@@ -254,14 +259,14 @@
         return 0
 
     lax.fori_loop(0, BLOCK // PAIRS, body, 0)
-    lat_filter((1, 2), rows, prm, u_ref, e_ref)
+    lat_filter((1, 2), rows, prm, u_ref, e_ref, p_ref)
 
 
 def lat_balance(
-    rows, pairs, prm, sigma, vert, bal, plo, phi, clo, chi, temp, north, south, west, east, w_in, u_in, e_in,
-    w_ref, u_ref, e_ref, xs, wt, sg,
+    rows, pairs, prm, sigma, vert, bal, plo, phi, clo, chi, temp, north, south, west, east, w_in, u_in, e_in, p_in,
+    w_ref, u_ref, e_ref, p_ref, xs, wt, sg,
 ):
-    del w_in, u_in, e_in
+    del w_in, u_in, e_in, p_in
     g = pl.program_id(0)
 
     @pl.when(g == 0)
@@ -305,10 +310,10 @@
         return 0
 
     lax.fori_loop(0, BLOCK // PAIRS, body, 0)
-    lat_filter((0,), rows, prm, u_ref, e_ref)
-
-
-def lon_filter(prm, rb, o_ref, el_ref, es_ref, at):
+    lat_filter((0,), rows, prm, u_ref, e_ref, p_ref)
+
+
+def lon_filter(prm, rb, o_ref, el_ref, put, at):
     half = o_ref.shape[1]
     nv = len(ORDER)
     decay = [prm[v, 1:2, :] for v in ORDER]
@@ -336,13 +341,13 @@
         t4 = e4 + k3 * c1 + k2 * c2 + k1 * c3
         c4 = jnp.where(low, swap(t4), 0.0)
         t4 = t4 + span * c4
-        es_ref[2 * k, at, :] = jnp.where(low, t2, t1)
-        es_ref[2 * k + 1, at, :] = jnp.where(low, t4, t3)
+        put(2 * k, jnp.where(low, t2, t1))
+        put(2 * k + 1, jnp.where(low, t4, t3))
         for e, x in enumerate((e1, e2, e3, e4)):
             el_ref[k, e, at, :] = x
 
 
-def lon_kernel(rb, prm, sigma, u_ref, o_ref, el_ref, es_ref):
+def lon_kernel(rows, rb, prm, sigma, u_ref, w_ref, o_ref, el_ref, es_ref, px_ref, dot_ref, rx_ref, ry_ref):
     g = pl.program_id(0)
     half = u_ref.shape[2]
 
@@ -351,6 +356,12 @@
         x = sigma[0]
         lon = x.shape[1]
         es_ref[6] = jnp.where(low_lanes((x.shape[0], LANES)), x[:, 0:1], x[:, lon - 1 : lon])
+        dot_ref[...] = jnp.zeros_like(dot_ref)
+        for k, v in enumerate(ORDER):
+            for e, r in enumerate(responses(prm[v, 0:1, :], prm[v, 1:2, :], half)):
+                rx_ref[k, e] = r
+            for e, r in enumerate(responses(prm[v, 0:1, :], prm[v, 1:2, :], rows)):
+                ry_ref[k, e] = r
 
     def turn(b, _):
         at = pl.ds(pl.multiple_of(b * 8, 8), 8)
@@ -360,7 +371,30 @@
         return 0
 
     lax.fori_loop(0, half // 8, turn, 0)
-    lon_filter(prm, rb, o_ref, el_ref, es_ref, pl.ds(pl.multiple_of(g * rb, 8), rb))
+    at = pl.ds(pl.multiple_of(g * rb, 8), rb)
+
+    def put(i, x):
+        es_ref[i, at, :] = x
+
+    lon_filter(prm, rb, o_ref, el_ref, put, at)
+    zero = jnp.zeros((rb, LANES), f32)
+    for k in range(len(ORDER)):
+
+        def body(b, sums, k=k):
+            base = pl.multiple_of(b * 8, 8)
+            rx = [rx_ref[k, e, pl.ds(base, 8), :] for e in range(4)]
+            sums = list(sums)
+            for o in range(8):
+                x = w_ref[k, base + o]
+                sums[4] = sums[4] + x * o_ref[k, base + o]
+                for e in range(4):
+                    sums[e] = sums[e] + x * rx[e][o : o + 1, :]
+            return tuple(sums)
+
+        sums = lax.fori_loop(0, half // 8, body, (zero,) * 5)
+        for e in range(4):
+            px_ref[k, e, at, :] = sums[e]
+        dot_ref[k] += jnp.sum(sums[4].reshape(rb // 8, 8, LANES), axis=0)
 
 
 def solve_kernel(n_lat, rows, prm, edges, carries):
@@ -387,108 +421,80 @@
         return 0
 
     lax.fori_loop(0, carries.shape[0], body, 0)
-    lon_filter(prm, 8, o_ref, el_ref, es_ref, slice(0, 8))
-
-
-def join_kernel(n_lon, rows, packed, rq, place, prm, u_ref, w_ref, x_ref, el, elc, *rest):
-    sent, sent_x = rest[:n_lon], rest[n_lon : 2 * n_lon]
-    y_ref, yx_ref, col_ref, side_ref, energy, carry, extra, resp_x, resp_y, esm, esx = rest[2 * n_lon :]
-    g = pl.program_id(0)
-    half = resp_x.shape[2]
-    lat, me = place[0], place[1]
-
-    @pl.when(g == 0)
-    def _():
-        energy[...] = jnp.zeros_like(energy)
-        for s in range(n_lon):
-            t = lax.rem(me - s + n_lon, n_lon)
-            esm[t] = sent[s][...]
-            esx[t] = sent_x[s][...]
-        side_ref[0] = esm[jnp.maximum(me - 1, 0), 6]
-        side_ref[1] = esm[jnp.minimum(me + 1, n_lon - 1), 6]
-        length = jnp.stack([prm[v, 0:1, :] for v in ORDER])
-        decay = jnp.stack([prm[v, 1:2, :] for v in ORDER])
-        whole = constants(length, decay, 2 * half)
-        span, k1, k2, k3 = constants(length, decay, half)
-        low = low_lanes((len(ORDER), rows + 8, LANES))
-        cache = {}
-
-        def both(main, more):
-            parts = [jnp.concatenate([main(k), more(k)], axis=0) for k in range(len(ORDER))]
-            return jnp.stack(parts)
-
-        def edge(t, e):
-            i = e // 2
-            if (t, i) not in cache:
-                x = both(lambda k: esm[t, 2 * k + i], lambda k: esx[t, 2 * k + i])
-                y = swap(x)
-                cache[t, i] = (jnp.where(low, y, x), jnp.where(low, x, y))
-            return cache[t, i][e % 2]
-
-        d1, d2, d3, d4 = pick(solve_carries(n_lon, edge, whole), me)
-        e1, e2, e3, e4 = (both(lambda k, e=e: el[k, e], lambda k, e=e: elc[k, e]) for e in range(4))
-        c1 = jnp.where(low, d1, swap(e1 + span * d1))
-        c2 = jnp.where(low, swap(e2 + k1 * c1 + span * d2), d2)
-        c3 = jnp.where(low, d3, swap(e3 + k2 * c1 + k1 * c2 + span * d3))
-        c4 = jnp.where(low, swap(e4 + k3 * c1 + k2 * c2 + k1 * c3 + span * d4), d4)
-        for k, v in enumerate(ORDER):
-            for e, r in enumerate(responses(prm[v, 0:1, :], prm[v, 1:2, :], half)):
-                resp_x[k, e] = r
-            ry = responses(prm[v, 0:1, :], prm[v, 1:2, :], rows)
-            for e in range(4):
-                resp_y[k, e] = ry[e]
-
-            def total(x, ry=ry):
-                y = x[:rows]
+
+    def put(i, x):
+        for t in range(es_ref.shape[0]):
+            es_ref[t, i] = x
+
+    lon_filter(prm, 8, o_ref, el_ref, put, slice(0, 8))
+
+
+def close_kernel(
+    n_lon, rows, place, prm, x_ref, proj, px, dots, rx, ry, el, elc, esx, *rest
+):
+    sent = rest[:n_lon]
+    carry, full_ref, col_ref, side_ref, energy, esm = rest[n_lon:]
+    half = rx.shape[2]
+    me = place[1]
+    for d in range(n_lon):
+        esm[me ^ d] = sent[d][...]
+    side_ref[0] = esm[jnp.maximum(me - 1, 0), 6]
+    side_ref[1] = esm[jnp.minimum(me + 1, n_lon - 1), 6]
+    length = jnp.stack([prm[v, 0:1, :] for v in ORDER])
+    decay = jnp.stack([prm[v, 1:2, :] for v in ORDER])
+    whole = constants(length, decay, 2 * half)
+    span, k1, k2, k3 = constants(length, decay, half)
+    low = low_lanes((len(ORDER), rows + 8, LANES))
+    cache = {}
+
+    def both(main, more):
+        parts = [jnp.concatenate([main(k), more(k)], axis=0) for k in range(len(ORDER))]
+        return jnp.stack(parts)
+
+    def edge(t, e):
+        i = e // 2
+        if (t, i) not in cache:
+            x = both(lambda k: esm[t, 2 * k + i], lambda k: esx[t, 2 * k + i])
+            y = swap(x)
+            cache[t, i] = (jnp.where(low, y, x), jnp.where(low, x, y))
+        return cache[t, i][e % 2]
+
+    d1, d2, d3, d4 = pick(solve_carries(n_lon, edge, whole), me)
+    e1, e2, e3, e4 = (both(lambda k, e=e: el[k, e], lambda k, e=e: elc[k, e]) for e in range(4))
+    c1 = jnp.where(low, d1, swap(e1 + span * d1))
+    c2 = jnp.where(low, swap(e2 + k1 * c1 + span * d2), d2)
+    c3 = jnp.where(low, d3, swap(e3 + k2 * c1 + k1 * c2 + span * d3))
+    c4 = jnp.where(low, swap(e4 + k3 * c1 + k2 * c2 + k1 * c3 + span * d4), d4)
+    for k, v in enumerate(ORDER):
+        more = [c[k, rows:] for c in (c1, c2, c3, c4)]
+        sums = jnp.zeros((rows, LANES), f32)
+        for e, c in enumerate((c1, c2, c3, c4)):
+            carry[k, e] = c[k, :rows]
+            sums = sums + c[k, :rows] * px[k, e]
+
+        def body(b, total, k=k, more=more):
+            base = pl.multiple_of(b * 8, 8)
+            r = [rx[k, e, pl.ds(base, 8), :] for e in range(4)]
+            for o in range(8):
+                x = x_ref[k, base + o]
                 for e in range(4):
-                    y = y + ry[e] * x[rows + e : rows + e + 1]
-                return y
-
-            for e, c in enumerate((c1, c2, c3, c4)):
-                extra[k, e] = c[k, rows:]
-                carry[k, e] = total(c[k])
-            if v == 0:
-                col_ref[0] = total(d3[k])
-                col_ref[1] = total(d4[k])
-
-    row8 = lax.broadcasted_iota(jnp.int32, (8, LANES), 0)
-    for k, v in enumerate(ORDER):
-        total = jnp.zeros((rq, LANES), f32)
-        for q in range(0, rows, rq):
-            at = slice(q, q + rq)
-            c = [carry[k, e, at, :] for e in range(4)]
-            ry = [resp_y[k, e, at, :] for e in range(4)]
-
-            def body(b, total, k=k, v=v, q=q, at=at, c=c, ry=ry):
-                base = g * packed + b * 8
-                rx = [resp_x[k, e, pl.ds(pl.multiple_of(base, 8), 8), :] for e in range(4)]
-                for o in range(8):
-                    p = b * 8 + o
-                    x = x_ref[k, p]
-                    y = u_ref[k, p, at, :]
-                    for e in range(4):
-                        y = y + rx[e][o : o + 1, :] * c[e] + ry[e] * x[e : e + 1, :]
-                    y_ref[k, p, at, :] = y
-                    total = total + y * w_ref[k, p, at, :]
-                    if v == 0 and q == 0:
-                        for e in range(4):
-                            x = x + rx[e][o : o + 1, :] * extra[k, e]
-                        x = pltpu.roll(x, 6, 0)
-                        above = jnp.where(lat > 0, x + prm[0, 1:2, :] * y[0:1, :], 0.0)
-                        yx_ref[p] = jnp.where(row8 == 0, above, jnp.where(row8 == 1, x, 0.0))
-                return total
-
-            total = lax.fori_loop(0, packed // 8, body, total)
-        energy[v] += jnp.sum(total.reshape(rq // 8, 8, LANES), axis=0)
-
-    @pl.when(g == 0)
-    def _():
-        beside = col_ref[0] + prm[0, 1:2, :] * y_ref[ORDER.index(0), 0]
-        col_ref[0] = jnp.where(me > 0, beside, 0.0)
+                    x = x + r[e][o : o + 1, :] * more[e]
+                full_ref[k, base + o] = x
+                total = total + x * proj[k, base + o]
+            return total
+
+        total = lax.fori_loop(0, half // 8, body, dots[k])
+        energy[v] = total + jnp.sum(sums.reshape(rows // 8, 8, LANES), axis=0)
+        if v == 0:
+            for i, d in enumerate((d3, d4)):
+                y = d[k, :rows]
+                for e in range(4):
+                    y = y + ry[k, e] * d[k, rows + e : rows + e + 1]
+                col_ref[i] = y
 
 
 def end_kernel(
-    rows, pairs, prm, sigma, north, south, vert, bal, col, side, y_ref, yx_ref,
+    rows, pairs, rq, place, prm, sigma, north, south, vert, bal, col, side, carry, rx_ref, ry_ref, u_ref, x_ref,
     out, xs, zx, zc, wt, sg, sx,
 ):
     g = pl.program_id(0)
@@ -507,22 +513,45 @@
             width = min(LANES, lon - at)
             sx[at // LANES, 0:1, 0:width] = north[:, merged + at : merged + at + width]
             sx[at // LANES, 1:2, 0:width] = south[:, merged + at : merged + at + width]
-        lhs = jnp.where(low_lanes((rows, LANES)), col[0], col[1])
+
+    lane = lax.broadcasted_iota(jnp.int32, (rows, LANES), 1)
+    high = (lane >= 64).astype(jnp.int32)
+    high8 = high[0:8]
+    chi_row = prm[0, 2:3, :]
+
+    def at_tile(m):
+        return pl.ds(pl.multiple_of(m * LANES, LANES), LANES)
+
+    row8 = lax.broadcasted_iota(jnp.int32, (8, LANES), 0)
+    beyond = [None] * (2 * PAIRS)
+    for k, v in enumerate(ORDER):
+        for q in range(0, rows, rq):
+            c = [carry[k, e, q : q + rq, :] for e in range(4)]
+            ry = [ry_ref[k, e, q : q + rq, :] for e in range(4)]
+            rx = [rx_ref[k, e, pl.ds(pl.multiple_of(g * 2 * PAIRS, 8), 2 * PAIRS), :] for e in range(4)]
+            for p in range(2 * PAIRS):
+                x = x_ref[k, p]
+                y = u_ref[k, p, q : q + rq, :]
+                for e in range(4):
+                    y = y + rx[e][p : p + 1, :] * c[e] + ry[e] * x[e : e + 1, :]
+                at = (p // 2) * rows + q
+                xs[k, at : at + rq, (p % 2) * LANES : (p % 2 + 1) * LANES] = y
+                if v == 0 and q == 0:
+                    x = pltpu.roll(x, 6, 0)
+                    above = jnp.where(place[0] > 0, x + prm[0, 1:2, :] * y[0:1, :], 0.0)
+                    beyond[p] = jnp.where(row8 == 0, above, jnp.where(row8 == 1, x, 0.0))
+
+    @pl.when(g == 0)
+    def _():
+        first = col[0] + prm[0, 1:2, :] * xs[ORDER.index(0), 0:rows, 0:LANES]
+        lhs = jnp.where(lane < 64, jnp.where(place[1] > 0, first, 0.0), col[1])
         lhs = jnp.concatenate([lhs, jnp.zeros_like(lhs)], axis=1)
         res = product(lhs, weight(wt, 0))
         zc[0] = swap(res[:, :LANES] * swap(side[0]))
         zc[1] = res[:, LANES:] * side[1]
 
-    lane = lax.broadcasted_iota(jnp.int32, (rows, LANES), 1)
-    high = (lane >= 64).astype(jnp.int32)
-    high8 = high[0:8]
-    chi_row = prm[0, 2:3, :]
-
-    def at_tile(m):
-        return pl.ds(pl.multiple_of(m * LANES, LANES), LANES)
-
     lhs = jnp.concatenate(
-        [jnp.concatenate([yx_ref[2 * p], yx_ref[2 * p + 1]], axis=1) for p in range(PAIRS)], axis=0
+        [jnp.concatenate(beyond[2 * p : 2 * p + 2], axis=1) for p in range(PAIRS)], axis=0
     )
     res = product(lhs, weight(wt, 0))
     for p in range(PAIRS):
@@ -531,11 +560,7 @@
             tile = m + side * pairs
             s = jnp.take_along_axis(sx[tile >> 6], 2 * (tile & 63) + high8, axis=1, mode="promise_in_bounds")
             part = res[p * 8 : (p + 1) * 8, side * LANES : (side + 1) * LANES]
-            zx[:, at_tile(tile)] = jnp.where(lax.broadcasted_iota(jnp.int32, (8, LANES), 0) < 2, part * s, 0.0)
-    for k in range(3):
-        for p in range(2 * PAIRS):
-            at = slice((p // 2) * rows, (p // 2 + 1) * rows)
-            xs[k, at, (p % 2) * LANES : (p % 2 + 1) * LANES] = y_ref[k, p]
+            zx[:, at_tile(tile)] = jnp.where(row8 < 2, part * s, 0.0)
     results = {v: product(xs[k], weight(wt, v)) for k, v in enumerate(ORDER)}
     for p in range(PAIRS):
         m = g * PAIRS + p
@@ -613,6 +638,7 @@
 
     width = half // n_lat
     shapes = [(nvars, half, rows, LANES), (nvars, rows, half, LANES), (n_lat, nvars, 4 * width, LANES)]
+    shapes.append((nvars, half, 8, LANES))
 
     def lat_call(nv, first, body, arrays, specs, name, aliases, more=()):
         return pl.pallas_call(
@@ -623,6 +649,7 @@
                 pl.BlockSpec((nv, 2 * BLOCK, rows, LANES), lambda g: (first, g, 0, 0)),
                 pl.BlockSpec((nv, rows, 2 * BLOCK, LANES), lambda g: (first, 0, g, 0)),
                 pl.BlockSpec((2 * BLOCK // width, nv, 4 * width, LANES), lambda g: (g, first, 0, 0)),
+                pl.BlockSpec((nv, 2 * BLOCK, 8, LANES), lambda g: (first, g, 0, 0)),
             ]
             + [full(s) for s in more],
             out_shape=[pltpu.HBM(s, f32) for s in shapes[:2]]
@@ -646,46 +673,55 @@
     body = functools.partial(lat_plain, rows, pairs)
     *wue, prm = lat_call(2, 0, body, ins, specs, "lat_chi_temp", {}, [(nvars, 4, LANES)])
     ins = [prm, sigma, vert, bal_temp] + [in_hbm(state)] * 5 + [north, south, west, east]
-    ins += [in_hbm(wue[0]), in_hbm(wue[1]), wue[2]]
+    ins += [in_hbm(wue[0]), in_hbm(wue[1]), wue[2], wue[3]]
     specs = [full(x.shape) for x in ins[:4]] + [part(0, 0), part(0, 1), part(1, 0), part(1, 1)]
     specs += [pl.BlockSpec((1, rows, merged), lambda g: (2, 0, 0))]
-    specs += [full(x.shape) for x in (north, south, west, east)] + [anywhere] * 3
-    aliases = {13: 0, 14: 1, 15: 2}
-    w, u, edges = lat_call(1, 2, functools.partial(lat_balance, rows, pairs), ins, specs, "lat_psi", aliases)
-    def trade(x):
-        return lax.all_to_all(x, "lat", split_axis=0, concat_axis=0, tiled=True)
-
-    shares = trade(edges)
+    specs += [full(x.shape) for x in (north, south, west, east)] + [anywhere] * 4
+    aliases = {13: 0, 14: 1, 15: 2, 16: 3}
+    w, u, edges, proj = lat_call(1, 2, functools.partial(lat_balance, rows, pairs), ins, specs, "lat_psi", aliases)
+    def trade(x, axis):
+        return lax.all_to_all(x, axis, split_axis=0, concat_axis=0, tiled=True)
+
+    shares = trade(edges, "lat")
 
     rb = BLOCK
-    local, el, es = pl.pallas_call(
-        functools.partial(lon_kernel, rb),
+    local, el, es, px, dots, rx, ry = pl.pallas_call(
+        functools.partial(lon_kernel, rows, rb),
         grid=(rows // rb,),
         in_specs=[
             full(prm.shape),
             pl.BlockSpec((1, rows, lon), lambda g: (0, 0, 0)),
             pl.BlockSpec((nvars, rb, half, LANES), lambda g: (0, g, 0, 0)),
+            pl.BlockSpec((nvars, half, rb, LANES), lambda g: (0, 0, g, 0)),
         ],
         out_specs=[
             pl.BlockSpec((nvars, half, rb, LANES), lambda g: (0, 0, g, 0)),
             full((nvars, 4, rows, LANES)),
             full((7, rows, LANES)),
+            full((nvars, 4, rows, LANES)),
+            full((nvars, 8, LANES)),
+            full((nvars, 4, half, LANES)),
+            full((nvars, 4, rows, LANES)),
         ],
         out_shape=[
             pltpu.HBM((nvars, half, rows, LANES), f32),
             jax.ShapeDtypeStruct((nvars, 4, rows, LANES), f32),
             jax.ShapeDtypeStruct((7, rows, LANES), f32),
+            jax.ShapeDtypeStruct((nvars, 4, rows, LANES), f32),
+            jax.ShapeDtypeStruct((nvars, 8, LANES), f32),
+            jax.ShapeDtypeStruct((nvars, 4, half, LANES), f32),
+            jax.ShapeDtypeStruct((nvars, 4, rows, LANES), f32),
         ],
         compiler_params=params(),
         cost_estimate=pl.CostEstimate(
             flops=180000000, bytes_accessed=6 * rows * merged * 4, transcendentals=0
         ),
         name="lon_tile",
-    )(prm, sigma, in_hbm(u))
+    )(prm, sigma, in_hbm(u), in_hbm(w))
 
     def round_lon(x):
         return [x] + [
-            lax.ppermute(x, "lon", [(i, (i + s) % n_lon) for i in range(n_lon)]) for s in range(1, n_lon)
+            lax.ppermute(x, "lon", [(i, i ^ s) for i in range(n_lon)]) for s in range(1, n_lon)
         ]
 
     shares, _ = lax.optimization_barrier((shares, es))
@@ -700,17 +736,17 @@
         cost_estimate=pl.CostEstimate(flops=1000000, bytes_accessed=2 * shares.size * 4, transcendentals=0),
         name="solve",
     )(prm, shares)
-    carries = trade(carries)
+    carries = trade(carries, "lat")
 
     crossed, elc, esc = pl.pallas_call(
         carry_kernel,
         grid=(1,),
         in_specs=[full(prm.shape), full(carries.shape)],
-        out_specs=[full((nvars, half, 8, LANES)), full((nvars, 4, 8, LANES)), full((6, 8, LANES))],
+        out_specs=[full((nvars, half, 8, LANES)), full((nvars, 4, 8, LANES)), full((n_lon, 6, 8, LANES))],
         out_shape=[
             jax.ShapeDtypeStruct((nvars, half, 8, LANES), f32),
             jax.ShapeDtypeStruct((nvars, 4, 8, LANES), f32),
-            jax.ShapeDtypeStruct((6, 8, LANES), f32),
+            jax.ShapeDtypeStruct((n_lon, 6, 8, LANES), f32),
         ],
         compiler_params=params(),
         cost_estimate=pl.CostEstimate(
@@ -718,48 +754,33 @@
         ),
         name="lon_carry",
     )(prm, carries)
-    sent_x = round_lon(esc)
+    sent_x = trade(esc, "lon")
 
     packed = 2 * PAIRS
 
     def columns(r):
         return pl.BlockSpec((nvars, packed, r, LANES), lambda g: (0, g, 0, 0))
 
-    ins = [place, prm, in_hbm(local), in_hbm(w), crossed, el, elc] + sent + sent_x
+    ins = [place, prm, crossed, proj, px, dots, rx, ry, el, elc, sent_x] + sent
     specs = [full(x.shape) for x in ins]
     specs[0] = pl.BlockSpec(memory_space=pltpu.SMEM)
-    specs[2:5] = [columns(rows), columns(rows), columns(8)]
-    y, yx, col, side, energy = pl.pallas_call(
-        functools.partial(join_kernel, n_lon, rows, packed, 24),
-        grid=(half // packed,),
+    shapes = [
+        (nvars, 4, rows, LANES),
+        (nvars, half, 8, LANES),
+        (2, rows, LANES),
+        (2, rows, LANES),
+        (nvars, 8, LANES),
+    ]
+    carry, crossed, col, side, energy = pl.pallas_call(
+        functools.partial(close_kernel, n_lon, rows),
+        grid=(1,),
         in_specs=specs,
-        out_specs=[
-            columns(rows),
-            pl.BlockSpec((packed, 8, LANES), lambda g: (g, 0, 0)),
-            full((2, rows, LANES)),
-            full((2, rows, LANES)),
-            full((nvars, 8, LANES)),
-        ],
-        out_shape=[
-            pltpu.HBM((nvars, half, rows, LANES), f32),
-            jax.ShapeDtypeStruct((half, 8, LANES), f32),
-            jax.ShapeDtypeStruct((2, rows, LANES), f32),
-            jax.ShapeDtypeStruct((2, rows, LANES), f32),
-            jax.ShapeDtypeStruct((nvars, 8, LANES), f32),
-        ],
-        scratch_shapes=[
-            pltpu.VMEM((nvars, 4, rows, LANES), f32),
-            pltpu.VMEM((nvars, 4, 8, LANES), f32),
-            pltpu.VMEM((nvars, 4, half, LANES), f32),
-            pltpu.VMEM((nvars, 4, rows, LANES), f32),
-            pltpu.VMEM((n_lon, 7, rows, LANES), f32),
-            pltpu.VMEM((n_lon, 6, 8, LANES), f32),
-        ],
+        out_specs=[full(x) for x in shapes],
+        out_shape=[jax.ShapeDtypeStruct(x, f32) for x in shapes],
+        scratch_shapes=[pltpu.VMEM((n_lon, 7, rows, LANES), f32)],
         compiler_params=params(),
-        cost_estimate=pl.CostEstimate(
-            flops=60000000, bytes_accessed=9 * rows * merged * 4, transcendentals=0
-        ),
-        name="join",
+        cost_estimate=pl.CostEstimate(flops=10000000, bytes_accessed=4000000, transcendentals=0),
+        name="close",
     )(*ins)
 
     index = jnp.arange(count, dtype=jnp.int32)
@@ -773,12 +794,12 @@
     table = lax.all_to_all(table, ("lat", "lon"), split_axis=0, concat_axis=0, tiled=True)
     slab_energy = (jnp.sum(table, axis=0) / (devices * rows * lon))[None, :]
 
-    ins = [prm, sigma, north, south, vert, bal_temp, col, side, in_hbm(y), yx]
+    ins = [place, prm, sigma, north, south, vert, bal_temp, col, side, carry, rx, ry, in_hbm(local), crossed]
     specs = [full(x.shape) for x in ins]
-    specs[8] = columns(rows)
-    specs[9] = pl.BlockSpec((packed, 8, LANES), lambda g: (g, 0, 0))
+    specs[0] = pl.BlockSpec(memory_space=pltpu.SMEM)
+    specs[-2:] = [columns(rows), columns(8)]
     applied = pl.pallas_call(
-        functools.partial(end_kernel, rows, pairs),
+        functools.partial(end_kernel, rows, pairs, 24),
         grid=(half // packed,),
         in_specs=specs,
         out_specs=full(state.shape),

time: 111 us -> 129 us (1.16)
  local copies, waits for them, and re-layouts: 3.56 us -> 25.4 us
  starting transfers between devices: 36.7 us -> 33.5 us
  other arithmetic: 1.15 us -> 3.76 us
  Pallas kernels: 58.8 us -> 56.3 us
  waiting for transfers between devices: 9.66 us -> 8.22 us
    unnamed x8 -> x66, local copies, waits for them, and re-layouts: 0.02 us -> 21.3 us
    ppermute x6 -> x3, starting transfers between devices: 13.2 us -> 5.3 us  [round_lon(): lax.ppermute(x, 'lon', [(i, i ^ s) for i in range(n_lon)])]
    all_to_all x2 -> x3, starting transfers between devices: 9.8 us -> 16.4 us  [trade(): return lax.all_to_all(x, axis, split_axis=0, concat_axis=0, tiled=True)]
    ppermute x6 -> x3, waiting for transfers between devices: 3.96 us -> 0.01 us  [round_lon(): lax.ppermute(x, 'lon', [(i, i ^ s) for i in range(n_lon)])]
    pallas_call x3, Pallas kernels: 34.1 us -> 31.4 us  [the longest x1 16.9 us: shards(): pl.pallas_call(functools.partial(end_kernel, rows, pairs, 24), grid=(half...]
    all_to_all x2 -> x3, waiting for transfers between devices: 5.69 us -> 8.2 us  [trade(): return lax.all_to_all(x, axis, split_axis=0, concat_axis=0, tiled=True)]
    all_to_all x1, starting transfers between devices: 4.46 us -> 2.55 us  [shards(): lax.all_to_all(table, ('lat', 'lon'), split_axis=0, concat_axis=0, tiled=...]
  transfers between devices with their start and end apart: 13 -> 11, of which waited for: 3 -> 2; matrix products, arithmetic and copies ran while one was open for 1% -> 2% of each run, Pallas kernels for 32% -> 33%
where the time goes in v8:
time: 129 us; the launch traced here: 128 us
  Pallas kernels  56.3 us (44%)
  starting transfers between devices  33.5 us (26%)
  local copies, waits for them, and re-layouts  25.4 us (20%)
  waiting for transfers between devices  8.22 us (6%)
  other arithmetic  3.76 us (3%)
    pallas_call x2, Pallas kernels, lat_call(): pl.pallas_call(body, grid=(steps,), in_specs=specs, out_specs=[pl.BlockSp...  22.3 us
    unnamed x66, local copies, waits for them, and re-layouts  21.3 us
    pallas_call x1, Pallas kernels, shards(): pl.pallas_call(functools.partial(end_kernel, rows, pairs, 24), grid=(half...  16.9 us
    all_to_all x3, starting transfers between devices, trade(): return lax.all_to_all(x, axis, split_axis=0, concat_axis=0, tiled=True)  16.4 us
    pallas_call x1, Pallas kernels, shards(): pl.pallas_call(functools.partial(lon_kernel, rows, rb), grid=(rows // rb,...  12.2 us
    all_to_all x3, waiting for transfers between devices, trade(): return lax.all_to_all(x, axis, split_axis=0, concat_axis=0, tiled=True)  8.2 us
    ppermute x3, starting transfers between devices, round_lon(): lax.ppermute(x, 'lon', [(i, i ^ s) for i in range(n_lon)])  5.3 us
    ppermute x1, starting transfers between devices, shards(): west = lax.ppermute(state[2, :, merged - levels:], 'lon', up_lon)  4.3 us
  transfers between devices with their start and end apart: 11, of which 2 were waited for; matrix products, arithmetic and copies ran while one was open for 2% of the time, Pallas kernels for 33%

profile of v8, /device:TPU:0, one launch (start us, length us, event | category | flops | bytes accessed | tf_op | source)
XLA Modules:
  0.0 128.0 jit_solution(4540731364032340877)
XLA Ops:
  0.6 1.2 slice_bitcast_fusion
  1.8 0.7 slice_bitcast_fusion.4
  2.6 2.4 %collective-permute-start = (f32[1,12480]{1,0:T(1,128)S(1)}, f32[1,12480]{1,0:T(1,128)S(1)}, u32[]{:S(2)}, u32[]{:S(2)}) collective-permute-start(f32[1,12480]{1,0:T(1,128)S(1)} %pad_maximum_fusion), channel_id=1, source_target_pairs={{0,4},{4,8},{8,12},{12,16},{16,20},{20,24},{24,28},{1,5},{5,9},{9,... | collective-permute-start | bytes 149768 | tf_op jit(solution)/shard_map/ppermute | solution.py:627
  5.0 1.3 %collective-permute-start.1 = (f32[1,12480]{1,0:T(1,128)S(1)}, f32[1,12480]{1,0:T(1,128)S(1)}, u32[]{:S(2)}, u32[]{:S(2)}) collective-permute-start(f32[1,12480]{1,0:T(1,128)S(1)} %pad_maximum_fusion.1), channel_id=1, source_target_pairs={{4,0},{8,4},{12,8},{16,12},{20,16},{24,20},{28,24},{5,1},{9,5},{13... | collective-permute-start | bytes 149768 | tf_op jit(solution)/shard_map/ppermute | solution.py:628
  6.3 0.8 slice_bitcast_fusion.2
  7.1 4.3 %collective-permute-start.2 = (f32[48,64]{1,0:T(8,128)S(1)}, f32[48,64]{1,0:T(8,128)S(1)}, u32[]{:S(2)}, u32[]{:S(2)}) collective-permute-start(f32[48,64]{1,0:T(8,128)S(1)} %get-tuple-element.53), channel_id=1, source_target_pairs={{0,1},{1,2},{2,3},{4,5},{5,6},{6,7},{8,9},{9,10},{10,11},{12,13},{... | collective-permute-start | bytes 36872 | tf_op jit(solution)/shard_map/ppermute | solution.py:629
  11.5 1.3 %collective-permute-start.3 = (f32[48,64]{1,0:T(8,128)S(1)}, f32[48,64]{1,0:T(8,128)S(1)}, u32[]{:S(2)}, u32[]{:S(2)}) collective-permute-start(f32[48,64]{1,0:T(8,128)S(1)} %get-tuple-element.52), channel_id=1, source_target_pairs={{1,0},{2,1},{3,2},{5,4},{6,5},{7,6},{9,8},{10,9},{11,10},{13,12},{... | collective-permute-start | bytes 36872 | tf_op jit(solution)/shard_map/ppermute | solution.py:630
  12.8 0.0 copy-start
  12.8 0.0 copy-start.3
  12.8 11.6 %lat_chi_temp.1 = (f32[3,96,48,128]{3,2,1,0:T(8,128)}, f32[3,48,96,128]{3,2,1,0:T(8,128)}, f32[8,3,48,128]{3,2,1,0:T(8,128)}, f32[3,96,8,128]{3,2,1,0:T(8,128)S(1)}, f32[3,4,128]{2,1,0:T(4,128)S(1)}) custom-call(f32[1,8]{1,0:T(1,128)} %bitcast.23, s32[1,192]{1,0:T(1,128)} %bitcast.22, f32[1,64]{1,0:T(1,128)} %bitcast.24, f32[3,48,192]{2,1,0:T(8,128)} %sigma.7, ...), custom_call_target="tpu_custom_call" | custom-call | flops 120000000 | bytes 14155776 | tf_op jit(solution)/shard_map/lat_chi_temp/pallas_call | solution.py:644
  24.5 10.7 %lat_psi.1 = (f32[3,96,48,128]{3,2,1,0:T(8,128)}, f32[3,48,96,128]{3,2,1,0:T(8,128)}, f32[8,3,48,128]{3,2,1,0:T(8,128)}, f32[3,96,8,128]{3,2,1,0:T(8,128)S(1)}) custom-call(f32[3,4,128]{2,1,0:T(4,128)S(1)} %get-tuple-element.27.prm, f32[3,48,192]{2,1,0:T(8,128)S(1)} %copy-done, ...), custom_call_target="tpu_custom_call", output_to_operand_aliasing={{0}: (13, {}), {1}: (14, {}), {2}: (15, {}), {3}: (16, {})} | custom-call | flops 60000000 | bytes 7077888 | tf_op jit(solution)/shard_map/lat_psi/pallas_call | solution.py:644
  35.2 6.3 %all-to-all-start = ((f32[8,3,48,128]{3,2,1,0:T(8,128)}), f32[8,3,48,128]{3,2,1,0:T(8,128)S(1)}, u32[]{:S(2)}, u32[]{:S(2)}) async-start(f32[8,3,48,128]{3,2,1,0:T(8,128)} %get-tuple-element.32), calls=%async_computation | async-start | bytes 1179648 | tf_op jit(solution)/shard_map/all_to_all | solution.py:683
  41.4 12.2 %lon_tile.1 = (f32[3,96,48,128]{3,2,1,0:T(8,128)}, f32[3,4,48,128]{3,2,1,0:T(8,128)S(1)}, f32[7,48,128]{2,1,0:T(8,128)S(1)}, f32[3,4,48,128]{3,2,1,0:T(8,128)S(1...) custom-call(f32[3,4,128]{2,1,0:T(4,128)S(1)} %get-tuple-element.27.prm, ...), custom_call_target="tpu_custom_call" | custom-call | flops 180000000 | bytes 14155776 | tf_op jit(solution)/shard_map/lon_tile/pallas_call | solution.py:688
  53.7 0.7 copy-done.6
  54.4 0.7 copy-done.8
  55.1 0.6 copy-done.29
  55.7 1.0 solve.1
  56.7 4.2 %all-to-all-start.1 = ((f32[8,3,48,128]{3,2,1,0:T(8,128)}), f32[8,3,48,128]{3,2,1,0:T(8,128)S(1)}, u32[]{:S(2)}, u32[]{:S(2)}) async-start(f32[8,3,48,128]{3,2,1,0:T(8,128)} %solve.1), calls=%async_computation.1 | async-start | bytes 1179648 | tf_op jit(solution)/shard_map/all_to_all | solution.py:683
  60.9 0.2 convert_reduce_fusion
  61.1 2.7 %collective-permute-start.4 = (f32[7,48,128]{2,1,0:T(8,128)S(1)}, f32[7,48,128]{2,1,0:T(8,128)S(1)}, u32[]{:S(2)}, u32[]{:S(2)}) collective-permute-start(f32[7,48,128]{2,1,0:T(8,128)S(1)} %get-tuple-element.35.rest_0_), channel_id=1, source_target_pairs={{0,1},{1,0},{2,3},{3,2},{4,5},{5,4},{6,7},{7,6},{8,9},{9,8},{10,11... | collective-permute-start | bytes 516104 | tf_op jit(solution)/shard_map/ppermute | solution.py:724
  63.8 2.6 %collective-permute-start.5 = (f32[7,48,128]{2,1,0:T(8,128)S(1)}, f32[7,48,128]{2,1,0:T(8,128)S(1)}, u32[]{:S(2)}, u32[]{:S(2)}) collective-permute-start(f32[7,48,128]{2,1,0:T(8,128)S(1)} %get-tuple-element.35.rest_0_), channel_id=1, source_target_pairs={{0,2},{1,3},{2,0},{3,1},{4,6},{5,7},{6,4},{7,5},{8,10},{9,11},{10,... | collective-permute-start | bytes 516104 | tf_op jit(solution)/shard_map/ppermute | solution.py:724
  66.4 5.0 %all-to-all-done.1.carries = f32[8,3,48,128]{3,2,1,0:T(8,128)S(1)} async-done(((f32[8,3,48,128]{3,2,1,0:T(8,128)}), f32[8,3,48,128]{3,2,1,0:T(8,128)S(1)}, u32[]{:S(2)}, u32[]{:S(2)}) %all-to-all-start.1) | async-done | bytes 589856 | tf_op jit(solution)/shard_map/all_to_all | solution.py:683
  71.3 1.6 %lon_carry.1 = (f32[3,96,8,128]{3,2,1,0:T(8,128)S(1)}, f32[3,4,8,128]{3,2,1,0:T(8,128)S(1)}, f32[4,6,8,128]{3,2,1,0:T(8,128)S(1)}) custom-call(f32[3,4,128]{2,1,0:T(4,128)S(1)} %get-tuple-element.27.prm, f32[8,3,48,128]{3,2,1,0:T(8,128)S(1)} %all-to-all-done.1.carries), custom_call_target="tpu_custom_call" | custom-call | flops 30000000 | bytes 1769472 | tf_op jit(solution)/shard_map/lon_carry/pallas_call | solution.py:741
  72.9 1.0 copy-done.1
  73.9 0.6 copy-done.22
  74.6 0.6 copy-done.23
  75.2 5.9 %all-to-all-start.2 = ((f32[4,6,8,128]{3,2,1,0:T(8,128)}), f32[4,6,8,128]{3,2,1,0:T(8,128)S(1)}, u32[]{:S(2)}, u32[]{:S(2)}) async-start(f32[4,6,8,128]{3,2,1,0:T(8,128)} %copy-done.22), calls=%async_computation.2 | async-start | bytes 196608 | tf_op jit(solution)/shard_map/all_to_all | solution.py:683
  81.1 0.6 multiply_add_fusion
  81.7 0.6 slice.33
  82.3 0.1 pad_add_fusion.place
  82.4 0.7 copy-done.16
  83.1 0.7 copy-done.18
  83.7 3.2 %all-to-all-done.2.esx = f32[4,6,8,128]{3,2,1,0:T(8,128)S(1)} async-done(((f32[4,6,8,128]{3,2,1,0:T(8,128)}), f32[4,6,8,128]{3,2,1,0:T(8,128)S(1)}, u32[]{:S(2)}, u32[]{:S(2)}) %all-to-all-start.2) | async-done | bytes 98336 | tf_op jit(solution)/shard_map/all_to_all | solution.py:683
  87.0 0.6 copy-done.4
  87.6 1.3 copy-done.2
  88.9 0.9 copy-done.5
  89.8 1.0 copy-done.7
  90.7 1.0 copy-done.9
  91.7 0.9 copy-done.15
  92.6 0.9 copy-done.17
  93.5 0.9 copy-done.19
  94.5 0.8 copy-done.24
  95.3 0.7 copy-done.30
  96.0 2.2 %close.1 = (f32[3,4,48,128]{3,2,1,0:T(8,128)S(1)}, f32[3,96,8,128]{3,2,1,0:T(8,128)S(1)}, f32[2,48,128]{2,1,0:T(8,128)S(1)}, f32[2,48,128]{2,1,0:T(8,128)S(1)}, f32[3,8,128]{2,1,0:T(8,128)S(1)}) custom-call(s32[2]{0:T(128)S(1)} %pad_add_fusion.place, f32[3,4,128]{2,1,0:T(4,128)S(1)} %get-tuple-element.27.prm, f32[3,96,8,128]{3,2,1,0:T(8,128)S(1)} %copy-done.2, ...), custom_call_target="tpu_custom_call" | custom-call | flops 10000000 | bytes 4000000 | tf_op jit(solution)/shard_map/close/pallas_call | solution.py:774
  98.2 0.0 copy-start.10
  98.2 0.7 copy-done.10
  98.9 0.6 copy-done.25
  99.5 0.6 copy-done.27
  100.2 0.6 copy-done.31
  100.8 0.7 reduce_sum.37
  101.5 0.7 bitcast_multiply_fusion
  102.2 0.1 slice_add_fusion
  102.2 0.1 broadcast_in_dim.14
  102.3 0.8 select_reduce_fusion
  103.1 0.7 all_to_all.18
  103.8 2.5 %all-to-all-start.3 = ((f32[32,1,7]{2,1,0:T(1,128)}), f32[32,1,7]{2,1,0:T(1,128)S(1)}, u32[]{:S(2)}, u32[]{:S(2)}) async-start(f32[32,1,7]{2,1,0:T(1,128)} %bitcast.11), calls=%async_computation.3 | async-start | bytes 32768 | tf_op jit(solution)/shard_map/all_to_all | solution.py:794
  106.4 1.0 copy-done.11
  107.4 0.8 copy-done.13
  108.2 0.8 copy-done.21
  108.9 0.8 copy-done.26
  109.7 0.8 copy-done.28
  110.5 16.9 %finish.1 = f32[3,48,12288]{2,1,0:T(8,128)} custom-call(s32[2]{0:T(128)S(1)} %pad_add_fusion.place, f32[3,4,128]{2,1,0:T(4,128)S(1)} %get-tuple-element.27.prm, f32[3,48,192]{2,1,0:T(8,128)S(1)} %copy-done, f32[1,12480]{1,0:T(1,128)S(1)} %collective-permute-done.north, f32[1,12480]{1,0:T(1,128)S(1)} %copy-done.13, f32[3,64,64]{2,1,0:T(8,128)S(1)} %copy-done.3, ...), custom_call_target="tpu_custom_call" | custom-call | flops 300000000 | bytes 14155776 | tf_op jit(solution)/shard_map/finish/pallas_call | solution.py:801
  127.5 0.1 reduce_sum.39
  127.5 0.5 multiply_bitcast_fusion
  (48 shorter events, 0.2 us)
Async XLA Ops:
  2.6 21.8 %collective-permute-start = (f32[1,12480]{1,0:T(1,128)S(1)}, f32[1,12480]{1,0:T(1,128)S(1)}, u32[]{:S(2)}, u32[]{:S(2)}) collective-permute-start(f32[1,12480]{1,0:T(1,128)S(1)} %pad_maximum_fusion), channel_id=1, source_target_pairs={{0,4},{4,8},{8,12},{12,16},{16,20},{20,24},{24,28},{1,5},{5,9},{9,... | collective-permute-start | bytes 149768 | tf_op jit(solution)/shard_map/ppermute | solution.py:627
  5.0 19.4 %collective-permute-start.1 = (f32[1,12480]{1,0:T(1,128)S(1)}, f32[1,12480]{1,0:T(1,128)S(1)}, u32[]{:S(2)}, u32[]{:S(2)}) collective-permute-start(f32[1,12480]{1,0:T(1,128)S(1)} %pad_maximum_fusion.1), channel_id=1, source_target_pairs={{4,0},{8,4},{12,8},{16,12},{20,16},{24,20},{28,24},{5,1},{9,5},{13... | collective-permute-start | bytes 149768 | tf_op jit(solution)/shard_map/ppermute | solution.py:628
  7.1 17.2 %collective-permute-start.2 = (f32[48,64]{1,0:T(8,128)S(1)}, f32[48,64]{1,0:T(8,128)S(1)}, u32[]{:S(2)}, u32[]{:S(2)}) collective-permute-start(f32[48,64]{1,0:T(8,128)S(1)} %get-tuple-element.53), channel_id=1, source_target_pairs={{0,1},{1,2},{2,3},{4,5},{5,6},{6,7},{8,9},{9,10},{10,11},{12,13},{... | collective-permute-start | bytes 36872 | tf_op jit(solution)/shard_map/ppermute | solution.py:629
  11.5 12.9 %collective-permute-start.3 = (f32[48,64]{1,0:T(8,128)S(1)}, f32[48,64]{1,0:T(8,128)S(1)}, u32[]{:S(2)}, u32[]{:S(2)}) collective-permute-start(f32[48,64]{1,0:T(8,128)S(1)} %get-tuple-element.52), channel_id=1, source_target_pairs={{1,0},{2,1},{3,2},{5,4},{6,5},{7,6},{9,8},{10,9},{11,10},{13,12},{... | collective-permute-start | bytes 36872 | tf_op jit(solution)/shard_map/ppermute | solution.py:630
  12.8 11.7 %copy-start = (f32[3,48,192]{2,1,0:T(8,128)S(1)}, f32[3,48,192]{2,1,0:T(8,128)}, u32[]{:S(2)}) copy-start(f32[3,48,192]{2,1,0:T(8,128)} %sigma.7) | copy-start | bytes 331780
  12.8 11.7 %copy-start.3 = (f32[3,64,64]{2,1,0:T(8,128)S(1)}, f32[3,64,64]{2,1,0:T(8,128)}, u32[]{:S(2)}) copy-start(f32[3,64,64]{2,1,0:T(8,128)} %vert.5) | copy-start | bytes 147460
  12.8 11.7 %copy-start.20 = (f32[64,64]{1,0:T(8,128)S(1)}, f32[64,64]{1,0:T(8,128)}, u32[]{:S(2)}) copy-start(f32[64,64]{1,0:T(8,128)} %bal.3) | copy-start | bytes 49156
  24.4 10.7 %copy-start.12 = (f32[1,12480]{1,0:T(1,128)}, f32[1,12480]{1,0:T(1,128)S(1)}, u32[]{:S(2)}) copy-start(f32[1,12480]{1,0:T(1,128)S(1)} %collective-permute-done.1.south) | copy-start | bytes 149764
  35.2 20.6 %all-to-all-start = ((f32[8,3,48,128]{3,2,1,0:T(8,128)}), f32[8,3,48,128]{3,2,1,0:T(8,128)S(1)}, u32[]{:S(2)}, u32[]{:S(2)}) async-start(f32[8,3,48,128]{3,2,1,0:T(8,128)} %get-tuple-element.32), calls=%async_computation | async-start | bytes 1179648 | tf_op jit(solution)/shard_map/all_to_all | solution.py:683
  41.4 19.5 %copy-start.32 = (s32[192]{0:T(256)S(1)}, s32[192]{0:T(256)}, u32[]{:S(2)}) copy-start(s32[192]{0:T(256)} %param.15) | copy-start | bytes 2308
  53.7 0.7 copy-start.6
  54.4 0.7 copy-start.8
  55.1 0.6 copy-start.29
  55.7 31.9 %copy-start.14 = (f32[7,48,128]{2,1,0:T(8,128)}, f32[7,48,128]{2,1,0:T(8,128)S(1)}, u32[]{:S(2)}) copy-start(f32[7,48,128]{2,1,0:T(8,128)S(1)} %get-tuple-element.35.rest_0_) | copy-start | bytes 516100
  56.7 14.6 %all-to-all-start.1 = ((f32[8,3,48,128]{3,2,1,0:T(8,128)}), f32[8,3,48,128]{3,2,1,0:T(8,128)S(1)}, u32[]{:S(2)}, u32[]{:S(2)}) async-start(f32[8,3,48,128]{3,2,1,0:T(8,128)} %solve.1), calls=%async_computation.1 | async-start | bytes 1179648 | tf_op jit(solution)/shard_map/all_to_all | solution.py:683
  61.1 21.3 %collective-permute-start.4 = (f32[7,48,128]{2,1,0:T(8,128)S(1)}, f32[7,48,128]{2,1,0:T(8,128)S(1)}, u32[]{:S(2)}, u32[]{:S(2)}) collective-permute-start(f32[7,48,128]{2,1,0:T(8,128)S(1)} %get-tuple-element.35.rest_0_), channel_id=1, source_target_pairs={{0,1},{1,0},{2,3},{3,2},{4,5},{5,4},{6,7},{7,6},{8,9},{9,8},{10,11... | collective-permute-start | bytes 516104 | tf_op jit(solution)/shard_map/ppermute | solution.py:724
  63.8 19.3 %collective-permute-start.5 = (f32[7,48,128]{2,1,0:T(8,128)S(1)}, f32[7,48,128]{2,1,0:T(8,128)S(1)}, u32[]{:S(2)}, u32[]{:S(2)}) collective-permute-start(f32[7,48,128]{2,1,0:T(8,128)S(1)} %get-tuple-element.35.rest_0_), channel_id=1, source_target_pairs={{0,2},{1,3},{2,0},{3,1},{4,6},{5,7},{6,4},{7,5},{8,10},{9,11},{10,... | collective-permute-start | bytes 516104 | tf_op jit(solution)/shard_map/ppermute | solution.py:724
  66.4 17.3 %collective-permute-start.6 = (f32[7,48,128]{2,1,0:T(8,128)S(1)}, f32[7,48,128]{2,1,0:T(8,128)}, u32[]{:S(2)}, u32[]{:S(2)}) collective-permute-start(f32[7,48,128]{2,1,0:T(8,128)S(1)} %get-tuple-element.35.rest_0_), channel_id=1, source_target_pairs={{0,3},{1,2},{2,1},{3,0},{4,7},{5,6},{6,5},{7,4},{8,11},{9,10},{10,... | collective-permute-start | bytes 516104 | tf_op jit(solution)/shard_map/ppermute | solution.py:724
  72.9 1.0 copy-start.1
  73.9 0.6 copy-start.22
  74.6 0.6 copy-start.23
  75.2 11.8 %all-to-all-start.2 = ((f32[4,6,8,128]{3,2,1,0:T(8,128)}), f32[4,6,8,128]{3,2,1,0:T(8,128)S(1)}, u32[]{:S(2)}, u32[]{:S(2)}) async-start(f32[4,6,8,128]{3,2,1,0:T(8,128)} %copy-done.22), calls=%async_computation.2 | async-start | bytes 196608 | tf_op jit(solution)/shard_map/all_to_all | solution.py:683
  82.4 0.7 copy-start.16
  83.1 0.7 copy-start.18
  87.0 0.6 copy-start.4
  87.6 1.3 copy-start.2
  88.9 0.9 copy-start.5
  89.8 1.0 copy-start.7
  90.7 1.0 copy-start.9
  91.7 0.9 copy-start.15
  92.6 0.9 copy-start.17
  93.5 0.9 copy-start.19
  94.5 0.8 copy-start.24
  95.3 0.7 copy-start.30
  98.2 0.7 copy-start.10
  98.9 0.6 copy-start.25
  99.5 0.6 copy-start.27
  100.2 0.6 copy-start.31
  103.8 23.6 %all-to-all-start.3 = ((f32[32,1,7]{2,1,0:T(1,128)}), f32[32,1,7]{2,1,0:T(1,128)S(1)}, u32[]{:S(2)}, u32[]{:S(2)}) async-start(f32[32,1,7]{2,1,0:T(1,128)} %bitcast.11), calls=%async_computation.3 | async-start | bytes 32768 | tf_op jit(solution)/shard_map/all_to_all | solution.py:794
  106.4 1.0 copy-start.11
  107.4 0.8 copy-start.13
  108.2 0.8 copy-start.21
  108.9 0.8 copy-start.26
  109.7 0.8 copy-start.28

commit v9 on v8

--- a/solution.py
+++ b/solution.py
@@ -430,10 +430,10 @@
 
 
 def close_kernel(
-    n_lon, rows, place, prm, x_ref, proj, px, dots, rx, ry, el, elc, esx, *rest
+    n_lon, rows, devices, capacity, cells, place, target, prm, x_ref, proj, px, dots, rx, ry, el, elc, esx, *rest
 ):
     sent = rest[:n_lon]
-    carry, full_ref, col_ref, side_ref, energy, esm = rest[n_lon:]
+    carry, full_ref, col_ref, side_ref, table, esm = rest[n_lon:]
     half = rx.shape[2]
     me = place[1]
     for d in range(n_lon):
@@ -465,6 +465,9 @@
     c2 = jnp.where(low, swap(e2 + k1 * c1 + span * d2), d2)
     c3 = jnp.where(low, d3, swap(e3 + k2 * c1 + k1 * c2 + span * d3))
     c4 = jnp.where(low, swap(e4 + k3 * c1 + k2 * c2 + k1 * c3 + span * d4), d4)
+    lane = lax.broadcasted_iota(jnp.int32, (devices, LANES), 1)
+    first_slot = lax.broadcasted_iota(jnp.int32, (devices, LANES), 0) * capacity
+    owned = jnp.zeros((devices, LANES), f32)
     for k, v in enumerate(ORDER):
         more = [c[k, rows:] for c in (c1, c2, c3, c4)]
         sums = jnp.zeros((rows, LANES), f32)
@@ -484,23 +487,37 @@
             return total
 
         total = lax.fori_loop(0, half // 8, body, dots[k])
-        energy[v] = total + jnp.sum(sums.reshape(rows // 8, 8, LANES), axis=0)
+        total = total + jnp.sum(sums.reshape(rows // 8, 8, LANES), axis=0)
+        total = jnp.sum(total, axis=0, keepdims=True)
+        total = (total + swap(total)) * prm[v, 3:4, :] * (1.0 / cells)
+        where = target[:, 64 * v : 64 * (v + 1)]
+        where = jnp.concatenate([where, where], axis=1) - first_slot
+        for s in range(capacity):
+            mine = jnp.where((lane < 64) & (where == s), total, 0.0)
+            owned = owned + jnp.where(lane == s, jnp.sum(mine, axis=1, keepdims=True), 0.0)
         if v == 0:
             for i, d in enumerate((d3, d4)):
                 y = d[k, :rows]
                 for e in range(4):
                     y = y + ry[k, e] * d[k, rows + e : rows + e + 1]
                 col_ref[i] = y
+    table[...] = owned
 
 
 def end_kernel(
     rows, pairs, rq, place, prm, sigma, north, south, vert, bal, col, side, carry, rx_ref, ry_ref, u_ref, x_ref,
-    out, xs, zx, zc, wt, sg, sx,
+    out_ref, out, xs, zx, zc, wt, sg, sx, sems,
 ):
     g = pl.program_id(0)
     half = 2 * pairs
     lon = sigma.shape[2]
     merged = out.shape[2]
+    steps = pairs // PAIRS
+
+    def copy(v, side_at, step):
+        first = pl.multiple_of((step * PAIRS + side_at * pairs) * LANES, LANES)
+        cols = pl.ds(first, PAIRS * LANES)
+        return pltpu.make_async_copy(out.at[v, :, cols], out_ref.at[v, :, cols], sems.at[v, side_at, step])
 
     @pl.when(g == 0)
     def _():
@@ -574,6 +591,9 @@
             out[0, :, at] = z[0]
             out[1, :, at] = z[1] + chi_row * z[0]
             out[2, :, at] = z[2]
+    for v in range(2):
+        for side_at in range(2):
+            copy(v, side_at, g).start()
 
     @pl.when(g == pl.num_programs(0) - 1)
     def _():
@@ -598,9 +618,15 @@
                     at = at_tile(b * PAIRS + p + side * pairs)
                     part = res[p * rows : (p + 1) * rows, side * LANES : (side + 1) * LANES]
                     out[2, :, at] = out[2, :, at] + part
+            for side_at in range(2):
+                copy(2, side_at, b).start()
             return 0
 
-        lax.fori_loop(0, pairs // PAIRS, body, 0)
+        lax.fori_loop(0, steps, body, 0)
+        for v in range(3):
+            for side_at in range(2):
+                for step in range(steps):
+                    copy(v, side_at, step).wait()
 
 
 def shards(state, sigma, vert, bal_temp, chi_coef, scales, classes, owner):
@@ -652,8 +678,8 @@
                 pl.BlockSpec((nv, 2 * BLOCK, 8, LANES), lambda g: (first, g, 0, 0)),
             ]
             + [full(s) for s in more],
-            out_shape=[pltpu.HBM(s, f32) for s in shapes[:2]]
-            + [jax.ShapeDtypeStruct(s, f32) for s in shapes[2:] + list(more)],
+            out_shape=[jax.ShapeDtypeStruct(s, f32) if n == 2 else pltpu.HBM(s, f32) for n, s in enumerate(shapes)]
+            + [pltpu.HBM(s, f32) for s in more],
             scratch_shapes=[
                 pltpu.VMEM((2, PAIRS * rows, 256), f32),
                 pltpu.VMEM((2 * 768, 256), bf16),
@@ -672,8 +698,8 @@
     ins = [in_hbm(x) for x in ins]
     body = functools.partial(lat_plain, rows, pairs)
     *wue, prm = lat_call(2, 0, body, ins, specs, "lat_chi_temp", {}, [(nvars, 4, LANES)])
-    ins = [prm, sigma, vert, bal_temp] + [in_hbm(state)] * 5 + [north, south, west, east]
-    ins += [in_hbm(wue[0]), in_hbm(wue[1]), wue[2], wue[3]]
+    ins = [in_hbm(x) for x in [prm, sigma, vert, bal_temp] + [state] * 5] + [north, south, west, east]
+    ins += [in_hbm(wue[0]), in_hbm(wue[1]), wue[2], in_hbm(wue[3])]
     specs = [full(x.shape) for x in ins[:4]] + [part(0, 0), part(0, 1), part(1, 0), part(1, 1)]
     specs += [pl.BlockSpec((1, rows, merged), lambda g: (2, 0, 0))]
     specs += [full(x.shape) for x in (north, south, west, east)] + [anywhere] * 4
@@ -705,19 +731,19 @@
         ],
         out_shape=[
             pltpu.HBM((nvars, half, rows, LANES), f32),
-            jax.ShapeDtypeStruct((nvars, 4, rows, LANES), f32),
+            pltpu.HBM((nvars, 4, rows, LANES), f32),
             jax.ShapeDtypeStruct((7, rows, LANES), f32),
-            jax.ShapeDtypeStruct((nvars, 4, rows, LANES), f32),
-            jax.ShapeDtypeStruct((nvars, 8, LANES), f32),
-            jax.ShapeDtypeStruct((nvars, 4, half, LANES), f32),
-            jax.ShapeDtypeStruct((nvars, 4, rows, LANES), f32),
+            pltpu.HBM((nvars, 4, rows, LANES), f32),
+            pltpu.HBM((nvars, 8, LANES), f32),
+            pltpu.HBM((nvars, 4, half, LANES), f32),
+            pltpu.HBM((nvars, 4, rows, LANES), f32),
         ],
         compiler_params=params(),
         cost_estimate=pl.CostEstimate(
             flops=180000000, bytes_accessed=6 * rows * merged * 4, transcendentals=0
         ),
         name="lon_tile",
-    )(prm, sigma, in_hbm(u), in_hbm(w))
+    )(*[in_hbm(x) for x in (prm, sigma, u, w)])
 
     def round_lon(x):
         return [x] + [
@@ -735,7 +761,7 @@
         compiler_params=params(),
         cost_estimate=pl.CostEstimate(flops=1000000, bytes_accessed=2 * shares.size * 4, transcendentals=0),
         name="solve",
-    )(prm, shares)
+    )(in_hbm(prm), shares)
     carries = trade(carries, "lat")
 
     crossed, elc, esc = pl.pallas_call(
@@ -744,8 +770,8 @@
         in_specs=[full(prm.shape), full(carries.shape)],
         out_specs=[full((nvars, half, 8, LANES)), full((nvars, 4, 8, LANES)), full((n_lon, 6, 8, LANES))],
         out_shape=[
-            jax.ShapeDtypeStruct((nvars, half, 8, LANES), f32),
-            jax.ShapeDtypeStruct((nvars, 4, 8, LANES), f32),
+            pltpu.HBM((nvars, half, 8, LANES), f32),
+            pltpu.HBM((nvars, 4, 8, LANES), f32),
             jax.ShapeDtypeStruct((n_lon, 6, 8, LANES), f32),
         ],
         compiler_params=params(),
@@ -753,7 +779,7 @@
             flops=30000000, bytes_accessed=4 * nvars * 12 * half * LANES, transcendentals=0
         ),
         name="lon_carry",
-    )(prm, carries)
+    )(in_hbm(prm), carries)
     sent_x = trade(esc, "lon")
 
     packed = 2 * PAIRS
@@ -761,40 +787,31 @@
     def columns(r):
         return pl.BlockSpec((nvars, packed, r, LANES), lambda g: (0, g, 0, 0))
 
-    ins = [place, prm, crossed, proj, px, dots, rx, ry, el, elc, sent_x] + sent
+    index = jnp.arange(count, dtype=jnp.int32)
+    same = (owner[:, None] == owner[None, :]) & (index[None, :] < index[:, None])
+    target = (owner * capacity + jnp.sum(same.astype(jnp.int32), axis=1)).reshape(1, count)
+
+    ins = [in_hbm(x) for x in (prm, crossed, proj, px, dots, rx, ry, el, elc)]
+    ins = [place, target] + ins + [sent_x] + sent
     specs = [full(x.shape) for x in ins]
     specs[0] = pl.BlockSpec(memory_space=pltpu.SMEM)
-    shapes = [
-        (nvars, 4, rows, LANES),
-        (nvars, half, 8, LANES),
-        (2, rows, LANES),
-        (2, rows, LANES),
-        (nvars, 8, LANES),
-    ]
-    carry, crossed, col, side, energy = pl.pallas_call(
-        functools.partial(close_kernel, n_lon, rows),
+    shapes = [(nvars, 4, rows, LANES), (nvars, half, 8, LANES), (2, rows, LANES), (2, rows, LANES)]
+    carry, crossed, col, side, table = pl.pallas_call(
+        functools.partial(close_kernel, n_lon, rows, devices, capacity, devices * rows * lon),
         grid=(1,),
         in_specs=specs,
-        out_specs=[full(x) for x in shapes],
-        out_shape=[jax.ShapeDtypeStruct(x, f32) for x in shapes],
+        out_specs=[full(x) for x in shapes] + [full((devices, LANES))],
+        out_shape=[pltpu.HBM(x, f32) for x in shapes] + [jax.ShapeDtypeStruct((devices, LANES), f32)],
         scratch_shapes=[pltpu.VMEM((n_lon, 7, rows, LANES), f32)],
         compiler_params=params(),
         cost_estimate=pl.CostEstimate(flops=10000000, bytes_accessed=4000000, transcendentals=0),
         name="close",
     )(*ins)
-
-    index = jnp.arange(count, dtype=jnp.int32)
-    same = (owner[:, None] == owner[None, :]) & (index[None, :] < index[:, None])
-    slot = jnp.sum(same.astype(jnp.int32), axis=1)
-    target = owner * capacity + slot
-    hit = target[:, None] == jnp.arange(devices * capacity)[None, :]
-    energy = jnp.sum(energy, axis=1) * prm[:, 3]
-    energy = (energy[:, :levels] + energy[:, levels:]).reshape(count)
-    table = jnp.sum(jnp.where(hit, energy[:, None], 0.0), axis=0).reshape(devices, capacity)
-    table = lax.all_to_all(table, ("lat", "lon"), split_axis=0, concat_axis=0, tiled=True)
-    slab_energy = (jnp.sum(table, axis=0) / (devices * rows * lon))[None, :]
-
-    ins = [place, prm, sigma, north, south, vert, bal_temp, col, side, carry, rx, ry, in_hbm(local), crossed]
+    table = trade(table, ("lat", "lon"))
+    slab_energy = jnp.sum(table, axis=0, keepdims=True)[:, :capacity]
+
+    ins = [prm, sigma, north, south, vert, bal_temp, col, side, carry, rx, ry, local, crossed]
+    ins = [place] + [in_hbm(x) for x in ins]
     specs = [full(x.shape) for x in ins]
     specs[0] = pl.BlockSpec(memory_space=pltpu.SMEM)
     specs[-2:] = [columns(rows), columns(8)]
@@ -802,15 +819,17 @@
         functools.partial(end_kernel, rows, pairs, 24),
         grid=(half // packed,),
         in_specs=specs,
-        out_specs=full(state.shape),
+        out_specs=anywhere,
         out_shape=jax.ShapeDtypeStruct(state.shape, f32),
         scratch_shapes=[
+            pltpu.VMEM(state.shape, f32),
             pltpu.VMEM((nvars, PAIRS * rows, 256), f32),
             pltpu.VMEM((8, merged), f32),
             pltpu.VMEM((2, rows, LANES), f32),
             pltpu.VMEM((4 * 768, 256), bf16),
             pltpu.VMEM((nvars, pieces, rows, LANES), f32),
             pltpu.VMEM((pieces, 8, LANES), f32),
+            pltpu.SemaphoreType.DMA((3, 2, pairs // PAIRS)),
         ],
         compiler_params=params(),
         cost_estimate=pl.CostEstimate(

time: 129 us -> 110 us (0.85)
  local copies, waits for them, and re-layouts: 25.4 us -> 2.75 us
  Pallas kernels: 56.3 us -> 60.2 us
  other arithmetic: 3.76 us -> 0.91 us
  waiting for transfers between devices: 8.22 us -> 10.7 us
    unnamed x66 -> x6, local copies, waits for them, and re-layouts: 21.3 us -> 0.01 us
    all_to_all x3 -> x4, starting transfers between devices: 16.4 us -> 19.5 us  [trade(): return lax.all_to_all(x, axis, split_axis=0, concat_axis=0, tiled=True)]
    pallas_call x1, Pallas kernels: 2.24 us -> 4.88 us  [shards(): pl.pallas_call(functools.partial(close_kernel, n_lon, rows, devices, capa...]
    all_to_all x1 -> x0, starting transfers between devices: 2.55 us -> none  [shards(): lax.all_to_all(table, ('lat', 'lon'), split_axis=0, concat_axis=0, tiled=...]
    all_to_all x3 -> x4, waiting for transfers between devices: 8.2 us -> 10.7 us  [trade(): return lax.all_to_all(x, axis, split_axis=0, concat_axis=0, tiled=True)]
    pallas_call x1, Pallas kernels: 1.58 us -> 3.07 us  [shards(): pl.pallas_call(carry_kernel, grid=(1,), in_specs=[full(prm.shape), full(c...]
    pallas_call x1, Pallas kernels: 16.9 us -> 15.6 us  [shards(): pl.pallas_call(functools.partial(end_kernel, rows, pairs, 24), grid=(half...]
  transfers between devices with their start and end apart: 11 -> 11, of which waited for: 2 -> 2; matrix products, arithmetic and copies ran while one was open for 2% -> 1% of each run, Pallas kernels for 33% -> 39%
where the time goes in v9:
time: 110 us; the launch traced here: 109 us
  Pallas kernels  60.2 us (55%)
  starting transfers between devices  34 us (31%)
  waiting for transfers between devices  10.7 us (10%)
  local copies, waits for them, and re-layouts  2.75 us (2%)
    pallas_call x2, Pallas kernels, lat_call(): pl.pallas_call(body, grid=(steps,), in_specs=specs, out_specs=[pl.BlockSp...  22.2 us
    all_to_all x4, starting transfers between devices, trade(): return lax.all_to_all(x, axis, split_axis=0, concat_axis=0, tiled=True)  19.5 us
    pallas_call x1, Pallas kernels, shards(): pl.pallas_call(functools.partial(end_kernel, rows, pairs, 24), grid=(half...  15.6 us
    pallas_call x1, Pallas kernels, shards(): pl.pallas_call(functools.partial(lon_kernel, rows, rb), grid=(rows // rb,...  12.7 us
    all_to_all x4, waiting for transfers between devices, trade(): return lax.all_to_all(x, axis, split_axis=0, concat_axis=0, tiled=True)  10.7 us
    ppermute x3, starting transfers between devices, round_lon(): lax.ppermute(x, 'lon', [(i, i ^ s) for i in range(n_lon)])  5.3 us
    pallas_call x1, Pallas kernels, shards(): pl.pallas_call(functools.partial(close_kernel, n_lon, rows, devices, capa...  4.88 us
    ppermute x1, starting transfers between devices, shards(): west = lax.ppermute(state[2, :, merged - levels:], 'lon', up_lon)  4.3 us
  transfers between devices with their start and end apart: 11, of which 2 were waited for; matrix products, arithmetic and copies ran while one was open for 1% of the time, Pallas kernels for 39%

profile of v9, /device:TPU:0, one launch (start us, length us, event | category | flops | bytes accessed | tf_op | source)
XLA Modules:
  0.0 109.4 jit_solution(13628674494101934388)
XLA Ops:
  0.6 1.2 %slice_bitcast_fusion = (f32[1,12288]{1,0:T(1,128)S(1)}, f32[1,12288]{1,0:T(1,128)S(1)}) fusion(f32[3,48,12288]{2,1,0:T(8,128)} %temp.1), kind=kLoop, calls=%fused_computation.5 | loop fusion | bytes 196608 | tf_op jit(solution)/shard_map/squeeze | solution.py:651
  1.8 0.7 slice_bitcast_fusion.4
  2.6 2.4 %collective-permute-start = (f32[1,12480]{1,0:T(1,128)S(1)}, f32[1,12480]{1,0:T(1,128)S(1)}, u32[]{:S(2)}, u32[]{:S(2)}) collective-permute-start(f32[1,12480]{1,0:T(1,128)S(1)} %pad_maximum_fusion), channel_id=1, source_target_pairs={{0,4},{4,8},{8,12},{12,16},{16,20},{20,24},{24,28},{1,5},{5,9},{9,... | collective-permute-start | bytes 149768 | tf_op jit(solution)/shard_map/ppermute | solution.py:653
  5.0 1.3 %collective-permute-start.1 = (f32[1,12480]{1,0:T(1,128)S(1)}, f32[1,12480]{1,0:T(1,128)S(1)}, u32[]{:S(2)}, u32[]{:S(2)}) collective-permute-start(f32[1,12480]{1,0:T(1,128)S(1)} %pad_maximum_fusion.1), channel_id=1, source_target_pairs={{4,0},{8,4},{12,8},{16,12},{20,16},{24,20},{28,24},{5,1},{9,5},{13... | collective-permute-start | bytes 149768 | tf_op jit(solution)/shard_map/ppermute | solution.py:654
  6.3 0.8 slice_bitcast_fusion.2
  7.1 4.3 %collective-permute-start.2 = (f32[48,64]{1,0:T(8,128)S(1)}, f32[48,64]{1,0:T(8,128)S(1)}, u32[]{:S(2)}, u32[]{:S(2)}) collective-permute-start(f32[48,64]{1,0:T(8,128)S(1)} %get-tuple-element.53), channel_id=1, source_target_pairs={{0,1},{1,2},{2,3},{4,5},{5,6},{6,7},{8,9},{9,10},{10,11},{12,13},{... | collective-permute-start | bytes 36872 | tf_op jit(solution)/shard_map/ppermute | solution.py:655
  11.5 1.3 %collective-permute-start.3 = (f32[48,64]{1,0:T(8,128)S(1)}, f32[48,64]{1,0:T(8,128)S(1)}, u32[]{:S(2)}, u32[]{:S(2)}) collective-permute-start(f32[48,64]{1,0:T(8,128)S(1)} %get-tuple-element.52), channel_id=1, source_target_pairs={{1,0},{2,1},{3,2},{5,4},{6,5},{7,6},{9,8},{10,9},{11,10},{13,12},{... | collective-permute-start | bytes 36872 | tf_op jit(solution)/shard_map/ppermute | solution.py:656
  12.8 11.3 %lat_chi_temp.1 = (f32[3,96,48,128]{3,2,1,0:T(8,128)}, f32[3,48,96,128]{3,2,1,0:T(8,128)}, f32[8,3,48,128]{3,2,1,0:T(8,128)}, f32[3,96,8,128]{3,2,1,0:T(8,128)}, f32[3,4,128]{2,1,0:T(4,128)}) custom-call(f32[1,8]{1,0:T(1,128)} %bitcast.26, s32[1,192]{1,0:T(1,128)} %bitcast.24, f32[1,64]{1,0:T(1,128)} %bitcast.27, f32[3,48,192]{2,1,0:T(8,128)} %sigma.7, ...), custom_call_target="tpu_custom_call" | custom-call | flops 120000000 | bytes 14155776 | tf_op jit(solution)/shard_map/lat_chi_temp/pallas_call | solution.py:670
  24.1 0.0 collective-permute-done.2.west
  24.1 0.0 collective-permute-done.3.east
  24.1 0.0 collective-permute-done.north
  24.1 0.0 copy-start
  24.1 0.0 collective-permute-done.1.south
  24.2 0.0 copy-start.1
  24.2 10.9 %lat_psi.1 = (f32[3,96,48,128]{3,2,1,0:T(8,128)}, f32[3,48,96,128]{3,2,1,0:T(8,128)}, f32[8,3,48,128]{3,2,1,0:T(8,128)}, f32[3,96,8,128]{3,2,1,0:T(8,128)}) custom-call(f32[3,4,128]{2,1,0:T(4,128)} %get-tuple-element.27.prm, f32[3,48,192]{2,1,0:T(8,128)} %sigma.7, ...), custom_call_target="tpu_custom_call", output_to_operand_aliasing={{0}: (13, {}), {1}: (14, {}), {2}: (15, {}), {3}: (16, {})} | custom-call | flops 60000000 | bytes 7077888 | tf_op jit(solution)/shard_map/lat_psi/pallas_call | solution.py:670
  35.1 0.0 copy-done
  35.1 0.0 copy-done.1
  35.1 6.3 %all-to-all-start = ((f32[8,3,48,128]{3,2,1,0:T(8,128)}), f32[8,3,48,128]{3,2,1,0:T(8,128)S(1)}, u32[]{:S(2)}, u32[]{:S(2)}) async-start(f32[8,3,48,128]{3,2,1,0:T(8,128)} %get-tuple-element.32), calls=%async_computation | async-start | bytes 1179648 | tf_op jit(solution)/shard_map/all_to_all | solution.py:709
  41.3 0.0 copy-start.2
  41.3 12.7 %lon_tile.1 = (f32[3,96,48,128]{3,2,1,0:T(8,128)}, f32[3,4,48,128]{3,2,1,0:T(8,128)}, f32[7,48,128]{2,1,0:T(8,128)S(1)}, f32[3,4,48,128]{3,2,1,0:T(8,128)}, f32[...) custom-call(f32[3,4,128]{2,1,0:T(4,128)} %get-tuple-element.27.prm, f32[3,48,192]{2,1,0:T(8,128)} %sigma.7, ...), custom_call_target="tpu_custom_call" | custom-call | flops 180000000 | bytes 14155776 | tf_op jit(solution)/shard_map/lon_tile/pallas_call | solution.py:714
  54.1 0.0 all-to-all-done.edges
  54.1 1.7 %solve.1 = f32[8,3,48,128]{3,2,1,0:T(8,128)} custom-call(f32[3,4,128]{2,1,0:T(4,128)} %get-tuple-element.27.prm, f32[8,3,48,128]{3,2,1,0:T(8,128)S(1)} %all-to-all-done.edges), custom_call_target="tpu_custom_call" | custom-call | flops 1000000 | bytes 1179648 | tf_op jit(solution)/shard_map/solve/pallas_call | solution.py:755
  55.7 4.2 %all-to-all-start.1 = ((f32[8,3,48,128]{3,2,1,0:T(8,128)}), f32[8,3,48,128]{3,2,1,0:T(8,128)S(1)}, u32[]{:S(2)}, u32[]{:S(2)}) async-start(f32[8,3,48,128]{3,2,1,0:T(8,128)} %solve.1), calls=%async_computation.1 | async-start | bytes 1179648 | tf_op jit(solution)/shard_map/all_to_all | solution.py:709
  59.9 0.0 copy-done.2
  59.9 0.2 convert_reduce_fusion
  60.1 2.7 %collective-permute-start.4 = (f32[7,48,128]{2,1,0:T(8,128)S(1)}, f32[7,48,128]{2,1,0:T(8,128)S(1)}, u32[]{:S(2)}, u32[]{:S(2)}) collective-permute-start(f32[7,48,128]{2,1,0:T(8,128)S(1)} %get-tuple-element.35.rest_0_), channel_id=1, source_target_pairs={{0,1},{1,0},{2,3},{3,2},{4,5},{5,4},{6,7},{7,6},{8,9},{9,8},{10,11... | collective-permute-start | bytes 516104 | tf_op jit(solution)/shard_map/ppermute | solution.py:750
  62.8 2.6 %collective-permute-start.5 = (f32[7,48,128]{2,1,0:T(8,128)S(1)}, f32[7,48,128]{2,1,0:T(8,128)S(1)}, u32[]{:S(2)}, u32[]{:S(2)}) collective-permute-start(f32[7,48,128]{2,1,0:T(8,128)S(1)} %get-tuple-element.35.rest_0_), channel_id=1, source_target_pairs={{0,2},{1,3},{2,0},{3,1},{4,6},{5,7},{6,4},{7,5},{8,10},{9,11},{10,... | collective-permute-start | bytes 516104 | tf_op jit(solution)/shard_map/ppermute | solution.py:750
  65.4 0.0 collective-permute-start.6
  65.4 5.0 %all-to-all-done.1.carries = f32[8,3,48,128]{3,2,1,0:T(8,128)S(1)} async-done(((f32[8,3,48,128]{3,2,1,0:T(8,128)}), f32[8,3,48,128]{3,2,1,0:T(8,128)S(1)}, u32[]{:S(2)}, u32[]{:S(2)}) %all-to-all-start.1) | async-done | bytes 589856 | tf_op jit(solution)/shard_map/all_to_all | solution.py:709
  70.4 3.1 %lon_carry.1 = (f32[3,96,8,128]{3,2,1,0:T(8,128)}, f32[3,4,8,128]{3,2,1,0:T(8,128)}, f32[4,6,8,128]{3,2,1,0:T(8,128)}) custom-call(f32[3,4,128]{2,1,0:T(4,128)} %get-tuple-element.27.prm, f32[8,3,48,128]{3,2,1,0:T(8,128)S(1)} %all-to-all-done.1.carries), custom_call_target="tpu_custom_call" | custom-call | flops 30000000 | bytes 1769472 | tf_op jit(solution)/shard_map/lon_carry/pallas_call | solution.py:767
  73.5 5.9 %all-to-all-start.2 = ((f32[4,6,8,128]{3,2,1,0:T(8,128)}), f32[4,6,8,128]{3,2,1,0:T(8,128)S(1)}, u32[]{:S(2)}, u32[]{:S(2)}) async-start(f32[4,6,8,128]{3,2,1,0:T(8,128)} %get-tuple-element.45), calls=%async_computation.2 | async-start | bytes 196608 | tf_op jit(solution)/shard_map/all_to_all | solution.py:709
  79.4 0.1 pad_add_fusion.place
  79.5 0.0 collective-permute-done.4.rest_1_
  79.5 0.0 collective-permute-done.5.rest_2_
  79.5 0.0 collective-permute-done.6.rest_3_
  79.5 5.7 %all-to-all-done.2.esx = f32[4,6,8,128]{3,2,1,0:T(8,128)S(1)} async-done(((f32[4,6,8,128]{3,2,1,0:T(8,128)}), f32[4,6,8,128]{3,2,1,0:T(8,128)S(1)}, u32[]{:S(2)}, u32[]{:S(2)}) %all-to-all-start.2) | async-done | bytes 98336 | tf_op jit(solution)/shard_map/all_to_all | solution.py:709
  85.2 4.9 %close.1 = (f32[3,4,48,128]{3,2,1,0:T(8,128)}, f32[3,96,8,128]{3,2,1,0:T(8,128)}, f32[2,48,128]{2,1,0:T(8,128)}, f32[2,48,128]{2,1,0:T(8,128)}, f32[32,128]{1,0:T(8,128)}) custom-call(s32[2]{0:T(128)S(1)} %pad_add_fusion.place, s32[1,192]{1,0:T(1,128)S(1)} %bitcast.23, f32[3,4,128]{2,1,0:T(4,128)} %get-tuple-element.27.prm, ...), custom_call_target="tpu_custom_call" | custom-call | flops 10000000 | bytes 4000000 | tf_op jit(solution)/shard_map/close/pallas_call | solution.py:799
  90.1 3.1 %all-to-all-start.3 = ((f32[32,1,128]{2,1,0:T(1,128)}), f32[32,1,128]{2,1,0:T(1,128)S(1)}, u32[]{:S(2)}, u32[]{:S(2)}) async-start(f32[32,1,128]{2,1,0:T(1,128)} %bitcast.13), calls=%async_computation.3 | async-start | bytes 32768 | tf_op jit(solution)/shard_map/all_to_all | solution.py:709
  93.2 15.6 %finish.1 = f32[3,48,12288]{2,1,0:T(8,128)} custom-call(s32[2]{0:T(128)S(1)} %pad_add_fusion.place, f32[3,4,128]{2,1,0:T(4,128)} %get-tuple-element.27.prm, f32[3,48,192]{2,1,0:T(8,128)} %sigma.7, f32[1,12480]{1,0:T(1,128)} %copy-done, f32[1,12480]{1,0:T(1,128)} %copy-done.1, f32[3,64,64]{2,1,0:T(8,128)} %vert.5, f32[64,64]{1,0:T(8,128)} %bal.3, ...), custom_call_target="tpu_custom_call" | custom-call | flops 300000000 | bytes 14155776 | tf_op jit(solution)/shard_map/finish/pallas_call | solution.py:818
  108.8 0.0 all-to-all-done.3
  108.8 0.6 reduce_sum.19
  (3 shorter events, 0.1 us)
Async XLA Ops:
  2.6 21.5 %collective-permute-start = (f32[1,12480]{1,0:T(1,128)S(1)}, f32[1,12480]{1,0:T(1,128)S(1)}, u32[]{:S(2)}, u32[]{:S(2)}) collective-permute-start(f32[1,12480]{1,0:T(1,128)S(1)} %pad_maximum_fusion), channel_id=1, source_target_pairs={{0,4},{4,8},{8,12},{12,16},{16,20},{20,24},{24,28},{1,5},{5,9},{9,... | collective-permute-start | bytes 149768 | tf_op jit(solution)/shard_map/ppermute | solution.py:653
  5.0 19.1 %collective-permute-start.1 = (f32[1,12480]{1,0:T(1,128)S(1)}, f32[1,12480]{1,0:T(1,128)S(1)}, u32[]{:S(2)}, u32[]{:S(2)}) collective-permute-start(f32[1,12480]{1,0:T(1,128)S(1)} %pad_maximum_fusion.1), channel_id=1, source_target_pairs={{4,0},{8,4},{12,8},{16,12},{20,16},{24,20},{28,24},{5,1},{9,5},{13... | collective-permute-start | bytes 149768 | tf_op jit(solution)/shard_map/ppermute | solution.py:654
  7.1 17.0 %collective-permute-start.2 = (f32[48,64]{1,0:T(8,128)S(1)}, f32[48,64]{1,0:T(8,128)S(1)}, u32[]{:S(2)}, u32[]{:S(2)}) collective-permute-start(f32[48,64]{1,0:T(8,128)S(1)} %get-tuple-element.53), channel_id=1, source_target_pairs={{0,1},{1,2},{2,3},{4,5},{5,6},{6,7},{8,9},{9,10},{10,11},{12,13},{... | collective-permute-start | bytes 36872 | tf_op jit(solution)/shard_map/ppermute | solution.py:655
  11.5 12.7 %collective-permute-start.3 = (f32[48,64]{1,0:T(8,128)S(1)}, f32[48,64]{1,0:T(8,128)S(1)}, u32[]{:S(2)}, u32[]{:S(2)}) collective-permute-start(f32[48,64]{1,0:T(8,128)S(1)} %get-tuple-element.52), channel_id=1, source_target_pairs={{1,0},{2,1},{3,2},{5,4},{6,5},{7,6},{9,8},{10,9},{11,10},{13,12},{... | collective-permute-start | bytes 36872 | tf_op jit(solution)/shard_map/ppermute | solution.py:656
  24.1 10.9 %copy-start = (f32[1,12480]{1,0:T(1,128)}, f32[1,12480]{1,0:T(1,128)S(1)}, u32[]{:S(2)}) copy-start(f32[1,12480]{1,0:T(1,128)S(1)} %collective-permute-done.north) | copy-start | bytes 149764
  24.2 10.9 %copy-start.1 = (f32[1,12480]{1,0:T(1,128)}, f32[1,12480]{1,0:T(1,128)S(1)}, u32[]{:S(2)}) copy-start(f32[1,12480]{1,0:T(1,128)S(1)} %collective-permute-done.1.south) | copy-start | bytes 149764
  35.1 19.0 %all-to-all-start = ((f32[8,3,48,128]{3,2,1,0:T(8,128)}), f32[8,3,48,128]{3,2,1,0:T(8,128)S(1)}, u32[]{:S(2)}, u32[]{:S(2)}) async-start(f32[8,3,48,128]{3,2,1,0:T(8,128)} %get-tuple-element.32), calls=%async_computation | async-start | bytes 1179648 | tf_op jit(solution)/shard_map/all_to_all | solution.py:709
  41.3 18.6 %copy-start.2 = (s32[192]{0:T(256)S(1)}, s32[192]{0:T(256)}, u32[]{:S(2)}) copy-start(s32[192]{0:T(256)} %param.15) | copy-start | bytes 2308
  55.7 14.6 %all-to-all-start.1 = ((f32[8,3,48,128]{3,2,1,0:T(8,128)}), f32[8,3,48,128]{3,2,1,0:T(8,128)S(1)}, u32[]{:S(2)}, u32[]{:S(2)}) async-start(f32[8,3,48,128]{3,2,1,0:T(8,128)} %solve.1), calls=%async_computation.1 | async-start | bytes 1179648 | tf_op jit(solution)/shard_map/all_to_all | solution.py:709
  60.1 19.4 %collective-permute-start.4 = (f32[7,48,128]{2,1,0:T(8,128)S(1)}, f32[7,48,128]{2,1,0:T(8,128)S(1)}, u32[]{:S(2)}, u32[]{:S(2)}) collective-permute-start(f32[7,48,128]{2,1,0:T(8,128)S(1)} %get-tuple-element.35.rest_0_), channel_id=1, source_target_pairs={{0,1},{1,0},{2,3},{3,2},{4,5},{5,4},{6,7},{7,6},{8,9},{9,8},{10,11... | collective-permute-start | bytes 516104 | tf_op jit(solution)/shard_map/ppermute | solution.py:750
  62.8 16.6 %collective-permute-start.5 = (f32[7,48,128]{2,1,0:T(8,128)S(1)}, f32[7,48,128]{2,1,0:T(8,128)S(1)}, u32[]{:S(2)}, u32[]{:S(2)}) collective-permute-start(f32[7,48,128]{2,1,0:T(8,128)S(1)} %get-tuple-element.35.rest_0_), channel_id=1, source_target_pairs={{0,2},{1,3},{2,0},{3,1},{4,6},{5,7},{6,4},{7,5},{8,10},{9,11},{10,... | collective-permute-start | bytes 516104 | tf_op jit(solution)/shard_map/ppermute | solution.py:750
  65.4 14.1 %collective-permute-start.6 = (f32[7,48,128]{2,1,0:T(8,128)S(1)}, f32[7,48,128]{2,1,0:T(8,128)S(1)}, u32[]{:S(2)}, u32[]{:S(2)}) collective-permute-start(f32[7,48,128]{2,1,0:T(8,128)S(1)} %get-tuple-element.35.rest_0_), channel_id=1, source_target_pairs={{0,3},{1,2},{2,1},{3,0},{4,7},{5,6},{6,5},{7,4},{8,11},{9,10},{10,... | collective-permute-start | bytes 516104 | tf_op jit(solution)/shard_map/ppermute | solution.py:750
  73.5 11.8 %all-to-all-start.2 = ((f32[4,6,8,128]{3,2,1,0:T(8,128)}), f32[4,6,8,128]{3,2,1,0:T(8,128)S(1)}, u32[]{:S(2)}, u32[]{:S(2)}) async-start(f32[4,6,8,128]{3,2,1,0:T(8,128)} %get-tuple-element.45), calls=%async_computation.2 | async-start | bytes 196608 | tf_op jit(solution)/shard_map/all_to_all | solution.py:709
  90.1 18.7 %all-to-all-start.3 = ((f32[32,1,128]{2,1,0:T(1,128)}), f32[32,1,128]{2,1,0:T(1,128)S(1)}, u32[]{:S(2)}, u32[]{:S(2)}) async-start(f32[32,1,128]{2,1,0:T(1,128)} %bitcast.13), calls=%async_computation.3 | async-start | bytes 32768 | tf_op jit(solution)/shard_map/all_to_all | solution.py:709

commit v10 on v9

--- a/solution.py
+++ b/solution.py
@@ -176,6 +176,14 @@
     return weights[768 * k : 768 * (k + 1)]
 
 
+def store_start(w_ref, w_hbm, first, sem):
+    nv, count = w_ref.shape[:2]
+    at = pl.ds(pl.multiple_of(pl.program_id(0) * count, 8), count)
+    copy = pltpu.make_async_copy(w_ref, w_hbm.at[first : first + nv, at], sem)
+    copy.start()
+    return copy
+
+
 def lat_filter(vs, rows, prm, u_ref, e_ref, p_ref):
     nv = len(vs)
     decay = [prm[v, 1:2, :] for v in vs]
@@ -231,7 +239,7 @@
 
 def lat_plain(
     rows, pairs, scales, classes, chi_coef, sigma, vert, b1lo, b1hi, b2lo, b2hi,
-    w_ref, u_ref, e_ref, p_ref, prm, xs, wt, sg,
+    w_hbm, u_ref, e_ref, p_ref, prm, xs, wt, sg, w_ref, sem,
 ):
     g = pl.program_id(0)
 
@@ -259,12 +267,14 @@
         return 0
 
     lax.fori_loop(0, BLOCK // PAIRS, body, 0)
+    copy = store_start(w_ref, w_hbm, 0, sem)
     lat_filter((1, 2), rows, prm, u_ref, e_ref, p_ref)
+    copy.wait()
 
 
 def lat_balance(
     rows, pairs, prm, sigma, vert, bal, plo, phi, clo, chi, temp, north, south, west, east, w_in, u_in, e_in, p_in,
-    w_ref, u_ref, e_ref, p_ref, xs, wt, sg,
+    w_hbm, u_ref, e_ref, p_ref, xs, wt, sg, w_ref, sem,
 ):
     del w_in, u_in, e_in, p_in
     g = pl.program_id(0)
@@ -310,7 +320,9 @@
         return 0
 
     lax.fori_loop(0, BLOCK // PAIRS, body, 0)
+    copy = store_start(w_ref, w_hbm, 2, sem)
     lat_filter((0,), rows, prm, u_ref, e_ref, p_ref)
+    copy.wait()
 
 
 def lon_filter(prm, rb, o_ref, el_ref, put, at):
@@ -347,9 +359,14 @@
             el_ref[k, e, at, :] = x
 
 
-def lon_kernel(rows, rb, prm, sigma, u_ref, w_ref, o_ref, el_ref, es_ref, px_ref, dot_ref, rx_ref, ry_ref):
+def lon_kernel(
+    rows, rb, prm, sigma, u_ref, w_hbm, o_hbm, el_ref, es_ref, px_ref, dot_ref, rx_ref, ry_ref, w_ref, o_ref, sems
+):
     g = pl.program_id(0)
     half = u_ref.shape[2]
+    at = pl.ds(pl.multiple_of(g * rb, 8), rb)
+    load_w = pltpu.make_async_copy(w_hbm.at[:, :, at, :], w_ref, sems.at[0])
+    load_w.start()
 
     @pl.when(g == 0)
     def _():
@@ -371,12 +388,14 @@
         return 0
 
     lax.fori_loop(0, half // 8, turn, 0)
-    at = pl.ds(pl.multiple_of(g * rb, 8), rb)
 
     def put(i, x):
         es_ref[i, at, :] = x
 
     lon_filter(prm, rb, o_ref, el_ref, put, at)
+    store_o = pltpu.make_async_copy(o_ref, o_hbm.at[:, :, at, :], sems.at[1])
+    store_o.start()
+    load_w.wait()
     zero = jnp.zeros((rb, LANES), f32)
     for k in range(len(ORDER)):
 
@@ -395,6 +414,7 @@
         for e in range(4):
             px_ref[k, e, at, :] = sums[e]
         dot_ref[k] += jnp.sum(sums[4].reshape(rb // 8, 8, LANES), axis=0)
+    store_o.wait()
 
 
 def solve_kernel(n_lat, rows, prm, edges, carries):
@@ -423,21 +443,21 @@
     lax.fori_loop(0, carries.shape[0], body, 0)
 
     def put(i, x):
-        for t in range(es_ref.shape[0]):
-            es_ref[t, i] = x
+        es_ref[i] = x
 
     lon_filter(prm, 8, o_ref, el_ref, put, slice(0, 8))
 
 
 def close_kernel(
-    n_lon, rows, devices, capacity, cells, place, target, prm, x_ref, proj, px, dots, rx, ry, el, elc, esx, *rest
+    n_lon, rows, devices, capacity, cells, place, target, prm, x_ref, proj, px, dots, rx, ry, el, elc, *rest
 ):
-    sent = rest[:n_lon]
-    carry, full_ref, col_ref, side_ref, table, esm = rest[n_lon:]
+    sent, sent_x = rest[:n_lon], rest[n_lon : 2 * n_lon]
+    carry, full_ref, col_ref, side_ref, table, esm, esx = rest[2 * n_lon :]
     half = rx.shape[2]
     me = place[1]
     for d in range(n_lon):
         esm[me ^ d] = sent[d][...]
+        esx[me ^ d] = sent_x[d][...]
     side_ref[0] = esm[jnp.maximum(me - 1, 0), 6]
     side_ref[1] = esm[jnp.minimum(me + 1, n_lon - 1), 6]
     length = jnp.stack([prm[v, 0:1, :] for v in ORDER])
@@ -672,18 +692,20 @@
             grid=(steps,),
             in_specs=specs,
             out_specs=[
-                pl.BlockSpec((nv, 2 * BLOCK, rows, LANES), lambda g: (first, g, 0, 0)),
+                anywhere,
                 pl.BlockSpec((nv, rows, 2 * BLOCK, LANES), lambda g: (first, 0, g, 0)),
                 pl.BlockSpec((2 * BLOCK // width, nv, 4 * width, LANES), lambda g: (g, first, 0, 0)),
                 pl.BlockSpec((nv, 2 * BLOCK, 8, LANES), lambda g: (first, g, 0, 0)),
             ]
             + [full(s) for s in more],
             out_shape=[jax.ShapeDtypeStruct(s, f32) if n == 2 else pltpu.HBM(s, f32) for n, s in enumerate(shapes)]
-            + [pltpu.HBM(s, f32) for s in more],
+            + [jax.ShapeDtypeStruct(s, f32) for s in more],
             scratch_shapes=[
                 pltpu.VMEM((2, PAIRS * rows, 256), f32),
                 pltpu.VMEM((2 * 768, 256), bf16),
                 pltpu.VMEM((nvars, pieces, rows, LANES), f32),
+                pltpu.VMEM((nv, 2 * BLOCK, rows, LANES), f32),
+                pltpu.SemaphoreType.DMA(()),
             ],
             compiler_params=params(),
             cost_estimate=pl.CostEstimate(
@@ -698,7 +720,7 @@
     ins = [in_hbm(x) for x in ins]
     body = functools.partial(lat_plain, rows, pairs)
     *wue, prm = lat_call(2, 0, body, ins, specs, "lat_chi_temp", {}, [(nvars, 4, LANES)])
-    ins = [in_hbm(x) for x in [prm, sigma, vert, bal_temp] + [state] * 5] + [north, south, west, east]
+    ins = [prm] + [in_hbm(x) for x in [sigma, vert, bal_temp] + [state] * 5] + [north, south, west, east]
     ins += [in_hbm(wue[0]), in_hbm(wue[1]), wue[2], in_hbm(wue[3])]
     specs = [full(x.shape) for x in ins[:4]] + [part(0, 0), part(0, 1), part(1, 0), part(1, 1)]
     specs += [pl.BlockSpec((1, rows, merged), lambda g: (2, 0, 0))]
@@ -718,10 +740,10 @@
             full(prm.shape),
             pl.BlockSpec((1, rows, lon), lambda g: (0, 0, 0)),
             pl.BlockSpec((nvars, rb, half, LANES), lambda g: (0, g, 0, 0)),
-            pl.BlockSpec((nvars, half, rb, LANES), lambda g: (0, 0, g, 0)),
+            anywhere,
         ],
         out_specs=[
-            pl.BlockSpec((nvars, half, rb, LANES), lambda g: (0, 0, g, 0)),
+            anywhere,
             full((nvars, 4, rows, LANES)),
             full((7, rows, LANES)),
             full((nvars, 4, rows, LANES)),
@@ -738,12 +760,13 @@
             pltpu.HBM((nvars, 4, half, LANES), f32),
             pltpu.HBM((nvars, 4, rows, LANES), f32),
         ],
+        scratch_shapes=[pltpu.VMEM((nvars, half, rb, LANES), f32)] * 2 + [pltpu.SemaphoreType.DMA((2,))],
         compiler_params=params(),
         cost_estimate=pl.CostEstimate(
             flops=180000000, bytes_accessed=6 * rows * merged * 4, transcendentals=0
         ),
         name="lon_tile",
-    )(*[in_hbm(x) for x in (prm, sigma, u, w)])
+    )(prm, *[in_hbm(x) for x in (sigma, u, w)])
 
     def round_lon(x):
         return [x] + [
@@ -761,26 +784,26 @@
         compiler_params=params(),
         cost_estimate=pl.CostEstimate(flops=1000000, bytes_accessed=2 * shares.size * 4, transcendentals=0),
         name="solve",
-    )(in_hbm(prm), shares)
+    )(prm, shares)
     carries = trade(carries, "lat")
 
     crossed, elc, esc = pl.pallas_call(
         carry_kernel,
         grid=(1,),
         in_specs=[full(prm.shape), full(carries.shape)],
-        out_specs=[full((nvars, half, 8, LANES)), full((nvars, 4, 8, LANES)), full((n_lon, 6, 8, LANES))],
+        out_specs=[full((nvars, half, 8, LANES)), full((nvars, 4, 8, LANES)), full((6, 8, LANES))],
         out_shape=[
-            pltpu.HBM((nvars, half, 8, LANES), f32),
-            pltpu.HBM((nvars, 4, 8, LANES), f32),
-            jax.ShapeDtypeStruct((n_lon, 6, 8, LANES), f32),
+            jax.ShapeDtypeStruct((nvars, half, 8, LANES), f32),
+            jax.ShapeDtypeStruct((nvars, 4, 8, LANES), f32),
+            jax.ShapeDtypeStruct((6, 8, LANES), f32),
         ],
         compiler_params=params(),
         cost_estimate=pl.CostEstimate(
             flops=30000000, bytes_accessed=4 * nvars * 12 * half * LANES, transcendentals=0
         ),
         name="lon_carry",
-    )(in_hbm(prm), carries)
-    sent_x = trade(esc, "lon")
+    )(prm, carries)
+    sent_x = round_lon(esc)
 
     packed = 2 * PAIRS
 
@@ -791,8 +814,8 @@
     same = (owner[:, None] == owner[None, :]) & (index[None, :] < index[:, None])
     target = (owner * capacity + jnp.sum(same.astype(jnp.int32), axis=1)).reshape(1, count)
 
-    ins = [in_hbm(x) for x in (prm, crossed, proj, px, dots, rx, ry, el, elc)]
-    ins = [place, target] + ins + [sent_x] + sent
+    ins = [in_hbm(x) for x in (proj, px, dots, rx, ry, el)]
+    ins = [place, target, prm, crossed] + ins + [elc] + sent + sent_x
     specs = [full(x.shape) for x in ins]
     specs[0] = pl.BlockSpec(memory_space=pltpu.SMEM)
     shapes = [(nvars, 4, rows, LANES), (nvars, half, 8, LANES), (2, rows, LANES), (2, rows, LANES)]
@@ -802,7 +825,7 @@
         in_specs=specs,
         out_specs=[full(x) for x in shapes] + [full((devices, LANES))],
         out_shape=[pltpu.HBM(x, f32) for x in shapes] + [jax.ShapeDtypeStruct((devices, LANES), f32)],
-        scratch_shapes=[pltpu.VMEM((n_lon, 7, rows, LANES), f32)],
+        scratch_shapes=[pltpu.VMEM((n_lon, 7, rows, LANES), f32), pltpu.VMEM((n_lon, 6, 8, LANES), f32)],
         compiler_params=params(),
         cost_estimate=pl.CostEstimate(flops=10000000, bytes_accessed=4000000, transcendentals=0),
         name="close",

time: 110 us -> 108 us (0.982)
  Pallas kernels: 60.2 us -> 56.7 us
  starting transfers between devices: 34 us -> 35.1 us
    ppermute x3 -> x6, waiting for transfers between devices: 0.01 us -> 5.91 us  [round_lon(): lax.ppermute(x, 'lon', [(i, i ^ s) for i in range(n_lon)])]
    all_to_all x4 -> x3, waiting for transfers between devices: 10.7 us -> 4.95 us  [trade(): return lax.all_to_all(x, axis, split_axis=0, concat_axis=0, tiled=True)]
    ppermute x3 -> x6, starting transfers between devices: 5.3 us -> 10.5 us  [round_lon(): lax.ppermute(x, 'lon', [(i, i ^ s) for i in range(n_lon)])]
    all_to_all x4 -> x3, starting transfers between devices: 19.5 us -> 15.3 us  [trade(): return lax.all_to_all(x, axis, split_axis=0, concat_axis=0, tiled=True)]
    pallas_call x1, Pallas kernels: 12.7 us -> 11 us  [shards(): pl.pallas_call(functools.partial(lon_kernel, rows, rb), grid=(rows // rb,...]
    pallas_call x1, Pallas kernels: 3.07 us -> 1.58 us  [shards(): pl.pallas_call(carry_kernel, grid=(1,), in_specs=[full(prm.shape), full(c...]
  transfers between devices with their start and end apart: 11 -> 13, of which waited for: 2 -> 3; matrix products, arithmetic and copies ran while one was open for 1% -> 1% of each run, Pallas kernels for 39% -> 37%
where the time goes in v10:
time: 108 us; the launch traced here: 107 us
  Pallas kernels  56.7 us (52%)
  starting transfers between devices  35.1 us (32%)
  waiting for transfers between devices  10.9 us (10%)
  local copies, waits for them, and re-layouts  2.76 us (3%)
    pallas_call x2, Pallas kernels, lat_call(): pl.pallas_call(body, grid=(steps,), in_specs=specs, out_specs=[anywhere,...  23.1 us
    pallas_call x1, Pallas kernels, shards(): pl.pallas_call(functools.partial(end_kernel, rows, pairs, 24), grid=(half...  15.6 us
    all_to_all x3, starting transfers between devices, trade(): return lax.all_to_all(x, axis, split_axis=0, concat_axis=0, tiled=True)  15.3 us
    pallas_call x1, Pallas kernels, shards(): pl.pallas_call(functools.partial(lon_kernel, rows, rb), grid=(rows // rb,...  11 us
    ppermute x6, starting transfers between devices, round_lon(): lax.ppermute(x, 'lon', [(i, i ^ s) for i in range(n_lon)])  10.5 us
    ppermute x6, waiting for transfers between devices, round_lon(): lax.ppermute(x, 'lon', [(i, i ^ s) for i in range(n_lon)])  5.91 us
    all_to_all x3, waiting for transfers between devices, trade(): return lax.all_to_all(x, axis, split_axis=0, concat_axis=0, tiled=True)  4.95 us
    pallas_call x1, Pallas kernels, shards(): pl.pallas_call(functools.partial(close_kernel, n_lon, rows, devices, capa...  4.49 us
  transfers between devices with their start and end apart: 13, of which 3 were waited for; matrix products, arithmetic and copies ran while one was open for 1% of the time, Pallas kernels for 37%

profile of v10, /device:TPU:0, one launch (start us, length us, event | category | flops | bytes accessed | tf_op | source)
XLA Modules:
  0.0 107.2 jit_solution(11305405476978836186)
XLA Ops:
  0.6 1.2 %slice_bitcast_fusion = (f32[1,12288]{1,0:T(1,128)S(1)}, f32[1,12288]{1,0:T(1,128)S(1)}) fusion(f32[3,48,12288]{2,1,0:T(8,128)} %temp.1), kind=kLoop, calls=%fused_computation.5 | loop fusion | bytes 196608 | tf_op jit(solution)/shard_map/squeeze | solution.py:671
  1.8 0.7 slice_bitcast_fusion.4
  2.6 2.4 %collective-permute-start = (f32[1,12480]{1,0:T(1,128)S(1)}, f32[1,12480]{1,0:T(1,128)S(1)}, u32[]{:S(2)}, u32[]{:S(2)}) collective-permute-start(f32[1,12480]{1,0:T(1,128)S(1)} %pad_maximum_fusion), channel_id=1, source_target_pairs={{0,4},{4,8},{8,12},{12,16},{16,20},{20,24},{24,28},{1,5},{5,9},{9,... | collective-permute-start | bytes 149768 | tf_op jit(solution)/shard_map/ppermute | solution.py:673
  5.0 1.3 %collective-permute-start.1 = (f32[1,12480]{1,0:T(1,128)S(1)}, f32[1,12480]{1,0:T(1,128)S(1)}, u32[]{:S(2)}, u32[]{:S(2)}) collective-permute-start(f32[1,12480]{1,0:T(1,128)S(1)} %pad_maximum_fusion.1), channel_id=1, source_target_pairs={{4,0},{8,4},{12,8},{16,12},{20,16},{24,20},{28,24},{5,1},{9,5},{13... | collective-permute-start | bytes 149768 | tf_op jit(solution)/shard_map/ppermute | solution.py:674
  6.3 0.8 slice_bitcast_fusion.2
  7.1 4.3 %collective-permute-start.2 = (f32[48,64]{1,0:T(8,128)S(1)}, f32[48,64]{1,0:T(8,128)S(1)}, u32[]{:S(2)}, u32[]{:S(2)}) collective-permute-start(f32[48,64]{1,0:T(8,128)S(1)} %get-tuple-element.53), channel_id=1, source_target_pairs={{0,1},{1,2},{2,3},{4,5},{5,6},{6,7},{8,9},{9,10},{10,11},{12,13},{... | collective-permute-start | bytes 36872 | tf_op jit(solution)/shard_map/ppermute | solution.py:675
  11.5 1.3 %collective-permute-start.3 = (f32[48,64]{1,0:T(8,128)S(1)}, f32[48,64]{1,0:T(8,128)S(1)}, u32[]{:S(2)}, u32[]{:S(2)}) collective-permute-start(f32[48,64]{1,0:T(8,128)S(1)} %get-tuple-element.52), channel_id=1, source_target_pairs={{1,0},{2,1},{3,2},{5,4},{6,5},{7,6},{9,8},{10,9},{11,10},{13,12},{... | collective-permute-start | bytes 36872 | tf_op jit(solution)/shard_map/ppermute | solution.py:676
  12.8 11.6 %lat_chi_temp.1 = (f32[3,96,48,128]{3,2,1,0:T(8,128)}, f32[3,48,96,128]{3,2,1,0:T(8,128)}, f32[8,3,48,128]{3,2,1,0:T(8,128)}, f32[3,96,8,128]{3,2,1,0:T(8,128)}, f32[3,4,128]{2,1,0:T(4,128)S(1)}) custom-call(f32[1,8]{1,0:T(1,128)} %bitcast.26, s32[1,192]{1,0:T(1,128)} %bitcast.24, f32[1,64]{1,0:T(1,128)} %bitcast.27, f32[3,48,192]{2,1,0:T(8,128)} %sigma.7, ...), custom_call_target="tpu_custom_call" | custom-call | flops 120000000 | bytes 14155776 | tf_op jit(solution)/shard_map/lat_chi_temp/pallas_call | solution.py:690
  24.3 0.0 copy-start
  24.4 0.0 collective-permute-done.2.west
  24.4 0.0 collective-permute-done.3.east
  24.4 0.0 collective-permute-done.north
  24.4 0.0 copy-start.1
  24.4 0.0 collective-permute-done.1.south
  24.4 0.0 copy-start.2
  24.4 11.5 %lat_psi.1 = (f32[3,96,48,128]{3,2,1,0:T(8,128)}, f32[3,48,96,128]{3,2,1,0:T(8,128)}, f32[8,3,48,128]{3,2,1,0:T(8,128)}, f32[3,96,8,128]{3,2,1,0:T(8,128)}) custom-call(f32[3,4,128]{2,1,0:T(4,128)S(1)} %get-tuple-element.27.prm, f32[3,48,192]{2,1,0:T(8,128)} %sigma.7, ...), custom_call_target="tpu_custom_call", output_to_operand_aliasing={{0}: (13, {}), {1}: (14, {}), {2}: (15, {}), {3}: (16, {})} | custom-call | flops 60000000 | bytes 7077888 | tf_op jit(solution)/shard_map/lat_psi/pallas_call | solution.py:690
  35.9 0.0 copy-done.1
  35.9 0.0 copy-done.2
  36.0 6.3 %all-to-all-start = ((f32[8,3,48,128]{3,2,1,0:T(8,128)}), f32[8,3,48,128]{3,2,1,0:T(8,128)S(1)}, u32[]{:S(2)}, u32[]{:S(2)}) async-start(f32[8,3,48,128]{3,2,1,0:T(8,128)} %get-tuple-element.32), calls=%async_computation | async-start | bytes 1179648 | tf_op jit(solution)/shard_map/all_to_all | solution.py:731
  42.2 0.0 copy-start.3
  42.2 11.0 %lon_tile.1 = (f32[3,96,48,128]{3,2,1,0:T(8,128)}, f32[3,4,48,128]{3,2,1,0:T(8,128)}, f32[7,48,128]{2,1,0:T(8,128)S(1)}, f32[3,4,48,128]{3,2,1,0:T(8,128)}, f32[...) custom-call(f32[3,4,128]{2,1,0:T(4,128)S(1)} %get-tuple-element.27.prm, ...), custom_call_target="tpu_custom_call" | custom-call | flops 180000000 | bytes 14155776 | tf_op jit(solution)/shard_map/lon_tile/pallas_call | solution.py:736
  53.2 0.0 all-to-all-done.edges
  53.2 1.0 solve.1
  54.2 4.2 %all-to-all-start.1 = ((f32[8,3,48,128]{3,2,1,0:T(8,128)}), f32[8,3,48,128]{3,2,1,0:T(8,128)S(1)}, u32[]{:S(2)}, u32[]{:S(2)}) async-start(f32[8,3,48,128]{3,2,1,0:T(8,128)} %solve.1), calls=%async_computation.1 | async-start | bytes 1179648 | tf_op jit(solution)/shard_map/all_to_all | solution.py:731
  58.4 0.0 copy-done.3
  58.4 0.2 convert_reduce_fusion
  58.6 2.7 %collective-permute-start.4 = (f32[7,48,128]{2,1,0:T(8,128)S(1)}, f32[7,48,128]{2,1,0:T(8,128)S(1)}, u32[]{:S(2)}, u32[]{:S(2)}) collective-permute-start(f32[7,48,128]{2,1,0:T(8,128)S(1)} %get-tuple-element.35.rest_0_), channel_id=1, source_target_pairs={{0,1},{1,0},{2,3},{3,2},{4,5},{5,4},{6,7},{7,6},{8,9},{9,8},{10,11... | collective-permute-start | bytes 516104 | tf_op jit(solution)/shard_map/ppermute | solution.py:773
  61.3 2.6 %collective-permute-start.5 = (f32[7,48,128]{2,1,0:T(8,128)S(1)}, f32[7,48,128]{2,1,0:T(8,128)S(1)}, u32[]{:S(2)}, u32[]{:S(2)}) collective-permute-start(f32[7,48,128]{2,1,0:T(8,128)S(1)} %get-tuple-element.35.rest_0_), channel_id=1, source_target_pairs={{0,2},{1,3},{2,0},{3,1},{4,6},{5,7},{6,4},{7,5},{8,10},{9,11},{10,... | collective-permute-start | bytes 516104 | tf_op jit(solution)/shard_map/ppermute | solution.py:773
  63.9 0.0 collective-permute-start.6
  63.9 4.9 %all-to-all-done.1.carries = f32[8,3,48,128]{3,2,1,0:T(8,128)S(1)} async-done(((f32[8,3,48,128]{3,2,1,0:T(8,128)}), f32[8,3,48,128]{3,2,1,0:T(8,128)S(1)}, u32[]{:S(2)}, u32[]{:S(2)}) %all-to-all-start.1) | async-done | bytes 589856 | tf_op jit(solution)/shard_map/all_to_all | solution.py:731
  68.8 1.6 %lon_carry.1 = (f32[3,96,8,128]{3,2,1,0:T(8,128)S(1)}, f32[3,4,8,128]{3,2,1,0:T(8,128)S(1)}, f32[6,8,128]{2,1,0:T(8,128)S(1)}) custom-call(f32[3,4,128]{2,1,0:T(4,128)S(1)} %get-tuple-element.27.prm, f32[8,3,48,128]{3,2,1,0:T(8,128)S(1)} %all-to-all-done.1.carries), custom_call_target="tpu_custom_call" | custom-call | flops 30000000 | bytes 1769472 | tf_op jit(solution)/shard_map/lon_carry/pallas_call | solution.py:790
  70.4 2.6 %collective-permute-start.7 = (f32[6,8,128]{2,1,0:T(8,128)S(1)}, f32[6,8,128]{2,1,0:T(8,128)S(1)}, u32[]{:S(2)}, u32[]{:S(2)}) collective-permute-start(f32[6,8,128]{2,1,0:T(8,128)S(1)} %get-tuple-element.45.rest_4_), channel_id=1, source_target_pairs={{0,1},{1,0},{2,3},{3,2},{4,5},{5,4},{6,7},{7,6},{8,9},{9,8},{10,11... | collective-permute-start | bytes 73736 | tf_op jit(solution)/shard_map/ppermute | solution.py:773
  73.0 2.6 %collective-permute-start.8 = (f32[6,8,128]{2,1,0:T(8,128)S(1)}, f32[6,8,128]{2,1,0:T(8,128)S(1)}, u32[]{:S(2)}, u32[]{:S(2)}) collective-permute-start(f32[6,8,128]{2,1,0:T(8,128)S(1)} %get-tuple-element.45.rest_4_), channel_id=1, source_target_pairs={{0,2},{1,3},{2,0},{3,1},{4,6},{5,7},{6,4},{7,5},{8,10},{9,11},{10,... | collective-permute-start | bytes 73736 | tf_op jit(solution)/shard_map/ppermute | solution.py:773
  75.6 0.0 collective-permute-done.4.rest_1_
  75.6 0.0 collective-permute-start.9
  75.6 0.1 pad_add_fusion.place
  75.7 1.6 %collective-permute-done.5.rest_2_ = f32[7,48,128]{2,1,0:T(8,128)S(1)} collective-permute-done((f32[7,48,128]{2,1,0:T(8,128)S(1)}, f32[7,48,128]{2,1,0:T(8,128)S(1)}, u32[]{:S(2)}, u32[]{:S(2)}) %collective-permute-start.5) | collective-permute-done | bytes 172064 | tf_op jit(solution)/shard_map/ppermute | solution.py:773
  77.3 0.0 collective-permute-done.6.rest_3_
  77.3 0.0 collective-permute-done.7.rest_5_
  77.3 4.3 %collective-permute-done.8.rest_6_ = f32[6,8,128]{2,1,0:T(8,128)S(1)} collective-permute-done((f32[6,8,128]{2,1,0:T(8,128)S(1)}, f32[6,8,128]{2,1,0:T(8,128)S(1)}, u32[]{:S(2)}, u32[]{:S(2)}) %collective-permute-start.8) | collective-permute-done | bytes 24608 | tf_op jit(solution)/shard_map/ppermute | solution.py:773
  81.6 0.0 collective-permute-done.9.rest_7_
  81.6 0.0 copy-done
  81.6 4.5 %close.1 = (f32[3,4,48,128]{3,2,1,0:T(8,128)}, f32[3,96,8,128]{3,2,1,0:T(8,128)}, f32[2,48,128]{2,1,0:T(8,128)}, f32[2,48,128]{2,1,0:T(8,128)}, f32[32,128]{1,0:T(8,128)}) custom-call(s32[2]{0:T(128)S(1)} %pad_add_fusion.place, s32[1,192]{1,0:T(1,128)S(1)} %bitcast.23, f32[3,4,128]{2,1,0:T(4,128)S(1)} %get-tuple-element.27.prm, ...), custom_call_target="tpu_custom_call" | custom-call | flops 10000000 | bytes 4000000 | tf_op jit(solution)/shard_map/close/pallas_call | solution.py:822
  86.1 4.9 %all-to-all-start.2 = ((f32[32,1,128]{2,1,0:T(1,128)}), f32[32,1,128]{2,1,0:T(1,128)S(1)}, u32[]{:S(2)}, u32[]{:S(2)}) async-start(f32[32,1,128]{2,1,0:T(1,128)} %bitcast.13), calls=%async_computation.2 | async-start | bytes 32768 | tf_op jit(solution)/shard_map/all_to_all | solution.py:731
  91.0 15.6 %finish.1 = f32[3,48,12288]{2,1,0:T(8,128)} custom-call(s32[2]{0:T(128)S(1)} %pad_add_fusion.place, f32[3,4,128]{2,1,0:T(4,128)} %copy-done, f32[3,48,192]{2,1,0:T(8,128)} %sigma.7, f32[1,12480]{1,0:T(1,128)} %copy-done.1, f32[1,12480]{1,0:T(1,128)} %copy-done.2, f32[3,64,64]{2,1,0:T(8,128)} %vert.5, f32[64,64]{1,0:T(8,128)} %bal.3, ...), custom_call_target="tpu_custom_call" | custom-call | flops 300000000 | bytes 14155776 | tf_op jit(solution)/shard_map/finish/pallas_call | solution.py:841
  106.6 0.0 all-to-all-done.2
  106.6 0.6 reduce_sum.19
  (3 shorter events, 0.1 us)
Async XLA Ops:
  2.6 21.8 %collective-permute-start = (f32[1,12480]{1,0:T(1,128)S(1)}, f32[1,12480]{1,0:T(1,128)S(1)}, u32[]{:S(2)}, u32[]{:S(2)}) collective-permute-start(f32[1,12480]{1,0:T(1,128)S(1)} %pad_maximum_fusion), channel_id=1, source_target_pairs={{0,4},{4,8},{8,12},{12,16},{16,20},{20,24},{24,28},{1,5},{5,9},{9,... | collective-permute-start | bytes 149768 | tf_op jit(solution)/shard_map/ppermute | solution.py:673
  5.0 19.4 %collective-permute-start.1 = (f32[1,12480]{1,0:T(1,128)S(1)}, f32[1,12480]{1,0:T(1,128)S(1)}, u32[]{:S(2)}, u32[]{:S(2)}) collective-permute-start(f32[1,12480]{1,0:T(1,128)S(1)} %pad_maximum_fusion.1), channel_id=1, source_target_pairs={{4,0},{8,4},{12,8},{16,12},{20,16},{24,20},{28,24},{5,1},{9,5},{13... | collective-permute-start | bytes 149768 | tf_op jit(solution)/shard_map/ppermute | solution.py:674
  7.1 17.2 %collective-permute-start.2 = (f32[48,64]{1,0:T(8,128)S(1)}, f32[48,64]{1,0:T(8,128)S(1)}, u32[]{:S(2)}, u32[]{:S(2)}) collective-permute-start(f32[48,64]{1,0:T(8,128)S(1)} %get-tuple-element.53), channel_id=1, source_target_pairs={{0,1},{1,2},{2,3},{4,5},{5,6},{6,7},{8,9},{9,10},{10,11},{12,13},{... | collective-permute-start | bytes 36872 | tf_op jit(solution)/shard_map/ppermute | solution.py:675
  11.5 12.9 %collective-permute-start.3 = (f32[48,64]{1,0:T(8,128)S(1)}, f32[48,64]{1,0:T(8,128)S(1)}, u32[]{:S(2)}, u32[]{:S(2)}) collective-permute-start(f32[48,64]{1,0:T(8,128)S(1)} %get-tuple-element.52), channel_id=1, source_target_pairs={{1,0},{2,1},{3,2},{5,4},{6,5},{7,6},{9,8},{10,9},{11,10},{13,12},{... | collective-permute-start | bytes 36872 | tf_op jit(solution)/shard_map/ppermute | solution.py:676
  24.3 57.3 %copy-start = (f32[3,4,128]{2,1,0:T(4,128)}, f32[3,4,128]{2,1,0:T(4,128)S(1)}, u32[]{:S(2)}) copy-start(f32[3,4,128]{2,1,0:T(4,128)S(1)} %get-tuple-element.27.prm) | copy-start | bytes 18436
  24.4 11.6 %copy-start.1 = (f32[1,12480]{1,0:T(1,128)}, f32[1,12480]{1,0:T(1,128)S(1)}, u32[]{:S(2)}) copy-start(f32[1,12480]{1,0:T(1,128)S(1)} %collective-permute-done.north) | copy-start | bytes 149764
  24.4 11.5 %copy-start.2 = (f32[1,12480]{1,0:T(1,128)}, f32[1,12480]{1,0:T(1,128)S(1)}, u32[]{:S(2)}) copy-start(f32[1,12480]{1,0:T(1,128)S(1)} %collective-permute-done.1.south) | copy-start | bytes 149764
  36.0 17.2 %all-to-all-start = ((f32[8,3,48,128]{3,2,1,0:T(8,128)}), f32[8,3,48,128]{3,2,1,0:T(8,128)S(1)}, u32[]{:S(2)}, u32[]{:S(2)}) async-start(f32[8,3,48,128]{3,2,1,0:T(8,128)} %get-tuple-element.32), calls=%async_computation | async-start | bytes 1179648 | tf_op jit(solution)/shard_map/all_to_all | solution.py:731
  42.2 16.2 %copy-start.3 = (s32[192]{0:T(256)S(1)}, s32[192]{0:T(256)}, u32[]{:S(2)}) copy-start(s32[192]{0:T(256)} %param.15) | copy-start | bytes 2308
  54.2 14.6 %all-to-all-start.1 = ((f32[8,3,48,128]{3,2,1,0:T(8,128)}), f32[8,3,48,128]{3,2,1,0:T(8,128)S(1)}, u32[]{:S(2)}, u32[]{:S(2)}) async-start(f32[8,3,48,128]{3,2,1,0:T(8,128)} %solve.1), calls=%async_computation.1 | async-start | bytes 1179648 | tf_op jit(solution)/shard_map/all_to_all | solution.py:731
  58.6 17.1 %collective-permute-start.4 = (f32[7,48,128]{2,1,0:T(8,128)S(1)}, f32[7,48,128]{2,1,0:T(8,128)S(1)}, u32[]{:S(2)}, u32[]{:S(2)}) collective-permute-start(f32[7,48,128]{2,1,0:T(8,128)S(1)} %get-tuple-element.35.rest_0_), channel_id=1, source_target_pairs={{0,1},{1,0},{2,3},{3,2},{4,5},{5,4},{6,7},{7,6},{8,9},{9,8},{10,11... | collective-permute-start | bytes 516104 | tf_op jit(solution)/shard_map/ppermute | solution.py:773
  61.3 16.1 %collective-permute-start.5 = (f32[7,48,128]{2,1,0:T(8,128)S(1)}, f32[7,48,128]{2,1,0:T(8,128)S(1)}, u32[]{:S(2)}, u32[]{:S(2)}) collective-permute-start(f32[7,48,128]{2,1,0:T(8,128)S(1)} %get-tuple-element.35.rest_0_), channel_id=1, source_target_pairs={{0,2},{1,3},{2,0},{3,1},{4,6},{5,7},{6,4},{7,5},{8,10},{9,11},{10,... | collective-permute-start | bytes 516104 | tf_op jit(solution)/shard_map/ppermute | solution.py:773
  63.9 13.5 %collective-permute-start.6 = (f32[7,48,128]{2,1,0:T(8,128)S(1)}, f32[7,48,128]{2,1,0:T(8,128)S(1)}, u32[]{:S(2)}, u32[]{:S(2)}) collective-permute-start(f32[7,48,128]{2,1,0:T(8,128)S(1)} %get-tuple-element.35.rest_0_), channel_id=1, source_target_pairs={{0,3},{1,2},{2,1},{3,0},{4,7},{5,6},{6,5},{7,4},{8,11},{9,10},{10,... | collective-permute-start | bytes 516104 | tf_op jit(solution)/shard_map/ppermute | solution.py:773
  70.4 6.9 %collective-permute-start.7 = (f32[6,8,128]{2,1,0:T(8,128)S(1)}, f32[6,8,128]{2,1,0:T(8,128)S(1)}, u32[]{:S(2)}, u32[]{:S(2)}) collective-permute-start(f32[6,8,128]{2,1,0:T(8,128)S(1)} %get-tuple-element.45.rest_4_), channel_id=1, source_target_pairs={{0,1},{1,0},{2,3},{3,2},{4,5},{5,4},{6,7},{7,6},{8,9},{9,8},{10,11... | collective-permute-start | bytes 73736 | tf_op jit(solution)/shard_map/ppermute | solution.py:773
  73.0 8.6 %collective-permute-start.8 = (f32[6,8,128]{2,1,0:T(8,128)S(1)}, f32[6,8,128]{2,1,0:T(8,128)S(1)}, u32[]{:S(2)}, u32[]{:S(2)}) collective-permute-start(f32[6,8,128]{2,1,0:T(8,128)S(1)} %get-tuple-element.45.rest_4_), channel_id=1, source_target_pairs={{0,2},{1,3},{2,0},{3,1},{4,6},{5,7},{6,4},{7,5},{8,10},{9,11},{10,... | collective-permute-start | bytes 73736 | tf_op jit(solution)/shard_map/ppermute | solution.py:773
  75.6 6.0 %collective-permute-start.9 = (f32[6,8,128]{2,1,0:T(8,128)S(1)}, f32[6,8,128]{2,1,0:T(8,128)S(1)}, u32[]{:S(2)}, u32[]{:S(2)}) collective-permute-start(f32[6,8,128]{2,1,0:T(8,128)S(1)} %get-tuple-element.45.rest_4_), channel_id=1, source_target_pairs={{0,3},{1,2},{2,1},{3,0},{4,7},{5,6},{6,5},{7,4},{8,11},{9,10},{10,... | collective-permute-start | bytes 73736 | tf_op jit(solution)/shard_map/ppermute | solution.py:773
  86.1 20.5 %all-to-all-start.2 = ((f32[32,1,128]{2,1,0:T(1,128)}), f32[32,1,128]{2,1,0:T(1,128)S(1)}, u32[]{:S(2)}, u32[]{:S(2)}) async-start(f32[32,1,128]{2,1,0:T(1,128)} %bitcast.13), calls=%async_computation.2 | async-start | bytes 32768 | tf_op jit(solution)/shard_map/all_to_all | solution.py:731

commit v11 on v10

--- a/solution.py
+++ b/solution.py
@@ -176,14 +176,6 @@
     return weights[768 * k : 768 * (k + 1)]
 
 
-def store_start(w_ref, w_hbm, first, sem):
-    nv, count = w_ref.shape[:2]
-    at = pl.ds(pl.multiple_of(pl.program_id(0) * count, 8), count)
-    copy = pltpu.make_async_copy(w_ref, w_hbm.at[first : first + nv, at], sem)
-    copy.start()
-    return copy
-
-
 def lat_filter(vs, rows, prm, u_ref, e_ref, p_ref):
     nv = len(vs)
     decay = [prm[v, 1:2, :] for v in vs]
@@ -239,7 +231,7 @@
 
 def lat_plain(
     rows, pairs, scales, classes, chi_coef, sigma, vert, b1lo, b1hi, b2lo, b2hi,
-    w_hbm, u_ref, e_ref, p_ref, prm, xs, wt, sg, w_ref, sem,
+    w_ref, u_ref, e_ref, p_ref, prm, xs, wt, sg,
 ):
     g = pl.program_id(0)
 
@@ -267,14 +259,12 @@
         return 0
 
     lax.fori_loop(0, BLOCK // PAIRS, body, 0)
-    copy = store_start(w_ref, w_hbm, 0, sem)
     lat_filter((1, 2), rows, prm, u_ref, e_ref, p_ref)
-    copy.wait()
 
 
 def lat_balance(
-    rows, pairs, prm, sigma, vert, bal, plo, phi, clo, chi, temp, north, south, west, east, w_in, u_in, e_in, p_in,
-    w_hbm, u_ref, e_ref, p_ref, xs, wt, sg, w_ref, sem,
+    rows, pairs, prm, sigma, vert, bal, plo, phi, clo, chi, tlo, thi, tll, tlr, thl, thr, north, south, west, east, w_in, u_in, e_in, p_in,
+    w_ref, u_ref, e_ref, p_ref, xs, wt, sg,
 ):
     del w_in, u_in, e_in, p_in
     g = pl.program_id(0)
@@ -296,10 +286,23 @@
     def at_tile(m):
         return pl.ds(pl.multiple_of(m * LANES, LANES), LANES)
 
-    def laplace(m):
-        x = temp[0, :, at_tile(m)]
-        left = jnp.where(m == 0, beyond[0], temp[0, :, at_tile(jnp.maximum(m - 1, 0))])
-        right = jnp.where(m == last, beyond[1], temp[0, :, at_tile(jnp.minimum(m + 1, last))])
+    sides = ((tlo, tll, tlr), (thi, thl, thr))
+
+    def laplace(b, o, side):
+        temp, before, after = sides[side]
+        p = b * PAIRS + o
+        m = g * BLOCK + p + side * pairs
+        x = temp[0, :, at_tile(p)]
+        left = temp[0, :, at_tile(jnp.maximum(p - 1, 0))]
+        if o == 0:
+            left = jnp.where(p == 0, before[0], left)
+            if side == 0:
+                left = jnp.where(m == 0, beyond[0], left)
+        right = temp[0, :, at_tile(jnp.minimum(p + 1, BLOCK - 1))]
+        if o == PAIRS - 1:
+            right = jnp.where(p == BLOCK - 1, after[0], right)
+            if side == 1:
+                right = jnp.where(m == last, beyond[1], right)
         beside = swap(x + jnp.where(lane >= 64, left, right))
         above = jnp.where(row_id == 0, north[:, at_tile(m)], pltpu.roll(x, 1, 0))
         below = jnp.where(row_id == rows - 1, south[:, at_tile(m)], pltpu.roll(x, rows - 1, 0))
@@ -314,15 +317,13 @@
                 s = sigma_tile(sg, 0, m + side * pairs, high)
                 to = slice(side * LANES, (side + 1) * LANES)
                 xs[0, at, to] = (pr[0, :, cols] + chi_row * cr[0, :, cols]) * s
-                xs[1, at, to] = laplace(m + side * pairs) * s
+                xs[1, at, to] = laplace(b, p, side) * s
         res = dot(jnp.concatenate([split(xs[0]), split(xs[1])], axis=1), wt[...])
         put_mixed(0, b, rows, res, w_ref, u_ref)
         return 0
 
     lax.fori_loop(0, BLOCK // PAIRS, body, 0)
-    copy = store_start(w_ref, w_hbm, 2, sem)
     lat_filter((0,), rows, prm, u_ref, e_ref, p_ref)
-    copy.wait()
 
 
 def lon_filter(prm, rb, o_ref, el_ref, put, at):
@@ -360,7 +361,7 @@
 
 
 def lon_kernel(
-    rows, rb, prm, sigma, u_ref, w_hbm, o_hbm, el_ref, es_ref, px_ref, dot_ref, rx_ref, ry_ref, w_ref, o_ref, sems
+    rows, rb, prm, u_ref, w_hbm, o_hbm, el_ref, es_ref, px_ref, dot_ref, rx_ref, ry_ref, w_ref, o_ref, sems
 ):
     g = pl.program_id(0)
     half = u_ref.shape[2]
@@ -370,9 +371,6 @@
 
     @pl.when(g == 0)
     def _():
-        x = sigma[0]
-        lon = x.shape[1]
-        es_ref[6] = jnp.where(low_lanes((x.shape[0], LANES)), x[:, 0:1], x[:, lon - 1 : lon])
         dot_ref[...] = jnp.zeros_like(dot_ref)
         for k, v in enumerate(ORDER):
             for e, r in enumerate(responses(prm[v, 0:1, :], prm[v, 1:2, :], half)):
@@ -427,7 +425,7 @@
                 carries[t, k, e * width : (e + 1) * width, :] = c[e][t]
 
 
-def carry_kernel(prm, carries, o_ref, el_ref, es_ref):
+def carry_kernel(prm, sigma, carries, o_ref, el_ref, es_ref):
     width = carries.shape[2] // 4
     zero = jnp.zeros((8, LANES), f32)
 
@@ -446,6 +444,11 @@
         es_ref[i] = x
 
     lon_filter(prm, 8, o_ref, el_ref, put, slice(0, 8))
+    x = sigma[0]
+    rows, lon = x.shape
+    outer = jnp.where(low_lanes((rows, LANES)), x[:, 0:1], x[:, lon - 1 : lon])
+    outer = jnp.concatenate([outer, jnp.zeros((LANES - rows, LANES), f32)], axis=0).T
+    es_ref[6] = jnp.concatenate([outer[0:1], outer[64:65], jnp.zeros((6, LANES), f32)], axis=0)
 
 
 def close_kernel(
@@ -458,8 +461,10 @@
     for d in range(n_lon):
         esm[me ^ d] = sent[d][...]
         esx[me ^ d] = sent_x[d][...]
-    side_ref[0] = esm[jnp.maximum(me - 1, 0), 6]
-    side_ref[1] = esm[jnp.minimum(me + 1, n_lon - 1), 6]
+    pad = jnp.zeros((LANES - 8, LANES), f32)
+    for i, t in enumerate((jnp.maximum(me - 1, 0), jnp.minimum(me + 1, n_lon - 1))):
+        outer = jnp.concatenate([esx[t, 6], pad], axis=0).T[:rows, 1 - i : 2 - i]
+        side_ref[i] = jnp.broadcast_to(outer, (rows, LANES))
     length = jnp.stack([prm[v, 0:1, :] for v in ORDER])
     decay = jnp.stack([prm[v, 1:2, :] for v in ORDER])
     whole = constants(length, decay, 2 * half)
@@ -692,7 +697,7 @@
             grid=(steps,),
             in_specs=specs,
             out_specs=[
-                anywhere,
+                pl.BlockSpec((nv, 2 * BLOCK, rows, LANES), lambda g: (first, g, 0, 0)),
                 pl.BlockSpec((nv, rows, 2 * BLOCK, LANES), lambda g: (first, 0, g, 0)),
                 pl.BlockSpec((2 * BLOCK // width, nv, 4 * width, LANES), lambda g: (g, first, 0, 0)),
                 pl.BlockSpec((nv, 2 * BLOCK, 8, LANES), lambda g: (first, g, 0, 0)),
@@ -704,8 +709,6 @@
                 pltpu.VMEM((2, PAIRS * rows, 256), f32),
                 pltpu.VMEM((2 * 768, 256), bf16),
                 pltpu.VMEM((nvars, pieces, rows, LANES), f32),
-                pltpu.VMEM((nv, 2 * BLOCK, rows, LANES), f32),
-                pltpu.SemaphoreType.DMA(()),
             ],
             compiler_params=params(),
             cost_estimate=pl.CostEstimate(
@@ -720,12 +723,19 @@
     ins = [in_hbm(x) for x in ins]
     body = functools.partial(lat_plain, rows, pairs)
     *wue, prm = lat_call(2, 0, body, ins, specs, "lat_chi_temp", {}, [(nvars, 4, LANES)])
-    ins = [prm] + [in_hbm(x) for x in [sigma, vert, bal_temp] + [state] * 5] + [north, south, west, east]
+    ins = [prm] + [in_hbm(x) for x in [sigma, vert, bal_temp] + [state] * 10] + [north, south, west, east]
     ins += [in_hbm(wue[0]), in_hbm(wue[1]), wue[2], in_hbm(wue[3])]
     specs = [full(x.shape) for x in ins[:4]] + [part(0, 0), part(0, 1), part(1, 0), part(1, 1)]
-    specs += [pl.BlockSpec((1, rows, merged), lambda g: (2, 0, 0))]
+
+    def tile(side, step):
+        last = 2 * pairs - 1
+        return pl.BlockSpec(
+            (1, rows, LANES), lambda g: (2, 0, jnp.clip(g * BLOCK + side * pairs + step, 0, last))
+        )
+
+    specs += [part(2, 0), part(2, 1), tile(0, -1), tile(0, BLOCK), tile(1, -1), tile(1, BLOCK)]
     specs += [full(x.shape) for x in (north, south, west, east)] + [anywhere] * 4
-    aliases = {13: 0, 14: 1, 15: 2, 16: 3}
+    aliases = {18: 0, 19: 1, 20: 2, 21: 3}
     w, u, edges, proj = lat_call(1, 2, functools.partial(lat_balance, rows, pairs), ins, specs, "lat_psi", aliases)
     def trade(x, axis):
         return lax.all_to_all(x, axis, split_axis=0, concat_axis=0, tiled=True)
@@ -738,14 +748,13 @@
         grid=(rows // rb,),
         in_specs=[
             full(prm.shape),
-            pl.BlockSpec((1, rows, lon), lambda g: (0, 0, 0)),
             pl.BlockSpec((nvars, rb, half, LANES), lambda g: (0, g, 0, 0)),
             anywhere,
         ],
         out_specs=[
             anywhere,
             full((nvars, 4, rows, LANES)),
-            full((7, rows, LANES)),
+            full((6, rows, LANES)),
             full((nvars, 4, rows, LANES)),
             full((nvars, 8, LANES)),
             full((nvars, 4, half, LANES)),
@@ -754,7 +763,7 @@
         out_shape=[
             pltpu.HBM((nvars, half, rows, LANES), f32),
             pltpu.HBM((nvars, 4, rows, LANES), f32),
-            jax.ShapeDtypeStruct((7, rows, LANES), f32),
+            jax.ShapeDtypeStruct((6, rows, LANES), f32),
             pltpu.HBM((nvars, 4, rows, LANES), f32),
             pltpu.HBM((nvars, 8, LANES), f32),
             pltpu.HBM((nvars, 4, half, LANES), f32),
@@ -766,7 +775,7 @@
             flops=180000000, bytes_accessed=6 * rows * merged * 4, transcendentals=0
         ),
         name="lon_tile",
-    )(prm, *[in_hbm(x) for x in (sigma, u, w)])
+    )(prm, *[in_hbm(x) for x in (u, w)])
 
     def round_lon(x):
         return [x] + [
@@ -790,19 +799,19 @@
     crossed, elc, esc = pl.pallas_call(
         carry_kernel,
         grid=(1,),
-        in_specs=[full(prm.shape), full(carries.shape)],
-        out_specs=[full((nvars, half, 8, LANES)), full((nvars, 4, 8, LANES)), full((6, 8, LANES))],
+        in_specs=[full(prm.shape), pl.BlockSpec((1, rows, lon), lambda g: (0, 0, 0)), full(carries.shape)],
+        out_specs=[full((nvars, half, 8, LANES)), full((nvars, 4, 8, LANES)), full((7, 8, LANES))],
         out_shape=[
             jax.ShapeDtypeStruct((nvars, half, 8, LANES), f32),
             jax.ShapeDtypeStruct((nvars, 4, 8, LANES), f32),
-            jax.ShapeDtypeStruct((6, 8, LANES), f32),
+            jax.ShapeDtypeStruct((7, 8, LANES), f32),
         ],
         compiler_params=params(),
         cost_estimate=pl.CostEstimate(
             flops=30000000, bytes_accessed=4 * nvars * 12 * half * LANES, transcendentals=0
         ),
         name="lon_carry",
-    )(prm, carries)
+    )(prm, in_hbm(sigma), carries)
     sent_x = round_lon(esc)
 
     packed = 2 * PAIRS
@@ -825,7 +834,7 @@
         in_specs=specs,
         out_specs=[full(x) for x in shapes] + [full((devices, LANES))],
         out_shape=[pltpu.HBM(x, f32) for x in shapes] + [jax.ShapeDtypeStruct((devices, LANES), f32)],
-        scratch_shapes=[pltpu.VMEM((n_lon, 7, rows, LANES), f32), pltpu.VMEM((n_lon, 6, 8, LANES), f32)],
+        scratch_shapes=[pltpu.VMEM((n_lon, 6, rows, LANES), f32), pltpu.VMEM((n_lon, 7, 8, LANES), f32)],
         compiler_params=params(),
         cost_estimate=pl.CostEstimate(flops=10000000, bytes_accessed=4000000, transcendentals=0),
         name="close",

time: 108 us -> 105 us (0.972)
  starting transfers between devices: 35.1 us -> 32.8 us
    all_to_all x3, starting transfers between devices: 15.3 us -> 13 us  [trade(): return lax.all_to_all(x, axis, split_axis=0, concat_axis=0, tiled=True)]
  transfers between devices with their start and end apart: 13 -> 13, of which waited for: 3 -> 3; matrix products, arithmetic and copies ran while one was open for 1% -> 1% of each run, Pallas kernels for 37% -> 39%
where the time goes in v11:
time: 105 us
  Pallas kernels  56.7 us (54%)
  starting transfers between devices  32.8 us (31%)
  waiting for transfers between devices  10.6 us (10%)
  local copies, waits for them, and re-layouts  2.76 us (3%)
    pallas_call x2, Pallas kernels, lat_call(): pl.pallas_call(body, grid=(steps,), in_specs=specs, out_specs=[pl.BlockSp...  22.2 us
    pallas_call x1, Pallas kernels, shards(): pl.pallas_call(functools.partial(end_kernel, rows, pairs, 24), grid=(half...  15.6 us
    all_to_all x3, starting transfers between devices, trade(): return lax.all_to_all(x, axis, split_axis=0, concat_axis=0, tiled=True)  13 us
    pallas_call x1, Pallas kernels, shards(): pl.pallas_call(functools.partial(lon_kernel, rows, rb), grid=(rows // rb,...  11 us
    ppermute x6, starting transfers between devices, round_lon(): lax.ppermute(x, 'lon', [(i, i ^ s) for i in range(n_lon)])  10.6 us
    ppermute x6, waiting for transfers between devices, round_lon(): lax.ppermute(x, 'lon', [(i, i ^ s) for i in range(n_lon)])  5.59 us
    all_to_all x3, waiting for transfers between devices, trade(): return lax.all_to_all(x, axis, split_axis=0, concat_axis=0, tiled=True)  4.96 us
    pallas_call x1, Pallas kernels, shards(): pl.pallas_call(functools.partial(close_kernel, n_lon, rows, devices, capa...  4.55 us
  transfers between devices with their start and end apart: 13, of which 3 were waited for; matrix products, arithmetic and copies ran while one was open for 1% of the time, Pallas kernels for 39%

profile of v11, /device:TPU:0, one launch (start us, length us, event | category | flops | bytes accessed | tf_op | source)
XLA Modules:
  0.0 104.6 jit_solution(10472018148093506953)
XLA Ops:
  0.6 1.2 %slice_bitcast_fusion = (f32[1,12288]{1,0:T(1,128)S(1)}, f32[1,12288]{1,0:T(1,128)S(1)}) fusion(f32[3,48,12288]{2,1,0:T(8,128)} %thr.1), kind=kLoop, calls=%fused_computation.5 | loop fusion | bytes 196608 | tf_op jit(solution)/shard_map/squeeze | solution.py:676
  1.8 0.7 slice_bitcast_fusion.4
  2.6 2.4 %collective-permute-start = (f32[1,12480]{1,0:T(1,128)S(1)}, f32[1,12480]{1,0:T(1,128)S(1)}, u32[]{:S(2)}, u32[]{:S(2)}) collective-permute-start(f32[1,12480]{1,0:T(1,128)S(1)} %pad_maximum_fusion), channel_id=1, source_target_pairs={{0,4},{4,8},{8,12},{12,16},{16,20},{20,24},{24,28},{1,5},{5,9},{9,... | collective-permute-start | bytes 149768 | tf_op jit(solution)/shard_map/ppermute | solution.py:678
  5.0 1.3 %collective-permute-start.1 = (f32[1,12480]{1,0:T(1,128)S(1)}, f32[1,12480]{1,0:T(1,128)S(1)}, u32[]{:S(2)}, u32[]{:S(2)}) collective-permute-start(f32[1,12480]{1,0:T(1,128)S(1)} %pad_maximum_fusion.1), channel_id=1, source_target_pairs={{4,0},{8,4},{12,8},{16,12},{20,16},{24,20},{28,24},{5,1},{9,5},{13... | collective-permute-start | bytes 149768 | tf_op jit(solution)/shard_map/ppermute | solution.py:679
  6.3 0.8 slice_bitcast_fusion.2
  7.1 4.3 %collective-permute-start.2 = (f32[48,64]{1,0:T(8,128)S(1)}, f32[48,64]{1,0:T(8,128)S(1)}, u32[]{:S(2)}, u32[]{:S(2)}) collective-permute-start(f32[48,64]{1,0:T(8,128)S(1)} %get-tuple-element.53), channel_id=1, source_target_pairs={{0,1},{1,2},{2,3},{4,5},{5,6},{6,7},{8,9},{9,10},{10,11},{12,13},{... | collective-permute-start | bytes 36872 | tf_op jit(solution)/shard_map/ppermute | solution.py:680
  11.5 1.3 %collective-permute-start.3 = (f32[48,64]{1,0:T(8,128)S(1)}, f32[48,64]{1,0:T(8,128)S(1)}, u32[]{:S(2)}, u32[]{:S(2)}) collective-permute-start(f32[48,64]{1,0:T(8,128)S(1)} %get-tuple-element.52), channel_id=1, source_target_pairs={{1,0},{2,1},{3,2},{5,4},{6,5},{7,6},{9,8},{10,9},{11,10},{13,12},{... | collective-permute-start | bytes 36872 | tf_op jit(solution)/shard_map/ppermute | solution.py:681
  12.8 11.4 %lat_chi_temp.1 = (f32[3,96,48,128]{3,2,1,0:T(8,128)}, f32[3,48,96,128]{3,2,1,0:T(8,128)}, f32[8,3,48,128]{3,2,1,0:T(8,128)}, f32[3,96,8,128]{3,2,1,0:T(8,128)}, f32[3,4,128]{2,1,0:T(4,128)S(1)}) custom-call(f32[1,8]{1,0:T(1,128)} %bitcast.26, s32[1,192]{1,0:T(1,128)} %bitcast.24, f32[1,64]{1,0:T(1,128)} %bitcast.27, f32[3,48,192]{2,1,0:T(8,128)} %sigma.7, ...), custom_call_target="tpu_custom_call" | custom-call | flops 120000000 | bytes 14155776 | tf_op jit(solution)/shard_map/lat_chi_temp/pallas_call | solution.py:695
  24.1 0.0 copy-start
  24.1 0.0 collective-permute-done.2.west
  24.1 0.0 collective-permute-done.3.east
  24.1 0.0 collective-permute-done.north
  24.1 0.0 copy-start.1
  24.2 0.0 collective-permute-done.1.south
  24.2 0.0 copy-start.2
  24.2 10.9 %lat_psi.1 = (f32[3,96,48,128]{3,2,1,0:T(8,128)}, f32[3,48,96,128]{3,2,1,0:T(8,128)}, f32[8,3,48,128]{3,2,1,0:T(8,128)}, f32[3,96,8,128]{3,2,1,0:T(8,128)}) custom-call(f32[3,4,128]{2,1,0:T(4,128)S(1)} %get-tuple-element.27.prm, f32[3,48,192]{2,1,0:T(8,128)} %sigma.7, ...), custom_call_target="tpu_custom_call", output_to_operand_aliasing={{0}: (18, {}), {1}: (19, {}), {2}: (20, {}), {3}: (21, {})} | custom-call | flops 60000000 | bytes 7077888 | tf_op jit(solution)/shard_map/lat_psi/pallas_call | solution.py:695
  35.0 0.0 copy-done.1
  35.1 0.0 copy-done.2
  35.1 6.3 %all-to-all-start = ((f32[8,3,48,128]{3,2,1,0:T(8,128)}), f32[8,3,48,128]{3,2,1,0:T(8,128)S(1)}, u32[]{:S(2)}, u32[]{:S(2)}) async-start(f32[8,3,48,128]{3,2,1,0:T(8,128)} %get-tuple-element.32), calls=%async_computation | async-start | bytes 1179648 | tf_op jit(solution)/shard_map/all_to_all | solution.py:741
  41.3 0.0 copy-start.3
  41.3 11.0 %lon_tile.1 = (f32[3,96,48,128]{3,2,1,0:T(8,128)}, f32[3,4,48,128]{3,2,1,0:T(8,128)}, f32[6,48,128]{2,1,0:T(8,128)S(1)}, f32[3,4,48,128]{3,2,1,0:T(8,128)}, f32[...) custom-call(f32[3,4,128]{2,1,0:T(4,128)S(1)} %get-tuple-element.27.prm, ...), custom_call_target="tpu_custom_call" | custom-call | flops 180000000 | bytes 14155776 | tf_op jit(solution)/shard_map/lon_tile/pallas_call | solution.py:746
  52.3 0.0 all-to-all-done.edges
  52.3 1.0 solve.1
  53.3 4.2 %all-to-all-start.1 = ((f32[8,3,48,128]{3,2,1,0:T(8,128)}), f32[8,3,48,128]{3,2,1,0:T(8,128)S(1)}, u32[]{:S(2)}, u32[]{:S(2)}) async-start(f32[8,3,48,128]{3,2,1,0:T(8,128)} %solve.1), calls=%async_computation.1 | async-start | bytes 1179648 | tf_op jit(solution)/shard_map/all_to_all | solution.py:741
  57.5 0.0 copy-done.3
  57.5 0.2 convert_reduce_fusion
  57.7 2.7 %collective-permute-start.4 = (f32[6,48,128]{2,1,0:T(8,128)S(1)}, f32[6,48,128]{2,1,0:T(8,128)S(1)}, u32[]{:S(2)}, u32[]{:S(2)}) collective-permute-start(f32[6,48,128]{2,1,0:T(8,128)S(1)} %get-tuple-element.35.rest_0_), channel_id=1, source_target_pairs={{0,1},{1,0},{2,3},{3,2},{4,5},{5,4},{6,7},{7,6},{8,9},{9,8},{10,11... | collective-permute-start | bytes 442376 | tf_op jit(solution)/shard_map/ppermute | solution.py:782
  60.4 2.6 %collective-permute-start.5 = (f32[6,48,128]{2,1,0:T(8,128)S(1)}, f32[6,48,128]{2,1,0:T(8,128)S(1)}, u32[]{:S(2)}, u32[]{:S(2)}) collective-permute-start(f32[6,48,128]{2,1,0:T(8,128)S(1)} %get-tuple-element.35.rest_0_), channel_id=1, source_target_pairs={{0,2},{1,3},{2,0},{3,1},{4,6},{5,7},{6,4},{7,5},{8,10},{9,11},{10,... | collective-permute-start | bytes 442376 | tf_op jit(solution)/shard_map/ppermute | solution.py:782
  63.0 0.0 collective-permute-start.6
  63.0 5.0 %all-to-all-done.1.carries = f32[8,3,48,128]{3,2,1,0:T(8,128)S(1)} async-done(((f32[8,3,48,128]{3,2,1,0:T(8,128)}), f32[8,3,48,128]{3,2,1,0:T(8,128)S(1)}, u32[]{:S(2)}, u32[]{:S(2)}) %all-to-all-start.1) | async-done | bytes 589856 | tf_op jit(solution)/shard_map/all_to_all | solution.py:741
  67.9 2.4 %lon_carry.1 = (f32[3,96,8,128]{3,2,1,0:T(8,128)S(1)}, f32[3,4,8,128]{3,2,1,0:T(8,128)S(1)}, f32[7,8,128]{2,1,0:T(8,128)S(1)}) custom-call(f32[3,4,128]{2,1,0:T(4,128)S(1)} %get-tuple-element.27.prm, f32[3,48,192]{2,1,0:T(8,128)} %sigma.7, f32[8,3,48,128]{3,2,1,0:T(8,128)S(1)} %all-to-all-done.1.carries), custom_call_target="tpu_custom_call" | custom-call | flops 30000000 | bytes 1769472 | tf_op jit(solution)/shard_map/lon_carry/pallas_call | solution.py:799
  70.3 2.7 %collective-permute-start.7 = (f32[7,8,128]{2,1,0:T(8,128)S(1)}, f32[7,8,128]{2,1,0:T(8,128)S(1)}, u32[]{:S(2)}, u32[]{:S(2)}) collective-permute-start(f32[7,8,128]{2,1,0:T(8,128)S(1)} %get-tuple-element.45.rest_4_), channel_id=1, source_target_pairs={{0,1},{1,0},{2,3},{3,2},{4,5},{5,4},{6,7},{7,6},{8,9},{9,8},{10,11... | collective-permute-start | bytes 86024 | tf_op jit(solution)/shard_map/ppermute | solution.py:782
  73.0 2.6 %collective-permute-start.8 = (f32[7,8,128]{2,1,0:T(8,128)S(1)}, f32[7,8,128]{2,1,0:T(8,128)S(1)}, u32[]{:S(2)}, u32[]{:S(2)}) collective-permute-start(f32[7,8,128]{2,1,0:T(8,128)S(1)} %get-tuple-element.45.rest_4_), channel_id=1, source_target_pairs={{0,2},{1,3},{2,0},{3,1},{4,6},{5,7},{6,4},{7,5},{8,10},{9,11},{10,... | collective-permute-start | bytes 86024 | tf_op jit(solution)/shard_map/ppermute | solution.py:782
  75.6 0.0 collective-permute-done.4.rest_1_
  75.6 0.0 collective-permute-start.9
  75.6 0.1 pad_add_fusion.place
  75.7 0.0 collective-permute-done.5.rest_2_
  75.7 0.0 collective-permute-done.6.rest_3_
  75.7 0.0 collective-permute-done.7.rest_5_
  75.7 3.0 %collective-permute-done.8.rest_6_ = f32[7,8,128]{2,1,0:T(8,128)S(1)} collective-permute-done((f32[7,8,128]{2,1,0:T(8,128)S(1)}, f32[7,8,128]{2,1,0:T(8,128)S(1)}, u32[]{:S(2)}, u32[]{:S(2)}) %collective-permute-start.8) | collective-permute-done | bytes 28704 | tf_op jit(solution)/shard_map/ppermute | solution.py:782
  78.7 2.6 %collective-permute-done.9.rest_7_ = f32[7,8,128]{2,1,0:T(8,128)S(1)} collective-permute-done((f32[7,8,128]{2,1,0:T(8,128)S(1)}, f32[7,8,128]{2,1,0:T(8,128)S(1)}, u32[]{:S(2)}, u32[]{:S(2)}) %collective-permute-start.9) | collective-permute-done | bytes 28704 | tf_op jit(solution)/shard_map/ppermute | solution.py:782
  81.3 0.0 copy-done
  81.3 4.6 %close.1 = (f32[3,4,48,128]{3,2,1,0:T(8,128)}, f32[3,96,8,128]{3,2,1,0:T(8,128)}, f32[2,48,128]{2,1,0:T(8,128)}, f32[2,48,128]{2,1,0:T(8,128)}, f32[32,128]{1,0:T(8,128)}) custom-call(s32[2]{0:T(128)S(1)} %pad_add_fusion.place, s32[1,192]{1,0:T(1,128)S(1)} %bitcast.23, f32[3,4,128]{2,1,0:T(4,128)S(1)} %get-tuple-element.27.prm, ...), custom_call_target="tpu_custom_call" | custom-call | flops 10000000 | bytes 4000000 | tf_op jit(solution)/shard_map/close/pallas_call | solution.py:831
  85.8 2.5 %all-to-all-start.2 = ((f32[32,1,128]{2,1,0:T(1,128)}), f32[32,1,128]{2,1,0:T(1,128)S(1)}, u32[]{:S(2)}, u32[]{:S(2)}) async-start(f32[32,1,128]{2,1,0:T(1,128)} %bitcast.13), calls=%async_computation.2 | async-start | bytes 32768 | tf_op jit(solution)/shard_map/all_to_all | solution.py:741
  88.4 15.6 %finish.1 = f32[3,48,12288]{2,1,0:T(8,128)} custom-call(s32[2]{0:T(128)S(1)} %pad_add_fusion.place, f32[3,4,128]{2,1,0:T(4,128)} %copy-done, f32[3,48,192]{2,1,0:T(8,128)} %sigma.7, f32[1,12480]{1,0:T(1,128)} %copy-done.1, f32[1,12480]{1,0:T(1,128)} %copy-done.2, f32[3,64,64]{2,1,0:T(8,128)} %vert.5, f32[64,64]{1,0:T(8,128)} %bal.3, ...), custom_call_target="tpu_custom_call" | custom-call | flops 300000000 | bytes 14155776 | tf_op jit(solution)/shard_map/finish/pallas_call | solution.py:850
  104.0 0.0 all-to-all-done.2
  104.0 0.6 reduce_sum.19
  (3 shorter events, 0.1 us)
Async XLA Ops:
  2.6 21.6 %collective-permute-start = (f32[1,12480]{1,0:T(1,128)S(1)}, f32[1,12480]{1,0:T(1,128)S(1)}, u32[]{:S(2)}, u32[]{:S(2)}) collective-permute-start(f32[1,12480]{1,0:T(1,128)S(1)} %pad_maximum_fusion), channel_id=1, source_target_pairs={{0,4},{4,8},{8,12},{12,16},{16,20},{20,24},{24,28},{1,5},{5,9},{9,... | collective-permute-start | bytes 149768 | tf_op jit(solution)/shard_map/ppermute | solution.py:678
  5.0 19.1 %collective-permute-start.1 = (f32[1,12480]{1,0:T(1,128)S(1)}, f32[1,12480]{1,0:T(1,128)S(1)}, u32[]{:S(2)}, u32[]{:S(2)}) collective-permute-start(f32[1,12480]{1,0:T(1,128)S(1)} %pad_maximum_fusion.1), channel_id=1, source_target_pairs={{4,0},{8,4},{12,8},{16,12},{20,16},{24,20},{28,24},{5,1},{9,5},{13... | collective-permute-start | bytes 149768 | tf_op jit(solution)/shard_map/ppermute | solution.py:679
  7.1 17.0 %collective-permute-start.2 = (f32[48,64]{1,0:T(8,128)S(1)}, f32[48,64]{1,0:T(8,128)S(1)}, u32[]{:S(2)}, u32[]{:S(2)}) collective-permute-start(f32[48,64]{1,0:T(8,128)S(1)} %get-tuple-element.53), channel_id=1, source_target_pairs={{0,1},{1,2},{2,3},{4,5},{5,6},{6,7},{8,9},{9,10},{10,11},{12,13},{... | collective-permute-start | bytes 36872 | tf_op jit(solution)/shard_map/ppermute | solution.py:680
  11.5 12.7 %collective-permute-start.3 = (f32[48,64]{1,0:T(8,128)S(1)}, f32[48,64]{1,0:T(8,128)S(1)}, u32[]{:S(2)}, u32[]{:S(2)}) collective-permute-start(f32[48,64]{1,0:T(8,128)S(1)} %get-tuple-element.52), channel_id=1, source_target_pairs={{1,0},{2,1},{3,2},{5,4},{6,5},{7,6},{9,8},{10,9},{11,10},{13,12},{... | collective-permute-start | bytes 36872 | tf_op jit(solution)/shard_map/ppermute | solution.py:681
  24.1 57.2 %copy-start = (f32[3,4,128]{2,1,0:T(4,128)}, f32[3,4,128]{2,1,0:T(4,128)S(1)}, u32[]{:S(2)}) copy-start(f32[3,4,128]{2,1,0:T(4,128)S(1)} %get-tuple-element.27.prm) | copy-start | bytes 18436
  24.1 10.9 %copy-start.1 = (f32[1,12480]{1,0:T(1,128)}, f32[1,12480]{1,0:T(1,128)S(1)}, u32[]{:S(2)}) copy-start(f32[1,12480]{1,0:T(1,128)S(1)} %collective-permute-done.north) | copy-start | bytes 149764
  24.2 10.9 %copy-start.2 = (f32[1,12480]{1,0:T(1,128)}, f32[1,12480]{1,0:T(1,128)S(1)}, u32[]{:S(2)}) copy-start(f32[1,12480]{1,0:T(1,128)S(1)} %collective-permute-done.1.south) | copy-start | bytes 149764
  35.1 17.2 %all-to-all-start = ((f32[8,3,48,128]{3,2,1,0:T(8,128)}), f32[8,3,48,128]{3,2,1,0:T(8,128)S(1)}, u32[]{:S(2)}, u32[]{:S(2)}) async-start(f32[8,3,48,128]{3,2,1,0:T(8,128)} %get-tuple-element.32), calls=%async_computation | async-start | bytes 1179648 | tf_op jit(solution)/shard_map/all_to_all | solution.py:741
  41.3 16.2 %copy-start.3 = (s32[192]{0:T(256)S(1)}, s32[192]{0:T(256)}, u32[]{:S(2)}) copy-start(s32[192]{0:T(256)} %param.15) | copy-start | bytes 2308
  53.3 14.6 %all-to-all-start.1 = ((f32[8,3,48,128]{3,2,1,0:T(8,128)}), f32[8,3,48,128]{3,2,1,0:T(8,128)S(1)}, u32[]{:S(2)}, u32[]{:S(2)}) async-start(f32[8,3,48,128]{3,2,1,0:T(8,128)} %solve.1), calls=%async_computation.1 | async-start | bytes 1179648 | tf_op jit(solution)/shard_map/all_to_all | solution.py:741
  57.7 17.9 %collective-permute-start.4 = (f32[6,48,128]{2,1,0:T(8,128)S(1)}, f32[6,48,128]{2,1,0:T(8,128)S(1)}, u32[]{:S(2)}, u32[]{:S(2)}) collective-permute-start(f32[6,48,128]{2,1,0:T(8,128)S(1)} %get-tuple-element.35.rest_0_), channel_id=1, source_target_pairs={{0,1},{1,0},{2,3},{3,2},{4,5},{5,4},{6,7},{7,6},{8,9},{9,8},{10,11... | collective-permute-start | bytes 442376 | tf_op jit(solution)/shard_map/ppermute | solution.py:782
  60.4 15.3 %collective-permute-start.5 = (f32[6,48,128]{2,1,0:T(8,128)S(1)}, f32[6,48,128]{2,1,0:T(8,128)S(1)}, u32[]{:S(2)}, u32[]{:S(2)}) collective-permute-start(f32[6,48,128]{2,1,0:T(8,128)S(1)} %get-tuple-element.35.rest_0_), channel_id=1, source_target_pairs={{0,2},{1,3},{2,0},{3,1},{4,6},{5,7},{6,4},{7,5},{8,10},{9,11},{10,... | collective-permute-start | bytes 442376 | tf_op jit(solution)/shard_map/ppermute | solution.py:782
  63.0 12.7 %collective-permute-start.6 = (f32[6,48,128]{2,1,0:T(8,128)S(1)}, f32[6,48,128]{2,1,0:T(8,128)S(1)}, u32[]{:S(2)}, u32[]{:S(2)}) collective-permute-start(f32[6,48,128]{2,1,0:T(8,128)S(1)} %get-tuple-element.35.rest_0_), channel_id=1, source_target_pairs={{0,3},{1,2},{2,1},{3,0},{4,7},{5,6},{6,5},{7,4},{8,11},{9,10},{10,... | collective-permute-start | bytes 442376 | tf_op jit(solution)/shard_map/ppermute | solution.py:782
  70.3 5.4 %collective-permute-start.7 = (f32[7,8,128]{2,1,0:T(8,128)S(1)}, f32[7,8,128]{2,1,0:T(8,128)S(1)}, u32[]{:S(2)}, u32[]{:S(2)}) collective-permute-start(f32[7,8,128]{2,1,0:T(8,128)S(1)} %get-tuple-element.45.rest_4_), channel_id=1, source_target_pairs={{0,1},{1,0},{2,3},{3,2},{4,5},{5,4},{6,7},{7,6},{8,9},{9,8},{10,11... | collective-permute-start | bytes 86024 | tf_op jit(solution)/shard_map/ppermute | solution.py:782
  73.0 5.6 %collective-permute-start.8 = (f32[7,8,128]{2,1,0:T(8,128)S(1)}, f32[7,8,128]{2,1,0:T(8,128)S(1)}, u32[]{:S(2)}, u32[]{:S(2)}) collective-permute-start(f32[7,8,128]{2,1,0:T(8,128)S(1)} %get-tuple-element.45.rest_4_), channel_id=1, source_target_pairs={{0,2},{1,3},{2,0},{3,1},{4,6},{5,7},{6,4},{7,5},{8,10},{9,11},{10,... | collective-permute-start | bytes 86024 | tf_op jit(solution)/shard_map/ppermute | solution.py:782
  75.6 5.7 %collective-permute-start.9 = (f32[7,8,128]{2,1,0:T(8,128)S(1)}, f32[7,8,128]{2,1,0:T(8,128)S(1)}, u32[]{:S(2)}, u32[]{:S(2)}) collective-permute-start(f32[7,8,128]{2,1,0:T(8,128)S(1)} %get-tuple-element.45.rest_4_), channel_id=1, source_target_pairs={{0,3},{1,2},{2,1},{3,0},{4,7},{5,6},{6,5},{7,4},{8,11},{9,10},{10,... | collective-permute-start | bytes 86024 | tf_op jit(solution)/shard_map/ppermute | solution.py:782
  85.8 18.2 %all-to-all-start.2 = ((f32[32,1,128]{2,1,0:T(1,128)}), f32[32,1,128]{2,1,0:T(1,128)S(1)}, u32[]{:S(2)}, u32[]{:S(2)}) async-start(f32[32,1,128]{2,1,0:T(1,128)} %bitcast.13), calls=%async_computation.2 | async-start | bytes 32768 | tf_op jit(solution)/shard_map/all_to_all | solution.py:741

commit v12 on v11

--- a/solution.py
+++ b/solution.py
@@ -132,10 +132,18 @@
     return c1, c2, c3, c4
 
 
-def cascade(count, load, store, decay, start):
+def cascade(count, turn, load, store, decay, start):
     step = 24
-    edges = []
-    for stage in range(4):
+
+    def first(b, states):
+        blocks = turn(b)
+        for o in range(8):
+            states = [a * s + x[o] for a, s, x in zip(decay, states, blocks)]
+            store(b * 8 + o, states)
+        return tuple(states)
+
+    edges = [list(lax.fori_loop(0, count // 8, first, tuple(start)))]
+    for stage in range(1, 4):
         back = stage % 2 == 1
 
         def body(b, states, back=back):
@@ -176,7 +184,7 @@
     return weights[768 * k : 768 * (k + 1)]
 
 
-def lat_filter(vs, rows, prm, u_ref, e_ref, p_ref):
+def lat_filter(vs, rows, prm, w_ref, u_ref, e_ref, p_ref):
     nv = len(vs)
     decay = [prm[v, 1:2, :] for v in vs]
 
@@ -187,8 +195,12 @@
         for k in range(nv):
             u_ref[k, i] = values[k]
 
+    def turn(b):
+        at = pl.ds(pl.multiple_of(b * 8, 8), 8)
+        return [jnp.swapaxes(w_ref[k, :, at, :], 0, 1) for k in range(nv)]
+
     zero = jnp.zeros((u_ref.shape[2], LANES), f32)
-    edges = cascade(rows, load, store, decay, [zero] * nv)
+    edges = cascade(rows, turn, load, store, decay, [zero] * nv)
     for k in range(nv):
         for j in range(0, u_ref.shape[2], 8):
             block = [edges[3 - e][k][j : j + 8] * decay[k] for e in range(4)]
@@ -201,14 +213,12 @@
                 e_ref[c, k, e * width : (e + 1) * width] = edges[e][k][c * width : (c + 1) * width]
 
 
-def put_mixed(k, b, rows, res, w_ref, u_ref):
+def put_mixed(k, b, rows, res, w_ref):
     base = b * 2 * PAIRS
     for p in range(PAIRS):
         part = res[p * rows : (p + 1) * rows]
         w_ref[k, base + 2 * p] = part[:, :LANES]
         w_ref[k, base + 2 * p + 1] = part[:, LANES:]
-    at = pl.ds(pl.multiple_of(base, 2 * PAIRS), 2 * PAIRS)
-    u_ref[k, :, at, :] = jnp.swapaxes(w_ref[k, at], 0, 1)
 
 
 def set_params(scales, classes, chi_coef, prm):
@@ -255,11 +265,11 @@
                     s = sigma_tile(sg, k + 1, m + side * pairs, high)
                     xs[k, at, side * LANES : (side + 1) * LANES] = sides[side][0, :, cols] * s
         for k in range(2):
-            put_mixed(k, b, rows, product(xs[k], weight(wt, k)), w_ref, u_ref)
+            put_mixed(k, b, rows, product(xs[k], weight(wt, k)), w_ref)
         return 0
 
     lax.fori_loop(0, BLOCK // PAIRS, body, 0)
-    lat_filter((1, 2), rows, prm, u_ref, e_ref, p_ref)
+    lat_filter((1, 2), rows, prm, w_ref, u_ref, e_ref, p_ref)
 
 
 def lat_balance(
@@ -319,14 +329,14 @@
                 xs[0, at, to] = (pr[0, :, cols] + chi_row * cr[0, :, cols]) * s
                 xs[1, at, to] = laplace(b, p, side) * s
         res = dot(jnp.concatenate([split(xs[0]), split(xs[1])], axis=1), wt[...])
-        put_mixed(0, b, rows, res, w_ref, u_ref)
+        put_mixed(0, b, rows, res, w_ref)
         return 0
 
     lax.fori_loop(0, BLOCK // PAIRS, body, 0)
-    lat_filter((0,), rows, prm, u_ref, e_ref, p_ref)
-
-
-def lon_filter(prm, rb, o_ref, el_ref, put, at):
+    lat_filter((0,), rows, prm, w_ref, u_ref, e_ref, p_ref)
+
+
+def lon_filter(prm, rb, turn, o_ref, el_ref, put, at):
     half = o_ref.shape[1]
     nv = len(ORDER)
     decay = [prm[v, 1:2, :] for v in ORDER]
@@ -338,7 +348,7 @@
         for k in range(nv):
             o_ref[k, j] = values[k]
 
-    edges = cascade(half, load, store, decay, [jnp.zeros((rb, LANES), f32)] * nv)
+    edges = cascade(half, turn, load, store, decay, [jnp.zeros((rb, LANES), f32)] * nv)
     low = low_lanes((rb, LANES))
     for k, v in enumerate(ORDER):
         span, k1, k2, k3 = constants(prm[v, 0:1, :], prm[v, 1:2, :], half)
@@ -361,16 +371,19 @@
 
 
 def lon_kernel(
-    rows, rb, prm, u_ref, w_hbm, o_hbm, el_ref, es_ref, px_ref, dot_ref, rx_ref, ry_ref, w_ref, o_ref, sems
+    rows, rb, prm, u_hbm, w_hbm, o_hbm, el_ref, es_ref, px_ref, dot_ref, rx_ref, ry_ref, u_all, w_ref, o_ref, sems
 ):
     g = pl.program_id(0)
-    half = u_ref.shape[2]
+    half = o_ref.shape[1]
     at = pl.ds(pl.multiple_of(g * rb, 8), rb)
-    load_w = pltpu.make_async_copy(w_hbm.at[:, :, at, :], w_ref, sems.at[0])
-    load_w.start()
+
+    def load_u(step):
+        return pltpu.make_async_copy(u_hbm.at[:, pl.ds(step * rb, rb)], u_all.at[step], sems.at[2 + step])
 
     @pl.when(g == 0)
     def _():
+        for step in range(rows // rb):
+            load_u(step).start()
         dot_ref[...] = jnp.zeros_like(dot_ref)
         for k, v in enumerate(ORDER):
             for e, r in enumerate(responses(prm[v, 0:1, :], prm[v, 1:2, :], half)):
@@ -378,19 +391,19 @@
             for e, r in enumerate(responses(prm[v, 0:1, :], prm[v, 1:2, :], rows)):
                 ry_ref[k, e] = r
 
-    def turn(b, _):
-        at = pl.ds(pl.multiple_of(b * 8, 8), 8)
-        for k in range(len(ORDER)):
-            for q in range(0, rb, 8):
-                o_ref[k, at, q : q + 8, :] = jnp.swapaxes(u_ref[k, q : q + 8, at, :], 0, 1)
-        return 0
-
-    lax.fori_loop(0, half // 8, turn, 0)
+    load_u(g).wait()
+    load_w = pltpu.make_async_copy(w_hbm.at[:, :, at, :], w_ref, sems.at[0])
+    load_w.start()
+    u_ref = u_all.at[g]
+
+    def turn(b):
+        cols = pl.ds(pl.multiple_of(b * 8, 8), 8)
+        return [jnp.swapaxes(u_ref[k, :, cols, :], 0, 1) for k in range(len(ORDER))]
 
     def put(i, x):
         es_ref[i, at, :] = x
 
-    lon_filter(prm, rb, o_ref, el_ref, put, at)
+    lon_filter(prm, rb, turn, o_ref, el_ref, put, at)
     store_o = pltpu.make_async_copy(o_ref, o_hbm.at[:, :, at, :], sems.at[1])
     store_o.start()
     load_w.wait()
@@ -443,7 +456,10 @@
     def put(i, x):
         es_ref[i] = x
 
-    lon_filter(prm, 8, o_ref, el_ref, put, slice(0, 8))
+    def turn(b):
+        return [o_ref[k, pl.ds(pl.multiple_of(b * 8, 8), 8)] for k in range(len(ORDER))]
+
+    lon_filter(prm, 8, turn, o_ref, el_ref, put, slice(0, 8))
     x = sigma[0]
     rows, lon = x.shape
     outer = jnp.where(low_lanes((rows, LANES)), x[:, 0:1], x[:, lon - 1 : lon])
@@ -748,7 +764,7 @@
         grid=(rows // rb,),
         in_specs=[
             full(prm.shape),
-            pl.BlockSpec((nvars, rb, half, LANES), lambda g: (0, g, 0, 0)),
+            anywhere,
             anywhere,
         ],
         out_specs=[
@@ -769,7 +785,9 @@
             pltpu.HBM((nvars, 4, half, LANES), f32),
             pltpu.HBM((nvars, 4, rows, LANES), f32),
         ],
-        scratch_shapes=[pltpu.VMEM((nvars, half, rb, LANES), f32)] * 2 + [pltpu.SemaphoreType.DMA((2,))],
+        scratch_shapes=[pltpu.VMEM((rows // rb, nvars, rb, half, LANES), f32)]
+        + [pltpu.VMEM((nvars, half, rb, LANES), f32)] * 2
+        + [pltpu.SemaphoreType.DMA((2 + rows // rb,))],
         compiler_params=params(),
         cost_estimate=pl.CostEstimate(
             flops=180000000, bytes_accessed=6 * rows * merged * 4, transcendentals=0

time: 105 us -> 107 us (1.019)
  Pallas kernels: 56.7 us -> 58 us
where the time goes in v12:
time: 107 us; the launch traced here: 106 us
  Pallas kernels  58 us (54%)
  starting transfers between devices  32.8 us (31%)
  waiting for transfers between devices  10.6 us (10%)
  local copies, waits for them, and re-layouts  2.76 us (3%)
    pallas_call x2, Pallas kernels, lat_call(): pl.pallas_call(body, grid=(steps,), in_specs=specs, out_specs=[pl.BlockSp...  23.1 us
    pallas_call x1, Pallas kernels, shards(): pl.pallas_call(functools.partial(end_kernel, rows, pairs, 24), grid=(half...  15.6 us
    all_to_all x3, starting transfers between devices, trade(): return lax.all_to_all(x, axis, split_axis=0, concat_axis=0, tiled=True)  13 us
    pallas_call x1, Pallas kernels, shards(): pl.pallas_call(functools.partial(lon_kernel, rows, rb), grid=(rows // rb,...  11.3 us
    ppermute x6, starting transfers between devices, round_lon(): lax.ppermute(x, 'lon', [(i, i ^ s) for i in range(n_lon)])  10.6 us
    ppermute x6, waiting for transfers between devices, round_lon(): lax.ppermute(x, 'lon', [(i, i ^ s) for i in range(n_lon)])  5.59 us
    all_to_all x3, waiting for transfers between devices, trade(): return lax.all_to_all(x, axis, split_axis=0, concat_axis=0, tiled=True)  4.96 us
    pallas_call x1, Pallas kernels, shards(): pl.pallas_call(functools.partial(close_kernel, n_lon, rows, devices, capa...  4.55 us
  transfers between devices with their start and end apart: 13, of which 3 were waited for; matrix products, arithmetic and copies ran while one was open for 1% of the time, Pallas kernels for 39%

profile of v12, /device:TPU:0, one launch (start us, length us, event | category | flops | bytes accessed | tf_op | source)
XLA Modules:
  0.0 105.9 jit_solution(3770005455135350433)
XLA Ops:
  0.6 1.2 %slice_bitcast_fusion = (f32[1,12288]{1,0:T(1,128)S(1)}, f32[1,12288]{1,0:T(1,128)S(1)}) fusion(f32[3,48,12288]{2,1,0:T(8,128)} %thr.1), kind=kLoop, calls=%fused_computation.5 | loop fusion | bytes 196608 | tf_op jit(solution)/shard_map/squeeze | solution.py:692
  1.8 0.7 slice_bitcast_fusion.4
  2.6 2.4 %collective-permute-start = (f32[1,12480]{1,0:T(1,128)S(1)}, f32[1,12480]{1,0:T(1,128)S(1)}, u32[]{:S(2)}, u32[]{:S(2)}) collective-permute-start(f32[1,12480]{1,0:T(1,128)S(1)} %pad_maximum_fusion), channel_id=1, source_target_pairs={{0,4},{4,8},{8,12},{12,16},{16,20},{20,24},{24,28},{1,5},{5,9},{9,... | collective-permute-start | bytes 149768 | tf_op jit(solution)/shard_map/ppermute | solution.py:694
  5.0 1.3 %collective-permute-start.1 = (f32[1,12480]{1,0:T(1,128)S(1)}, f32[1,12480]{1,0:T(1,128)S(1)}, u32[]{:S(2)}, u32[]{:S(2)}) collective-permute-start(f32[1,12480]{1,0:T(1,128)S(1)} %pad_maximum_fusion.1), channel_id=1, source_target_pairs={{4,0},{8,4},{12,8},{16,12},{20,16},{24,20},{28,24},{5,1},{9,5},{13... | collective-permute-start | bytes 149768 | tf_op jit(solution)/shard_map/ppermute | solution.py:695
  6.3 0.8 slice_bitcast_fusion.2
  7.1 4.3 %collective-permute-start.2 = (f32[48,64]{1,0:T(8,128)S(1)}, f32[48,64]{1,0:T(8,128)S(1)}, u32[]{:S(2)}, u32[]{:S(2)}) collective-permute-start(f32[48,64]{1,0:T(8,128)S(1)} %get-tuple-element.53), channel_id=1, source_target_pairs={{0,1},{1,2},{2,3},{4,5},{5,6},{6,7},{8,9},{9,10},{10,11},{12,13},{... | collective-permute-start | bytes 36872 | tf_op jit(solution)/shard_map/ppermute | solution.py:696
  11.5 1.3 %collective-permute-start.3 = (f32[48,64]{1,0:T(8,128)S(1)}, f32[48,64]{1,0:T(8,128)S(1)}, u32[]{:S(2)}, u32[]{:S(2)}) collective-permute-start(f32[48,64]{1,0:T(8,128)S(1)} %get-tuple-element.52), channel_id=1, source_target_pairs={{1,0},{2,1},{3,2},{5,4},{6,5},{7,6},{9,8},{10,9},{11,10},{13,12},{... | collective-permute-start | bytes 36872 | tf_op jit(solution)/shard_map/ppermute | solution.py:697
  12.8 11.9 %lat_chi_temp.1 = (f32[3,96,48,128]{3,2,1,0:T(8,128)}, f32[3,48,96,128]{3,2,1,0:T(8,128)}, f32[8,3,48,128]{3,2,1,0:T(8,128)}, f32[3,96,8,128]{3,2,1,0:T(8,128)}, f32[3,4,128]{2,1,0:T(4,128)S(1)}) custom-call(f32[1,8]{1,0:T(1,128)} %bitcast.26, s32[1,192]{1,0:T(1,128)} %bitcast.24, f32[1,64]{1,0:T(1,128)} %bitcast.27, f32[3,48,192]{2,1,0:T(8,128)} %sigma.7, ...), custom_call_target="tpu_custom_call" | custom-call | flops 120000000 | bytes 14155776 | tf_op jit(solution)/shard_map/lat_chi_temp/pallas_call | solution.py:711
  24.7 0.0 copy-start
  24.7 0.0 collective-permute-done.2.west
  24.7 0.0 collective-permute-done.3.east
  24.7 0.0 collective-permute-done.north
  24.7 0.0 copy-start.1
  24.7 0.0 collective-permute-done.1.south
  24.7 0.0 copy-start.2
  24.7 11.2 %lat_psi.1 = (f32[3,96,48,128]{3,2,1,0:T(8,128)}, f32[3,48,96,128]{3,2,1,0:T(8,128)}, f32[8,3,48,128]{3,2,1,0:T(8,128)}, f32[3,96,8,128]{3,2,1,0:T(8,128)}) custom-call(f32[3,4,128]{2,1,0:T(4,128)S(1)} %get-tuple-element.27.prm, f32[3,48,192]{2,1,0:T(8,128)} %sigma.7, ...), custom_call_target="tpu_custom_call", output_to_operand_aliasing={{0}: (18, {}), {1}: (19, {}), {2}: (20, {}), {3}: (21, {})} | custom-call | flops 60000000 | bytes 7077888 | tf_op jit(solution)/shard_map/lat_psi/pallas_call | solution.py:711
  35.9 0.0 copy-done.1
  35.9 0.0 copy-done.2
  36.0 6.3 %all-to-all-start = ((f32[8,3,48,128]{3,2,1,0:T(8,128)}), f32[8,3,48,128]{3,2,1,0:T(8,128)S(1)}, u32[]{:S(2)}, u32[]{:S(2)}) async-start(f32[8,3,48,128]{3,2,1,0:T(8,128)} %get-tuple-element.32), calls=%async_computation | async-start | bytes 1179648 | tf_op jit(solution)/shard_map/all_to_all | solution.py:757
  42.2 0.0 copy-start.3
  42.2 11.3 %lon_tile.1 = (f32[3,96,48,128]{3,2,1,0:T(8,128)}, f32[3,4,48,128]{3,2,1,0:T(8,128)}, f32[6,48,128]{2,1,0:T(8,128)S(1)}, f32[3,4,48,128]{3,2,1,0:T(8,128)}, f32[...) custom-call(f32[3,4,128]{2,1,0:T(4,128)S(1)} %get-tuple-element.27.prm, ...), custom_call_target="tpu_custom_call" | custom-call | flops 180000000 | bytes 14155776 | tf_op jit(solution)/shard_map/lon_tile/pallas_call | solution.py:762
  53.6 0.0 all-to-all-done.edges
  53.6 1.0 solve.1
  54.5 4.2 %all-to-all-start.1 = ((f32[8,3,48,128]{3,2,1,0:T(8,128)}), f32[8,3,48,128]{3,2,1,0:T(8,128)S(1)}, u32[]{:S(2)}, u32[]{:S(2)}) async-start(f32[8,3,48,128]{3,2,1,0:T(8,128)} %solve.1), calls=%async_computation.1 | async-start | bytes 1179648 | tf_op jit(solution)/shard_map/all_to_all | solution.py:757
  58.7 0.0 copy-done.3
  58.7 0.2 convert_reduce_fusion
  58.9 2.7 %collective-permute-start.4 = (f32[6,48,128]{2,1,0:T(8,128)S(1)}, f32[6,48,128]{2,1,0:T(8,128)S(1)}, u32[]{:S(2)}, u32[]{:S(2)}) collective-permute-start(f32[6,48,128]{2,1,0:T(8,128)S(1)} %get-tuple-element.35.rest_0_), channel_id=1, source_target_pairs={{0,1},{1,0},{2,3},{3,2},{4,5},{5,4},{6,7},{7,6},{8,9},{9,8},{10,11... | collective-permute-start | bytes 442376 | tf_op jit(solution)/shard_map/ppermute | solution.py:800
  61.6 2.6 %collective-permute-start.5 = (f32[6,48,128]{2,1,0:T(8,128)S(1)}, f32[6,48,128]{2,1,0:T(8,128)S(1)}, u32[]{:S(2)}, u32[]{:S(2)}) collective-permute-start(f32[6,48,128]{2,1,0:T(8,128)S(1)} %get-tuple-element.35.rest_0_), channel_id=1, source_target_pairs={{0,2},{1,3},{2,0},{3,1},{4,6},{5,7},{6,4},{7,5},{8,10},{9,11},{10,... | collective-permute-start | bytes 442376 | tf_op jit(solution)/shard_map/ppermute | solution.py:800
  64.2 0.0 collective-permute-start.6
  64.2 5.0 %all-to-all-done.1.carries = f32[8,3,48,128]{3,2,1,0:T(8,128)S(1)} async-done(((f32[8,3,48,128]{3,2,1,0:T(8,128)}), f32[8,3,48,128]{3,2,1,0:T(8,128)S(1)}, u32[]{:S(2)}, u32[]{:S(2)}) %all-to-all-start.1) | async-done | bytes 589856 | tf_op jit(solution)/shard_map/all_to_all | solution.py:757
  69.2 2.4 %lon_carry.1 = (f32[3,96,8,128]{3,2,1,0:T(8,128)S(1)}, f32[3,4,8,128]{3,2,1,0:T(8,128)S(1)}, f32[7,8,128]{2,1,0:T(8,128)S(1)}) custom-call(f32[3,4,128]{2,1,0:T(4,128)S(1)} %get-tuple-element.27.prm, f32[3,48,192]{2,1,0:T(8,128)} %sigma.7, f32[8,3,48,128]{3,2,1,0:T(8,128)S(1)} %all-to-all-done.1.carries), custom_call_target="tpu_custom_call" | custom-call | flops 30000000 | bytes 1769472 | tf_op jit(solution)/shard_map/lon_carry/pallas_call | solution.py:817
  71.6 2.7 %collective-permute-start.7 = (f32[7,8,128]{2,1,0:T(8,128)S(1)}, f32[7,8,128]{2,1,0:T(8,128)S(1)}, u32[]{:S(2)}, u32[]{:S(2)}) collective-permute-start(f32[7,8,128]{2,1,0:T(8,128)S(1)} %get-tuple-element.45.rest_4_), channel_id=1, source_target_pairs={{0,1},{1,0},{2,3},{3,2},{4,5},{5,4},{6,7},{7,6},{8,9},{9,8},{10,11... | collective-permute-start | bytes 86024 | tf_op jit(solution)/shard_map/ppermute | solution.py:800
  74.3 2.6 %collective-permute-start.8 = (f32[7,8,128]{2,1,0:T(8,128)S(1)}, f32[7,8,128]{2,1,0:T(8,128)S(1)}, u32[]{:S(2)}, u32[]{:S(2)}) collective-permute-start(f32[7,8,128]{2,1,0:T(8,128)S(1)} %get-tuple-element.45.rest_4_), channel_id=1, source_target_pairs={{0,2},{1,3},{2,0},{3,1},{4,6},{5,7},{6,4},{7,5},{8,10},{9,11},{10,... | collective-permute-start | bytes 86024 | tf_op jit(solution)/shard_map/ppermute | solution.py:800
  76.9 0.0 collective-permute-done.4.rest_1_
  76.9 0.0 collective-permute-start.9
  76.9 0.1 pad_add_fusion.place
  77.0 0.0 collective-permute-done.5.rest_2_
  77.0 0.0 collective-permute-done.6.rest_3_
  77.0 0.0 collective-permute-done.7.rest_5_
  77.0 2.9 %collective-permute-done.8.rest_6_ = f32[7,8,128]{2,1,0:T(8,128)S(1)} collective-permute-done((f32[7,8,128]{2,1,0:T(8,128)S(1)}, f32[7,8,128]{2,1,0:T(8,128)S(1)}, u32[]{:S(2)}, u32[]{:S(2)}) %collective-permute-start.8) | collective-permute-done | bytes 28704 | tf_op jit(solution)/shard_map/ppermute | solution.py:800
  79.9 2.6 %collective-permute-done.9.rest_7_ = f32[7,8,128]{2,1,0:T(8,128)S(1)} collective-permute-done((f32[7,8,128]{2,1,0:T(8,128)S(1)}, f32[7,8,128]{2,1,0:T(8,128)S(1)}, u32[]{:S(2)}, u32[]{:S(2)}) %collective-permute-start.9) | collective-permute-done | bytes 28704 | tf_op jit(solution)/shard_map/ppermute | solution.py:800
  82.6 0.0 copy-done
  82.6 4.6 %close.1 = (f32[3,4,48,128]{3,2,1,0:T(8,128)}, f32[3,96,8,128]{3,2,1,0:T(8,128)}, f32[2,48,128]{2,1,0:T(8,128)}, f32[2,48,128]{2,1,0:T(8,128)}, f32[32,128]{1,0:T(8,128)}) custom-call(s32[2]{0:T(128)S(1)} %pad_add_fusion.place, s32[1,192]{1,0:T(1,128)S(1)} %bitcast.23, f32[3,4,128]{2,1,0:T(4,128)S(1)} %get-tuple-element.27.prm, ...), custom_call_target="tpu_custom_call" | custom-call | flops 10000000 | bytes 4000000 | tf_op jit(solution)/shard_map/close/pallas_call | solution.py:849
  87.1 2.5 %all-to-all-start.2 = ((f32[32,1,128]{2,1,0:T(1,128)}), f32[32,1,128]{2,1,0:T(1,128)S(1)}, u32[]{:S(2)}, u32[]{:S(2)}) async-start(f32[32,1,128]{2,1,0:T(1,128)} %bitcast.13), calls=%async_computation.2 | async-start | bytes 32768 | tf_op jit(solution)/shard_map/all_to_all | solution.py:757
  89.7 15.6 %finish.1 = f32[3,48,12288]{2,1,0:T(8,128)} custom-call(s32[2]{0:T(128)S(1)} %pad_add_fusion.place, f32[3,4,128]{2,1,0:T(4,128)} %copy-done, f32[3,48,192]{2,1,0:T(8,128)} %sigma.7, f32[1,12480]{1,0:T(1,128)} %copy-done.1, f32[1,12480]{1,0:T(1,128)} %copy-done.2, f32[3,64,64]{2,1,0:T(8,128)} %vert.5, f32[64,64]{1,0:T(8,128)} %bal.3, ...), custom_call_target="tpu_custom_call" | custom-call | flops 300000000 | bytes 14155776 | tf_op jit(solution)/shard_map/finish/pallas_call | solution.py:868
  105.3 0.0 all-to-all-done.2
  105.3 0.6 reduce_sum.19
  (3 shorter events, 0.1 us)
Async XLA Ops:
  2.6 22.1 %collective-permute-start = (f32[1,12480]{1,0:T(1,128)S(1)}, f32[1,12480]{1,0:T(1,128)S(1)}, u32[]{:S(2)}, u32[]{:S(2)}) collective-permute-start(f32[1,12480]{1,0:T(1,128)S(1)} %pad_maximum_fusion), channel_id=1, source_target_pairs={{0,4},{4,8},{8,12},{12,16},{16,20},{20,24},{24,28},{1,5},{5,9},{9,... | collective-permute-start | bytes 149768 | tf_op jit(solution)/shard_map/ppermute | solution.py:694
  5.0 19.7 %collective-permute-start.1 = (f32[1,12480]{1,0:T(1,128)S(1)}, f32[1,12480]{1,0:T(1,128)S(1)}, u32[]{:S(2)}, u32[]{:S(2)}) collective-permute-start(f32[1,12480]{1,0:T(1,128)S(1)} %pad_maximum_fusion.1), channel_id=1, source_target_pairs={{4,0},{8,4},{12,8},{16,12},{20,16},{24,20},{28,24},{5,1},{9,5},{13... | collective-permute-start | bytes 149768 | tf_op jit(solution)/shard_map/ppermute | solution.py:695
  7.1 17.5 %collective-permute-start.2 = (f32[48,64]{1,0:T(8,128)S(1)}, f32[48,64]{1,0:T(8,128)S(1)}, u32[]{:S(2)}, u32[]{:S(2)}) collective-permute-start(f32[48,64]{1,0:T(8,128)S(1)} %get-tuple-element.53), channel_id=1, source_target_pairs={{0,1},{1,2},{2,3},{4,5},{5,6},{6,7},{8,9},{9,10},{10,11},{12,13},{... | collective-permute-start | bytes 36872 | tf_op jit(solution)/shard_map/ppermute | solution.py:696
  11.5 13.2 %collective-permute-start.3 = (f32[48,64]{1,0:T(8,128)S(1)}, f32[48,64]{1,0:T(8,128)S(1)}, u32[]{:S(2)}, u32[]{:S(2)}) collective-permute-start(f32[48,64]{1,0:T(8,128)S(1)} %get-tuple-element.52), channel_id=1, source_target_pairs={{1,0},{2,1},{3,2},{5,4},{6,5},{7,6},{9,8},{10,9},{11,10},{13,12},{... | collective-permute-start | bytes 36872 | tf_op jit(solution)/shard_map/ppermute | solution.py:697
  24.7 57.9 %copy-start = (f32[3,4,128]{2,1,0:T(4,128)}, f32[3,4,128]{2,1,0:T(4,128)S(1)}, u32[]{:S(2)}) copy-start(f32[3,4,128]{2,1,0:T(4,128)S(1)} %get-tuple-element.27.prm) | copy-start | bytes 18436
  24.7 11.2 %copy-start.1 = (f32[1,12480]{1,0:T(1,128)}, f32[1,12480]{1,0:T(1,128)S(1)}, u32[]{:S(2)}) copy-start(f32[1,12480]{1,0:T(1,128)S(1)} %collective-permute-done.north) | copy-start | bytes 149764
  24.7 11.2 %copy-start.2 = (f32[1,12480]{1,0:T(1,128)}, f32[1,12480]{1,0:T(1,128)S(1)}, u32[]{:S(2)}) copy-start(f32[1,12480]{1,0:T(1,128)S(1)} %collective-permute-done.1.south) | copy-start | bytes 149764
  36.0 17.6 %all-to-all-start = ((f32[8,3,48,128]{3,2,1,0:T(8,128)}), f32[8,3,48,128]{3,2,1,0:T(8,128)S(1)}, u32[]{:S(2)}, u32[]{:S(2)}) async-start(f32[8,3,48,128]{3,2,1,0:T(8,128)} %get-tuple-element.32), calls=%async_computation | async-start | bytes 1179648 | tf_op jit(solution)/shard_map/all_to_all | solution.py:757
  42.2 16.5 %copy-start.3 = (s32[192]{0:T(256)S(1)}, s32[192]{0:T(256)}, u32[]{:S(2)}) copy-start(s32[192]{0:T(256)} %param.15) | copy-start | bytes 2308
  54.5 14.6 %all-to-all-start.1 = ((f32[8,3,48,128]{3,2,1,0:T(8,128)}), f32[8,3,48,128]{3,2,1,0:T(8,128)S(1)}, u32[]{:S(2)}, u32[]{:S(2)}) async-start(f32[8,3,48,128]{3,2,1,0:T(8,128)} %solve.1), calls=%async_computation.1 | async-start | bytes 1179648 | tf_op jit(solution)/shard_map/all_to_all | solution.py:757
  58.9 18.0 %collective-permute-start.4 = (f32[6,48,128]{2,1,0:T(8,128)S(1)}, f32[6,48,128]{2,1,0:T(8,128)S(1)}, u32[]{:S(2)}, u32[]{:S(2)}) collective-permute-start(f32[6,48,128]{2,1,0:T(8,128)S(1)} %get-tuple-element.35.rest_0_), channel_id=1, source_target_pairs={{0,1},{1,0},{2,3},{3,2},{4,5},{5,4},{6,7},{7,6},{8,9},{9,8},{10,11... | collective-permute-start | bytes 442376 | tf_op jit(solution)/shard_map/ppermute | solution.py:800
  61.6 15.3 %collective-permute-start.5 = (f32[6,48,128]{2,1,0:T(8,128)S(1)}, f32[6,48,128]{2,1,0:T(8,128)S(1)}, u32[]{:S(2)}, u32[]{:S(2)}) collective-permute-start(f32[6,48,128]{2,1,0:T(8,128)S(1)} %get-tuple-element.35.rest_0_), channel_id=1, source_target_pairs={{0,2},{1,3},{2,0},{3,1},{4,6},{5,7},{6,4},{7,5},{8,10},{9,11},{10,... | collective-permute-start | bytes 442376 | tf_op jit(solution)/shard_map/ppermute | solution.py:800
  64.2 12.8 %collective-permute-start.6 = (f32[6,48,128]{2,1,0:T(8,128)S(1)}, f32[6,48,128]{2,1,0:T(8,128)S(1)}, u32[]{:S(2)}, u32[]{:S(2)}) collective-permute-start(f32[6,48,128]{2,1,0:T(8,128)S(1)} %get-tuple-element.35.rest_0_), channel_id=1, source_target_pairs={{0,3},{1,2},{2,1},{3,0},{4,7},{5,6},{6,5},{7,4},{8,11},{9,10},{10,... | collective-permute-start | bytes 442376 | tf_op jit(solution)/shard_map/ppermute | solution.py:800
  71.6 5.4 %collective-permute-start.7 = (f32[7,8,128]{2,1,0:T(8,128)S(1)}, f32[7,8,128]{2,1,0:T(8,128)S(1)}, u32[]{:S(2)}, u32[]{:S(2)}) collective-permute-start(f32[7,8,128]{2,1,0:T(8,128)S(1)} %get-tuple-element.45.rest_4_), channel_id=1, source_target_pairs={{0,1},{1,0},{2,3},{3,2},{4,5},{5,4},{6,7},{7,6},{8,9},{9,8},{10,11... | collective-permute-start | bytes 86024 | tf_op jit(solution)/shard_map/ppermute | solution.py:800
  74.3 5.6 %collective-permute-start.8 = (f32[7,8,128]{2,1,0:T(8,128)S(1)}, f32[7,8,128]{2,1,0:T(8,128)S(1)}, u32[]{:S(2)}, u32[]{:S(2)}) collective-permute-start(f32[7,8,128]{2,1,0:T(8,128)S(1)} %get-tuple-element.45.rest_4_), channel_id=1, source_target_pairs={{0,2},{1,3},{2,0},{3,1},{4,6},{5,7},{6,4},{7,5},{8,10},{9,11},{10,... | collective-permute-start | bytes 86024 | tf_op jit(solution)/shard_map/ppermute | solution.py:800
  76.9 5.7 %collective-permute-start.9 = (f32[7,8,128]{2,1,0:T(8,128)S(1)}, f32[7,8,128]{2,1,0:T(8,128)S(1)}, u32[]{:S(2)}, u32[]{:S(2)}) collective-permute-start(f32[7,8,128]{2,1,0:T(8,128)S(1)} %get-tuple-element.45.rest_4_), channel_id=1, source_target_pairs={{0,3},{1,2},{2,1},{3,0},{4,7},{5,6},{6,5},{7,4},{8,11},{9,10},{10,... | collective-permute-start | bytes 86024 | tf_op jit(solution)/shard_map/ppermute | solution.py:800
  87.1 18.2 %all-to-all-start.2 = ((f32[32,1,128]{2,1,0:T(1,128)}), f32[32,1,128]{2,1,0:T(1,128)S(1)}, u32[]{:S(2)}, u32[]{:S(2)}) async-start(f32[32,1,128]{2,1,0:T(1,128)} %bitcast.13), calls=%async_computation.2 | async-start | bytes 32768 | tf_op jit(solution)/shard_map/all_to_all | solution.py:757

commit v13 on v11

--- a/solution.py
+++ b/solution.py
@@ -361,17 +361,14 @@
 
 
 def lon_kernel(
-    rows, rb, prm, u_ref, w_hbm, o_hbm, el_ref, es_ref, px_ref, dot_ref, rx_ref, ry_ref, w_ref, o_ref, sems
+    rows, rb, prm, u_ref, o_ref, el_ref, es_ref, rx_ref, ry_ref
 ):
     g = pl.program_id(0)
     half = u_ref.shape[2]
     at = pl.ds(pl.multiple_of(g * rb, 8), rb)
-    load_w = pltpu.make_async_copy(w_hbm.at[:, :, at, :], w_ref, sems.at[0])
-    load_w.start()
 
     @pl.when(g == 0)
     def _():
-        dot_ref[...] = jnp.zeros_like(dot_ref)
         for k, v in enumerate(ORDER):
             for e, r in enumerate(responses(prm[v, 0:1, :], prm[v, 1:2, :], half)):
                 rx_ref[k, e] = r
@@ -391,28 +388,29 @@
         es_ref[i, at, :] = x
 
     lon_filter(prm, rb, o_ref, el_ref, put, at)
-    store_o = pltpu.make_async_copy(o_ref, o_hbm.at[:, :, at, :], sems.at[1])
-    store_o.start()
-    load_w.wait()
-    zero = jnp.zeros((rb, LANES), f32)
+
+
+def energy_kernel(rows, rq, w_ref, u_ref, rx_ref, px_ref, dot_ref):
+    g = pl.program_id(0)
+    count = w_ref.shape[1]
+
+    @pl.when(g == 0)
+    def _():
+        px_ref[...] = jnp.zeros_like(px_ref)
+        dot_ref[...] = jnp.zeros_like(dot_ref)
+
     for k in range(len(ORDER)):
-
-        def body(b, sums, k=k):
-            base = pl.multiple_of(b * 8, 8)
-            rx = [rx_ref[k, e, pl.ds(base, 8), :] for e in range(4)]
-            sums = list(sums)
-            for o in range(8):
-                x = w_ref[k, base + o]
-                sums[4] = sums[4] + x * o_ref[k, base + o]
+        rx = [rx_ref[k, e, pl.ds(pl.multiple_of(g * count, 8), count), :] for e in range(4)]
+        for q in range(0, rows, rq):
+            sums = [px_ref[k, e, q : q + rq, :] for e in range(4)] + [jnp.zeros((rq, LANES), f32)]
+            for p in range(count):
+                x = w_ref[k, p, q : q + rq, :]
+                sums[4] = sums[4] + x * u_ref[k, p, q : q + rq, :]
                 for e in range(4):
-                    sums[e] = sums[e] + x * rx[e][o : o + 1, :]
-            return tuple(sums)
-
-        sums = lax.fori_loop(0, half // 8, body, (zero,) * 5)
-        for e in range(4):
-            px_ref[k, e, at, :] = sums[e]
-        dot_ref[k] += jnp.sum(sums[4].reshape(rb // 8, 8, LANES), axis=0)
-    store_o.wait()
+                    sums[e] = sums[e] + x * rx[e][p : p + 1, :]
+            for e in range(4):
+                px_ref[k, e, q : q + rq, :] = sums[e]
+            dot_ref[k] += jnp.sum(sums[4].reshape(rq // 8, 8, LANES), axis=0)
 
 
 def solve_kernel(n_lat, rows, prm, edges, carries):
@@ -743,20 +741,17 @@
     shares = trade(edges, "lat")
 
     rb = BLOCK
-    local, el, es, px, dots, rx, ry = pl.pallas_call(
+    local, el, es, rx, ry = pl.pallas_call(
         functools.partial(lon_kernel, rows, rb),
         grid=(rows // rb,),
         in_specs=[
             full(prm.shape),
             pl.BlockSpec((nvars, rb, half, LANES), lambda g: (0, g, 0, 0)),
-            anywhere,
         ],
         out_specs=[
-            anywhere,
+            pl.BlockSpec((nvars, half, rb, LANES), lambda g: (0, 0, g, 0)),
             full((nvars, 4, rows, LANES)),
             full((6, rows, LANES)),
-            full((nvars, 4, rows, LANES)),
-            full((nvars, 8, LANES)),
             full((nvars, 4, half, LANES)),
             full((nvars, 4, rows, LANES)),
         ],
@@ -764,18 +759,15 @@
             pltpu.HBM((nvars, half, rows, LANES), f32),
             pltpu.HBM((nvars, 4, rows, LANES), f32),
             jax.ShapeDtypeStruct((6, rows, LANES), f32),
-            pltpu.HBM((nvars, 4, rows, LANES), f32),
-            pltpu.HBM((nvars, 8, LANES), f32),
             pltpu.HBM((nvars, 4, half, LANES), f32),
             pltpu.HBM((nvars, 4, rows, LANES), f32),
         ],
-        scratch_shapes=[pltpu.VMEM((nvars, half, rb, LANES), f32)] * 2 + [pltpu.SemaphoreType.DMA((2,))],
         compiler_params=params(),
         cost_estimate=pl.CostEstimate(
             flops=180000000, bytes_accessed=6 * rows * merged * 4, transcendentals=0
         ),
         name="lon_tile",
-    )(prm, *[in_hbm(x) for x in (u, w)])
+    )(prm, in_hbm(u))
 
     def round_lon(x):
         return [x] + [
@@ -795,6 +787,23 @@
         name="solve",
     )(prm, shares)
     carries = trade(carries, "lat")
+
+    packed = 2 * PAIRS
+
+    def columns(r):
+        return pl.BlockSpec((nvars, packed, r, LANES), lambda g: (0, g, 0, 0))
+
+    px, dots = pl.pallas_call(
+        functools.partial(energy_kernel, rows, 24),
+        grid=(half // packed,),
+        in_specs=[columns(rows), columns(rows), full(rx.shape)],
+        out_specs=[full((nvars, 4, rows, LANES)), full((nvars, 8, LANES))],
+        out_shape=[pltpu.HBM((nvars, 4, rows, LANES), f32), pltpu.HBM((nvars, 8, LANES), f32)],
+        compiler_params=params(),
+        cost_estimate=pl.CostEstimate(flops=20000000, bytes_accessed=6 * rows * merged * 4, transcendentals=0),
+        name="energy",
+    )(in_hbm(w), in_hbm(local), in_hbm(rx))
+    carries, _ = lax.optimization_barrier((carries, px))
 
     crossed, elc, esc = pl.pallas_call(
         carry_kernel,
@@ -813,11 +822,6 @@
         name="lon_carry",
     )(prm, in_hbm(sigma), carries)
     sent_x = round_lon(esc)
-
-    packed = 2 * PAIRS
-
-    def columns(r):
-        return pl.BlockSpec((nvars, packed, r, LANES), lambda g: (0, g, 0, 0))
 
     index = jnp.arange(count, dtype=jnp.int32)
     same = (owner[:, None] == owner[None, :]) & (index[None, :] < index[:, None])

time: 105 us -> 107 us (1.019)
  Pallas kernels: 56.7 us -> 62.7 us
  waiting for transfers between devices: 10.6 us -> 7.34 us
    pallas_call x0 -> x1, Pallas kernels: none -> 8.2 us  [shards(): pl.pallas_call(functools.partial(energy_kernel, rows, 24), grid=(half //...]
    all_to_all x3, waiting for transfers between devices: 4.96 us -> 1.75 us  [trade(): return lax.all_to_all(x, axis, split_axis=0, concat_axis=0, tiled=True)]
    pallas_call x1, Pallas kernels: 11 us -> 8.7 us  [shards(): pl.pallas_call(functools.partial(lon_kernel, rows, rb), grid=(rows // rb,...]
  transfers between devices with their start and end apart: 13 -> 13, of which waited for: 3 -> 3; matrix products, arithmetic and copies ran while one was open for 1% -> 1% of each run, Pallas kernels for 39% -> 43%
where the time goes in v13:
time: 107 us
  Pallas kernels  62.7 us (59%)
  starting transfers between devices  32 us (30%)
  waiting for transfers between devices  7.34 us (7%)
  local copies, waits for them, and re-layouts  2.76 us (3%)
    pallas_call x2, Pallas kernels, lat_call(): pl.pallas_call(body, grid=(steps,), in_specs=specs, out_specs=[pl.BlockSp...  22.2 us
    pallas_call x1, Pallas kernels, shards(): pl.pallas_call(functools.partial(end_kernel, rows, pairs, 24), grid=(half...  15.6 us
    all_to_all x3, starting transfers between devices, trade(): return lax.all_to_all(x, axis, split_axis=0, concat_axis=0, tiled=True)  13 us
    ppermute x6, starting transfers between devices, round_lon(): lax.ppermute(x, 'lon', [(i, i ^ s) for i in range(n_lon)])  9.76 us
    pallas_call x1, Pallas kernels, shards(): pl.pallas_call(functools.partial(lon_kernel, rows, rb), grid=(rows // rb,...  8.7 us
    pallas_call x1, Pallas kernels, shards(): pl.pallas_call(functools.partial(energy_kernel, rows, 24), grid=(half //...  8.2 us
    ppermute x6, waiting for transfers between devices, round_lon(): lax.ppermute(x, 'lon', [(i, i ^ s) for i in range(n_lon)])  5.57 us
    pallas_call x1, Pallas kernels, shards(): pl.pallas_call(functools.partial(close_kernel, n_lon, rows, devices, capa...  4.6 us
  transfers between devices with their start and end apart: 13, of which 3 were waited for; matrix products, arithmetic and copies ran while one was open for 1% of the time, Pallas kernels for 43%

profile of v13, /device:TPU:0, one launch (start us, length us, event | category | flops | bytes accessed | tf_op | source)
XLA Modules:
  0.0 106.5 jit_solution(8541455497741021922)
XLA Ops:
  0.6 1.2 %slice_bitcast_fusion = (f32[1,12288]{1,0:T(1,128)S(1)}, f32[1,12288]{1,0:T(1,128)S(1)}) fusion(f32[3,48,12288]{2,1,0:T(8,128)} %thr.1), kind=kLoop, calls=%fused_computation.5 | loop fusion | bytes 196608 | tf_op jit(solution)/shard_map/squeeze | solution.py:674
  1.8 0.7 slice_bitcast_fusion.4
  2.6 2.4 %collective-permute-start = (f32[1,12480]{1,0:T(1,128)S(1)}, f32[1,12480]{1,0:T(1,128)S(1)}, u32[]{:S(2)}, u32[]{:S(2)}) collective-permute-start(f32[1,12480]{1,0:T(1,128)S(1)} %pad_maximum_fusion), channel_id=1, source_target_pairs={{0,4},{4,8},{8,12},{12,16},{16,20},{20,24},{24,28},{1,5},{5,9},{9,... | collective-permute-start | bytes 149768 | tf_op jit(solution)/shard_map/ppermute | solution.py:676
  5.0 1.3 %collective-permute-start.1 = (f32[1,12480]{1,0:T(1,128)S(1)}, f32[1,12480]{1,0:T(1,128)S(1)}, u32[]{:S(2)}, u32[]{:S(2)}) collective-permute-start(f32[1,12480]{1,0:T(1,128)S(1)} %pad_maximum_fusion.1), channel_id=1, source_target_pairs={{4,0},{8,4},{12,8},{16,12},{20,16},{24,20},{28,24},{5,1},{9,5},{13... | collective-permute-start | bytes 149768 | tf_op jit(solution)/shard_map/ppermute | solution.py:677
  6.3 0.8 slice_bitcast_fusion.2
  7.1 4.3 %collective-permute-start.2 = (f32[48,64]{1,0:T(8,128)S(1)}, f32[48,64]{1,0:T(8,128)S(1)}, u32[]{:S(2)}, u32[]{:S(2)}) collective-permute-start(f32[48,64]{1,0:T(8,128)S(1)} %get-tuple-element.55), channel_id=1, source_target_pairs={{0,1},{1,2},{2,3},{4,5},{5,6},{6,7},{8,9},{9,10},{10,11},{12,13},{... | collective-permute-start | bytes 36872 | tf_op jit(solution)/shard_map/ppermute | solution.py:678
  11.5 1.3 %collective-permute-start.3 = (f32[48,64]{1,0:T(8,128)S(1)}, f32[48,64]{1,0:T(8,128)S(1)}, u32[]{:S(2)}, u32[]{:S(2)}) collective-permute-start(f32[48,64]{1,0:T(8,128)S(1)} %get-tuple-element.54), channel_id=1, source_target_pairs={{1,0},{2,1},{3,2},{5,4},{6,5},{7,6},{9,8},{10,9},{11,10},{13,12},{... | collective-permute-start | bytes 36872 | tf_op jit(solution)/shard_map/ppermute | solution.py:679
  12.8 11.4 %lat_chi_temp.1 = (f32[3,96,48,128]{3,2,1,0:T(8,128)}, f32[3,48,96,128]{3,2,1,0:T(8,128)}, f32[8,3,48,128]{3,2,1,0:T(8,128)}, f32[3,96,8,128]{3,2,1,0:T(8,128)}, f32[3,4,128]{2,1,0:T(4,128)S(1)}) custom-call(f32[1,8]{1,0:T(1,128)} %bitcast.26, s32[1,192]{1,0:T(1,128)} %bitcast.24, f32[1,64]{1,0:T(1,128)} %bitcast.27, f32[3,48,192]{2,1,0:T(8,128)} %sigma.7, ...), custom_call_target="tpu_custom_call" | custom-call | flops 120000000 | bytes 14155776 | tf_op jit(solution)/shard_map/lat_chi_temp/pallas_call | solution.py:693
  24.1 0.0 copy-start
  24.1 0.0 collective-permute-done.2.west
  24.1 0.0 collective-permute-done.3.east
  24.1 0.0 collective-permute-done.north
  24.1 0.0 copy-start.1
  24.2 0.0 collective-permute-done.1.south
  24.2 0.0 copy-start.2
  24.2 10.9 %lat_psi.1 = (f32[3,96,48,128]{3,2,1,0:T(8,128)}, f32[3,48,96,128]{3,2,1,0:T(8,128)}, f32[8,3,48,128]{3,2,1,0:T(8,128)}, f32[3,96,8,128]{3,2,1,0:T(8,128)}) custom-call(f32[3,4,128]{2,1,0:T(4,128)S(1)} %get-tuple-element.28.prm, f32[3,48,192]{2,1,0:T(8,128)} %sigma.7, ...), custom_call_target="tpu_custom_call", output_to_operand_aliasing={{0}: (18, {}), {1}: (19, {}), {2}: (20, {}), {3}: (21, {})} | custom-call | flops 60000000 | bytes 7077888 | tf_op jit(solution)/shard_map/lat_psi/pallas_call | solution.py:693
  35.0 0.0 copy-done.1
  35.0 0.0 copy-done.2
  35.0 0.0 copy-start.3
  35.1 6.3 %all-to-all-start = ((f32[8,3,48,128]{3,2,1,0:T(8,128)}), f32[8,3,48,128]{3,2,1,0:T(8,128)S(1)}, u32[]{:S(2)}, u32[]{:S(2)}) async-start(f32[8,3,48,128]{3,2,1,0:T(8,128)} %get-tuple-element.33), calls=%async_computation | async-start | bytes 1179648 | tf_op jit(solution)/shard_map/all_to_all | solution.py:739
  41.3 8.7 %lon_tile.1 = (f32[3,96,48,128]{3,2,1,0:T(8,128)}, f32[3,4,48,128]{3,2,1,0:T(8,128)}, f32[6,48,128]{2,1,0:T(8,128)S(1)}, f32[3,4,96,128]{3,2,1,0:T(8,128)}, f32[3,4,48,128]{3,2,1,0:T(8,128)}) custom-call(f32[3,4,128]{2,1,0:T(4,128)S(1)} %get-tuple-element.28.prm, f32[3,48,96,128]{3,2,1,0:T(8,128)} %get-tuple-element.34.u_ref), custom_call_target="tpu_custom_call" | custom-call | flops 180000000 | bytes 14155776 | tf_op jit(solution)/shard_map/lon_tile/pallas_call | solution.py:744
  50.0 1.7 %all-to-all-done.edges = f32[8,3,48,128]{3,2,1,0:T(8,128)S(1)} async-done(((f32[8,3,48,128]{3,2,1,0:T(8,128)}), f32[8,3,48,128]{3,2,1,0:T(8,128)S(1)}, u32[]{:S(2)}, u32[]{:S(2)}) %all-to-all-start) | async-done | bytes 589856 | tf_op jit(solution)/shard_map/all_to_all | solution.py:739
  51.8 1.0 solve.1
  52.8 3.5 %all-to-all-start.1 = ((f32[8,3,48,128]{3,2,1,0:T(8,128)}), f32[8,3,48,128]{3,2,1,0:T(8,128)S(1)}, u32[]{:S(2)}, u32[]{:S(2)}) async-start(f32[8,3,48,128]{3,2,1,0:T(8,128)} %solve.1), calls=%async_computation.1 | async-start | bytes 1179648 | tf_op jit(solution)/shard_map/all_to_all | solution.py:739
  56.3 0.0 copy-done.3
  56.3 0.2 convert_reduce_fusion
  56.5 2.7 %collective-permute-start.4 = (f32[6,48,128]{2,1,0:T(8,128)S(1)}, f32[6,48,128]{2,1,0:T(8,128)S(1)}, u32[]{:S(2)}, u32[]{:S(2)}) collective-permute-start(f32[6,48,128]{2,1,0:T(8,128)S(1)} %get-tuple-element.35.rest_0_), channel_id=1, source_target_pairs={{0,1},{1,0},{2,3},{3,2},{4,5},{5,4},{6,7},{7,6},{8,9},{9,8},{10,11... | collective-permute-start | bytes 442376 | tf_op jit(solution)/shard_map/ppermute | solution.py:774
  59.2 2.6 %collective-permute-start.5 = (f32[6,48,128]{2,1,0:T(8,128)S(1)}, f32[6,48,128]{2,1,0:T(8,128)S(1)}, u32[]{:S(2)}, u32[]{:S(2)}) collective-permute-start(f32[6,48,128]{2,1,0:T(8,128)S(1)} %get-tuple-element.35.rest_0_), channel_id=1, source_target_pairs={{0,2},{1,3},{2,0},{3,1},{4,6},{5,7},{6,4},{7,5},{8,10},{9,11},{10,... | collective-permute-start | bytes 442376 | tf_op jit(solution)/shard_map/ppermute | solution.py:774
  61.8 0.0 collective-permute-start.6
  61.8 8.2 %energy.1 = (f32[3,4,48,128]{3,2,1,0:T(8,128)}, f32[3,8,128]{2,1,0:T(8,128)}) custom-call(f32[3,96,48,128]{3,2,1,0:T(8,128)} %get-tuple-element.37.w_ref, f32[3,96,48,128]{3,2,1,0:T(8,128)} %get-tuple-element.38.u_ref, f32[3,4,96,128]{3,2,1,0:T(8,128)} %get-tuple-element.39.rx_ref.rx), custom_call_target="tpu_custom_call" | custom-call | flops 20000000 | bytes 14155776 | tf_op jit(solution)/shard_map/energy/pallas_call | solution.py:796
  70.0 0.0 all-to-all-done.1.carries
  70.0 2.4 %lon_carry.1 = (f32[3,96,8,128]{3,2,1,0:T(8,128)S(1)}, f32[3,4,8,128]{3,2,1,0:T(8,128)S(1)}, f32[7,8,128]{2,1,0:T(8,128)S(1)}) custom-call(f32[3,4,128]{2,1,0:T(4,128)S(1)} %get-tuple-element.28.prm, f32[3,48,192]{2,1,0:T(8,128)} %sigma.7, f32[8,3,48,128]{3,2,1,0:T(8,128)S(1)} %all-to-all-done.1.carries), custom_call_target="tpu_custom_call" | custom-call | flops 30000000 | bytes 1769472 | tf_op jit(solution)/shard_map/lon_carry/pallas_call | solution.py:808
  72.4 0.9 collective-permute-start.7
  73.3 3.5 %collective-permute-start.8 = (f32[7,8,128]{2,1,0:T(8,128)S(1)}, f32[7,8,128]{2,1,0:T(8,128)S(1)}, u32[]{:S(2)}, u32[]{:S(2)}) collective-permute-start(f32[7,8,128]{2,1,0:T(8,128)S(1)} %get-tuple-element.48.rest_4_), channel_id=1, source_target_pairs={{0,2},{1,3},{2,0},{3,1},{4,6},{5,7},{6,4},{7,5},{8,10},{9,11},{10,... | collective-permute-start | bytes 86024 | tf_op jit(solution)/shard_map/ppermute | solution.py:774
  76.8 0.0 collective-permute-done.4.rest_1_
  76.8 0.0 collective-permute-start.9
  76.9 0.1 pad_add_fusion.place
  76.9 0.0 collective-permute-done.5.rest_2_
  76.9 0.0 collective-permute-done.6.rest_3_
  76.9 0.0 collective-permute-done.7.rest_5_
  76.9 2.2 %collective-permute-done.8.rest_6_ = f32[7,8,128]{2,1,0:T(8,128)S(1)} collective-permute-done((f32[7,8,128]{2,1,0:T(8,128)S(1)}, f32[7,8,128]{2,1,0:T(8,128)S(1)}, u32[]{:S(2)}, u32[]{:S(2)}) %collective-permute-start.8) | collective-permute-done | bytes 28704 | tf_op jit(solution)/shard_map/ppermute | solution.py:774
  79.2 3.3 %collective-permute-done.9.rest_7_ = f32[7,8,128]{2,1,0:T(8,128)S(1)} collective-permute-done((f32[7,8,128]{2,1,0:T(8,128)S(1)}, f32[7,8,128]{2,1,0:T(8,128)S(1)}, u32[]{:S(2)}, u32[]{:S(2)}) %collective-permute-start.9) | collective-permute-done | bytes 28704 | tf_op jit(solution)/shard_map/ppermute | solution.py:774
  82.5 0.0 copy-done
  82.5 4.6 %close.1 = (f32[3,4,48,128]{3,2,1,0:T(8,128)}, f32[3,96,8,128]{3,2,1,0:T(8,128)}, f32[2,48,128]{2,1,0:T(8,128)}, f32[2,48,128]{2,1,0:T(8,128)}, f32[32,128]{1,0:T(8,128)}) custom-call(s32[2]{0:T(128)S(1)} %pad_add_fusion.place, s32[1,192]{1,0:T(1,128)S(1)} %bitcast.23, f32[3,4,128]{2,1,0:T(4,128)S(1)} %get-tuple-element.28.prm, ...), custom_call_target="tpu_custom_call" | custom-call | flops 10000000 | bytes 4000000 | tf_op jit(solution)/shard_map/close/pallas_call | solution.py:835
  87.1 3.2 %all-to-all-start.2 = ((f32[32,1,128]{2,1,0:T(1,128)}), f32[32,1,128]{2,1,0:T(1,128)S(1)}, u32[]{:S(2)}, u32[]{:S(2)}) async-start(f32[32,1,128]{2,1,0:T(1,128)} %bitcast.13), calls=%async_computation.2 | async-start | bytes 32768 | tf_op jit(solution)/shard_map/all_to_all | solution.py:739
  90.3 15.6 %finish.1 = f32[3,48,12288]{2,1,0:T(8,128)} custom-call(s32[2]{0:T(128)S(1)} %pad_add_fusion.place, f32[3,4,128]{2,1,0:T(4,128)} %copy-done, f32[3,48,192]{2,1,0:T(8,128)} %sigma.7, f32[1,12480]{1,0:T(1,128)} %copy-done.1, f32[1,12480]{1,0:T(1,128)} %copy-done.2, f32[3,64,64]{2,1,0:T(8,128)} %vert.5, f32[64,64]{1,0:T(8,128)} %bal.3, ...), custom_call_target="tpu_custom_call" | custom-call | flops 300000000 | bytes 14155776 | tf_op jit(solution)/shard_map/finish/pallas_call | solution.py:854
  105.9 0.0 all-to-all-done.2
  106.0 0.6 reduce_sum.19
  (3 shorter events, 0.1 us)
Async XLA Ops:
  2.6 21.5 %collective-permute-start = (f32[1,12480]{1,0:T(1,128)S(1)}, f32[1,12480]{1,0:T(1,128)S(1)}, u32[]{:S(2)}, u32[]{:S(2)}) collective-permute-start(f32[1,12480]{1,0:T(1,128)S(1)} %pad_maximum_fusion), channel_id=1, source_target_pairs={{0,4},{4,8},{8,12},{12,16},{16,20},{20,24},{24,28},{1,5},{5,9},{9,... | collective-permute-start | bytes 149768 | tf_op jit(solution)/shard_map/ppermute | solution.py:676
  5.0 19.1 %collective-permute-start.1 = (f32[1,12480]{1,0:T(1,128)S(1)}, f32[1,12480]{1,0:T(1,128)S(1)}, u32[]{:S(2)}, u32[]{:S(2)}) collective-permute-start(f32[1,12480]{1,0:T(1,128)S(1)} %pad_maximum_fusion.1), channel_id=1, source_target_pairs={{4,0},{8,4},{12,8},{16,12},{20,16},{24,20},{28,24},{5,1},{9,5},{13... | collective-permute-start | bytes 149768 | tf_op jit(solution)/shard_map/ppermute | solution.py:677
  7.1 17.0 %collective-permute-start.2 = (f32[48,64]{1,0:T(8,128)S(1)}, f32[48,64]{1,0:T(8,128)S(1)}, u32[]{:S(2)}, u32[]{:S(2)}) collective-permute-start(f32[48,64]{1,0:T(8,128)S(1)} %get-tuple-element.55), channel_id=1, source_target_pairs={{0,1},{1,2},{2,3},{4,5},{5,6},{6,7},{8,9},{9,10},{10,11},{12,13},{... | collective-permute-start | bytes 36872 | tf_op jit(solution)/shard_map/ppermute | solution.py:678
  11.5 12.7 %collective-permute-start.3 = (f32[48,64]{1,0:T(8,128)S(1)}, f32[48,64]{1,0:T(8,128)S(1)}, u32[]{:S(2)}, u32[]{:S(2)}) collective-permute-start(f32[48,64]{1,0:T(8,128)S(1)} %get-tuple-element.54), channel_id=1, source_target_pairs={{1,0},{2,1},{3,2},{5,4},{6,5},{7,6},{9,8},{10,9},{11,10},{13,12},{... | collective-permute-start | bytes 36872 | tf_op jit(solution)/shard_map/ppermute | solution.py:679
  24.1 58.4 %copy-start = (f32[3,4,128]{2,1,0:T(4,128)}, f32[3,4,128]{2,1,0:T(4,128)S(1)}, u32[]{:S(2)}) copy-start(f32[3,4,128]{2,1,0:T(4,128)S(1)} %get-tuple-element.28.prm) | copy-start | bytes 18436
  24.1 10.9 %copy-start.1 = (f32[1,12480]{1,0:T(1,128)}, f32[1,12480]{1,0:T(1,128)S(1)}, u32[]{:S(2)}) copy-start(f32[1,12480]{1,0:T(1,128)S(1)} %collective-permute-done.north) | copy-start | bytes 149764
  24.2 10.9 %copy-start.2 = (f32[1,12480]{1,0:T(1,128)}, f32[1,12480]{1,0:T(1,128)S(1)}, u32[]{:S(2)}) copy-start(f32[1,12480]{1,0:T(1,128)S(1)} %collective-permute-done.1.south) | copy-start | bytes 149764
  35.0 21.2 %copy-start.3 = (s32[192]{0:T(256)S(1)}, s32[192]{0:T(256)}, u32[]{:S(2)}) copy-start(s32[192]{0:T(256)} %param.15) | copy-start | bytes 2308
  35.1 16.7 %all-to-all-start = ((f32[8,3,48,128]{3,2,1,0:T(8,128)}), f32[8,3,48,128]{3,2,1,0:T(8,128)S(1)}, u32[]{:S(2)}, u32[]{:S(2)}) async-start(f32[8,3,48,128]{3,2,1,0:T(8,128)} %get-tuple-element.33), calls=%async_computation | async-start | bytes 1179648 | tf_op jit(solution)/shard_map/all_to_all | solution.py:739
  52.8 17.3 %all-to-all-start.1 = ((f32[8,3,48,128]{3,2,1,0:T(8,128)}), f32[8,3,48,128]{3,2,1,0:T(8,128)S(1)}, u32[]{:S(2)}, u32[]{:S(2)}) async-start(f32[8,3,48,128]{3,2,1,0:T(8,128)} %solve.1), calls=%async_computation.1 | async-start | bytes 1179648 | tf_op jit(solution)/shard_map/all_to_all | solution.py:739
  56.5 20.3 %collective-permute-start.4 = (f32[6,48,128]{2,1,0:T(8,128)S(1)}, f32[6,48,128]{2,1,0:T(8,128)S(1)}, u32[]{:S(2)}, u32[]{:S(2)}) collective-permute-start(f32[6,48,128]{2,1,0:T(8,128)S(1)} %get-tuple-element.35.rest_0_), channel_id=1, source_target_pairs={{0,1},{1,0},{2,3},{3,2},{4,5},{5,4},{6,7},{7,6},{8,9},{9,8},{10,11... | collective-permute-start | bytes 442376 | tf_op jit(solution)/shard_map/ppermute | solution.py:774
  59.2 17.7 %collective-permute-start.5 = (f32[6,48,128]{2,1,0:T(8,128)S(1)}, f32[6,48,128]{2,1,0:T(8,128)S(1)}, u32[]{:S(2)}, u32[]{:S(2)}) collective-permute-start(f32[6,48,128]{2,1,0:T(8,128)S(1)} %get-tuple-element.35.rest_0_), channel_id=1, source_target_pairs={{0,2},{1,3},{2,0},{3,1},{4,6},{5,7},{6,4},{7,5},{8,10},{9,11},{10,... | collective-permute-start | bytes 442376 | tf_op jit(solution)/shard_map/ppermute | solution.py:774
  61.8 15.1 %collective-permute-start.6 = (f32[6,48,128]{2,1,0:T(8,128)S(1)}, f32[6,48,128]{2,1,0:T(8,128)S(1)}, u32[]{:S(2)}, u32[]{:S(2)}) collective-permute-start(f32[6,48,128]{2,1,0:T(8,128)S(1)} %get-tuple-element.35.rest_0_), channel_id=1, source_target_pairs={{0,3},{1,2},{2,1},{3,0},{4,7},{5,6},{6,5},{7,4},{8,11},{9,10},{10,... | collective-permute-start | bytes 442376 | tf_op jit(solution)/shard_map/ppermute | solution.py:774
  72.4 4.5 %collective-permute-start.7 = (f32[7,8,128]{2,1,0:T(8,128)S(1)}, f32[7,8,128]{2,1,0:T(8,128)S(1)}, u32[]{:S(2)}, u32[]{:S(2)}) collective-permute-start(f32[7,8,128]{2,1,0:T(8,128)S(1)} %get-tuple-element.48.rest_4_), channel_id=1, source_target_pairs={{0,1},{1,0},{2,3},{3,2},{4,5},{5,4},{6,7},{7,6},{8,9},{9,8},{10,11... | collective-permute-start | bytes 86024 | tf_op jit(solution)/shard_map/ppermute | solution.py:774
  73.3 5.8 %collective-permute-start.8 = (f32[7,8,128]{2,1,0:T(8,128)S(1)}, f32[7,8,128]{2,1,0:T(8,128)S(1)}, u32[]{:S(2)}, u32[]{:S(2)}) collective-permute-start(f32[7,8,128]{2,1,0:T(8,128)S(1)} %get-tuple-element.48.rest_4_), channel_id=1, source_target_pairs={{0,2},{1,3},{2,0},{3,1},{4,6},{5,7},{6,4},{7,5},{8,10},{9,11},{10,... | collective-permute-start | bytes 86024 | tf_op jit(solution)/shard_map/ppermute | solution.py:774
  76.8 5.7 %collective-permute-start.9 = (f32[7,8,128]{2,1,0:T(8,128)S(1)}, f32[7,8,128]{2,1,0:T(8,128)S(1)}, u32[]{:S(2)}, u32[]{:S(2)}) collective-permute-start(f32[7,8,128]{2,1,0:T(8,128)S(1)} %get-tuple-element.48.rest_4_), channel_id=1, source_target_pairs={{0,3},{1,2},{2,1},{3,0},{4,7},{5,6},{6,5},{7,4},{8,11},{9,10},{10,... | collective-permute-start | bytes 86024 | tf_op jit(solution)/shard_map/ppermute | solution.py:774
  87.1 18.8 %all-to-all-start.2 = ((f32[32,1,128]{2,1,0:T(1,128)}), f32[32,1,128]{2,1,0:T(1,128)S(1)}, u32[]{:S(2)}, u32[]{:S(2)}) async-start(f32[32,1,128]{2,1,0:T(1,128)} %bitcast.13), calls=%async_computation.2 | async-start | bytes 32768 | tf_op jit(solution)/shard_map/all_to_all | solution.py:739

commit v14 on v13

--- a/solution.py
+++ b/solution.py
@@ -399,7 +399,7 @@
         px_ref[...] = jnp.zeros_like(px_ref)
         dot_ref[...] = jnp.zeros_like(dot_ref)
 
-    for k in range(len(ORDER)):
+    for k in range(w_ref.shape[0]):
         rx = [rx_ref[k, e, pl.ds(pl.multiple_of(g * count, 8), count), :] for e in range(4)]
         for q in range(0, rows, rq):
             sums = [px_ref[k, e, q : q + rq, :] for e in range(4)] + [jnp.zeros((rq, LANES), f32)]
@@ -450,7 +450,7 @@
 
 
 def close_kernel(
-    n_lon, rows, devices, capacity, cells, place, target, prm, x_ref, proj, px, dots, rx, ry, el, elc, *rest
+    n_lon, rows, devices, capacity, cells, place, target, prm, x_ref, proj, px, dots, px0, dots0, rx, ry, el, elc, *rest
 ):
     sent, sent_x = rest[:n_lon], rest[n_lon : 2 * n_lon]
     carry, full_ref, col_ref, side_ref, table, esm, esx = rest[2 * n_lon :]
@@ -496,7 +496,7 @@
         sums = jnp.zeros((rows, LANES), f32)
         for e, c in enumerate((c1, c2, c3, c4)):
             carry[k, e] = c[k, :rows]
-            sums = sums + c[k, :rows] * px[k, e]
+            sums = sums + c[k, :rows] * (px[k, e] if k < 2 else px0[0, e])
 
         def body(b, total, k=k, more=more):
             base = pl.multiple_of(b * 8, 8)
@@ -509,7 +509,7 @@
                 total = total + x * proj[k, base + o]
             return total
 
-        total = lax.fori_loop(0, half // 8, body, dots[k])
+        total = lax.fori_loop(0, half // 8, body, dots[k] if k < 2 else dots0[0])
         total = total + jnp.sum(sums.reshape(rows // 8, 8, LANES), axis=0)
         total = jnp.sum(total, axis=0, keepdims=True)
         total = (total + swap(total)) * prm[v, 3:4, :] * (1.0 / cells)
@@ -793,16 +793,28 @@
     def columns(r):
         return pl.BlockSpec((nvars, packed, r, LANES), lambda g: (0, g, 0, 0))
 
-    px, dots = pl.pallas_call(
-        functools.partial(energy_kernel, rows, 24),
-        grid=(half // packed,),
-        in_specs=[columns(rows), columns(rows), full(rx.shape)],
-        out_specs=[full((nvars, 4, rows, LANES)), full((nvars, 8, LANES))],
-        out_shape=[pltpu.HBM((nvars, 4, rows, LANES), f32), pltpu.HBM((nvars, 8, LANES), f32)],
-        compiler_params=params(),
-        cost_estimate=pl.CostEstimate(flops=20000000, bytes_accessed=6 * rows * merged * 4, transcendentals=0),
-        name="energy",
-    )(in_hbm(w), in_hbm(local), in_hbm(rx))
+    def energy_call(nv, first, table, name):
+        def block(r):
+            return pl.BlockSpec((nv, packed, r, LANES), lambda g: (first, g, 0, 0))
+
+        return pl.pallas_call(
+            functools.partial(energy_kernel, rows, 24),
+            grid=(half // packed,),
+            in_specs=[
+                block(rows),
+                block(rows),
+                pl.BlockSpec((nv, 4, half, LANES), lambda g: (first, 0, 0, 0)),
+            ],
+            out_specs=[full((nv, 4, rows, LANES)), full((nv, 8, LANES))],
+            out_shape=[pltpu.HBM((nv, 4, rows, LANES), f32), pltpu.HBM((nv, 8, LANES), f32)],
+            compiler_params=params(),
+            cost_estimate=pl.CostEstimate(
+                flops=nv * 7000000, bytes_accessed=2 * nv * rows * merged * 4, transcendentals=0
+            ),
+            name=name,
+        )(in_hbm(w), in_hbm(local), in_hbm(table))
+
+    px, dots = energy_call(2, 0, rx, "energy_chi_temp")
     carries, _ = lax.optimization_barrier((carries, px))
 
     crossed, elc, esc = pl.pallas_call(
@@ -822,12 +834,14 @@
         name="lon_carry",
     )(prm, in_hbm(sigma), carries)
     sent_x = round_lon(esc)
+    table, _ = lax.optimization_barrier((rx, esc))
+    px0, dots0 = energy_call(1, 2, table, "energy_psi")
 
     index = jnp.arange(count, dtype=jnp.int32)
     same = (owner[:, None] == owner[None, :]) & (index[None, :] < index[:, None])
     target = (owner * capacity + jnp.sum(same.astype(jnp.int32), axis=1)).reshape(1, count)
 
-    ins = [in_hbm(x) for x in (proj, px, dots, rx, ry, el)]
+    ins = [in_hbm(x) for x in (proj, px, dots, px0, dots0, rx, ry, el)]
     ins = [place, target, prm, crossed] + ins + [elc] + sent + sent_x
     specs = [full(x.shape) for x in ins]
     specs[0] = pl.BlockSpec(memory_space=pltpu.SMEM)

time: 107 us -> 109 us (1.019)
  waiting for transfers between devices: 7.34 us -> 2.35 us
  Pallas kernels: 62.7 us -> 66.1 us
  starting transfers between devices: 32 us -> 34.6 us
    ppermute x6, waiting for transfers between devices: 5.57 us -> 0.68 us  [round_lon(): lax.ppermute(x, 'lon', [(i, i ^ s) for i in range(n_lon)])]
    pallas_call x1 -> x2, Pallas kernels: 8.2 us -> 11.5 us  [energy_call(): pl.pallas_call(functools.partial(energy_kernel, rows, 24), grid=(half //...]
    all_to_all x3, starting transfers between devices: 13 us -> 15.6 us  [trade(): return lax.all_to_all(x, axis, split_axis=0, concat_axis=0, tiled=True)]
  transfers between devices with their start and end apart: 13 -> 13, of which waited for: 3 -> 2; matrix products, arithmetic and copies ran while one was open for 1% -> 1% of each run, Pallas kernels for 43% -> 46%
where the time goes in v14:
time: 109 us; the launch traced here: 108 us
  Pallas kernels  66.1 us (61%)
  starting transfers between devices  34.6 us (32%)
  local copies, waits for them, and re-layouts  2.76 us (3%)
  waiting for transfers between devices  2.35 us (2%)
    pallas_call x2, Pallas kernels, lat_call(): pl.pallas_call(body, grid=(steps,), in_specs=specs, out_specs=[pl.BlockSp...  22.2 us
    all_to_all x3, starting transfers between devices, trade(): return lax.all_to_all(x, axis, split_axis=0, concat_axis=0, tiled=True)  15.6 us
    pallas_call x1, Pallas kernels, shards(): pl.pallas_call(functools.partial(end_kernel, rows, pairs, 24), grid=(half...  15.6 us
    pallas_call x2, Pallas kernels, energy_call(): pl.pallas_call(functools.partial(energy_kernel, rows, 24), grid=(half //...  11.5 us
    ppermute x6, starting transfers between devices, round_lon(): lax.ppermute(x, 'lon', [(i, i ^ s) for i in range(n_lon)])  9.76 us
    pallas_call x1, Pallas kernels, shards(): pl.pallas_call(functools.partial(lon_kernel, rows, rb), grid=(rows // rb,...  8.79 us
    pallas_call x1, Pallas kernels, shards(): pl.pallas_call(functools.partial(close_kernel, n_lon, rows, devices, capa...  4.69 us
    ppermute x1, starting transfers between devices, shards(): west = lax.ppermute(state[2, :, merged - levels:], 'lon', up_lon)  4.3 us
  transfers between devices with their start and end apart: 13, of which 2 were waited for; matrix products, arithmetic and copies ran while one was open for 1% of the time, Pallas kernels for 46%

profile of v14, /device:TPU:0, one launch (start us, length us, event | category | flops | bytes accessed | tf_op | source)
XLA Modules:
  0.0 107.6 jit_solution(7248180219772195727)
XLA Ops:
  0.6 1.2 %slice_bitcast_fusion = (f32[1,12288]{1,0:T(1,128)S(1)}, f32[1,12288]{1,0:T(1,128)S(1)}) fusion(f32[3,48,12288]{2,1,0:T(8,128)} %thr.1), kind=kLoop, calls=%fused_computation.5 | loop fusion | bytes 196608 | tf_op jit(solution)/shard_map/squeeze | solution.py:674
  1.8 0.7 slice_bitcast_fusion.4
  2.6 2.4 %collective-permute-start = (f32[1,12480]{1,0:T(1,128)S(1)}, f32[1,12480]{1,0:T(1,128)S(1)}, u32[]{:S(2)}, u32[]{:S(2)}) collective-permute-start(f32[1,12480]{1,0:T(1,128)S(1)} %pad_maximum_fusion), channel_id=1, source_target_pairs={{0,4},{4,8},{8,12},{12,16},{16,20},{20,24},{24,28},{1,5},{5,9},{9,... | collective-permute-start | bytes 149768 | tf_op jit(solution)/shard_map/ppermute | solution.py:676
  5.0 1.3 %collective-permute-start.1 = (f32[1,12480]{1,0:T(1,128)S(1)}, f32[1,12480]{1,0:T(1,128)S(1)}, u32[]{:S(2)}, u32[]{:S(2)}) collective-permute-start(f32[1,12480]{1,0:T(1,128)S(1)} %pad_maximum_fusion.1), channel_id=1, source_target_pairs={{4,0},{8,4},{12,8},{16,12},{20,16},{24,20},{28,24},{5,1},{9,5},{13... | collective-permute-start | bytes 149768 | tf_op jit(solution)/shard_map/ppermute | solution.py:677
  6.3 0.8 slice_bitcast_fusion.2
  7.1 4.3 %collective-permute-start.2 = (f32[48,64]{1,0:T(8,128)S(1)}, f32[48,64]{1,0:T(8,128)S(1)}, u32[]{:S(2)}, u32[]{:S(2)}) collective-permute-start(f32[48,64]{1,0:T(8,128)S(1)} %get-tuple-element.61), channel_id=1, source_target_pairs={{0,1},{1,2},{2,3},{4,5},{5,6},{6,7},{8,9},{9,10},{10,11},{12,13},{... | collective-permute-start | bytes 36872 | tf_op jit(solution)/shard_map/ppermute | solution.py:678
  11.5 1.3 %collective-permute-start.3 = (f32[48,64]{1,0:T(8,128)S(1)}, f32[48,64]{1,0:T(8,128)S(1)}, u32[]{:S(2)}, u32[]{:S(2)}) collective-permute-start(f32[48,64]{1,0:T(8,128)S(1)} %get-tuple-element.60), channel_id=1, source_target_pairs={{1,0},{2,1},{3,2},{5,4},{6,5},{7,6},{9,8},{10,9},{11,10},{13,12},{... | collective-permute-start | bytes 36872 | tf_op jit(solution)/shard_map/ppermute | solution.py:679
  12.8 11.4 %lat_chi_temp.1 = (f32[3,96,48,128]{3,2,1,0:T(8,128)}, f32[3,48,96,128]{3,2,1,0:T(8,128)}, f32[8,3,48,128]{3,2,1,0:T(8,128)}, f32[3,96,8,128]{3,2,1,0:T(8,128)}, f32[3,4,128]{2,1,0:T(4,128)S(1)}) custom-call(f32[1,8]{1,0:T(1,128)} %bitcast.26, s32[1,192]{1,0:T(1,128)} %bitcast.24, f32[1,64]{1,0:T(1,128)} %bitcast.27, f32[3,48,192]{2,1,0:T(8,128)} %sigma.7, ...), custom_call_target="tpu_custom_call" | custom-call | flops 120000000 | bytes 14155776 | tf_op jit(solution)/shard_map/lat_chi_temp/pallas_call | solution.py:693
  24.1 0.0 copy-start
  24.1 0.0 collective-permute-done.2.west
  24.1 0.0 collective-permute-done.3.east
  24.1 0.0 collective-permute-done.north
  24.2 0.0 copy-start.1
  24.2 0.0 collective-permute-done.1.south
  24.2 0.0 copy-start.2
  24.2 10.9 %lat_psi.1 = (f32[3,96,48,128]{3,2,1,0:T(8,128)}, f32[3,48,96,128]{3,2,1,0:T(8,128)}, f32[8,3,48,128]{3,2,1,0:T(8,128)}, f32[3,96,8,128]{3,2,1,0:T(8,128)}) custom-call(f32[3,4,128]{2,1,0:T(4,128)S(1)} %get-tuple-element.31.prm, f32[3,48,192]{2,1,0:T(8,128)} %sigma.7, ...), custom_call_target="tpu_custom_call", output_to_operand_aliasing={{0}: (18, {}), {1}: (19, {}), {2}: (20, {}), {3}: (21, {})} | custom-call | flops 60000000 | bytes 7077888 | tf_op jit(solution)/shard_map/lat_psi/pallas_call | solution.py:693
  35.1 0.0 copy-done.1
  35.1 0.0 copy-done.2
  35.1 0.0 copy-start.3
  35.1 6.3 %all-to-all-start = ((f32[8,3,48,128]{3,2,1,0:T(8,128)}), f32[8,3,48,128]{3,2,1,0:T(8,128)S(1)}, u32[]{:S(2)}, u32[]{:S(2)}) async-start(f32[8,3,48,128]{3,2,1,0:T(8,128)} %get-tuple-element.36), calls=%async_computation | async-start | bytes 1179648 | tf_op jit(solution)/shard_map/all_to_all | solution.py:739
  41.3 8.8 %lon_tile.1 = (f32[3,96,48,128]{3,2,1,0:T(8,128)}, f32[3,4,48,128]{3,2,1,0:T(8,128)}, f32[6,48,128]{2,1,0:T(8,128)S(1)}, f32[3,4,96,128]{3,2,1,0:T(8,128)}, f32[3,4,48,128]{3,2,1,0:T(8,128)}) custom-call(f32[3,4,128]{2,1,0:T(4,128)S(1)} %get-tuple-element.31.prm, f32[3,48,96,128]{3,2,1,0:T(8,128)} %get-tuple-element.37.u_ref), custom_call_target="tpu_custom_call" | custom-call | flops 180000000 | bytes 14155776 | tf_op jit(solution)/shard_map/lon_tile/pallas_call | solution.py:744
  50.1 1.7 %all-to-all-done.edges = f32[8,3,48,128]{3,2,1,0:T(8,128)S(1)} async-done(((f32[8,3,48,128]{3,2,1,0:T(8,128)}), f32[8,3,48,128]{3,2,1,0:T(8,128)S(1)}, u32[]{:S(2)}, u32[]{:S(2)}) %all-to-all-start) | async-done | bytes 589856 | tf_op jit(solution)/shard_map/all_to_all | solution.py:739
  51.8 1.0 solve.1
  52.8 3.5 %all-to-all-start.1 = ((f32[8,3,48,128]{3,2,1,0:T(8,128)}), f32[8,3,48,128]{3,2,1,0:T(8,128)S(1)}, u32[]{:S(2)}, u32[]{:S(2)}) async-start(f32[8,3,48,128]{3,2,1,0:T(8,128)} %solve.1), calls=%async_computation.1 | async-start | bytes 1179648 | tf_op jit(solution)/shard_map/all_to_all | solution.py:739
  56.3 0.0 copy-done.3
  56.3 0.2 convert_reduce_fusion
  56.5 2.7 %collective-permute-start.4 = (f32[6,48,128]{2,1,0:T(8,128)S(1)}, f32[6,48,128]{2,1,0:T(8,128)S(1)}, u32[]{:S(2)}, u32[]{:S(2)}) collective-permute-start(f32[6,48,128]{2,1,0:T(8,128)S(1)} %get-tuple-element.38.rest_0_), channel_id=1, source_target_pairs={{0,1},{1,0},{2,3},{3,2},{4,5},{5,4},{6,7},{7,6},{8,9},{9,8},{10,11... | collective-permute-start | bytes 442376 | tf_op jit(solution)/shard_map/ppermute | solution.py:774
  59.2 2.6 %collective-permute-start.5 = (f32[6,48,128]{2,1,0:T(8,128)S(1)}, f32[6,48,128]{2,1,0:T(8,128)S(1)}, u32[]{:S(2)}, u32[]{:S(2)}) collective-permute-start(f32[6,48,128]{2,1,0:T(8,128)S(1)} %get-tuple-element.38.rest_0_), channel_id=1, source_target_pairs={{0,2},{1,3},{2,0},{3,1},{4,6},{5,7},{6,4},{7,5},{8,10},{9,11},{10,... | collective-permute-start | bytes 442376 | tf_op jit(solution)/shard_map/ppermute | solution.py:774
  61.8 0.0 collective-permute-start.6
  61.8 6.6 %energy_chi_temp.1 = (f32[2,4,48,128]{3,2,1,0:T(8,128)}, f32[2,8,128]{2,1,0:T(8,128)}) custom-call(f32[3,96,48,128]{3,2,1,0:T(8,128)} %get-tuple-element.40.w_ref, f32[3,96,48,128]{3,2,1,0:T(8,128)} %get-tuple-element.41.u_ref, f32[3,4,96,128]{3,2,1,0:T(8,128)} %get-tuple-element.49.rx_ref.rx), custom_call_target="tpu_custom_call" | custom-call | flops 14000000 | bytes 9437184 | tf_op jit(solution)/shard_map/energy_chi_temp/pallas_call | solution.py:800
  68.4 0.0 all-to-all-done.1.carries
  68.4 2.4 %lon_carry.1 = (f32[3,96,8,128]{3,2,1,0:T(8,128)S(1)}, f32[3,4,8,128]{3,2,1,0:T(8,128)S(1)}, f32[7,8,128]{2,1,0:T(8,128)S(1)}) custom-call(f32[3,4,128]{2,1,0:T(4,128)S(1)} %get-tuple-element.31.prm, f32[3,48,192]{2,1,0:T(8,128)} %sigma.7, f32[8,3,48,128]{3,2,1,0:T(8,128)S(1)} %all-to-all-done.1.carries), custom_call_target="tpu_custom_call" | custom-call | flops 30000000 | bytes 1769472 | tf_op jit(solution)/shard_map/lon_carry/pallas_call | solution.py:820
  70.8 1.0 collective-permute-start.7
  71.8 3.4 %collective-permute-start.8 = (f32[7,8,128]{2,1,0:T(8,128)S(1)}, f32[7,8,128]{2,1,0:T(8,128)S(1)}, u32[]{:S(2)}, u32[]{:S(2)}) collective-permute-start(f32[7,8,128]{2,1,0:T(8,128)S(1)} %get-tuple-element.48.rest_4_), channel_id=1, source_target_pairs={{0,2},{1,3},{2,0},{3,1},{4,6},{5,7},{6,4},{7,5},{8,10},{9,11},{10,... | collective-permute-start | bytes 86024 | tf_op jit(solution)/shard_map/ppermute | solution.py:774
  75.2 0.0 collective-permute-done.4.rest_1_
  75.2 0.0 collective-permute-start.9
  75.3 0.1 pad_add_fusion.place
  75.3 4.9 %energy_psi.1 = (f32[1,4,48,128]{3,2,1,0:T(8,128)}, f32[1,8,128]{2,1,0:T(8,128)}) custom-call(f32[3,96,48,128]{3,2,1,0:T(8,128)} %get-tuple-element.40.w_ref, f32[3,96,48,128]{3,2,1,0:T(8,128)} %get-tuple-element.41.u_ref, f32[3,4,96,128]{3,2,1,0:T(8,128)} %get-tuple-element.49.rx_ref.rx), custom_call_target="tpu_custom_call" | custom-call | flops 7000000 | bytes 4718592 | tf_op jit(solution)/shard_map/energy_psi/pallas_call | solution.py:800
  80.2 0.0 collective-permute-done.5.rest_2_
  80.2 0.0 collective-permute-done.6.rest_3_
  80.2 0.0 collective-permute-done.7.rest_5_
  80.2 0.0 collective-permute-done.8.rest_6_
  80.2 0.7 collective-permute-done.9.rest_7_
  80.9 0.0 copy-done
  80.9 4.7 %close.1 = (f32[3,4,48,128]{3,2,1,0:T(8,128)}, f32[3,96,8,128]{3,2,1,0:T(8,128)}, f32[2,48,128]{2,1,0:T(8,128)}, f32[2,48,128]{2,1,0:T(8,128)}, f32[32,128]{1,0:T(8,128)}) custom-call(s32[2]{0:T(128)S(1)} %pad_add_fusion.place, s32[1,192]{1,0:T(1,128)S(1)} %bitcast.23, f32[3,4,128]{2,1,0:T(4,128)S(1)} %get-tuple-element.31.prm, ...), custom_call_target="tpu_custom_call" | custom-call | flops 10000000 | bytes 4000000 | tf_op jit(solution)/shard_map/close/pallas_call | solution.py:849
  85.6 5.8 %all-to-all-start.2 = ((f32[32,1,128]{2,1,0:T(1,128)}), f32[32,1,128]{2,1,0:T(1,128)S(1)}, u32[]{:S(2)}, u32[]{:S(2)}) async-start(f32[32,1,128]{2,1,0:T(1,128)} %bitcast.13), calls=%async_computation.2 | async-start | bytes 32768 | tf_op jit(solution)/shard_map/all_to_all | solution.py:739
  91.4 15.6 %finish.1 = f32[3,48,12288]{2,1,0:T(8,128)} custom-call(s32[2]{0:T(128)S(1)} %pad_add_fusion.place, f32[3,4,128]{2,1,0:T(4,128)} %copy-done, f32[3,48,192]{2,1,0:T(8,128)} %sigma.7, f32[1,12480]{1,0:T(1,128)} %copy-done.1, f32[1,12480]{1,0:T(1,128)} %copy-done.2, f32[3,64,64]{2,1,0:T(8,128)} %vert.5, f32[64,64]{1,0:T(8,128)} %bal.3, ...), custom_call_target="tpu_custom_call" | custom-call | flops 300000000 | bytes 14155776 | tf_op jit(solution)/shard_map/finish/pallas_call | solution.py:868
  107.0 0.0 all-to-all-done.2
  107.0 0.6 reduce_sum.19
  (3 shorter events, 0.1 us)
Async XLA Ops:
  2.6 21.6 %collective-permute-start = (f32[1,12480]{1,0:T(1,128)S(1)}, f32[1,12480]{1,0:T(1,128)S(1)}, u32[]{:S(2)}, u32[]{:S(2)}) collective-permute-start(f32[1,12480]{1,0:T(1,128)S(1)} %pad_maximum_fusion), channel_id=1, source_target_pairs={{0,4},{4,8},{8,12},{12,16},{16,20},{20,24},{24,28},{1,5},{5,9},{9,... | collective-permute-start | bytes 149768 | tf_op jit(solution)/shard_map/ppermute | solution.py:676
  5.0 19.2 %collective-permute-start.1 = (f32[1,12480]{1,0:T(1,128)S(1)}, f32[1,12480]{1,0:T(1,128)S(1)}, u32[]{:S(2)}, u32[]{:S(2)}) collective-permute-start(f32[1,12480]{1,0:T(1,128)S(1)} %pad_maximum_fusion.1), channel_id=1, source_target_pairs={{4,0},{8,4},{12,8},{16,12},{20,16},{24,20},{28,24},{5,1},{9,5},{13... | collective-permute-start | bytes 149768 | tf_op jit(solution)/shard_map/ppermute | solution.py:677
  7.1 17.0 %collective-permute-start.2 = (f32[48,64]{1,0:T(8,128)S(1)}, f32[48,64]{1,0:T(8,128)S(1)}, u32[]{:S(2)}, u32[]{:S(2)}) collective-permute-start(f32[48,64]{1,0:T(8,128)S(1)} %get-tuple-element.61), channel_id=1, source_target_pairs={{0,1},{1,2},{2,3},{4,5},{5,6},{6,7},{8,9},{9,10},{10,11},{12,13},{... | collective-permute-start | bytes 36872 | tf_op jit(solution)/shard_map/ppermute | solution.py:678
  11.5 12.7 %collective-permute-start.3 = (f32[48,64]{1,0:T(8,128)S(1)}, f32[48,64]{1,0:T(8,128)S(1)}, u32[]{:S(2)}, u32[]{:S(2)}) collective-permute-start(f32[48,64]{1,0:T(8,128)S(1)} %get-tuple-element.60), channel_id=1, source_target_pairs={{1,0},{2,1},{3,2},{5,4},{6,5},{7,6},{9,8},{10,9},{11,10},{13,12},{... | collective-permute-start | bytes 36872 | tf_op jit(solution)/shard_map/ppermute | solution.py:679
  24.1 56.8 %copy-start = (f32[3,4,128]{2,1,0:T(4,128)}, f32[3,4,128]{2,1,0:T(4,128)S(1)}, u32[]{:S(2)}) copy-start(f32[3,4,128]{2,1,0:T(4,128)S(1)} %get-tuple-element.31.prm) | copy-start | bytes 18436
  24.2 10.9 %copy-start.1 = (f32[1,12480]{1,0:T(1,128)}, f32[1,12480]{1,0:T(1,128)S(1)}, u32[]{:S(2)}) copy-start(f32[1,12480]{1,0:T(1,128)S(1)} %collective-permute-done.north) | copy-start | bytes 149764
  24.2 10.9 %copy-start.2 = (f32[1,12480]{1,0:T(1,128)}, f32[1,12480]{1,0:T(1,128)S(1)}, u32[]{:S(2)}) copy-start(f32[1,12480]{1,0:T(1,128)S(1)} %collective-permute-done.1.south) | copy-start | bytes 149764
  35.1 21.2 %copy-start.3 = (s32[192]{0:T(256)S(1)}, s32[192]{0:T(256)}, u32[]{:S(2)}) copy-start(s32[192]{0:T(256)} %param.15) | copy-start | bytes 2308
  35.1 16.7 %all-to-all-start = ((f32[8,3,48,128]{3,2,1,0:T(8,128)}), f32[8,3,48,128]{3,2,1,0:T(8,128)S(1)}, u32[]{:S(2)}, u32[]{:S(2)}) async-start(f32[8,3,48,128]{3,2,1,0:T(8,128)} %get-tuple-element.36), calls=%async_computation | async-start | bytes 1179648 | tf_op jit(solution)/shard_map/all_to_all | solution.py:739
  52.8 15.6 %all-to-all-start.1 = ((f32[8,3,48,128]{3,2,1,0:T(8,128)}), f32[8,3,48,128]{3,2,1,0:T(8,128)S(1)}, u32[]{:S(2)}, u32[]{:S(2)}) async-start(f32[8,3,48,128]{3,2,1,0:T(8,128)} %solve.1), calls=%async_computation.1 | async-start | bytes 1179648 | tf_op jit(solution)/shard_map/all_to_all | solution.py:739
  56.5 18.7 %collective-permute-start.4 = (f32[6,48,128]{2,1,0:T(8,128)S(1)}, f32[6,48,128]{2,1,0:T(8,128)S(1)}, u32[]{:S(2)}, u32[]{:S(2)}) collective-permute-start(f32[6,48,128]{2,1,0:T(8,128)S(1)} %get-tuple-element.38.rest_0_), channel_id=1, source_target_pairs={{0,1},{1,0},{2,3},{3,2},{4,5},{5,4},{6,7},{7,6},{8,9},{9,8},{10,11... | collective-permute-start | bytes 442376 | tf_op jit(solution)/shard_map/ppermute | solution.py:774
  59.2 21.0 %collective-permute-start.5 = (f32[6,48,128]{2,1,0:T(8,128)S(1)}, f32[6,48,128]{2,1,0:T(8,128)S(1)}, u32[]{:S(2)}, u32[]{:S(2)}) collective-permute-start(f32[6,48,128]{2,1,0:T(8,128)S(1)} %get-tuple-element.38.rest_0_), channel_id=1, source_target_pairs={{0,2},{1,3},{2,0},{3,1},{4,6},{5,7},{6,4},{7,5},{8,10},{9,11},{10,... | collective-permute-start | bytes 442376 | tf_op jit(solution)/shard_map/ppermute | solution.py:774
  61.8 18.4 %collective-permute-start.6 = (f32[6,48,128]{2,1,0:T(8,128)S(1)}, f32[6,48,128]{2,1,0:T(8,128)S(1)}, u32[]{:S(2)}, u32[]{:S(2)}) collective-permute-start(f32[6,48,128]{2,1,0:T(8,128)S(1)} %get-tuple-element.38.rest_0_), channel_id=1, source_target_pairs={{0,3},{1,2},{2,1},{3,0},{4,7},{5,6},{6,5},{7,4},{8,11},{9,10},{10,... | collective-permute-start | bytes 442376 | tf_op jit(solution)/shard_map/ppermute | solution.py:774
  70.8 9.4 %collective-permute-start.7 = (f32[7,8,128]{2,1,0:T(8,128)S(1)}, f32[7,8,128]{2,1,0:T(8,128)S(1)}, u32[]{:S(2)}, u32[]{:S(2)}) collective-permute-start(f32[7,8,128]{2,1,0:T(8,128)S(1)} %get-tuple-element.48.rest_4_), channel_id=1, source_target_pairs={{0,1},{1,0},{2,3},{3,2},{4,5},{5,4},{6,7},{7,6},{8,9},{9,8},{10,11... | collective-permute-start | bytes 86024 | tf_op jit(solution)/shard_map/ppermute | solution.py:774
  71.8 8.4 %collective-permute-start.8 = (f32[7,8,128]{2,1,0:T(8,128)S(1)}, f32[7,8,128]{2,1,0:T(8,128)S(1)}, u32[]{:S(2)}, u32[]{:S(2)}) collective-permute-start(f32[7,8,128]{2,1,0:T(8,128)S(1)} %get-tuple-element.48.rest_4_), channel_id=1, source_target_pairs={{0,2},{1,3},{2,0},{3,1},{4,6},{5,7},{6,4},{7,5},{8,10},{9,11},{10,... | collective-permute-start | bytes 86024 | tf_op jit(solution)/shard_map/ppermute | solution.py:774
  75.2 5.7 %collective-permute-start.9 = (f32[7,8,128]{2,1,0:T(8,128)S(1)}, f32[7,8,128]{2,1,0:T(8,128)S(1)}, u32[]{:S(2)}, u32[]{:S(2)}) collective-permute-start(f32[7,8,128]{2,1,0:T(8,128)S(1)} %get-tuple-element.48.rest_4_), channel_id=1, source_target_pairs={{0,3},{1,2},{2,1},{3,0},{4,7},{5,6},{6,5},{7,4},{8,11},{9,10},{10,... | collective-permute-start | bytes 86024 | tf_op jit(solution)/shard_map/ppermute | solution.py:774
  85.6 21.4 %all-to-all-start.2 = ((f32[32,1,128]{2,1,0:T(1,128)}), f32[32,1,128]{2,1,0:T(1,128)S(1)}, u32[]{:S(2)}, u32[]{:S(2)}) async-start(f32[32,1,128]{2,1,0:T(1,128)} %bitcast.13), calls=%async_computation.2 | async-start | bytes 32768 | tf_op jit(solution)/shard_map/all_to_all | solution.py:739
